TPU v7x, 32 devices: a whole 2x2x4 slice. The times are simulated.
32 devices in a mesh: dp: 8 (over y, x, core), tensor: 4 (over z).
Axes of the slice: x: 2, y: 2, z: 4, core: 2. Of those that a mesh axis runs over, the one named last changes fastest.
Arguments:
- inputs: bfloat16 [8, 1024, 1536], P('dp', 'tensor'), may hold values from -6 to 6
- context: bfloat16 [8, 130, 1536], P('dp', None, 'tensor'), may hold values from -6 to 6
- positions: int32 [8, 1024], P('dp'), may hold values from 0 to 3069, as said below
- adapter_index: int32 [8], P('dp'), may hold values from 0 to 7
- self_in_weight: bfloat16 [1536, 3, 1536], P('dp', None, 'tensor'), may hold values from -0.15625 to 0.15625
- self_out_weight: bfloat16 [1536, 1536], P('tensor', 'dp'), may hold values from -3 to 3
- cross_query_weight: bfloat16 [1536, 1536], P('dp', 'tensor'), may hold values from -0.15625 to 0.15625
- cross_keyval_weight: bfloat16 [1536, 2, 1536], P('dp', None, 'tensor'), may hold values from -0.15625 to 0.15625
- cross_out_weight: bfloat16 [1536, 1536], P('tensor', 'dp'), may hold values from -1 to 1
- feed_in_weight: bfloat16 [1536, 2, 6144], P('dp', None, 'tensor'), may hold values from -0.15625 to 0.15625
- feed_out_weight: bfloat16 [6144, 1536], P('tensor', 'dp'), may hold values from -0.078125 to 0.078125
- norm_gains: float32 [3, 1536], replicated, may hold values from 0.25 to 1.75
- norm_biases: float32 [3, 1536], replicated, may hold values from -1.75 to 1.75
- adapter_down: bfloat16 [8, 6, 1536, 16], replicated, may hold values from -0.15625 to 0.15625
- adapter_down_hidden: bfloat16 [8, 6144, 16], replicated, may hold values from -0.078125 to 0.078125
- adapter_up: bfloat16 [8, 16, 9, 1536], replicated, may hold values from -1.5 to 1.5
- adapter_up_hidden: bfloat16 [8, 16, 2, 6144], replicated, may hold values from -1.5 to 1.5
- out_cotangent: bfloat16 [8, 1024, 1536], P('dp', 'tensor'), may hold values from -6 to 6
Outputs:
- block_output: bfloat16 [8, 1024, 1536], P('dp', 'tensor')
- grad_inputs: float32 [8, 1024, 1536], P('dp', 'tensor')
- grad_context: float32 [8, 130, 1536], P('dp', None, 'tensor')
- grad_adapter_down: float32 [8, 6, 1536, 16], P(None, None, 'tensor')
- grad_adapter_down_hidden: float32 [8, 6144, 16], P(None, 'tensor')
- grad_adapter_up: float32 [8, 16, 9, 1536], P(None, None, None, 'tensor')
- grad_adapter_up_hidden: float32 [8, 16, 2, 6144], P(None, None, None, 'tensor')
Inputs may be any that keep to these rules, and one draw needn't show every extreme that they name: Within each sequence the positions start at 0 and rise by 1 to 3 from one token to the next.
All inputs are finite; a program needn't handle non-finite values.
Results may differ from a plain program's by a relative error of at most 0.03.
Values may be sent and summed in bfloat16 or wider, within the bound.
No kernel may reach another device: no remote copies, remote signals or barrier semaphores. Data moves between devices by JAX's collectives and lax.ppermute only.
A program may use at most 256 MiB of HBM per device.

v0:
```python
import jax
import jax.numpy as jnp
from jax import lax
from jax.sharding import PartitionSpec as P

HEAD_DIM = 64
ROT = 32


EPSILON = 1e-05
HIGHEST = lax.Precision.HIGHEST
FLOAT_KIND = jnp.float32
BFLOAT = jnp.bfloat16


def layer_norm(stream, norm_gain, norm_bias):
    average = jnp.mean(stream, axis=-1, keepdims=True)
    centred = stream - average
    variance = jnp.mean(centred * centred, axis=-1, keepdims=True)
    return centred * lax.rsqrt(variance + EPSILON) * norm_gain + norm_bias


def norm_backward(stream, norm_gain, norm_bias, grad_normed):

    def normalize(values):
        return layer_norm(values, norm_gain, norm_bias)

    outcome, pullback = jax.vjp(normalize, stream)
    return pullback(grad_normed)[0]


def gate_backward(gate_part, up_part, grad_hidden):

    def gated(gate_in, up_in):
        return jax.nn.silu(gate_in) * up_in

    outcome, pullback = jax.vjp(gated, gate_part, up_part)
    return pullback(grad_hidden)


def rotate(values, cosines, sines):
    half_rot = cosines.shape[-1]
    leading = values[..., :half_rot]
    second = values[..., half_rot : 2 * half_rot]
    return jnp.concatenate(
        [
            leading * cosines - second * sines,
            second * cosines + leading * sines,
            values[..., 2 * half_rot :],
        ],
        axis=-1,
    )


def select(onehot, lookup):
    return jnp.einsum("sa,a...->s...", onehot, lookup.astype(FLOAT_KIND))


def scatter_slots(onehot, per_sequence):
    return jnp.einsum("sa,s...->a...", onehot, per_sequence, precision=HIGHEST)


def own_part(source, along, breadth):
    return lax.dynamic_slice_in_dim(source, lax.axis_index("tensor") * breadth, breadth, along)


def unpack_weights(gathered):
    self_in = gathered[0].reshape(gathered[0].shape[0], -1)
    cross_keyval = gathered[3].reshape(gathered[3].shape[0], -1)
    feed_in = gathered[5].reshape(gathered[5].shape[0], -1)
    return (self_in, gathered[1], gathered[2], cross_keyval, gathered[4], feed_in, gathered[6])


def attend_forward(query, keys, values):
    sequences, row_count, head_count, breadth = query.shape
    block_rows = min(512, row_count)
    block_count = row_count // block_rows
    scaling = breadth ** (-0.5)
    query_blocks = query.reshape(sequences * block_count, block_rows, head_count, breadth)

    def forward_block(packed):
        number, query_block = packed
        keys_here = lax.dynamic_index_in_dim(keys, number // block_count, 0, keepdims=False)
        values_here = lax.dynamic_index_in_dim(values, number // block_count, 0, keepdims=False)
        scores = (
            jnp.einsum("qhe,khe->hqk", query_block, keys_here, preferred_element_type=FLOAT_KIND)
            * scaling
        )
        row_max = jnp.max(scores, axis=-1, keepdims=True)
        exponentials = jnp.exp(scores - row_max)
        denominator = jnp.sum(exponentials, axis=-1, keepdims=True)
        probabilities = (exponentials / denominator).astype(BFLOAT)
        result = jnp.einsum(
            "hqk,khe->qhe", probabilities, values_here, preferred_element_type=FLOAT_KIND
        )
        return (result.astype(BFLOAT), row_max + jnp.log(denominator))

    numbers = jnp.arange(sequences * block_count, dtype=jnp.int32)
    results, logsums = lax.map(forward_block, (numbers, query_blocks))
    return (results.reshape(sequences, row_count, head_count, breadth), logsums)


def attend_backward(query, keys, values, logsums, grad_out):
    sequences, row_count, head_count, breadth = query.shape
    key_count = keys.shape[1]
    block_rows = min(512, row_count)
    block_count = row_count // block_rows
    scaling = breadth ** (-0.5)
    query_blocks = query.reshape(sequences * block_count, block_rows, head_count, breadth)
    grad_blocks = grad_out.reshape(sequences * block_count, block_rows, head_count, breadth)

    def backward_block(packed):
        number, query_block, grad_block, logsum = packed
        keys_here = lax.dynamic_index_in_dim(keys, number // block_count, 0, keepdims=False)
        values_here = lax.dynamic_index_in_dim(values, number // block_count, 0, keepdims=False)
        scores = (
            jnp.einsum("qhe,khe->hqk", query_block, keys_here, preferred_element_type=FLOAT_KIND)
            * scaling
        )
        probabilities = jnp.exp(scores - logsum)
        grad_probs = jnp.einsum(
            "qhe,khe->hqk", grad_block, values_here, preferred_element_type=FLOAT_KIND
        )
        deltas = jnp.sum(probabilities * grad_probs, axis=-1, keepdims=True)
        grad_scores = (probabilities * (grad_probs - deltas)).astype(BFLOAT)
        grad_query = (
            jnp.einsum("hqk,khe->qhe", grad_scores, keys_here, preferred_element_type=FLOAT_KIND)
            * scaling
        )
        grad_keys = (
            jnp.einsum("hqk,qhe->khe", grad_scores, query_block, preferred_element_type=FLOAT_KIND)
            * scaling
        )
        grad_values = jnp.einsum(
            "hqk,qhe->khe",
            probabilities.astype(BFLOAT),
            grad_block,
            preferred_element_type=FLOAT_KIND,
        )
        return (grad_query, grad_keys, grad_values)

    numbers = jnp.arange(sequences * block_count, dtype=jnp.int32)
    grad_query, grad_keys, grad_values = lax.map(
        backward_block, (numbers, query_blocks, grad_blocks, logsums)
    )
    grad_query = grad_query.reshape(sequences, row_count, head_count, breadth)
    grad_keys = grad_keys.reshape(sequences, block_count, key_count, head_count, breadth).sum(
        axis=1
    )
    grad_values = grad_values.reshape(sequences, block_count, key_count, head_count, breadth).sum(
        axis=1
    )
    return (grad_query, grad_keys, grad_values)


def spread_rows(normed_own):
    return lax.all_gather(normed_own, "tensor", axis=1, tiled=True)


def return_rows(grad_partial):
    return lax.psum_scatter(grad_partial, "tensor", scatter_dimension=1, tiled=True)


def head_forward(normed_all, in_weight, down_full, up_part):
    lowrank = jnp.einsum(
        "snd,sdr->snr", normed_all, down_full, preferred_element_type=FLOAT_KIND
    ).astype(BFLOAT)
    mixed = jnp.einsum("snd,dk->snk", normed_all, in_weight, preferred_element_type=FLOAT_KIND)
    mixed = mixed + jnp.einsum("snr,srk->snk", lowrank, up_part, preferred_element_type=FLOAT_KIND)
    return (mixed, lowrank)


def head_backward(grad_mixed, normed_all, lowrank, in_weight, down_full, up_part):
    grad_lowrank = jnp.einsum(
        "snk,srk->snr", grad_mixed, up_part, preferred_element_type=FLOAT_KIND
    )
    grad_normed = jnp.einsum(
        "snk,dk->snd", grad_mixed, in_weight, preferred_element_type=FLOAT_KIND
    )
    grad_normed = grad_normed + jnp.einsum(
        "snr,sdr->snd", grad_lowrank, down_full.astype(FLOAT_KIND), precision=HIGHEST
    )
    up_weight_gradient = jnp.einsum(
        "snr,snk->srk", lowrank, grad_mixed, preferred_element_type=FLOAT_KIND
    )
    grad_down = jnp.einsum(
        "snd,snr->sdr", normed_all.astype(FLOAT_KIND), grad_lowrank, precision=HIGHEST
    )
    return (grad_normed, up_weight_gradient, grad_down)


def branch_tail(heads_every_token, down_rows, output_weight, up_weight_rows):
    partial_total_sum = jnp.einsum(
        "xvr,rb->xvb", heads_every_token, output_weight, preferred_element_type=FLOAT_KIND
    )
    lowrank = jnp.einsum(
        "snd,sdr->snr", heads_every_token, down_rows, preferred_element_type=FLOAT_KIND
    )
    reduced_sum, low_rank_local = (
        lax.psum_scatter(partial_total_sum, "tensor", scatter_dimension=1, tiled=True),
        lax.psum_scatter(lowrank, "tensor", scatter_dimension=1, tiled=True),
    )
    low_rank_local = low_rank_local.astype(BFLOAT)
    adapter_branch = reduced_sum + jnp.einsum(
        "ack,akw->acw", low_rank_local, up_weight_rows, preferred_element_type=FLOAT_KIND
    )
    return (adapter_branch, low_rank_local)


def tail_backward(
    grad_stream, heads_every_token, low_rank_local, down_rows, output_weight, up_weight_rows
):
    branch_gradient = grad_stream.astype(BFLOAT)
    grad_lowrank = jnp.einsum(
        "kpd,kvd->kpv", branch_gradient, up_weight_rows, preferred_element_type=FLOAT_KIND
    ).astype(BFLOAT)
    up_weight_gradient = jnp.einsum(
        "hfy,hfo->hyo", low_rank_local, branch_gradient, preferred_element_type=FLOAT_KIND
    )
    branch_every_token, lowrank_all = (
        lax.all_gather(branch_gradient, "tensor", axis=1, tiled=True),
        lax.all_gather(grad_lowrank, "tensor", axis=1, tiled=True),
    )
    heads_gradient = jnp.einsum(
        "ofm,cm->ofc", branch_every_token, output_weight, preferred_element_type=FLOAT_KIND
    )
    heads_gradient = heads_gradient + jnp.einsum(
        "snr,sdr->snd", lowrank_all, down_rows, preferred_element_type=FLOAT_KIND
    )
    grad_down = jnp.einsum(
        "snd,snr->sdr", heads_every_token, lowrank_all, preferred_element_type=FLOAT_KIND
    )
    return (heads_gradient, up_weight_gradient, grad_down)


def body(
    inputs,
    context,
    positions,
    adapter_index,
    self_in_weight,
    self_out_weight,
    cross_query_weight,
    cross_keyval_weight,
    cross_out_weight,
    feed_in_weight,
    feed_out_weight,
    norm_gains,
    norm_biases,
    adapter_down,
    adapter_down_hidden,
    adapter_up,
    adapter_up_hidden,
    out_cotangent,
):
    sequences = inputs.shape[0]
    local_width = self_in_weight.shape[2]
    local_hidden = feed_in_weight.shape[2]
    local_heads = local_width // HEAD_DIM
    rank_size = adapter_down.shape[3]
    onehot = (
        adapter_index[:, None] == jnp.arange(adapter_down.shape[0], dtype=jnp.int32)[None, :]
    ).astype(FLOAT_KIND)
    chosen_down = select(onehot, adapter_down).astype(BFLOAT)
    self_down = own_part(chosen_down[:, 1], 1, local_width)
    cross_down = own_part(chosen_down[:, 4], 1, local_width)
    feed_down = own_part(select(onehot, adapter_down_hidden), 1, local_hidden).astype(BFLOAT)
    up_full = select(onehot, adapter_up).astype(BFLOAT)
    up_columns = own_part(up_full, 3, local_width)
    self_up = up_columns[:, :, 0:3].reshape(sequences, rank_size, 3 * local_width)
    query_up = up_columns[:, :, 4]
    keyval_up = up_columns[:, :, 5:7].reshape(sequences, rank_size, 2 * local_width)
    feed_up = own_part(select(onehot, adapter_up_hidden), 3, local_hidden).astype(BFLOAT)
    feed_up = feed_up.reshape(sequences, rank_size, 2 * local_hidden)
    gathered = (
        lax.all_gather(self_in_weight, "dp", axis=0, tiled=True),
        lax.all_gather(self_out_weight, "dp", axis=1, tiled=True),
        lax.all_gather(cross_query_weight, "dp", axis=0, tiled=True),
        lax.all_gather(cross_keyval_weight, "dp", axis=0, tiled=True),
        lax.all_gather(cross_out_weight, "dp", axis=1, tiled=True),
        lax.all_gather(feed_in_weight, "dp", axis=0, tiled=True),
        lax.all_gather(feed_out_weight, "dp", axis=1, tiled=True),
    )
    self_in, self_out, cross_query, cross_keyval, cross_out, feed_in, feed_out = unpack_weights(
        gathered
    )
    half_rot = ROT // 2
    inverse = 10000.0 ** (-jnp.arange(half_rot, dtype=FLOAT_KIND) / half_rot)
    angles = positions.astype(FLOAT_KIND)[:, :, None, None] * inverse
    cosines = jnp.cos(angles)
    sines = jnp.sin(angles)
    stream_zero = inputs.astype(FLOAT_KIND)
    normed_one = spread_rows(layer_norm(stream_zero, norm_gains[0], norm_biases[0]).astype(BFLOAT))
    row_count = normed_one.shape[1]
    mixed, lowrank_one = head_forward(normed_one, self_in, chosen_down[:, 0], self_up)
    mixed = mixed.reshape(sequences, row_count, 3, local_heads, HEAD_DIM)
    query_self = rotate(mixed[:, :, 0], cosines, sines).astype(BFLOAT)
    keys_self = rotate(mixed[:, :, 1], cosines, sines).astype(BFLOAT)
    values_self = mixed[:, :, 2].astype(BFLOAT)
    heads_self, logsum_self = attend_forward(query_self, keys_self, values_self)
    heads_self = heads_self.reshape(sequences, row_count, local_width)
    adapter_branch, lowrank_two = branch_tail(heads_self, self_down, self_out, up_full[:, :, 3])
    stream_one = stream_zero + adapter_branch
    normed_two = spread_rows(layer_norm(stream_one, norm_gains[1], norm_biases[1]).astype(BFLOAT))
    query_mixed, lowrank_three = head_forward(normed_two, cross_query, chosen_down[:, 2], query_up)
    query_cross = query_mixed.astype(BFLOAT).reshape(sequences, row_count, local_heads, HEAD_DIM)
    context_all = lax.all_gather(context, "tensor", axis=2, tiled=True)
    context_count = context_all.shape[1]
    keyval_mixed, lowrank_context = head_forward(
        context_all, cross_keyval, chosen_down[:, 3], keyval_up
    )
    keyval = keyval_mixed.astype(BFLOAT).reshape(sequences, context_count, 2, local_heads, HEAD_DIM)
    keys_cross = keyval[:, :, 0]
    values_cross = keyval[:, :, 1]
    heads_cross, logsum_cross = attend_forward(query_cross, keys_cross, values_cross)
    heads_cross = heads_cross.reshape(sequences, row_count, local_width)
    adapter_branch, lowrank_four = branch_tail(heads_cross, cross_down, cross_out, up_full[:, :, 7])
    stream_two = stream_one + adapter_branch
    normed_three = spread_rows(layer_norm(stream_two, norm_gains[2], norm_biases[2]).astype(BFLOAT))
    gate_up, lowrank_five = head_forward(normed_three, feed_in, chosen_down[:, 5], feed_up)
    gate_up = gate_up.reshape(sequences, row_count, 2, local_hidden)
    hidden = (jax.nn.silu(gate_up[:, :, 0]) * gate_up[:, :, 1]).astype(BFLOAT)
    adapter_branch, lowrank_six = branch_tail(hidden, feed_down, feed_out, up_full[:, :, 8])
    stream_three = stream_two + adapter_branch
    block_output = stream_three.astype(BFLOAT)
    grad_stream = out_cotangent.astype(FLOAT_KIND)
    grad_hidden, grad_up_eight, grad_down_feed = tail_backward(
        grad_stream, hidden, lowrank_six, feed_down, feed_out, up_full[:, :, 8]
    )
    grad_gate, grad_upper = gate_backward(gate_up[:, :, 0], gate_up[:, :, 1], grad_hidden)
    grad_mixed = (
        jnp.stack([grad_gate, grad_upper], axis=2)
        .astype(BFLOAT)
        .reshape(sequences, row_count, 2 * local_hidden)
    )
    grad_normed, grad_up_feed, grad_down_five = head_backward(
        grad_mixed, normed_three, lowrank_five, feed_in, chosen_down[:, 5], feed_up
    )
    grad_stream = grad_stream + norm_backward(
        stream_two, norm_gains[2], norm_biases[2], return_rows(grad_normed)
    )
    heads_gradient, grad_up_seven, grad_down_four = tail_backward(
        grad_stream, heads_cross, lowrank_four, cross_down, cross_out, up_full[:, :, 7]
    )
    heads_gradient = heads_gradient.astype(BFLOAT).reshape(
        sequences, row_count, local_heads, HEAD_DIM
    )
    grad_query, grad_keys, grad_values = attend_backward(
        query_cross, keys_cross, values_cross, logsum_cross, heads_gradient
    )
    grad_query = grad_query.astype(BFLOAT).reshape(sequences, row_count, local_width)
    grad_keyval = (
        jnp.stack([grad_keys, grad_values], axis=2)
        .astype(BFLOAT)
        .reshape(sequences, context_count, 2 * local_width)
    )
    grad_normed, grad_up_four, grad_down_two = head_backward(
        grad_query, normed_two, lowrank_three, cross_query, chosen_down[:, 2], query_up
    )
    context_partial, grad_up_keyval, grad_down_three = head_backward(
        grad_keyval, context_all, lowrank_context, cross_keyval, chosen_down[:, 3], keyval_up
    )
    grad_context = lax.psum_scatter(
        context_partial.astype(jnp.bfloat16), "tensor", scatter_dimension=2, tiled=True
    ).astype(jnp.float32)
    grad_stream = grad_stream + norm_backward(
        stream_one, norm_gains[1], norm_biases[1], return_rows(grad_normed)
    )
    heads_gradient, grad_up_three, grad_down_one = tail_backward(
        grad_stream, heads_self, lowrank_two, self_down, self_out, up_full[:, :, 3]
    )
    heads_gradient = heads_gradient.astype(BFLOAT).reshape(
        sequences, row_count, local_heads, HEAD_DIM
    )
    grad_query, grad_keys, grad_values = attend_backward(
        query_self, keys_self, values_self, logsum_self, heads_gradient
    )
    grad_query = rotate(grad_query, cosines, -sines)
    grad_keys = rotate(grad_keys, cosines, -sines)
    grad_mixed = (
        jnp.stack([grad_query, grad_keys, grad_values], axis=2)
        .astype(BFLOAT)
        .reshape(sequences, row_count, 3 * local_width)
    )
    grad_normed, grad_up_self, grad_down_zero = head_backward(
        grad_mixed, normed_one, lowrank_one, self_in, chosen_down[:, 0], self_up
    )
    grad_inputs = grad_stream + norm_backward(
        stream_zero, norm_gains[0], norm_biases[0], return_rows(grad_normed)
    )
    partial_down = jnp.stack(
        [grad_down_zero, grad_down_two, grad_down_three, grad_down_five], axis=1
    )
    partial_up = jnp.stack([grad_up_three, grad_up_seven, grad_up_eight], axis=2)
    down_own, up_own = (
        lax.psum_scatter(
            partial_down.astype(jnp.bfloat16), "tensor", scatter_dimension=2, tiled=True
        ).astype(jnp.float32),
        lax.psum_scatter(
            partial_up.astype(jnp.bfloat16), "tensor", scatter_dimension=3, tiled=True
        ).astype(jnp.float32),
    )
    per_down = jnp.stack(
        [
            down_own[:, 0],
            grad_down_one,
            down_own[:, 1],
            down_own[:, 2],
            grad_down_four,
            down_own[:, 3],
        ],
        axis=1,
    )
    per_up = jnp.concatenate(
        [
            grad_up_self.reshape(sequences, rank_size, 3, local_width),
            up_own[:, :, 0:1],
            grad_up_four[:, :, None],
            grad_up_keyval.reshape(sequences, rank_size, 2, local_width),
            up_own[:, :, 1:3],
        ],
        axis=2,
    )
    per_up_hidden = grad_up_feed.reshape(sequences, rank_size, 2, local_hidden)
    grad_adapter_down, grad_adapter_down_hidden, grad_adapter_up, grad_adapter_up_hidden = (
        lax.psum(scatter_slots(onehot, per_down).astype(jnp.bfloat16), "dp").astype(jnp.float32),
        lax.psum(scatter_slots(onehot, grad_down_feed).astype(jnp.bfloat16), "dp").astype(
            jnp.float32
        ),
        lax.psum(scatter_slots(onehot, per_up).astype(jnp.bfloat16), "dp").astype(jnp.float32),
        lax.psum(scatter_slots(onehot, per_up_hidden).astype(jnp.bfloat16), "dp").astype(
            jnp.float32
        ),
    )
    return (
        block_output,
        grad_inputs,
        grad_context,
        grad_adapter_down,
        grad_adapter_down_hidden,
        grad_adapter_up,
        grad_adapter_up_hidden,
    )


def solution(mesh):
    in_specs = (
        P("dp", "tensor", None),
        P("dp", None, "tensor"),
        P("dp", None),
        P("dp"),
        P("dp", None, "tensor"),
        P("tensor", "dp"),
        P("dp", "tensor"),
        P("dp", None, "tensor"),
        P("tensor", "dp"),
        P("dp", None, "tensor"),
        P("tensor", "dp"),
        P(),
        P(),
        P(),
        P(),
        P(),
        P(),
        P("dp", "tensor", None),
    )
    out_specs = (
        P("dp", "tensor", None),
        P("dp", "tensor", None),
        P("dp", None, "tensor"),
        P(None, None, "tensor", None),
        P(None, "tensor", None),
        P(None, None, None, "tensor"),
        P(None, None, None, "tensor"),
    )
    return jax.shard_map(body, mesh=mesh, in_specs=in_specs, out_specs=out_specs, check_vma=False)
```

profile of v0, /device:TPU:0, one launch (start us, length us, event | category | flops | bytes accessed | tf_op | source)
XLA Modules:
  0.0 1804.4 jit_solution(6207867989564632781)
XLA Ops:
  31.3 50.5 %all-gather.17.cloned.1.call-done = bf16[1,1024,1536]{2,1,0:T(8,128)(2,1)} async-done(((bf16[1,256,1536]{2,1,0:T(8,128)(2,1)}), bf16[1,1024,1536]{2,1,0:T(8,128)(2,1)}) %all-gather.17.cloned.1.call-update) | async-done | bytes 3145744 | tf_op jit(solution)/shard_map/all_gather | solution.py:157
  84.6 31.7 %all-gather.19.cloned.1.call-done = bf16[1536,3,384]{2,0,1:T(8,128)(2,1)} async-done(((bf16[192,3,384]{2,0,1:T(8,128)(2,1)}), bf16[1536,3,384]{2,0,1:T(8,128)(2,1)}) %all-gather.19.cloned.1.call-update) | async-done | bytes 3538960 | tf_op jit(solution)/shard_map/all_gather | solution.py:276
  145.8 16.8 while.56
  184.4 111.2 %reduce-scatter.19.cloned.1.call-done = f32[1,256,1536]{2,1,0:T(8,128)} async-done(((f32[1,1024,1536]{2,1,0:T(8,128)}), f32[1,256,1536]{2,1,0:T(8,128)}) %reduce-scatter.19.cloned.1.call-update) | async-done | bytes 1572880 | tf_op jit(solution)/shard_map/reduce_scatter | solution.py:200
  300.7 15.1 all_gather.56
  333.1 59.7 %all-gather.23.cloned.1.call-done = bf16[1,1024,1536]{2,1,0:T(8,128)(2,1)} async-done(((bf16[1,256,1536]{2,1,0:T(8,128)(2,1)}), bf16[1,1024,1536]{2,1,0:T(8,128)(2,1)}) %all-gather.23.cloned.1.call-update) | async-done | bytes 3145744 | tf_op jit(solution)/shard_map/all_gather | solution.py:157
  395.8 21.8 %all-gather.25.cloned.1.call-done = bf16[1536,384]{1,0:T(8,128)(2,1)} async-done(((bf16[192,384]{1,0:T(8,128)(2,1)}), bf16[1536,384]{1,0:T(8,128)(2,1)}) %all-gather.25.cloned.1.call-update) | async-done | bytes 1179664 | tf_op jit(solution)/shard_map/all_gather | solution.py:278
  465.5 111.3 %reduce-scatter.23.cloned.1.call-done = f32[1,256,1536]{2,1,0:T(8,128)} async-done(((f32[1,1024,1536]{2,1,0:T(8,128)}), f32[1,256,1536]{2,1,0:T(8,128)}) %reduce-scatter.23.cloned.1.call-update) | async-done | bytes 1572880 | tf_op jit(solution)/shard_map/reduce_scatter | solution.py:200
  602.8 19.0 %copy.198 = bf16[1,6144,16]{1,2,0:T(8,128)(2,1)S(1)} copy(bf16[1,6144,16]{0,1,2:T(8,128)(2,1)} %fusion.157) | data formatting | bytes 393216 | tf_op jit(solution)/shard_map/sa,a...->s.../dot_general | solution.py:56
  642.7 39.5 %all-gather.35.cloned.1.call-done = bf16[1536,1536]{0,1:T(8,128)(2,1)} async-done(((bf16[1536,192]{0,1:T(8,128)(2,1)}), bf16[1536,1536]{0,1:T(8,128)(2,1)}) %all-gather.35.cloned.1.call-update) | async-done | bytes 4718608 | tf_op jit(solution)/shard_map/all_gather | solution.py:282
  694.1 48.8 %all-gather.33.cloned.1.call-done = bf16[1536,2,1536]{2,1,0:T(2,128)(2,1)} async-done(((bf16[192,2,1536]{2,1,0:T(2,128)(2,1)}), bf16[1536,2,1536]{2,1,0:T(2,128)(2,1)}) %all-gather.33.cloned.1.call-update) | async-done | bytes 9437200 | tf_op jit(solution)/shard_map/all_gather | solution.py:281
  752.7 55.7 %all-gather.31.cloned.1.call-done = bf16[1,1024,1536]{2,1,0:T(8,128)(2,1)} async-done(((bf16[1,256,1536]{2,1,0:T(8,128)(2,1)}), bf16[1,1024,1536]{2,1,0:T(8,128)(2,1)}) %all-gather.31.cloned.1.call-update) | async-done | bytes 3145744 | tf_op jit(solution)/shard_map/all_gather | solution.py:157
  830.2 16.9 reshape.1229
  911.8 109.3 %reduce-scatter.31.cloned.1.call-done = f32[1,256,1536]{2,1,0:T(8,128)} async-done(((f32[1,1024,1536]{2,1,0:T(8,128)}), f32[1,256,1536]{2,1,0:T(8,128)}) %reduce-scatter.31.cloned.1.call-update) | async-done | bytes 1572880 | tf_op jit(solution)/shard_map/reduce_scatter | solution.py:161
  1041.1 49.0 %all-gather.39.cloned.1.call-done = bf16[1,1024,1536]{2,1,0:T(8,128)(2,1)} async-done(((bf16[1,256,1536]{2,1,0:T(8,128)(2,1)}), bf16[1,1024,1536]{2,1,0:T(8,128)(2,1)}) %all-gather.39.cloned.1.call-update) | async-done | bytes 3145744 | tf_op jit(solution)/shard_map/all_gather | solution.py:221
  1096.8 20.9 %while.58 = (s32[]{:T(128)}, bf16[2,512,6,64]{1,3,2,0:T(8,128)(2,1)}, f32[2,130,6,64]{1,3,2,0:T(8,128)}, f32[2,130,6,64]{1,3,2,0:T(8,128)}, bf16[2,512,6,64]{1,3...) while((s32[]{:T(128)}, ...), condition=%wide.region_25.26_spmd, body=%wide.region_23.25_spmd.sunk | while | flops 259028736 | bytes 35000212 | solution.py:143
  1140.5 97.2 %reduce-scatter.33.cloned.1.call-done = f32[1,256,1536]{2,1,0:T(8,128)} async-done(((f32[1,1024,1536]{2,1,0:T(8,128)}), f32[1,256,1536]{2,1,0:T(8,128)}) %reduce-scatter.33.cloned.1.call-update) | async-done | bytes 1572880 | tf_op jit(solution)/shard_map/reduce_scatter | solution.py:161
  1294.8 29.5 %all-gather.41.cloned.1.call-done = bf16[1,1024,1536]{2,1,0:T(8,128)(2,1)} async-done(((bf16[1,256,1536]{2,1,0:T(8,128)(2,1)}), bf16[1,1024,1536]{2,1,0:T(8,128)(2,1)}) %all-gather.41.cloned.1.call-update) | async-done | bytes 3145744 | tf_op jit(solution)/shard_map/all_gather | solution.py:221
  1334.3 96.1 %while.59 = (s32[]{:T(128)}, f32[2,512,6,64]{1,0,3,2:T(2,128)}, f32[2,1024,6,64]{1,3,2,0:T(8,128)}, f32[2,1024,6,64]{1,3,2,0:T(8,128)}, bf16[2,512,6,64]{1,3,2,0...) while((s32[]{:T(128)}, f32[2,512,6,64]{1,0,3,2:T(2,128)}, ...), condition=%wide.region_31.32_spmd, body=%wide.region_29.31_spmd.sunk | while | flops 2051601408 | bytes 215578992 | solution.py:143
  1354.6 15.0 dynamic_update_slice.73
  1504.1 76.5 %reduce-scatter.27.cloned.1.call-done = f32[1,256,1536]{2,1,0:T(8,128)} async-done(((f32[1,1024,1536]{2,1,0:T(8,128)}), f32[1,256,1536]{2,1,0:T(8,128)}) %reduce-scatter.27.cloned.1.call-update) | async-done | bytes 1572880 | tf_op jit(solution)/shard_map/reduce_scatter | solution.py:200
  1583.3 24.0 %reduce-scatter.37.cloned.1.call-done = bf16[384,130]{1,0:T(8,128)(2,1)} async-done(((bf16[1536,130]{1,0:T(8,128)(2,1)}), bf16[384,130]{1,0:T(8,128)(2,1)}) %reduce-scatter.37.cloned.1.call-update) | async-done | bytes 99856
  1609.9 67.3 %all-reduce.3.cloned.1.call-done = (bf16[8,6,384,16]{2,3,1,0:T(8,128)(2,1)}, bf16[8,1536,16]{1,2,0:T(8,128)(2,1)}, bf16[8,16,9,384]{3,1,2,0:T(8,128)(2,1)}, bf16[8,16,2,1536]{3,2,1,0:T(2,128)(2,1)}) async-done(((bf16[8,6,384,16]{2,3,1,0:T(8,128)(2,1)}, bf16[8,1536,16]{1,2,0:T(8,128)(2,1)}, bf16[8,16,9,384]{3,1,2,0:T(8,128)(2,1)}, bf16[8,16,2,1536]{3,2,1,0:T(2,128)(2,1)}), ...) | async-done | bytes 2654224 | tf_op jit(solution)/shard_map/psum | solution.py:426
  1684.5 105.4 %reduce-scatter.35.cloned.1.call-done = f32[1,256,1536]{2,1,0:T(8,128)} async-done(((f32[1,1024,1536]{2,1,0:T(8,128)}), f32[1,256,1536]{2,1,0:T(8,128)}) %reduce-scatter.35.cloned.1.call-update) | async-done | bytes 1572880 | tf_op jit(solution)/shard_map/reduce_scatter | solution.py:161
  (647 shorter events, 636.7 us)
Async XLA Ops:
  16.1 149.2 %all-gather.21.cloned.1.call-start = ((), (), s32[]{:S(2)}) async-start(), calls=%async_computation.14 | async-start | bytes 1327104 | tf_op jit(solution)/shard_map/all_gather | solution.py:277
  16.9 167.5 %reduce-scatter.21.cloned.1.call-start = ((), (), s32[]{:S(2)}) async-start(), calls=%async_computation.16 | async-start | bytes 81920 | tf_op jit(solution)/shard_map/reduce_scatter | solution.py:201
  165.2 130.4 %reduce-scatter.19.cloned.1.call-start = ((), (), s32[]{:S(2)}) async-start(), calls=%async_computation.15 | async-start | bytes 7864320 | tf_op jit(solution)/shard_map/reduce_scatter | solution.py:200
  171.2 155.8 %all-gather.27.cloned.1.call-start = ((), (), s32[]{:S(2)}) async-start(), calls=%async_computation.19 | async-start | bytes 2654208 | tf_op jit(solution)/shard_map/all_gather | solution.py:279
  171.8 221.0 %all-gather.23.cloned.1.call-start = ((), (), s32[]{:S(2)}) async-start(), calls=%async_computation.17 | async-start | bytes 3932160 | tf_op jit(solution)/shard_map/all_gather | solution.py:157
  299.2 118.4 %all-gather.25.cloned.1.call-start = ((), (), s32[]{:S(2)}) async-start(), calls=%async_computation.18 | async-start | bytes 1327104 | tf_op jit(solution)/shard_map/all_gather | solution.py:278
  299.9 143.8 %all-gather.29.cloned.1.call-start = ((), (), s32[]{:S(2)}) async-start(), calls=%async_computation.20 | async-start | bytes 1327104 | tf_op jit(solution)/shard_map/all_gather | solution.py:280
  300.7 164.8 %reduce-scatter.25.cloned.1.call-start = ((), (), s32[]{:S(2)}) async-start(), calls=%async_computation.22 | async-start | bytes 81920 | tf_op jit(solution)/shard_map/reduce_scatter | solution.py:201
  429.1 147.7 %reduce-scatter.23.cloned.1.call-start = ((), (), s32[]{:S(2)}) async-start(), calls=%async_computation.21 | async-start | bytes 7864320 | tf_op jit(solution)/shard_map/reduce_scatter | solution.py:200
  449.5 193.2 %all-gather.37.cloned.1.call-start = ((), (), s32[]{:S(2)}) async-start(), calls=%async_computation.28 | async-start | bytes 3932160 | tf_op jit(solution)/shard_map/all_gather | solution.py:221
  450.1 232.1 %all-gather.35.cloned.1.call-start = ((), (), s32[]{:S(2)}) async-start(), calls=%async_computation.25 | async-start | bytes 5308416 | tf_op jit(solution)/shard_map/all_gather | solution.py:282
  450.8 292.1 %all-gather.33.cloned.1.call-start = ((), (), s32[]{:S(2)}) async-start(), calls=%async_computation.24 | async-start | bytes 10616832 | tf_op jit(solution)/shard_map/all_gather | solution.py:281
  451.4 357.0 %all-gather.31.cloned.1.call-start = ((), (), s32[]{:S(2)}) async-start(), calls=%async_computation.23 | async-start | bytes 3932160 | tf_op jit(solution)/shard_map/all_gather | solution.py:157
  581.1 439.9 %reduce-scatter.31.cloned.1.call-start = ((), (), s32[]{:S(2)}) async-start(), calls=%async_computation.29 | async-start | bytes 7864320 | tf_op jit(solution)/shard_map/reduce_scatter | solution.py:161
  911.5 178.6 %all-gather.39.cloned.1.call-start = ((), (), s32[]{:S(2)}) async-start(), calls=%async_computation.30 | async-start | bytes 3932160 | tf_op jit(solution)/shard_map/all_gather | solution.py:221
  1025.8 212.0 %reduce-scatter.33.cloned.1.call-start = ((), (), s32[]{:S(2)}) async-start(), calls=%async_computation.31 | async-start | bytes 7864320 | tf_op jit(solution)/shard_map/reduce_scatter | solution.py:161
  1128.2 131.9 %reduce-scatter.29.cloned.1.call-start = ((), (), s32[]{:S(2)}) async-start(), calls=%async_computation.27 | async-start | bytes 81920 | tf_op jit(solution)/shard_map/reduce_scatter | solution.py:201
  1140.5 183.8 %all-gather.41.cloned.1.call-start = ((), (), s32[]{:S(2)}) async-start(), calls=%async_computation.32 | async-start | bytes 3932160 | tf_op jit(solution)/shard_map/all_gather | solution.py:221
  1243.0 237.8 %reduce-scatter.41.cloned.1.call-start = ((), (), s32[]{:S(2)}) async-start(), calls=%async_computation.36 | async-start | bytes 491520
  1294.8 192.0 %reduce-scatter.39.cloned.1.call-start = ((), (), s32[]{:S(2)}) async-start(), calls=%async_computation.35 | async-start | bytes 491520
  1449.7 130.9 %reduce-scatter.27.cloned.1.call-start = ((), (), s32[]{:S(2)}) async-start(), calls=%async_computation.26 | async-start | bytes 7864320 | tf_op jit(solution)/shard_map/reduce_scatter | solution.py:200
  1462.5 144.8 %reduce-scatter.37.cloned.1.call-start = ((), (), s32[]{:S(2)}) async-start(), calls=%async_computation.34 | async-start | bytes 983040
  1480.5 196.6 %all-reduce.3.cloned.1.call-start = ((), (), s32[]{:S(2)}) async-start(), calls=%async_computation.37 | async-start | bytes 5308416 | tf_op jit(solution)/shard_map/psum | solution.py:426
  1492.1 297.8 %reduce-scatter.35.cloned.1.call-start = ((), (), s32[]{:S(2)}) async-start(), calls=%async_computation.33 | async-start | bytes 7864320 | tf_op jit(solution)/shard_map/reduce_scatter | solution.py:161
  (168 other events, 3799.3 us)
Sparse Core Ops, SparseCore 0:
  15.5 66.1 all-gather.16
  83.6 32.6 all-gather.18
  118.2 24.0 all-gather.20
  186.6 108.9 reduce-scatter.18
  297.5 29.5 all-gather.26
  329.3 63.4 all-gather.22
  394.8 22.6 all-gather.24
  419.6 24.0 all-gather.28
  467.8 108.9 reduce-scatter.22
  578.2 64.4 all-gather.36
  644.6 37.5 all-gather.34
  683.9 58.8 all-gather.32
  744.9 63.4 all-gather.30
  911.6 109.3 reduce-scatter.30
  1025.9 64.1 all-gather.38
  1128.3 109.4 reduce-scatter.32
  1240.6 19.4 reduce-scatter.28
  1262.2 62.1 all-gather.40
  1326.7 19.1 reduce-scatter.40
  1449.8 19.1 reduce-scatter.38
  1471.4 109.1 reduce-scatter.26
  1583.4 23.8 reduce-scatter.36
  1612.0 65.0 all-reduce.2
  1679.3 110.5 reduce-scatter.34
  (2 shorter events, 37.9 us)
where the time goes:
time: 1820 us; the launch traced here: 1800 us
  waiting for transfers between devices  1160 us (64%)
  matrix products  273 us (15%)
  local copies, waits for them, and re-layouts  192 us (11%)
  other arithmetic  100 us (5%)
  blocking collectives  56.3 us (3%)
    reduce_scatter x3, waiting for transfers between devices, return_rows(): lax.psum_scatter(grad_partial, 'tensor', scatter_dimension=1, tiled=True)  312 us
    reduce_scatter x3, waiting for transfers between devices, branch_tail(): lax.psum_scatter(partial_total_sum, 'tensor', scatter_dimension=1, tiled=...  299 us
    all_gather x3, waiting for transfers between devices, spread_rows(): return lax.all_gather(normed_own, 'tensor', axis=1, tiled=True)  166 us
    all_gather x3, waiting for transfers between devices, tail_backward(): lax.all_gather(branch_gradient, 'tensor', axis=1, tiled=True)  84.2 us
    psum x1, waiting for transfers between devices, body(): lax.psum(scatter_slots(onehot, per_down).astype(jnp.bfloat16), 'dp')  67.3 us
    all_gather x1, waiting for transfers between devices, body(): lax.all_gather(feed_in_weight, 'dp', axis=0, tiled=True)  48.8 us
    unnamed x288, local copies, waits for them, and re-layouts  45.3 us
    all_gather x3, blocking collectives, tail_backward(): lax.all_gather(grad_lowrank, 'tensor', axis=1, tiled=True)  41.2 us
  transfers between devices with their start and end apart: 26, of which 23 were waited for; matrix products, arithmetic and copies ran while one was open for 22% of the time, Pallas kernels for 0%

commit v1 on v0

v1 whole, which is shorter than its diff:
```python
import jax
import jax.numpy as jnp
from jax import lax
from jax.sharding import Mesh, PartitionSpec as P

HEAD_DIM = 64
ROT = 32
EPSILON = 1e-05
EXT = 128
CHUNKS = 3
F32 = jnp.float32
BF = jnp.bfloat16
SWAP = ((0, 1), (1, 0))


def dot(left, right):
    return jnp.dot(left, right, preferred_element_type=F32)


def dot_nt(left, right):
    return lax.dot_general(left, right, (((1,), (1,)), ((), ())), preferred_element_type=F32)


def dot_tn(left, right):
    return lax.dot_general(left, right, (((0,), (0,)), ((), ())), preferred_element_type=F32)


def core_swap(x):
    return lax.ppermute(x, "core", SWAP)


def xor_move(x, axis, size, k):
    return lax.ppermute(x, axis, [(i, i ^ k) for i in range(size)])


def home_swap(x):
    return lax.ppermute(x, ("core", "zhi"), [(0, 0), (1, 2), (2, 1), (3, 3)])


class Group:
    def __init__(self, pairs, chips):
        self.pairs, self.chips = pairs, chips
        self.core, self.zhi, self.p = (lax.axis_index(n) for n in ("core", "zhi", "p"))
        self.chip = lax.axis_index("chip")
        self.home = self.core == self.zhi
        self.pieces = [
            (self.core ^ kc) * pairs + (self.p ^ kp) for kp in range(pairs) for kc in (0, 1)
        ]

    def gather(self, own):
        blocks = [own, core_swap(own)]
        for k in range(1, self.pairs):
            far = xor_move(own, "p", self.pairs, k)
            blocks += [far, core_swap(far)]
        return blocks

    def scatter(self, partials):
        sums = [
            partials[2 * k].astype(F32) + core_swap(partials[2 * k + 1].astype(BF)).astype(F32)
            for k in range(self.pairs)
        ]
        total = sums[0]
        for k in range(1, self.pairs):
            total = total + xor_move(sums[k].astype(BF), "p", self.pairs, k).astype(F32)
        return total

    def spread_chips(self, block):
        got = {0: block}
        if self.chips == 4:
            got[1] = xor_move(block, "chip", 4, 1)
            got[2] = xor_move(block, "chip", 4, 2)
            half = block.shape[0] // 2
            got[3] = jnp.concatenate(
                [
                    xor_move(got[2][:half], "chip", 4, 1),
                    xor_move(got[1][half:], "chip", 4, 2),
                ],
                axis=0,
            )
        else:
            for k in range(1, self.chips):
                got[k] = xor_move(block, "chip", self.chips, k)
        return [got[k] for k in range(self.chips)]

    def gather_weights(self, shard):
        rows, columns = shard.shape
        other = core_swap(shard)
        both = jnp.zeros((2 * rows, columns), shard.dtype)
        both = lax.dynamic_update_slice(both, shard, (self.core * rows, 0))
        both = lax.dynamic_update_slice(both, other, ((1 - self.core) * rows, 0))
        far = lax.ppermute(both, ("core", "zhi"), [(0, 1), (3, 2)])
        both = jnp.where(self.home, both, far)
        blocks = self.spread_chips(both)
        whole = jnp.zeros((2 * rows * self.chips + EXT, columns), shard.dtype)
        for k, block in enumerate(blocks):
            whole = lax.dynamic_update_slice(whole, block, ((self.chip ^ k) * 2 * rows, 0))
        return whole


def stats(stream):
    average = jnp.mean(stream, axis=-1, keepdims=True)
    centred = stream - average
    variance = jnp.mean(centred * centred, axis=-1, keepdims=True)
    scale = lax.rsqrt(variance + EPSILON)
    return centred * scale, scale


def layer_norm(stream, gain, bias):
    return (stats(stream)[0] * gain + bias).astype(BF)


def norm_backward(stream, gain, grad):
    unit, scale = stats(stream)
    grad = grad * gain
    return scale * (
        grad
        - jnp.mean(grad, axis=-1, keepdims=True)
        - unit * jnp.mean(grad * unit, axis=-1, keepdims=True)
    )


def widen(rows, low):
    pad = jnp.zeros((rows.shape[0], EXT - low.shape[1]), rows.dtype)
    return jnp.concatenate([rows, low.astype(rows.dtype), pad], axis=1)


def rotate(values, cosines, sines):
    half = ROT // 2
    rows, width = values.shape
    values = values.reshape(rows, width // HEAD_DIM, HEAD_DIM)
    leading, second = values[..., :half], values[..., half:ROT]
    cosines, sines = cosines[:, None], sines[:, None]
    return jnp.concatenate(
        [
            leading * cosines - second * sines,
            second * cosines + leading * sines,
            values[..., ROT:],
        ],
        axis=-1,
    ).reshape(rows, width)


def split_heads(x):
    return x.reshape(x.shape[0], -1, HEAD_DIM)


def attend(query, keys, values):
    query, keys, values = split_heads(query), split_heads(keys), split_heads(values)
    scores = jnp.einsum("qhe,khe->hqk", query, keys, preferred_element_type=F32) * 0.125
    top = jnp.max(scores, axis=-1, keepdims=True)
    powers = jnp.exp(scores - top)
    total = jnp.sum(powers, axis=-1, keepdims=True)
    out = jnp.einsum(
        "hqk,khe->qhe", (powers / total).astype(BF), values, preferred_element_type=F32
    )
    return out.reshape(out.shape[0], -1).astype(BF), top + jnp.log(total)


def attend_backward(query, keys, values, logsum, grad):
    query, keys, values = split_heads(query), split_heads(keys), split_heads(values)
    grad = split_heads(grad)
    scores = jnp.einsum("qhe,khe->hqk", query, keys, preferred_element_type=F32) * 0.125
    probs = jnp.exp(scores - logsum)
    grad_probs = jnp.einsum("qhe,khe->hqk", grad, values, preferred_element_type=F32)
    delta = jnp.sum(probs * grad_probs, axis=-1, keepdims=True)
    grad_scores = (probs * (grad_probs - delta)).astype(BF)
    grad_query = jnp.einsum("hqk,khe->qhe", grad_scores, keys, preferred_element_type=F32) * 0.125
    grad_keys = jnp.einsum("hqk,qhe->khe", grad_scores, query, preferred_element_type=F32) * 0.125
    grad_values = jnp.einsum("hqk,qhe->khe", probs.astype(BF), grad, preferred_element_type=F32)
    return tuple(g.reshape(g.shape[0], -1) for g in (grad_query, grad_keys, grad_values))


def body(
    inputs,
    context,
    positions,
    adapter_index,
    self_in_weight,
    self_out_weight,
    cross_query_weight,
    cross_keyval_weight,
    cross_out_weight,
    feed_in_weight,
    feed_out_weight,
    norm_gains,
    norm_biases,
    adapter_down,
    adapter_down_hidden,
    adapter_up,
    adapter_up_hidden,
    out_cotangent,
    *,
    pairs,
    chips,
):
    group = Group(pairs, chips)
    members = 2 * pairs
    rows, width = inputs.shape[1], inputs.shape[2]
    local = self_in_weight.shape[2]
    hidden = feed_in_weight.shape[2]
    slots, rank = adapter_down.shape[0], adapter_down.shape[3]
    part = hidden // CHUNKS
    pieces = group.pieces
    gains, biases = norm_gains, norm_biases

    index = jnp.where(group.home, adapter_index, core_swap(adapter_index))[0]
    positions = jnp.where(group.home, positions, core_swap(positions))[0]
    stream = group.gather(home_swap(inputs[0]))
    cotangent = group.gather(home_swap(out_cotangent[0]))
    context_blocks = group.gather(home_swap(context[0]))

    down = lax.dynamic_index_in_dim(adapter_down.transpose(0, 1, 3, 2), index, 0, keepdims=False)
    down_hidden = lax.dynamic_index_in_dim(
        adapter_down_hidden.transpose(0, 2, 1), index, 0, keepdims=False
    )
    up = lax.dynamic_index_in_dim(adapter_up.transpose(0, 2, 1, 3), index, 0, keepdims=False)
    up_hidden = lax.dynamic_index_in_dim(
        adapter_up_hidden.transpose(0, 2, 1, 3), index, 0, keepdims=False
    )

    def piece(array, k, size):
        return lax.dynamic_slice_in_dim(array, pieces[k] * size, size, array.ndim - 1)

    def relative(array, size):
        return jnp.concatenate([piece(array, k, size) for k in range(members)], axis=-1)

    def own(array):
        return piece(array, 0, local)

    def weights(shards, low):
        whole = group.gather_weights(jnp.concatenate(shards, axis=1))
        return lax.dynamic_update_slice(whole, jnp.concatenate(low, axis=1), (width, 0))

    self_in = weights(
        [self_in_weight[:, i] for i in range(3)], [own(up[i]) for i in range(3)]
    )
    rest = weights(
        [
            self_out_weight.T,
            cross_query_weight,
            cross_out_weight.T,
            cross_keyval_weight[:, 0],
            cross_keyval_weight[:, 1],
        ],
        [own(down[1]), own(up[4]), own(down[4]), own(up[5]), own(up[6])],
    )
    self_out = rest[:, :local]
    cross_keyval = rest[:, 3 * local :]
    cross_blocks = group.gather(rest[:, local : 3 * local])
    cross_query = jnp.concatenate([b[:, :local] for b in cross_blocks], axis=1)
    cross_out = jnp.concatenate([b[:, local:] for b in cross_blocks], axis=1)
    feed_down = piece(down_hidden, 0, hidden)
    feed_up = piece(up_hidden, 0, hidden)
    feed = []
    for i in range(CHUNKS):
        at = slice(i * part, (i + 1) * part)
        feed.append(
            weights(
                [feed_in_weight[:, 0, at], feed_in_weight[:, 1, at], feed_out_weight.T[:, at]],
                [feed_up[0, :, at], feed_up[1, :, at], feed_down[:, at]],
            )
        )

    blocks_at = [
        lax.dynamic_slice_in_dim(positions, pieces[k] * rows, rows, 0) for k in range(members)
    ]
    half = ROT // 2
    inverse = 10000.0 ** (-jnp.arange(half, dtype=F32) / half)
    angles = jnp.concatenate(blocks_at).astype(F32)[:, None] * inverse
    cosines, sines = jnp.cos(angles), jnp.sin(angles)

    def project(normed, down_rows, weight):
        low = dot_nt(normed, down_rows).astype(BF)
        return dot(widen(normed, low), weight), low

    stream_zero = stream[0].astype(F32)
    normed_one = layer_norm(jnp.concatenate(stream, axis=0).astype(F32), gains[0], biases[0])
    mixed, low_one = project(normed_one, down[0], self_in)
    query = rotate(mixed[:, :local], cosines, sines).astype(BF)
    keys = rotate(mixed[:, local : 2 * local], cosines, sines).astype(BF)
    values = mixed[:, 2 * local :].astype(BF)
    heads, logsum = attend(query, keys, values)

    def split_rows(x):
        return [x[k * rows : (k + 1) * rows] for k in range(members)]

    def tail(partial, up_rows):
        total = group.scatter(partial)
        low = total[:, width : width + rank].astype(BF)
        return total[:, :width] + dot(low, up_rows), low

    branch, low_two = tail(split_rows(dot_nt(heads, self_out)), up[3])
    stream_one = stream_zero + branch

    normed_two = layer_norm(stream_one, gains[1], biases[1])
    query_cross, low_three = project(normed_two, down[2], cross_query)
    query_cross = query_cross.astype(BF)
    context_count = context_blocks[0].shape[0]
    context_all = jnp.zeros((members,) + context_blocks[0].shape, BF)
    for k in range(members):
        context_all = lax.dynamic_update_slice(
            context_all, context_blocks[k][None], (pieces[k], 0, 0)
        )
    context_all = context_all.transpose(1, 0, 2).reshape(context_count, width)
    keyval, low_context = project(context_all, down[3], cross_keyval)
    keyval_blocks = group.gather(keyval.astype(BF))
    keys_cross = jnp.concatenate([b[:, :local] for b in keyval_blocks], axis=1)
    values_cross = jnp.concatenate([b[:, local:] for b in keyval_blocks], axis=1)
    heads_cross, logsum_cross = attend(query_cross, keys_cross, values_cross)
    total = dot_nt(heads_cross, cross_out)
    low_four = total[:, width : width + rank].astype(BF)
    stream_two = stream_one + total[:, :width] + dot(low_four, up[7])

    normed_three = layer_norm(stream_two, gains[2], biases[2])
    low_own_five = dot_nt(normed_three, down[5]).astype(BF)
    normed_all = jnp.concatenate(group.gather(normed_three), axis=0)
    low_five = dot_nt(normed_all, down[5]).astype(BF)
    wide = widen(normed_all, low_five)
    cotangent_all = jnp.concatenate(cotangent, axis=0)
    grad_low = dot_nt(cotangent_all, up[8]).astype(BF)
    wide_grad = widen(cotangent_all, grad_low)
    feed_sum, grad_sum = 0.0, 0.0
    grad_feed_down, grad_gate_up, grad_upper_up = [], [], []
    for weight in feed:
        gate = dot(wide, weight[:, :part])
        upper = dot(wide, weight[:, part : 2 * part])
        sigmoid = 1.0 / (1.0 + jnp.exp(-gate))
        acted = gate * sigmoid
        unit = (acted * upper).astype(BF)
        feed_sum = feed_sum + dot_nt(unit, weight[:, 2 * part :])
        grad_unit = dot(wide_grad, weight[:, 2 * part :])
        grad_gate = (grad_unit * upper * (sigmoid + acted * (1.0 - sigmoid))).astype(BF)
        grad_upper = (grad_unit * acted).astype(BF)
        grad_sum = grad_sum + dot_nt(grad_gate, weight[:, :part])
        grad_sum = grad_sum + dot_nt(grad_upper, weight[:, part : 2 * part])
        grad_feed_down.append(dot_tn(grad_low, unit))
        grad_gate_up.append(dot_tn(low_five, grad_gate))
        grad_upper_up.append(dot_tn(low_five, grad_upper))

    def head(partial, down_rows):
        total = group.scatter(partial)
        grad_low = total[:, width : width + rank].astype(BF)
        return total[:, :width] + dot(grad_low, down_rows), grad_low

    grad_normed, grad_low_five = head(split_rows(grad_sum), down[5])
    grad_down_five = dot_tn(grad_low_five, normed_three)
    branch, low_six = tail(split_rows(feed_sum), up[8])
    block_output = home_swap((stream_two + branch).astype(BF))
    grad_up_eight = dot_tn(low_six, cotangent[0])
    grad_stream = cotangent[0].astype(F32) + norm_backward(stream_two, gains[2], grad_normed)

    branch_grad = grad_stream.astype(BF)
    grad_low_four = dot_nt(branch_grad, up[7]).astype(BF)
    grad_up_seven = dot_tn(low_four, branch_grad)
    grad_down_four = dot_tn(grad_low_four, heads_cross)
    grad_heads = dot(widen(branch_grad, grad_low_four), cross_out).astype(BF)
    grad_query, grad_keys, grad_values = attend_backward(
        query_cross, keys_cross, values_cross, logsum_cross, grad_heads
    )
    grad_query = grad_query.astype(BF)
    total = dot_nt(grad_query, cross_query)
    grad_low_two = total[:, width : width + rank].astype(BF)
    grad_up_four = dot_tn(low_three, grad_query)
    grad_down_two = dot_tn(grad_low_two, normed_two)
    grad_normed = total[:, :width] + dot(grad_low_two, down[2])
    grad_stream = grad_stream + norm_backward(stream_one, gains[1], grad_normed)
    grad_keyval = group.scatter(
        [
            jnp.concatenate([g[:, k * local : (k + 1) * local] for g in (grad_keys, grad_values)], axis=1)
            for k in range(members)
        ]
    ).astype(BF)
    total = dot_nt(grad_keyval, cross_keyval)
    grad_low_three = total[:, width : width + rank].astype(BF)
    grad_up_keyval = dot_tn(low_context, grad_keyval)
    grad_down_three = dot_tn(grad_low_three, context_all)
    context_partial = total[:, :width] + dot(grad_low_three, down[3])
    grad_context = home_swap(
        group.scatter([piece(context_partial, k, local) for k in range(members)]).astype(BF)
    ).astype(F32)

    branch_grad = jnp.concatenate(group.gather(grad_stream.astype(BF)), axis=0)
    grad_low_one = dot_nt(branch_grad, up[3]).astype(BF)
    grad_up_three = dot_tn(low_two, branch_grad[:rows])
    grad_down_one = dot_tn(grad_low_one, heads)
    grad_heads = dot(widen(branch_grad, grad_low_one), self_out).astype(BF)
    grad_query, grad_keys, grad_values = attend_backward(query, keys, values, logsum, grad_heads)
    grad_mixed = jnp.concatenate(
        [rotate(grad_query, cosines, -sines), rotate(grad_keys, cosines, -sines), grad_values],
        axis=1,
    ).astype(BF)
    grad_up_self = dot_tn(low_one, grad_mixed)
    grad_normed, grad_low_zero = head(split_rows(dot_nt(grad_mixed, self_in)), down[0])
    grad_down_zero = dot_tn(grad_low_zero, normed_one[:rows])
    grad_inputs = grad_stream + norm_backward(stream_zero, gains[0], grad_normed)
    grad_inputs = home_swap(grad_inputs.astype(BF)).astype(F32)

    summed = group.scatter(
        [
            jnp.concatenate(
                [
                    piece(g, k, local)
                    for g in (
                        grad_down_zero,
                        grad_down_two,
                        grad_down_three,
                        grad_down_five,
                        grad_up_three,
                        grad_up_seven,
                        grad_up_eight,
                    )
                ]
                + [g[:, k * local : (k + 1) * local] for g in (grad_down_four, grad_up_four)],
                axis=0,
            )
            for k in range(members)
        ]
    ).reshape(9, rank, local)
    fold = hidden // local

    def columns(array):
        return array.reshape(rank, -1, local).transpose(1, 0, 2)

    grads = jnp.concatenate(
        [
            summed[0:1],
            grad_down_one[None],
            summed[1:3],
            summed[7:8],
            summed[3:4],
            columns(grad_up_self),
            summed[4:5],
            summed[8:9],
            columns(grad_up_keyval),
            summed[5:7],
            columns(jnp.concatenate(grad_feed_down, axis=1)),
            columns(jnp.concatenate(grad_gate_up, axis=1)),
            columns(jnp.concatenate(grad_upper_up, axis=1)),
            jnp.full((1, rank, local), index, F32),
        ],
        axis=0,
    ).astype(BF)
    across = xor_move(grads, "zhi", 2, 1)
    both = jnp.stack([grads, across])
    both = jnp.where(group.home, both, core_swap(both))
    every = jnp.concatenate(group.spread_chips(both), axis=0)
    labels = every[:, -1, 0, 0]

    def settle(array):
        return jnp.stack(
            [
                sum(
                    jnp.where(labels[s] == slot, array[s], 0).astype(F32)
                    for s in range(array.shape[0])
                )
                for slot in range(slots)
            ]
        )

    grad_down = settle(every[:, 0:6]).transpose(0, 1, 3, 2)
    grad_up = settle(every[:, 6:15]).transpose(0, 2, 1, 3)
    grad_hidden = settle(every[:, 15 : 15 + fold]).transpose(0, 1, 3, 2)
    grad_hidden = grad_hidden.reshape(slots, hidden, rank)
    grad_gate = settle(every[:, 15 + fold : 15 + 3 * fold])
    grad_gate = grad_gate.reshape(slots, 2, fold, rank, local).transpose(0, 3, 1, 2, 4)
    return (
        block_output[None],
        grad_inputs[None],
        grad_context[None],
        grad_down,
        grad_hidden,
        grad_up,
        grad_gate.reshape(slots, rank, 2, hidden),
    )


def solution(mesh):
    members = mesh.shape["tensor"]
    chips = mesh.shape["dp"] // 2
    mesh = Mesh(
        mesh.devices.reshape(chips, 2, 2, members // 2), ("chip", "core", "zhi", "p")
    )
    dp, tensor = ("chip", "core"), ("zhi", "p")
    in_specs = (
        P(dp, tensor, None),
        P(dp, None, tensor),
        P(dp, None),
        P(dp),
        P(dp, None, tensor),
        P(tensor, dp),
        P(dp, tensor),
        P(dp, None, tensor),
        P(tensor, dp),
        P(dp, None, tensor),
        P(tensor, dp),
        P(),
        P(),
        P(),
        P(),
        P(),
        P(),
        P(dp, tensor, None),
    )
    out_specs = (
        P(dp, tensor, None),
        P(dp, tensor, None),
        P(dp, None, tensor),
        P(None, None, tensor, None),
        P(None, tensor, None),
        P(None, None, None, tensor),
        P(None, None, None, tensor),
    )

    def run(*args):
        return body(*args, pairs=members // 2, chips=chips)

    return jax.shard_map(run, mesh=mesh, in_specs=in_specs, out_specs=out_specs, check_vma=False)
```

time: 1820 us -> 1040 us (0.57)
  waiting for transfers between devices: 1160 us -> 283 us
  starting transfers between devices: 2.3 us -> 166 us
  blocking collectives: 56.3 us -> 0 us
  matrix products: 273 us -> 234 us
  between operations: 17 us -> 47.1 us
    reduce_scatter x9 -> x0, waiting for transfers between devices: 649 us -> none  [the longest x3 312 us: return_rows(): lax.psum_scatter(grad_partial, 'tensor', scatter_dimension=1, tiled=True)]
    all_gather x13 -> x0, waiting for transfers between devices: 417 us -> none  [the longest x3 166 us: spread_rows(): return lax.all_gather(normed_own, 'tensor', axis=1, tiled=True)]
    ppermute x0 -> x86, waiting for transfers between devices: none -> 283 us  [the longest x39 280 us: xor_move(): return lax.ppermute(x, axis, [(i, i ^ k) for i in range(size)])]
    ppermute x0 -> x86, starting transfers between devices: none -> 166 us  [the longest x36 75.5 us: core_swap(): return lax.ppermute(x, 'core', SWAP)]
    psum x1 -> x0, waiting for transfers between devices: 67.3 us -> none  [body(): lax.psum(scatter_slots(onehot, per_down).astype(jnp.bfloat16), 'dp')]
    all_gather x4 -> x0, blocking collectives: 56.3 us -> none  [the longest x3 41.2 us: tail_backward(): lax.all_gather(grad_lowrank, 'tensor', axis=1, tiled=True)]
    dot_general x88 -> x75, matrix products: 273 us -> 234 us  [the longest x21 82.6 us: dot_nt(): lax.dot_general(left, right, (((1,), (1,)), ((), ())), preferred_element_...]
    slice x12 -> x52, local copies, waits for them, and re-layouts: 17 us -> 53.2 us  [the longest x4 10.7 us: body(): cross_out = jnp.concatenate([b[:, local:] for b in cross_blocks], axis=1)]
  transfers between devices with their start and end apart: 26 -> 86, of which waited for: 23 -> 24; matrix products, arithmetic and copies ran while one was open for 22% -> 40% of each run, Pallas kernels for 0% -> 0%
where the time goes in v1:
time: 1040 us; the launch traced here: 1020 us
  waiting for transfers between devices  283 us (27%)
  matrix products  234 us (22%)
  local copies, waits for them, and re-layouts  183 us (18%)
  starting transfers between devices  166 us (16%)
  other arithmetic  108 us (10%)
  between operations  47.1 us (5%)
    ppermute x39, waiting for transfers between devices, xor_move(): return lax.ppermute(x, axis, [(i, i ^ k) for i in range(size)])  280 us
    dot_general x21, matrix products, dot_nt(): lax.dot_general(left, right, (((1,), (1,)), ((), ())), preferred_element_...  82.6 us
    ppermute x36, starting transfers between devices, core_swap(): return lax.ppermute(x, 'core', SWAP)  75.5 us
    dot_general x21, matrix products, dot(): return jnp.dot(left, right, preferred_element_type=F32)  60.2 us
    ppermute x39, starting transfers between devices, xor_move(): return lax.ppermute(x, axis, [(i, i ^ k) for i in range(size)])  51 us
    unnamed x424, local copies, waits for them, and re-layouts  39.4 us
    concatenate x7, local copies, waits for them, and re-layouts, widen(): return jnp.concatenate([rows, low.astype(rows.dtype), pad], axis=1)  26.9 us
    ppermute x5, starting transfers between devices, gather_weights(): far = lax.ppermute(both, ('core', 'zhi'), [(0, 1), (3, 2)])  24.7 us
  transfers between devices with their start and end apart: 86, of which 24 were waited for; matrix products, arithmetic and copies ran while one was open for 40% of the time, Pallas kernels for 0%

profile of v1, /device:TPU:0, one launch (start us, length us, event | category | flops | bytes accessed | tf_op | source)
XLA Modules:
  0.0 1021.3 jit_solution(7098724459657948805)
XLA Ops:
  89.7 62.9 %collective-permute-start.57 = (bf16[256,1536]{1,0:T(8,128)(2,1)S(1)}, bf16[256,1536]{1,0:T(8,128)(2,1)S(1)}, u32[]{:S(2)}, u32[]{:S(2)}) collective-permute-start(bf16[256,1536]{1,0:T(8,128)(2,1)S(1)} %collective-permute-done.56), channel_id=1, source_target_pairs={{0,4},{4,0},{1,5},{5,1},{2,6},{6,2},{3,7},{7,3},{8,12},{12,8},{9,1... | collective-permute-start | bytes 2359304 | tf_op jit(solution)/shard_map/ppermute | solution.py:29
  156.0 15.5 %collective-permute-start.13 = (bf16[384,1920]{1,0:T(8,128)(2,1)S(1)}, bf16[384,1920]{1,0:T(8,128)(2,1)S(1)}, u32[]{:S(2)}, u32[]{:S(2)}) collective-permute-start(bf16[384,1920]{1,0:T(8,128)(2,1)S(1)} %constant_dynamic-update-slice_fusion.129), channel_id=1, source_target_pairs={{0,2},{6,4},{1,3},{7,5},{8,10},{14,12},{9,11},{15,13},{16,18},{22,... | collective-permute-start | bytes 4423688 | tf_op jit(solution)/shard_map/ppermute | solution.py:91
  171.6 53.4 %collective-permute-done.58 = bf16[256,1536]{1,0:T(8,128)(2,1)} collective-permute-done((bf16[256,1536]{1,0:T(8,128)(2,1)S(1)}, bf16[256,1536]{1,0:T(8,128)(2,1)}, u32[]{:S(2)}, u32[]{:S(2)}) %collective-permute-start.58) | collective-permute-done | bytes 786464 | tf_op jit(solution)/shard_map/ppermute | solution.py:33
  293.6 22.1 %collective-permute-done.9 = bf16[192,1152]{1,0:T(8,128)(2,1)} collective-permute-done((bf16[192,1152]{1,0:T(8,128)(2,1)}, bf16[192,1152]{1,0:T(8,128)(2,1)}, u32[]{:S(2)}, u32[]{:S(2)}) %collective-permute-start.9) | collective-permute-done | bytes 442400 | tf_op jit(solution)/shard_map/ppermute | solution.py:33
  318.9 8.0 fusion.184
  337.6 10.1 multiply_reduce_fusion.1
  347.8 11.2 %fusion = f32[6,1024]{1,0:T(8,128)S(1)} fusion(f32[6,1024,1024]{1,2,0:T(8,128)} %get-tuple-element.195, f32[6,1024]{1,0:T(8,128)S(1)} %get-tuple-element.194), kind=kLoop, calls=%fused_computation.5 | loop fusion | flops 18868224 | bytes 25214976 | tf_op jit(solution)/shard_map/reduce_sum | solution.py:152
  362.6 10.9 %fusion.89 = bf16[6,64,1024]{2,1,0:T(8,128)(2,1)S(1)} fusion(bf16[1024,6,64]{0,2,1:T(8,128)(2,1)S(1)} %bitcast.488, f32[6,1024,1024]{1,2,0:T(8,128)} %get-tuple-element.195, f32[6,1024]{1,0:T(8,128)S(1)} %fusion, f32[6,1024]{1,0:T(8,128)S(1)} %get-tuple-element.194), kind=kOutput, calls=%fused_computation.157 | convolution fusion | flops 830865408 | bytes 26787840 | tf_op jit(solution)/shard_map/hqk,khe->qhe/dot_general | solution.py:153
  400.3 19.3 %collective-permute-done.15 = bf16[384,1920]{1,0:T(8,128)(2,1)S(1)} collective-permute-done((bf16[384,1920]{1,0:T(8,128)(2,1)S(1)}, bf16[384,1920]{1,0:T(8,128)(2,1)S(1)}, u32[]{:S(2)}, u32[]{:S(2)}) %collective-permute-start.15) | collective-permute-done | bytes 1474592 | tf_op jit(solution)/shard_map/ppermute | solution.py:33
  424.0 19.1 %collective-permute-done.17 = bf16[192,1920]{1,0:T(8,128)(2,1)S(1)} collective-permute-done((bf16[192,1920]{1,0:T(8,128)(2,1)S(1)}, bf16[192,1920]{1,0:T(8,128)(2,1)S(1)}, u32[]{:S(2)}, u32[]{:S(2)}) %collective-permute-start.17) | collective-permute-done | bytes 737312 | tf_op jit(solution)/shard_map/ppermute | solution.py:33
  463.6 64.2 %collective-permute-done.20 = bf16[256,1664]{1,0:T(8,128)(2,1)} collective-permute-done((bf16[256,1664]{1,0:T(8,128)(2,1)}, bf16[256,1664]{1,0:T(8,128)(2,1)}, u32[]{:S(2)}, u32[]{:S(2)}) %collective-permute-start.20) | collective-permute-done | bytes 852000 | tf_op jit(solution)/shard_map/ppermute | solution.py:33
  569.2 9.0 collective-permute-done.44
  658.3 7.8 fusion.179
  667.9 16.4 %fusion.180 = (bf16[1024,1664]{1,0:T(8,128)(2,1)}, f32[1024,1664]{1,0:T(8,128)}) fusion(bf16[1024,512]{1,0:T(8,128)(2,1)S(1)} %get-tuple-element.51, bf16[1664,1536]{1,0:T(8,128)(2,1)} %maximum_dynamic-update-slice_fusion.7, f32[1024,1664]{1,0:T(8,128)} %fusion.55, f32[1024,1664]{1,0:T(8,128)} %fusion.63, f32[1024,1664]{1,0:T(8,128)} %fusion.67, ...), kind=kOutput, calls=%fused_computation.553 | convolution fusion | flops 1755054080 | bytes 47054848 | tf_op jit(solution)/shard_map/dot_general | solution.py:21
  696.6 15.8 %collective-permute-done.62 = bf16[256,1664]{1,0:T(8,128)(2,1)S(1)} collective-permute-done((bf16[256,1664]{1,0:T(8,128)(2,1)S(1)}, bf16[256,1664]{1,0:T(8,128)(2,1)S(1)}, u32[]{:S(2)}, u32[]{:S(2)}) %collective-permute-start.62) | collective-permute-done | bytes 852000 | tf_op jit(solution)/shard_map/ppermute | solution.py:33
  747.8 7.6 collective-permute-start.55
  779.7 11.5 %fusion.86 = bf16[6,64,1024]{2,1,0:T(8,128)(2,1)} fusion(bf16[1024,6,64]{0,2,1:T(8,128)(2,1)S(1)} %bitcast.484, f32[6,1024,1024]{1,2,0:T(8,128)} %get-tuple-element.195, f32[6,1024]{1,0:T(8,128)S(1)} %copy-done.118), kind=kOutput, calls=%fused_computation.155 | convolution fusion | flops 824573952 | bytes 26763264 | tf_op jit(solution)/shard_map/hqk,qhe->khe/dot_general | solution.py:169
  791.2 19.8 %multiply_reduce_fusion = (f32[6,1024]{1,0:T(8,128)S(1)}, f32[6,1024,1024]{1,2,0:T(8,128)}) fusion(f32[6,1024,1024]{1,2,0:T(8,128)} %get-tuple-element.195, f32[6,1024]{1,0:T(8,128)S(1)} %copy-done.118, bf16[1024,6,64]{0,2,1:T(8,128)(2,1)S(1)} %bitcast.485, bf16[1024,6,64]{0,2,1:T(8,128)(2,1)S(1)} %bitcast.489), kind=kOutput, calls=%fused_computation.1 | convolution fusion | flops 830466048 | bytes 51953664 | tf_op jit(solution)/shard_map/qhe,khe->hqk/dot_general | solution.py:164
  811.0 21.7 %multiply_convert_fusion = bf16[6,1024,1024]{1,2,0:T(8,128)(2,1)} fusion(f32[6,1024,1024]{1,2,0:T(8,128)} %get-tuple-element.213, f32[6,1024,1024]{1,2,0:T(8,128)} %get-tuple-element.195, f32[6,1024]{1,0:T(8,128)S(1)} %get-tuple-element.212, f32[6,1024]{1,0:T(8,128)S(1)} %copy-done.118), kind=kLoop, calls=%fused_computation | loop fusion | flops 31457280 | bytes 62963712 | tf_op jit(solution)/shard_map/convert_element_type | solution.py:166
  832.7 8.6 multiply_bitcast_fusion
  862.1 8.8 collective-permute-done.72
  882.5 15.2 %collective-permute-done.68 = bf16[256,1664]{1,0:T(8,128)(2,1)} collective-permute-done((bf16[256,1664]{1,0:T(8,128)(2,1)}, bf16[256,1664]{1,0:T(8,128)(2,1)}, u32[]{:S(2)}, u32[]{:S(2)}) %collective-permute-start.68) | collective-permute-done | bytes 852000 | tf_op jit(solution)/shard_map/ppermute | solution.py:33
  915.8 14.8 %collective-permute-done.80 = bf16[28,16,384]{2,1,0:T(8,128)(2,1)S(1)} collective-permute-done((bf16[28,16,384]{2,1,0:T(8,128)(2,1)S(1)}, bf16[28,16,384]{2,1,0:T(8,128)(2,1)S(1)}, u32[]{:S(2)}, u32[]{:S(2)}) %collective-permute-start.80) | collective-permute-done | bytes 344096 | tf_op jit(solution)/shard_map/ppermute | solution.py:33
  944.0 7.3 collective-permute-done.83
  (894 shorter events, 513.4 us)
Async XLA Ops:
  11.2 74.2 %collective-permute-start.12 = (bf16[192,1920]{1,0:T(8,128)(2,1)}, bf16[192,1920]{1,0:T(8,128)(2,1)}, u32[]{:S(2)}, u32[]{:S(2)}) collective-permute-start(bf16[192,1920]{1,0:T(8,128)(2,1)} %constant_dynamic-update-slice_fusion), channel_id=1, source_target_pairs={{0,4},{4,0},{1,5},{5,1},{2,6},{6,2},{3,7},{7,3},{8,12},{12,8},{9,1... | collective-permute-start | bytes 2211848 | tf_op jit(solution)/shard_map/ppermute | solution.py:29
  77.0 76.6 %collective-permute-start.6 = (bf16[384,1152]{1,0:T(8,128)(2,1)}, bf16[384,1152]{1,0:T(8,128)(2,1)S(1)}, u32[]{:S(2)}, u32[]{:S(2)}) collective-permute-start(bf16[384,1152]{1,0:T(8,128)(2,1)} %constant_dynamic-update-slice_fusion.134), channel_id=1, source_target_pairs={{0,2},{6,4},{1,3},{7,5},{8,10},{14,12},{9,11},{15,13},{16,18},{22,... | collective-permute-start | bytes 2654216 | tf_op jit(solution)/shard_map/ppermute | solution.py:91
  84.0 148.4 %collective-permute-start.47 = (bf16[384,1536]{1,0:T(8,128)(2,1)}, bf16[384,1536]{1,0:T(8,128)(2,1)S(1)}, u32[]{:S(2)}, u32[]{:S(2)}) collective-permute-start(bf16[384,1536]{1,0:T(8,128)(2,1)} %constant_dynamic-update-slice_fusion.113), channel_id=1, source_target_pairs={{0,2},{6,4},{1,3},{7,5},{8,10},{14,12},{9,11},{15,13},{16,18},{22,... | collective-permute-start | bytes 3538952 | tf_op jit(solution)/shard_map/ppermute | solution.py:91
  85.5 152.4 %collective-permute-start.41 = (bf16[384,1536]{1,0:T(8,128)(2,1)S(1)}, bf16[384,1536]{1,0:T(8,128)(2,1)S(1)}, u32[]{:S(2)}, u32[]{:S(2)}) collective-permute-start(bf16[384,1536]{1,0:T(8,128)(2,1)S(1)} %constant_dynamic-update-slice_fusion.118), channel_id=1, source_target_pairs={{0,2},{6,4},{1,3},{7,5},{8,10},{14,12},{9,11},{15,13},{16,18},{22,... | collective-permute-start | bytes 3538952 | tf_op jit(solution)/shard_map/ppermute | solution.py:91
  88.1 138.1 %collective-permute-start.35 = (bf16[384,1536]{1,0:T(8,128)(2,1)}, bf16[384,1536]{1,0:T(8,128)(2,1)S(1)}, u32[]{:S(2)}, u32[]{:S(2)}) collective-permute-start(bf16[384,1536]{1,0:T(8,128)(2,1)} %constant_dynamic-update-slice_fusion.123), channel_id=1, source_target_pairs={{0,2},{6,4},{1,3},{7,5},{8,10},{14,12},{9,11},{15,13},{16,18},{22,... | collective-permute-start | bytes 3538952 | tf_op jit(solution)/shard_map/ppermute | solution.py:91
  89.7 66.3 %collective-permute-start.57 = (bf16[256,1536]{1,0:T(8,128)(2,1)S(1)}, bf16[256,1536]{1,0:T(8,128)(2,1)S(1)}, u32[]{:S(2)}, u32[]{:S(2)}) collective-permute-start(bf16[256,1536]{1,0:T(8,128)(2,1)S(1)} %collective-permute-done.56), channel_id=1, source_target_pairs={{0,4},{4,0},{1,5},{5,1},{2,6},{6,2},{3,7},{7,3},{8,12},{12,8},{9,1... | collective-permute-start | bytes 2359304 | tf_op jit(solution)/shard_map/ppermute | solution.py:29
  153.6 71.4 %collective-permute-start.58 = (bf16[256,1536]{1,0:T(8,128)(2,1)S(1)}, bf16[256,1536]{1,0:T(8,128)(2,1)}, u32[]{:S(2)}, u32[]{:S(2)}) collective-permute-start(bf16[256,1536]{1,0:T(8,128)(2,1)S(1)} %collective-permute-done.56), channel_id=1, source_target_pairs={{0,1},{1,0},{2,3},{3,2},{4,5},{5,4},{6,7},{7,6},{8,9},{9,8},{10,11... | collective-permute-start | bytes 2359304 | tf_op jit(solution)/shard_map/ppermute | solution.py:33
  156.0 100.3 %collective-permute-start.13 = (bf16[384,1920]{1,0:T(8,128)(2,1)S(1)}, bf16[384,1920]{1,0:T(8,128)(2,1)S(1)}, u32[]{:S(2)}, u32[]{:S(2)}) collective-permute-start(bf16[384,1920]{1,0:T(8,128)(2,1)S(1)} %constant_dynamic-update-slice_fusion.129), channel_id=1, source_target_pairs={{0,2},{6,4},{1,3},{7,5},{8,10},{14,12},{9,11},{15,13},{16,18},{22,... | collective-permute-start | bytes 4423688 | tf_op jit(solution)/shard_map/ppermute | solution.py:91
  254.7 104.2 %collective-permute-start.36 = (bf16[384,1536]{1,0:T(8,128)(2,1)}, bf16[384,1536]{1,0:T(8,128)(2,1)}, u32[]{:S(2)}, u32[]{:S(2)}) collective-permute-start(bf16[384,1536]{1,0:T(8,128)(2,1)} %get-tuple-element.42), channel_id=1, source_target_pairs={{0,8},{8,0},{16,24},{24,16},{1,9},{9,1},{17,25},{25,17},{2,10},{10... | collective-permute-start | bytes 3538952 | tf_op jit(solution)/shard_map/ppermute | solution.py:33
  256.4 104.2 %collective-permute-start.37 = (bf16[384,1536]{1,0:T(8,128)(2,1)}, bf16[384,1536]{1,0:T(8,128)(2,1)}, u32[]{:S(2)}, u32[]{:S(2)}) collective-permute-start(bf16[384,1536]{1,0:T(8,128)(2,1)} %get-tuple-element.42), channel_id=1, source_target_pairs={{0,16},{8,24},{16,0},{24,8},{1,17},{9,25},{17,1},{25,9},{2,18},{10... | collective-permute-start | bytes 3538952 | tf_op jit(solution)/shard_map/ppermute | solution.py:33
  260.0 102.1 %collective-permute-start.48 = (bf16[384,1536]{1,0:T(8,128)(2,1)}, bf16[384,1536]{1,0:T(8,128)(2,1)}, u32[]{:S(2)}, u32[]{:S(2)}) collective-permute-start(bf16[384,1536]{1,0:T(8,128)(2,1)} %get-tuple-element.38), channel_id=1, source_target_pairs={{0,8},{8,0},{16,24},{24,16},{1,9},{9,1},{17,25},{25,17},{2,10},{10... | collective-permute-start | bytes 3538952 | tf_op jit(solution)/shard_map/ppermute | solution.py:33
  292.0 87.9 %collective-permute-start.49 = (bf16[384,1536]{1,0:T(8,128)(2,1)}, bf16[384,1536]{1,0:T(8,128)(2,1)}, u32[]{:S(2)}, u32[]{:S(2)}) collective-permute-start(bf16[384,1536]{1,0:T(8,128)(2,1)} %get-tuple-element.38), channel_id=1, source_target_pairs={{0,16},{8,24},{16,0},{24,8},{1,17},{9,25},{17,1},{25,9},{2,18},{10... | collective-permute-start | bytes 3538952 | tf_op jit(solution)/shard_map/ppermute | solution.py:33
  315.6 67.8 %collective-permute-start.42 = (bf16[384,1536]{1,0:T(8,128)(2,1)}, bf16[384,1536]{1,0:T(8,128)(2,1)}, u32[]{:S(2)}, u32[]{:S(2)}) collective-permute-start(bf16[384,1536]{1,0:T(8,128)(2,1)} %get-tuple-element.40), channel_id=1, source_target_pairs={{0,8},{8,0},{16,24},{24,16},{1,9},{9,1},{17,25},{25,17},{2,10},{10... | collective-permute-start | bytes 3538952 | tf_op jit(solution)/shard_map/ppermute | solution.py:33
  362.1 57.5 %collective-permute-start.15 = (bf16[384,1920]{1,0:T(8,128)(2,1)S(1)}, bf16[384,1920]{1,0:T(8,128)(2,1)S(1)}, u32[]{:S(2)}, u32[]{:S(2)}) collective-permute-start(bf16[384,1920]{1,0:T(8,128)(2,1)S(1)} %copy-done.88), channel_id=1, source_target_pairs={{0,16},{8,24},{16,0},{24,8},{1,17},{9,25},{17,1},{25,9},{2,18},{10... | collective-permute-start | bytes 4423688 | tf_op jit(solution)/shard_map/ppermute | solution.py:33
  380.0 189.2 %collective-permute-start.39 = (bf16[192,1536]{1,0:T(8,128)(2,1)}, bf16[192,1536]{1,0:T(8,128)(2,1)}, u32[]{:S(2)}, u32[]{:S(2)}) collective-permute-start(bf16[192,1536]{1,0:T(8,128)(2,1)} %slice.1485), channel_id=1, source_target_pairs={{0,16},{8,24},{16,0},{24,8},{1,17},{9,25},{17,1},{25,9},{2,18},{10... | collective-permute-start | bytes 1769480 | tf_op jit(solution)/shard_map/ppermute | solution.py:33
  450.2 79.5 %collective-permute-start.29 = (bf16[1664,768]{1,0:T(8,128)(2,1)}, bf16[1664,768]{1,0:T(8,128)(2,1)}, u32[]{:S(2)}, u32[]{:S(2)}) collective-permute-start(bf16[1664,768]{1,0:T(8,128)(2,1)} %slice.1467), channel_id=1, source_target_pairs={{0,1},{1,0},{2,3},{3,2},{4,5},{5,4},{6,7},{7,6},{8,9},{9,8},{10,11... | collective-permute-start | bytes 7667720 | tf_op jit(solution)/shard_map/ppermute | solution.py:33
  455.4 72.4 %collective-permute-start.20 = (bf16[256,1664]{1,0:T(8,128)(2,1)}, bf16[256,1664]{1,0:T(8,128)(2,1)}, u32[]{:S(2)}, u32[]{:S(2)}) collective-permute-start(bf16[256,1664]{1,0:T(8,128)(2,1)} %fusion.27), channel_id=1, source_target_pairs={{0,1},{1,0},{2,3},{3,2},{4,5},{5,4},{6,7},{7,6},{8,9},{9,8},{10,11... | collective-permute-start | bytes 2555912 | tf_op jit(solution)/shard_map/ppermute | solution.py:33
  458.1 111.0 %collective-permute-start.38 = (bf16[192,1536]{1,0:T(8,128)(2,1)}, bf16[192,1536]{1,0:T(8,128)(2,1)}, u32[]{:S(2)}, u32[]{:S(2)}) collective-permute-start(bf16[192,1536]{1,0:T(8,128)(2,1)} %slice.1484), channel_id=1, source_target_pairs={{0,8},{8,0},{16,24},{24,16},{1,9},{9,1},{17,25},{25,17},{2,10},{10... | collective-permute-start | bytes 1769480 | tf_op jit(solution)/shard_map/ppermute | solution.py:33
  462.1 101.2 %collective-permute-start.51 = (bf16[192,1536]{1,0:T(8,128)(2,1)}, bf16[192,1536]{1,0:T(8,128)(2,1)}, u32[]{:S(2)}, u32[]{:S(2)}) collective-permute-start(bf16[192,1536]{1,0:T(8,128)(2,1)} %slice.1503), channel_id=1, source_target_pairs={{0,16},{8,24},{16,0},{24,8},{1,17},{9,25},{17,1},{25,9},{2,18},{10... | collective-permute-start | bytes 1769480 | tf_op jit(solution)/shard_map/ppermute | solution.py:33
  667.4 76.0 %collective-permute-start.52 = (bf16[256,1664]{1,0:T(8,128)(2,1)}, bf16[256,1664]{1,0:T(8,128)(2,1)}, u32[]{:S(2)}, u32[]{:S(2)}) collective-permute-start(bf16[256,1664]{1,0:T(8,128)(2,1)} %get-tuple-element.64), channel_id=1, source_target_pairs={{0,4},{4,0},{1,5},{5,1},{2,6},{6,2},{3,7},{7,3},{8,12},{12,8},{9,1... | collective-permute-start | bytes 2555912 | tf_op jit(solution)/shard_map/ppermute | solution.py:29
  747.8 196.3 %collective-permute-start.55 = (bf16[256,1536]{1,0:T(8,128)(2,1)}, bf16[256,1536]{1,0:T(8,128)(2,1)}, u32[]{:S(2)}, u32[]{:S(2)}) collective-permute-start(bf16[256,1536]{1,0:T(8,128)(2,1)} %fusion.44), channel_id=1, source_target_pairs={{0,0},{2,4},{4,2},{6,6},{1,1},{3,5},{5,3},{7,7},{8,8},{10,12},{12,... | collective-permute-start | bytes 2359304 | tf_op jit(solution)/shard_map/ppermute | solution.py:37
  756.5 100.5 %collective-permute-start.71 = (bf16[130,768]{0,1:T(8,128)(2,1)}, bf16[130,768]{0,1:T(8,128)(2,1)}, u32[]{:S(2)}, u32[]{:S(2)}) collective-permute-start(bf16[130,768]{0,1:T(8,128)(2,1)} %pad_maximum_fusion.24), channel_id=1, source_target_pairs={{0,4},{4,0},{1,5},{5,1},{2,6},{6,2},{3,7},{7,3},{8,12},{12,8},{9,1... | collective-permute-start | bytes 599048 | tf_op jit(solution)/shard_map/ppermute | solution.py:29
  764.7 97.3 %collective-permute-start.70 = (bf16[130,768]{0,1:T(8,128)(2,1)}, bf16[130,768]{0,1:T(8,128)(2,1)}, u32[]{:S(2)}, u32[]{:S(2)}) collective-permute-start(bf16[130,768]{0,1:T(8,128)(2,1)} %pad_maximum_fusion.23), channel_id=1, source_target_pairs={{0,4},{4,0},{1,5},{5,1},{2,6},{6,2},{3,7},{7,3},{8,12},{12,8},{9,1... | collective-permute-start | bytes 599048 | tf_op jit(solution)/shard_map/ppermute | solution.py:29
  879.3 56.8 %collective-permute-start.73 = (bf16[130,384]{1,0:T(8,128)(2,1)}, bf16[130,384]{1,0:T(8,128)(2,1)}, u32[]{:S(2)}, u32[]{:S(2)}) collective-permute-start(bf16[130,384]{1,0:T(8,128)(2,1)} %get-tuple-element.92), channel_id=1, source_target_pairs={{0,4},{4,0},{1,5},{5,1},{2,6},{6,2},{3,7},{7,3},{8,12},{12,8},{9,1... | collective-permute-start | bytes 299528 | tf_op jit(solution)/shard_map/ppermute | solution.py:29
  (240 other events, 3879.9 us)

commit v2 on v1

v2 whole, which is shorter than its diff:
```python
import functools

import jax
import jax.numpy as jnp
from jax import lax
from jax.experimental import pallas as pl
from jax.experimental.pallas import tpu as pltpu
from jax.sharding import Mesh, PartitionSpec as P

HEAD_DIM = 64
ROT = 32
EPSILON = 1e-05
EXT = 128
CHUNKS = 3
F32 = jnp.float32
BF = jnp.bfloat16
SWAP = ((0, 1), (1, 0))
VMEM_LIMIT = 56 * 1024 * 1024


def dot(left, right):
    return jnp.dot(left, right, preferred_element_type=F32)


def dot_nt(left, right):
    return lax.dot_general(left, right, (((1,), (1,)), ((), ())), preferred_element_type=F32)


def dot_tn(left, right):
    return lax.dot_general(left, right, (((0,), (0,)), ((), ())), preferred_element_type=F32)


def after(x, *earlier):
    return lax.optimization_barrier((x, *earlier))[0]


def core_swap(x):
    return lax.ppermute(x, "core", SWAP)


def xor_move(x, axis, size, k):
    return lax.ppermute(x, axis, [(i, i ^ k) for i in range(size)])


def home_swap(x):
    return lax.ppermute(x, ("core", "zhi"), [(0, 0), (1, 2), (2, 1), (3, 3)])


class Group:
    def __init__(self, pairs, chips):
        self.pairs, self.chips = pairs, chips
        self.core, self.zhi, self.p = (lax.axis_index(n) for n in ("core", "zhi", "p"))
        self.chip = lax.axis_index("chip")
        self.home = self.core == self.zhi
        self.pieces = [
            (self.core ^ kc) * pairs + (self.p ^ kp) for kp in range(pairs) for kc in (0, 1)
        ]

    def gather(self, own):
        blocks = [own, core_swap(own)]
        for k in range(1, self.pairs):
            far = xor_move(own, "p", self.pairs, k)
            blocks += [far, core_swap(far)]
        return blocks

    def scatter(self, partials):
        sums = [
            partials[2 * k].astype(F32) + core_swap(partials[2 * k + 1].astype(BF)).astype(F32)
            for k in reversed(range(self.pairs))
        ][::-1]
        total = sums[0]
        for k in range(1, self.pairs):
            total = total + xor_move(sums[k].astype(BF), "p", self.pairs, k).astype(F32)
        return total

    def spread_chips(self, block):
        got = {0: block}
        if self.chips == 4:
            got[1] = xor_move(block, "chip", 4, 1)
            got[2] = xor_move(block, "chip", 4, 2)
            half = block.shape[0] // 2
            got[3] = jnp.concatenate(
                [
                    xor_move(got[2][:half], "chip", 4, 1),
                    xor_move(got[1][half:], "chip", 4, 2),
                ],
                axis=0,
            )
        else:
            for k in range(1, self.chips):
                got[k] = xor_move(block, "chip", self.chips, k)
        return [got[k] for k in range(self.chips)]

    def pair_shard(self, shard):
        rows, columns = shard.shape
        other = core_swap(shard)
        both = jnp.zeros((2 * rows, columns), shard.dtype)
        both = lax.dynamic_update_slice(both, shard, (self.core * rows, 0))
        return lax.dynamic_update_slice(both, other, ((1 - self.core) * rows, 0))

    def cross_shard(self, both):
        far = lax.ppermute(both, ("core", "zhi"), [(0, 1), (3, 2)])
        return jnp.where(self.home, both, far)

    def assemble(self, blocks, low):
        rows, columns = blocks[0].shape
        whole = jnp.zeros((rows * self.chips + EXT, columns), blocks[0].dtype)
        for k, block in enumerate(blocks):
            whole = lax.dynamic_update_slice(whole, block, ((self.chip ^ k) * rows, 0))
        return lax.dynamic_update_slice(whole, low, (rows * self.chips, 0))


def stats(stream):
    average = jnp.mean(stream, axis=-1, keepdims=True)
    centred = stream - average
    variance = jnp.mean(centred * centred, axis=-1, keepdims=True)
    scale = lax.rsqrt(variance + EPSILON)
    return centred * scale, scale


def layer_norm(stream, gain, bias):
    return (stats(stream)[0] * gain + bias).astype(BF)


def norm_backward(stream, gain, grad):
    unit, scale = stats(stream)
    grad = grad * gain
    return scale * (
        grad
        - jnp.mean(grad, axis=-1, keepdims=True)
        - unit * jnp.mean(grad * unit, axis=-1, keepdims=True)
    )


def turn(x, cosines, left_sines, right_sines):
    breadth = 2 * HEAD_DIM if x.shape[1] % (2 * HEAD_DIM) == 0 else HEAD_DIM
    half = ROT // 2
    for at in range(0, x.shape[1], breadth):
        group = x[:, at : at + breadth]
        if breadth % 128 == 0:
            left, right = pltpu.roll(group, breadth - half, 1), pltpu.roll(group, half, 1)
        else:
            left = jnp.concatenate([group[:, half:], group[:, :half]], axis=1)
            right = jnp.concatenate([group[:, -half:], group[:, :-half]], axis=1)
        yield (
            at,
            breadth,
            group * cosines[:, :breadth]
            + left * left_sines[:, :breadth]
            + right * right_sines[:, :breadth],
        )


def whole_spec(shape):
    return pl.BlockSpec(shape, lambda *_: (0,) * len(shape))


def row_spec(rows, columns):
    return pl.BlockSpec((rows, columns), lambda t: (t, 0))


def params(semantics=1):
    return pltpu.CompilerParams(
        dimension_semantics=("arbitrary",) * semantics, vmem_limit_bytes=VMEM_LIMIT
    )


def cost(flops, moved, exps=0):
    return pl.CostEstimate(flops=int(flops), bytes_accessed=int(moved), transcendentals=int(exps))


def sds(shape, dtype):
    return jax.ShapeDtypeStruct(shape, dtype)


def query_kernel(
    x_ref, gain_ref, bias_ref, down_ref, w_ref, cos_ref, left_ref, right_ref,
    q_ref, k_ref, v_ref, low_ref,
):
    local, width = q_ref.shape[1], x_ref.shape[1]
    normed = layer_norm(x_ref[...].astype(F32), gain_ref[...], bias_ref[...])
    low = dot_nt(normed, down_ref[...]).astype(BF)
    low_ref[...] = low
    mixed = dot(normed, w_ref[:width, :]) + dot(low, w_ref[width:, :])
    tables = cos_ref[...], left_ref[...], right_ref[...]
    for at, breadth, turned in turn(mixed[:, :local], *tables):
        q_ref[:, at : at + breadth] = (turned * HEAD_DIM**-0.5).astype(BF)
    for at, breadth, turned in turn(mixed[:, local : 2 * local], *tables):
        k_ref[:, at : at + breadth] = turned.astype(BF)
    v_ref[...] = mixed[:, 2 * local :].astype(BF)


def project_self(x, gain, bias, down, weight, tables, rows):
    tokens, width = x.shape
    local = weight.shape[1] // 3
    return pl.pallas_call(
        query_kernel,
        grid=(tokens // rows,),
        in_specs=[
            row_spec(rows, width),
            whole_spec(gain.shape),
            whole_spec(bias.shape),
            whole_spec(down.shape),
            whole_spec(weight.shape),
            *[row_spec(rows, t.shape[1]) for t in tables],
        ],
        out_specs=[row_spec(rows, local)] * 3 + [row_spec(rows, EXT)],
        out_shape=[sds((tokens, local), BF)] * 3 + [sds((tokens, EXT), BF)],
        compiler_params=params(),
        cost_estimate=cost(2 * tokens * weight.size, 2 * (x.size + weight.size)),
    )(x, gain, bias, down, weight, *tables)


def attend_kernel(q_ref, k_ref, v_ref, w_ref, y_ref, o_ref, lse_ref):
    rows, local = q_ref.shape
    lanes = lax.broadcasted_iota(jnp.int32, (rows, EXT), 1)
    logsums = jnp.zeros((rows, EXT), F32)
    for head in range(local // HEAD_DIM):
        at = slice(head * HEAD_DIM, (head + 1) * HEAD_DIM)
        scores = dot_nt(q_ref[:, at], k_ref[:, at])
        top = jnp.max(scores, axis=1, keepdims=True)
        powers = jnp.exp(scores - top)
        total = jnp.sum(powers, axis=1, keepdims=True)
        out = dot(powers.astype(BF), v_ref[:, at]) / total
        o_ref[:, at] = out.astype(BF)
        logsums = jnp.where(lanes == head, top + jnp.log(total), logsums)
    lse_ref[...] = logsums.T[: lse_ref.shape[0]]
    y_ref[...] = dot_nt(o_ref[...], w_ref[...]).astype(BF)


def attend_self(query, keys, values, weight, rows):
    tokens, local = query.shape
    heads = -(-local // HEAD_DIM // 8) * 8
    return pl.pallas_call(
        attend_kernel,
        grid=(tokens // rows,),
        in_specs=[
            row_spec(rows, local),
            whole_spec(keys.shape),
            whole_spec(values.shape),
            whole_spec(weight.shape),
        ],
        out_specs=[
            row_spec(rows, weight.shape[0]),
            row_spec(rows, local),
            pl.BlockSpec((heads, rows), lambda t: (0, t)),
        ],
        out_shape=[
            sds((tokens, weight.shape[0]), BF),
            sds((tokens, local), BF),
            sds((heads, tokens), F32),
        ],
        compiler_params=params(),
        cost_estimate=cost(
            16 * tokens * tokens * local, 10 * query.size, tokens * tokens * local // HEAD_DIM
        ),
    )(query, keys, values, weight)


def attend_back_kernel(
    g_ref, up_ref, w_ref, q_ref, k_ref, v_ref, o_ref, lse_ref, cos_ref, left_ref, right_ref, low_ref,
    m_ref, down_ref, gup_ref, gk_ref, gv_ref,
):
    step, rows = pl.program_id(0), q_ref.shape[0]
    width, local = g_ref.shape[1], q_ref.shape[1]
    at_rows = pl.ds(pl.multiple_of(step * rows, rows), rows)

    @pl.when(step == 0)
    def _():
        gk_ref[...] = jnp.zeros_like(gk_ref)
        gv_ref[...] = jnp.zeros_like(gv_ref)
        down_ref[...] = jnp.zeros_like(down_ref)

    grad = g_ref[...]
    grad_low = dot_nt(grad, up_ref[...]).astype(BF)
    grad_out = (dot(grad, w_ref[:width, :]) + dot(grad_low, w_ref[width:, :])).astype(BF)
    out = o_ref[...]
    down_ref[...] += dot_tn(grad_low, out)[: down_ref.shape[0]]
    product = grad_out.astype(F32) * out.astype(F32)
    ones = jnp.ones((8, HEAD_DIM), F32)
    parts = []
    for head in range(local // HEAD_DIM):
        at = slice(head * HEAD_DIM, (head + 1) * HEAD_DIM)
        q, k, v, g = q_ref[:, at], k_ref[:, at], v_ref[:, at], grad_out[:, at]
        delta = lax.dot_general(
            ones, product[:, at], (((1,), (1,)), ((), ())),
            precision=lax.Precision.HIGHEST, preferred_element_type=F32,
        )[:1]
        probs = jnp.exp(dot_nt(k, q) - lse_ref[head : head + 1, :])
        grad_scores = (probs * (dot_nt(v, g) - delta)).astype(BF)
        gv_ref[:, at] += dot(probs.astype(BF), g)
        gk_ref[:, at] += dot(grad_scores, q)
        parts.append(dot_tn(grad_scores, k) * HEAD_DIM**-0.5)
    tables = cos_ref[at_rows, :], -left_ref[at_rows, :], -right_ref[at_rows, :]
    for at, breadth, turned in turn(jnp.concatenate(parts, axis=1), *tables):
        m_ref[at_rows, at : at + breadth] = turned.astype(BF)

    @pl.when(step == pl.num_programs(0) - 1)
    def _():
        tables = cos_ref[...], -left_ref[...], -right_ref[...]
        for at, breadth, turned in turn(gk_ref[...], *tables):
            m_ref[:, local + at : local + at + breadth] = turned.astype(BF)
        m_ref[:, 2 * local :] = gv_ref[...].astype(BF)
        gup_ref[...] = dot_tn(low_ref[...], m_ref[...])[: gup_ref.shape[0]]


def attend_back(grad, up, weight, query, keys, values, out, lse, tables, low, rank, rows):
    tokens, local = query.shape
    width = grad.shape[1]
    return pl.pallas_call(
        attend_back_kernel,
        grid=(tokens // rows,),
        in_specs=[
            row_spec(rows, width),
            whole_spec(up.shape),
            whole_spec(weight.shape),
            row_spec(rows, local),
            whole_spec(keys.shape),
            whole_spec(values.shape),
            row_spec(rows, local),
            pl.BlockSpec((lse.shape[0], rows), lambda t: (0, t)),
            *[whole_spec(t.shape) for t in tables],
            whole_spec(low.shape),
        ],
        out_specs=[
            whole_spec((tokens, 3 * local)),
            whole_spec((rank, local)),
            whole_spec((rank, 3 * local)),
        ],
        out_shape=[
            sds((tokens, 3 * local), BF),
            sds((rank, local), F32),
            sds((rank, 3 * local), F32),
        ],
        scratch_shapes=[pltpu.VMEM((tokens, local), F32)] * 2,
        compiler_params=params(),
        cost_estimate=cost(
            40 * tokens * tokens * local, 10 * query.size, tokens * tokens * local // HEAD_DIM
        ),
    )(grad, up, weight, query, keys, values, out, lse, *tables, low)


def cross_kernel(members, local, *refs):
    (x_ref, y_ref, up_self_ref, up_cross_ref, down_ref, gain_ref, bias_ref), refs = refs[:7], refs[7:]
    weights, refs = refs[:members], refs[members:]
    keyvals, refs = refs[:members], refs[members:]
    s1_ref, s2_ref, n2_ref, n3_ref, q_ref, o_ref, lse_ref, z2_ref, u_ref, z4_ref = refs
    width = x_ref.shape[1]
    rows = x_ref.shape[0]
    low = y_ref[:, width:].astype(BF)
    z2_ref[...] = low
    stream = x_ref[...].astype(F32) + y_ref[:, :width] + dot(low, up_self_ref[...])
    s1_ref[...] = stream
    normed = layer_norm(stream, gain_ref[1:2, :], bias_ref[1:2, :])
    n2_ref[...] = normed
    low = dot_nt(normed, down_ref[...]).astype(BF)
    u_ref[...] = low
    lanes = lax.broadcasted_iota(jnp.int32, (rows, EXT), 1)
    logsums = jnp.zeros((rows, EXT), F32)
    total = jnp.zeros((rows, width + EXT), F32)
    for k in range(members):
        weight, keyval = weights[k][...], keyvals[k][...]
        query = dot(normed, weight[:width, :local]) + dot(low, weight[width:, :local])
        query = (query * HEAD_DIM**-0.5).astype(BF)
        q_ref[:, k * local : (k + 1) * local] = query
        parts = []
        for head in range(local // HEAD_DIM):
            at = slice(head * HEAD_DIM, (head + 1) * HEAD_DIM)
            scores = dot_nt(query[:, at], keyval[:, at])
            top = jnp.max(scores, axis=1, keepdims=True)
            powers = jnp.exp(scores - top)
            sums = jnp.sum(powers, axis=1, keepdims=True)
            values = keyval[:, local + head * HEAD_DIM : local + (head + 1) * HEAD_DIM]
            parts.append((dot(powers.astype(BF), values) / sums).astype(BF))
            number = k * (local // HEAD_DIM) + head
            logsums = jnp.where(lanes == number, top + jnp.log(sums), logsums)
        out = jnp.concatenate(parts, axis=1)
        o_ref[:, k * local : (k + 1) * local] = out
        total = total + dot_nt(out, weight[:, local:])
    lse_ref[...] = logsums
    low = total[:, width:].astype(BF)
    z4_ref[...] = low
    stream = stream + total[:, :width] + dot(low, up_cross_ref[...])
    s2_ref[...] = stream
    n3_ref[...] = layer_norm(stream, gain_ref[2:3, :], bias_ref[2:3, :])


def cross_forward(x, y, up_self, up_cross, down, gains, biases, weights, keyvals):
    rows, width = x.shape
    members, local = len(weights), weights[0].shape[1] // 2
    plain, wide = sds((rows, width), BF), sds((rows, width), F32)
    low = sds((rows, EXT), BF)
    return pl.pallas_call(
        functools.partial(cross_kernel, members, local),
        out_shape=[wide, wide, plain, plain, plain, plain, sds((rows, EXT), F32), low, low, low],
        compiler_params=pltpu.CompilerParams(vmem_limit_bytes=VMEM_LIMIT),
        cost_estimate=cost(6 * rows * width * width, 8 * width * width),
    )(x, y, up_self, up_cross, down, gains, biases, *weights, *keyvals)


def cross_back_kernel(members, local, *refs):
    (
        g_ref, dn_ref, s1_ref, s2_ref, n2_ref, q_ref, o_ref, lse_ref, u_ref, z4_ref,
        up_ref, down5_ref, down2_ref, gain_ref, bias_ref,
    ), refs = refs[:15], refs[15:]
    weights, refs = refs[:members], refs[members:]
    keyvals, refs = refs[:members], refs[members:]
    r1_ref, r1b_ref, gup7_ref, gdown4_ref, gup4_ref, gdown2_ref, gdown5_ref, *gkv_refs = refs
    width = g_ref.shape[1]
    rank = gup7_ref.shape[0]
    stream = s2_ref[...]
    low = dn_ref[:, width:].astype(BF)
    grad_normed = dn_ref[:, :width] + dot(low, down5_ref[...])
    normed = layer_norm(stream, gain_ref[2:3, :], bias_ref[2:3, :])
    gdown5_ref[...] = dot_tn(low, normed)[:rank]
    grad = g_ref[...].astype(F32) + norm_backward(stream, gain_ref[2:3, :], grad_normed)
    branch = grad.astype(BF)
    low = dot_nt(branch, up_ref[...]).astype(BF)
    gup7_ref[...] = dot_tn(z4_ref[...], branch)[:rank]
    gdown4_ref[...] = dot_tn(low, o_ref[...])[:rank]
    total = jnp.zeros((g_ref.shape[0], width + EXT), F32)
    for k in range(members):
        weight, keyval = weights[k][...], keyvals[k][...]
        columns = slice(k * local, (k + 1) * local)
        grad_out = dot(branch, weight[:width, local:]) + dot(low, weight[width:, local:])
        grad_out = grad_out.astype(BF)
        out, query = o_ref[:, columns], q_ref[:, columns]
        product = grad_out.astype(F32) * out.astype(F32)
        queries, keys, values = [], [], []
        for head in range(local // HEAD_DIM):
            at = slice(head * HEAD_DIM, (head + 1) * HEAD_DIM)
            number = k * (local // HEAD_DIM) + head
            key, q, g = keyval[:, at], query[:, at], grad_out[:, at]
            value = keyval[:, local + head * HEAD_DIM : local + (head + 1) * HEAD_DIM]
            delta = jnp.sum(product[:, at], axis=1, keepdims=True)
            probs = jnp.exp(dot_nt(q, key) - lse_ref[:, number : number + 1])
            grad_scores = (probs * (dot_nt(g, value) - delta)).astype(BF)
            queries.append((dot(grad_scores, key) * HEAD_DIM**-0.5).astype(BF))
            keys.append(dot_tn(grad_scores, q))
            values.append(dot_tn(probs.astype(BF), g))
        grad_query = jnp.concatenate(queries, axis=1)
        gkv_refs[k][...] = jnp.concatenate(keys + values, axis=1).astype(BF)
        gup4_ref[:, columns] = dot_tn(u_ref[...], grad_query)[:rank]
        total = total + dot_nt(grad_query, weight[:, :local])
    low = total[:, width:].astype(BF)
    gdown2_ref[...] = dot_tn(low, n2_ref[...])[:rank]
    grad_normed = total[:, :width] + dot(low, down2_ref[...])
    grad = grad + norm_backward(s1_ref[...], gain_ref[1:2, :], grad_normed)
    r1_ref[...] = grad
    r1b_ref[...] = grad.astype(BF)


def cross_back(rank, g, dn, s1, s2, n2, q, o, lse, u, z4, up, down5, down2, gains, biases, weights, keyvals):
    rows, width = g.shape
    members, local = len(weights), weights[0].shape[1] // 2
    return pl.pallas_call(
        functools.partial(cross_back_kernel, members, local),
        out_shape=[sds((rows, width), F32), sds((rows, width), BF)]
        + [sds((rank, width), F32)] * 5
        + [sds(keyvals[0].shape, BF)] * members,
        compiler_params=pltpu.CompilerParams(vmem_limit_bytes=VMEM_LIMIT),
        cost_estimate=cost(8 * rows * width * width, 8 * width * width),
    )(g, dn, s1, s2, n2, q, o, lse, u, z4, up, down5, down2, gains, biases, *weights, *keyvals)


def feed_kernel(first, last, *refs):
    (n_ref, g_ref, down_ref, up_ref, gate_ref, upper_ref, out_ref), refs = refs[:7], refs[7:]
    if not first:
        (y_in, dn_in), refs = refs[:2], refs[2:]
    (y_ref, dn_ref, gdown_ref, ggate_ref, gupper_ref), refs = refs[:5], refs[5:]
    low_ref, glow_ref, y_sum, dn_sum = refs
    step, width = pl.program_id(0), n_ref.shape[1]
    rank = gdown_ref.shape[0]

    @pl.when(step == 0)
    def _():
        low_ref[...] = dot_nt(n_ref[...], down_ref[...]).astype(BF)
        glow_ref[...] = dot_nt(g_ref[...], up_ref[...]).astype(BF)
        if first:
            y_sum[...] = jnp.zeros_like(y_sum)
            dn_sum[...] = jnp.zeros_like(dn_sum)
        else:
            y_sum[...] = y_in[...]
            dn_sum[...] = dn_in[...]

    normed, low = n_ref[...], low_ref[...]
    grad, grad_low = g_ref[...], glow_ref[...]
    gate = dot(normed, gate_ref[:width, :]) + dot(low, gate_ref[width:, :])
    upper = dot(normed, upper_ref[:width, :]) + dot(low, upper_ref[width:, :])
    grad_unit = dot(grad, out_ref[:width, :]) + dot(grad_low, out_ref[width:, :])
    sigmoid = 1.0 / (1.0 + jnp.exp(-gate))
    acted = gate * sigmoid
    unit = (acted * upper).astype(BF)
    grad_gate = (grad_unit * upper * (sigmoid + acted * (1.0 - sigmoid))).astype(BF)
    grad_upper = (grad_unit * acted).astype(BF)
    y_sum[...] += dot_nt(unit, out_ref[...])
    dn_sum[...] += dot_nt(grad_gate, gate_ref[...]) + dot_nt(grad_upper, upper_ref[...])
    gdown_ref[...] = dot_tn(grad_low, unit)[:rank]
    ggate_ref[...] = dot_tn(low, grad_gate)[:rank]
    gupper_ref[...] = dot_tn(low, grad_upper)[:rank]

    @pl.when(step == pl.num_programs(0) - 1)
    def _():
        y_ref[...] = y_sum[...].astype(y_ref.dtype)
        dn_ref[...] = dn_sum[...].astype(dn_ref.dtype)


def feed(normed, grad, down, up, weight, rank, sums, last):
    tokens, width = normed.shape
    part = weight.shape[1] // 3
    block = min(256, part)
    steps = part // block
    deep = weight.shape[0]
    wide = sds((tokens, deep), BF if last else F32)
    narrow = sds((rank, part), F32)
    first = sums is None
    sums = () if first else sums

    def columns(number):
        return pl.BlockSpec((deep, block), lambda j: (0, number * steps + j))

    return pl.pallas_call(
        functools.partial(feed_kernel, first, last),
        grid=(steps,),
        in_specs=[whole_spec(a.shape) for a in (normed, grad, down, up)]
        + [columns(0), columns(1), columns(2)]
        + [whole_spec(a.shape) for a in sums],
        out_specs=[whole_spec(wide.shape)] * 2
        + [pl.BlockSpec((rank, block), lambda j: (0, j))] * 3,
        out_shape=[wide, wide, narrow, narrow, narrow],
        scratch_shapes=[pltpu.VMEM((tokens, EXT), BF)] * 2 + [pltpu.VMEM((tokens, deep), F32)] * 2,
        compiler_params=params(),
        cost_estimate=cost(4 * tokens * weight.size, 2 * weight.size + 16 * tokens * deep),
    )(normed, grad, down, up, weight, weight, weight, *sums)


def settle_kernel(fold, labels_ref, first_ref, second_ref, down_ref, up_ref, hid_ref, gate_ref):
    slot = pl.program_id(0)
    local = down_ref.shape[-1]
    for ref in (down_ref, up_ref, hid_ref, gate_ref):
        ref[...] = jnp.zeros_like(ref)
    for s in range(first_ref.shape[0]):

        @pl.when(labels_ref[s] == slot)
        def _(s=s):
            down_ref[0, 0:2] += second_ref[s, 0:2].astype(F32)
            down_ref[0, 2:6] += first_ref[s, 0:4].astype(F32)
            up_ref[0, 0:4] += second_ref[s, 2:6].astype(F32)
            up_ref[0, 4:9] += first_ref[s, 4:9].astype(F32)
            for k in range(fold):
                at = slice(k * local, (k + 1) * local)
                hid_ref[0, :, at] += first_ref[s, 9 + k].astype(F32)
                gate_ref[0, 0, :, at] += first_ref[s, 9 + fold + k].astype(F32)
                gate_ref[0, 1, :, at] += first_ref[s, 9 + 2 * fold + k].astype(F32)


def settle(labels, first, second, slots, fold):
    rank, local = first.shape[2:]
    hidden = fold * local
    shapes = [
        (slots, 6, rank, local),
        (slots, 9, rank, local),
        (slots, rank, hidden),
        (slots, 2, rank, hidden),
    ]
    return pl.pallas_call(
        functools.partial(settle_kernel, fold),
        grid_spec=pltpu.PrefetchScalarGridSpec(
            num_scalar_prefetch=1,
            grid=(slots,),
            in_specs=[whole_spec(first.shape), whole_spec(second.shape)],
            out_specs=[
                pl.BlockSpec((1,) + s[1:], lambda i, *_, n=len(s): (i,) + (0,) * (n - 1))
                for s in shapes
            ],
        ),
        out_shape=[sds(s, F32) for s in shapes],
        compiler_params=params(),
    )(labels, first, second)


def body(
    inputs,
    context,
    positions,
    adapter_index,
    self_in_weight,
    self_out_weight,
    cross_query_weight,
    cross_keyval_weight,
    cross_out_weight,
    feed_in_weight,
    feed_out_weight,
    norm_gains,
    norm_biases,
    adapter_down,
    adapter_down_hidden,
    adapter_up,
    adapter_up_hidden,
    out_cotangent,
    *,
    pairs,
    chips,
):
    group = Group(pairs, chips)
    members = 2 * pairs
    rows, width = inputs.shape[1], inputs.shape[2]
    local = self_in_weight.shape[2]
    hidden = feed_in_weight.shape[2]
    slots, rank = adapter_down.shape[0], adapter_down.shape[3]
    part = hidden // CHUNKS
    fold = hidden // local
    pieces = group.pieces
    gains, biases = norm_gains, norm_biases

    shards = [
        [self_in_weight[:, i] for i in range(3)],
        [
            self_out_weight.T,
            cross_query_weight,
            cross_out_weight.T,
            cross_keyval_weight[:, 0],
            cross_keyval_weight[:, 1],
        ],
    ]
    for i in range(CHUNKS):
        at = slice(i * part, (i + 1) * part)
        shards.append(
            [feed_in_weight[:, 0, at], feed_in_weight[:, 1, at], feed_out_weight.T[:, at]]
        )
    shards = [group.pair_shard(jnp.concatenate(s, axis=1)) for s in shards]

    index = jnp.where(group.home, adapter_index, core_swap(adapter_index))[0]
    positions = jnp.where(group.home, positions, core_swap(positions))[0]
    context_own = home_swap(context[0])
    ready = [group.cross_shard(shards[0])]
    stream_own = home_swap(after(inputs[0], ready[0]))
    ready.append(group.cross_shard(after(shards[1], stream_own)))
    cotangent_own = home_swap(after(out_cotangent[0], ready[1]))
    last = cotangent_own
    for shard in shards[2:]:
        ready.append(group.cross_shard(after(shard, last)))
        last = ready[-1]

    stream = group.gather(stream_own)
    context_blocks = group.gather(context_own)

    down = lax.dynamic_index_in_dim(adapter_down.transpose(0, 1, 3, 2), index, 0, keepdims=False)
    down_hidden = lax.dynamic_index_in_dim(
        adapter_down_hidden.transpose(0, 2, 1), index, 0, keepdims=False
    )
    up = lax.dynamic_index_in_dim(adapter_up.transpose(0, 2, 1, 3), index, 0, keepdims=False)
    up_hidden = lax.dynamic_index_in_dim(
        adapter_up_hidden.transpose(0, 2, 1, 3), index, 0, keepdims=False
    )

    def piece(array, k, size):
        return lax.dynamic_slice_in_dim(array, pieces[k] * size, size, array.ndim - 1)

    def own(array):
        return piece(array, 0, local)

    def tall(array):
        return jnp.pad(array, ((0, EXT - rank), (0, 0)))

    down_tall = [tall(down[i]) for i in range(6)]
    up_tall = {i: tall(up[i]) for i in (3, 7, 8)}
    feed_down = piece(down_hidden, 0, hidden)
    feed_up = piece(up_hidden, 0, hidden)
    lows = [
        [own(up[i]) for i in range(3)],
        [own(down[1]), own(up[4]), own(down[4]), own(up[5]), own(up[6])],
    ]
    for i in range(CHUNKS):
        at = slice(i * part, (i + 1) * part)
        lows.append([feed_up[0, :, at], feed_up[1, :, at], feed_down[:, at]])

    whole, last = [], None
    for shard, low in zip(ready, lows):
        blocks = group.spread_chips(shard if last is None else after(shard, last))
        last = blocks[1]
        whole.append(group.assemble(blocks, jnp.concatenate(low, axis=1)))
    self_in, rest, *feeds = whole
    self_out = rest[:, :local]
    cross_keyval = rest[:, 3 * local :]

    blocks_at = [
        lax.dynamic_slice_in_dim(positions, pieces[k] * rows, rows, 0) for k in range(members)
    ]
    half = ROT // 2
    lanes = jnp.arange(2 * HEAD_DIM)
    inverse = 10000.0 ** (-(lanes % half).astype(F32) / half)
    inverse = jnp.where(lanes % HEAD_DIM < ROT, inverse, 0.0)
    angles = jnp.concatenate(blocks_at).astype(F32)[:, None] * inverse
    sines = jnp.sin(angles)
    leading = lanes % HEAD_DIM < half
    tables = (
        jnp.cos(angles),
        jnp.where(leading, -sines, 0.0),
        jnp.where(leading, 0.0, sines),
    )

    tile = min(256, members * rows)
    stream_all = jnp.concatenate(stream, axis=0)
    query, keys, values, low_one = project_self(
        stream_all, gains[0:1], biases[0:1], down_tall[0], self_in, tables, tile
    )
    branch, heads, logsum = attend_self(query, keys, values, self_out, tile)

    def split_rows(x):
        return [x[k * rows : (k + 1) * rows] for k in range(members)]

    branch = group.scatter(split_rows(branch))

    cross_blocks = group.gather(rest[:, local : 3 * local])
    context_count = context_blocks[0].shape[0]
    context_all = jnp.zeros((members,) + context_blocks[0].shape, BF)
    for k in range(members):
        context_all = lax.dynamic_update_slice(
            context_all, context_blocks[k][None], (pieces[k], 0, 0)
        )
    context_all = context_all.transpose(1, 0, 2).reshape(context_count, width)
    low_context = dot_nt(context_all, down_tall[3]).astype(BF)
    keyval = dot(context_all, cross_keyval[:width]) + dot(low_context, cross_keyval[width:])
    keyval_blocks = group.gather(keyval.astype(BF))
    (
        stream_one, stream_two, normed_two, normed_three, query_cross, heads_cross, logsum_cross,
        low_two, low_three, low_four,
    ) = cross_forward(
        stream_own, branch, up_tall[3], up_tall[7], down_tall[2], gains, biases,
        cross_blocks, keyval_blocks,
    )

    def by_chip(blocks):
        return [
            jnp.concatenate(blocks[2 * k : 2 * k + 2], axis=0) for k in range(pairs)
        ]

    normed_parts = by_chip(group.gather(normed_three))
    cotangent_parts = by_chip(group.gather(cotangent_own))
    sums = [None] * pairs
    feed_grads = []
    for i, weight in enumerate(feeds):
        order = range(pairs)
        if i == CHUNKS - 1:
            order = reversed(order)
        found = []
        for k in order:
            y, dn, *grads = feed(
                normed_parts[k], cotangent_parts[k], down_tall[5], up_tall[8], weight, rank,
                sums[k], i == CHUNKS - 1,
            )
            sums[k] = (y, dn)
            found.append(grads)
        feed_grads.append([sum(g[1:], g[0]) for g in zip(*found)])

    def scatter_parts(parts):
        return group.scatter([p[at] for p in parts for at in (slice(0, rows), slice(rows, None))])

    grad_normed = scatter_parts([s[1] for s in sums])
    feed_sum = scatter_parts([s[0] for s in sums])
    low_six = feed_sum[:, width:].astype(BF)
    branch = feed_sum[:, :width] + dot(low_six, up_tall[8])
    block_output = home_swap((stream_two + branch).astype(BF))
    grad_up_eight = dot_tn(low_six, cotangent_own)[:rank]

    (
        grad_stream, branch_grad, grad_up_seven, grad_down_four, grad_up_four, grad_down_two,
        grad_down_five, *grad_keyval,
    ) = cross_back(
        rank, cotangent_own, grad_normed, stream_one, stream_two, normed_two, query_cross,
        heads_cross, logsum_cross, low_three, low_four, up_tall[7], down_tall[5], down_tall[2],
        gains, biases, cross_blocks, keyval_blocks,
    )

    branch_grads = group.gather(branch_grad)
    grad_up_three = dot_tn(low_two, branch_grad)[:rank]
    grad_mixed, grad_down_one, grad_up_self = attend_back(
        jnp.concatenate(branch_grads, axis=0), up_tall[3], self_out, query, keys, values, heads,
        logsum, tables, low_one, rank, tile,
    )
    grad_normed = scatter_parts(
        [
            dot_nt(grad_mixed[2 * k * rows : 2 * (k + 1) * rows], self_in).astype(BF)
            for k in range(pairs)
        ]
    )
    stream_zero = stream_own.astype(F32)
    grad_low = grad_normed[:, width:].astype(BF)
    grad_down_zero = dot_tn(grad_low, layer_norm(stream_zero, gains[0], biases[0]))[:rank]
    grad_normed = grad_normed[:, :width] + dot(grad_low, down_tall[0])
    grad_inputs = grad_stream + norm_backward(stream_zero, gains[0], grad_normed)
    grad_inputs = home_swap(grad_inputs.astype(BF)).astype(F32)

    grad_keyval = group.scatter(grad_keyval).astype(BF)
    total = dot_nt(grad_keyval, cross_keyval)
    grad_low = total[:, width:].astype(BF)
    grad_up_keyval = dot_tn(low_context, grad_keyval)[:rank]
    grad_down_three = dot_tn(grad_low, context_all)[:rank]
    context_partial = total[:, :width] + dot(grad_low, down_tall[3])
    grad_context = home_swap(
        group.scatter([piece(context_partial, k, local) for k in range(members)]).astype(BF)
    ).astype(F32)

    def gathered(partial, relative):
        return group.scatter(
            [
                jnp.concatenate(
                    [piece(g, k, local) for g in partial]
                    + [g[:, k * local : (k + 1) * local] for g in relative],
                    axis=0,
                )
                for k in range(members)
            ]
        ).reshape(-1, rank, local)

    def columns(array):
        return array.reshape(rank, -1, local).transpose(1, 0, 2)

    def every(parts):
        parts.append(jnp.full((1, rank, local), index, F32))
        grads = jnp.concatenate(parts, axis=0).astype(BF)
        both = jnp.stack([grads, xor_move(grads, "zhi", 2, 1)])
        both = jnp.where(group.home, both, core_swap(both))
        return jnp.concatenate(group.spread_chips(both), axis=0)

    summed = gathered(
        [grad_down_two, grad_down_three, grad_down_five, grad_up_seven, grad_up_eight],
        [grad_down_four, grad_up_four],
    )
    first = every(
        [
            summed[0:2],
            summed[5:6],
            summed[2:3],
            summed[6:7],
            columns(grad_up_keyval),
            summed[3:5],
            *[columns(jnp.concatenate(g, axis=1)) for g in zip(*feed_grads)],
        ]
    )
    summed = gathered([grad_down_zero, grad_up_three], [])
    second = every([summed[0:1], grad_down_one[None], columns(grad_up_self), summed[1:2]])
    grad_down, grad_up, grad_hidden, grad_gate = settle(
        first[:, -1, 0, 0].astype(jnp.int32), first, second, slots, fold
    )
    return (
        block_output[None],
        grad_inputs[None],
        grad_context[None],
        grad_down.transpose(0, 1, 3, 2),
        grad_hidden.transpose(0, 2, 1),
        grad_up.transpose(0, 2, 1, 3),
        grad_gate.transpose(0, 2, 1, 3),
    )


def solution(mesh):
    members = mesh.shape["tensor"]
    chips = mesh.shape["dp"] // 2
    mesh = Mesh(
        mesh.devices.reshape(chips, 2, 2, members // 2), ("chip", "core", "zhi", "p")
    )
    dp, tensor = ("chip", "core"), ("zhi", "p")
    in_specs = (
        P(dp, tensor, None),
        P(dp, None, tensor),
        P(dp, None),
        P(dp),
        P(dp, None, tensor),
        P(tensor, dp),
        P(dp, tensor),
        P(dp, None, tensor),
        P(tensor, dp),
        P(dp, None, tensor),
        P(tensor, dp),
        P(),
        P(),
        P(),
        P(),
        P(),
        P(),
        P(dp, tensor, None),
    )
    out_specs = (
        P(dp, tensor, None),
        P(dp, tensor, None),
        P(dp, None, tensor),
        P(None, None, tensor, None),
        P(None, tensor, None),
        P(None, None, None, tensor),
        P(None, None, None, tensor),
    )

    def run(*args):
        return body(*args, pairs=members // 2, chips=chips)

    return jax.shard_map(run, mesh=mesh, in_specs=in_specs, out_specs=out_specs, check_vma=False)
```

time: 1040 us -> 776 us (0.75)
  matrix products: 234 us -> 18.4 us
  Pallas kernels: 0 us -> 206 us
  local copies, waits for them, and re-layouts: 183 us -> 109 us
  other arithmetic: 108 us -> 42 us
  waiting for transfers between devices: 283 us -> 239 us
  between operations: 47.1 us -> 4.49 us
  starting transfers between devices: 166 us -> 147 us
    pallas_call x0 -> x12, Pallas kernels: none -> 206 us  [the longest x6 90.9 us: feed(): pl.pallas_call(functools.partial(feed_kernel, first, last), grid=(steps,)...]
    dot_general x12 -> x0, matrix products: 75 us -> none  [the longest x2 22.2 us: attend_backward(): jnp.einsum('qhe,khe->hqk', grad, values, preferred_element_type=F32)]
    ppermute x39 -> x45, waiting for transfers between devices: 280 us -> 210 us  [xor_move(): return lax.ppermute(x, axis, [(i, i ^ k) for i in range(size)])]
    dot_general x21 -> x4, matrix products: 82.6 us -> 14 us  [dot_nt(): lax.dot_general(left, right, (((1,), (1,)), ((), ())), preferred_element_...]
    dot_general x21 -> x5, matrix products: 60.2 us -> 1.95 us  [dot(): return jnp.dot(left, right, preferred_element_type=F32)]
    ppermute x36 -> x39, starting transfers between devices: 75.5 us -> 36.8 us  [core_swap(): return lax.ppermute(x, 'core', SWAP)]
    convert_element_type x8 -> x1, other arithmetic: 31.9 us -> 0.96 us  [body(): first[:, -1, 0, 0].astype(jnp.int32)]
    concatenate x14, local copies, waits for them, and re-layouts: 29.7 us -> 3.44 us  [the longest x4 2.63 us: by_chip(): jnp.concatenate(blocks[2 * k:2 * k + 2], axis=0)]
  transfers between devices with their start and end apart: 86 -> 95, of which waited for: 24 -> 32; matrix products, arithmetic and copies ran while one was open for 40% -> 19% of each run, Pallas kernels for 0% -> 21%
where the time goes in v2:
time: 776 us; the launch traced here: 765 us
  waiting for transfers between devices  239 us (31%)
  Pallas kernels  206 us (27%)
  starting transfers between devices  147 us (19%)
  local copies, waits for them, and re-layouts  109 us (14%)
  other arithmetic  42 us (5%)
  matrix products  18.4 us (2%)
    ppermute x45, waiting for transfers between devices, xor_move(): return lax.ppermute(x, axis, [(i, i ^ k) for i in range(size)])  210 us
    pallas_call x6, Pallas kernels, feed(): pl.pallas_call(functools.partial(feed_kernel, first, last), grid=(steps,)...  90.9 us
    ppermute x45, starting transfers between devices, xor_move(): return lax.ppermute(x, axis, [(i, i ^ k) for i in range(size)])  53.1 us
    ppermute x5, starting transfers between devices, cross_shard(): far = lax.ppermute(both, ('core', 'zhi'), [(0, 1), (3, 2)])  43.5 us
    ppermute x39, starting transfers between devices, core_swap(): return lax.ppermute(x, 'core', SWAP)  36.8 us
    pallas_call x1, Pallas kernels, attend_back(): pl.pallas_call(attend_back_kernel, grid=(tokens // rows,), in_specs=[row_...  31.3 us
    unnamed x284, local copies, waits for them, and re-layouts  29.7 us
    pallas_call x1, Pallas kernels, cross_back(): pl.pallas_call(functools.partial(cross_back_kernel, members, local), out_...  26.4 us
  transfers between devices with their start and end apart: 95, of which 32 were waited for; matrix products, arithmetic and copies ran while one was open for 19% of the time, Pallas kernels for 21%

profile of v2, /device:TPU:0, one launch (start us, length us, event | category | flops | bytes accessed | tf_op | source)
XLA Modules:
  0.0 765.4 jit_solution(11171612421469514783)
XLA Ops:
  54.9 10.6 %collective-permute-done.26 = bf16[130,384]{1,0:T(8,128)(2,1)S(1)} collective-permute-done((bf16[130,384]{1,0:T(8,128)(2,1)}, bf16[130,384]{1,0:T(8,128)(2,1)S(1)}, u32[]{:S(2)}, u32[]{:S(2)}) %collective-permute-start.26) | collective-permute-done | bytes 99872 | tf_op jit(solution)/shard_map/ppermute | solution.py:42
  98.8 15.6 %collective-permute-start.13 = (bf16[384,1920]{1,0:T(8,128)(2,1)S(1)}, bf16[384,1920]{1,0:T(8,128)(2,1)S(1)}, u32[]{:S(2)}, u32[]{:S(2)}) collective-permute-start(bf16[384,1920]{1,0:T(8,128)(2,1)S(1)} %constant_dynamic-update-slice_fusion.105), channel_id=1, source_target_pairs={{0,2},{6,4},{1,3},{7,5},{8,10},{14,12},{9,11},{15,13},{16,18},{22,... | collective-permute-start | bytes 4423688 | tf_op jit(solution)/shard_map/ppermute | solution.py:102
  133.1 16.2 %collective-permute-done.4 = bf16[256,1536]{1,0:T(8,128)(2,1)S(1)} collective-permute-done((bf16[256,1536]{1,0:T(8,128)(2,1)S(1)}, bf16[256,1536]{1,0:T(8,128)(2,1)S(1)}, u32[]{:S(2)}, u32[]{:S(2)}) %collective-permute-start.4) | collective-permute-done | bytes 786464 | tf_op jit(solution)/shard_map/ppermute | solution.py:42
  159.8 13.2 %shard_map.225 = (bf16[1024,384]{1,0:T(8,128)(2,1)}, bf16[1024,384]{1,0:T(8,128)(2,1)}, bf16[1024,384]{1,0:T(8,128)(2,1)}, bf16[1024,128]{1,0:T(8,128)(2,1)}) custom-call(bf16[1024,1536]{1,0:T(8,128)(2,1)} %pad_maximum_fusion.x_ref, f32[1,1536]{1,0:T(1,128)} %get-tuple-element.285.gain_ref, f32[1,1536]{1,0:T(1,128)} %get-tuple-element.272.bias_ref, ...), custom_call_target="tpu_custom_call" | custom-call | flops 3925868544 | bytes 6979584 | tf_op jit(solution)/shard_map/pallas_call | solution.py:196
  173.0 19.3 %collective-permute-start.37 = (bf16[384,1536]{1,0:T(8,128)(2,1)}, bf16[384,1536]{1,0:T(8,128)(2,1)S(1)}, u32[]{:S(2)}, u32[]{:S(2)}) collective-permute-start(bf16[384,1536]{1,0:T(8,128)(2,1)} %constant_dynamic-update-slice_fusion.95), channel_id=1, source_target_pairs={{0,2},{6,4},{1,3},{7,5},{8,10},{14,12},{9,11},{15,13},{16,18},{22,... | collective-permute-start | bytes 3538952 | tf_op jit(solution)/shard_map/ppermute | solution.py:102
  219.5 19.5 %shard_map.226 = (bf16[1024,1664]{1,0:T(8,128)(2,1)}, bf16[1024,384]{1,0:T(8,128)(2,1)}, f32[8,1024]{1,0:T(8,128)}) custom-call(bf16[1024,384]{1,0:T(8,128)(2,1)} %get-tuple-element.83.q_ref, bf16[1024,384]{1,0:T(8,128)(2,1)} %get-tuple-element.84.k_ref, bf16[1024,384]{1,0:T(8,128)(2,1)} %get-tuple-element.85.v_ref, bf16[1664,384]{1,0:T(8,128)(2,1)} %slice.492.w_ref), custom_call_target="tpu_custom_call" | custom-call | flops 6442450944 | bytes 3932160 | tf_op jit(solution)/shard_map/pallas_call | solution.py:234
  240.7 20.4 %collective-permute-start.19 = (bf16[256,1664]{1,0:T(8,128)(2,1)S(1)}, bf16[256,1664]{1,0:T(8,128)(2,1)S(1)}, u32[]{:S(2)}, u32[]{:S(2)}) collective-permute-start(bf16[256,1664]{1,0:T(8,128)(2,1)S(1)} %get-tuple-element.184), channel_id=1, source_target_pairs={{0,4},{4,0},{1,5},{5,1},{2,6},{6,2},{3,7},{7,3},{8,12},{12,8},{9,1... | collective-permute-start | bytes 2555912 | tf_op jit(solution)/shard_map/ppermute | solution.py:38
  276.9 19.0 %collective-permute-done.49 = bf16[384,1536]{1,0:T(8,128)(2,1)S(1)} collective-permute-done((bf16[384,1536]{1,0:T(8,128)(2,1)}, bf16[384,1536]{1,0:T(8,128)(2,1)S(1)}, u32[]{:S(2)}, u32[]{:S(2)}) %collective-permute-start.49) | collective-permute-done | bytes 1179680 | tf_op jit(solution)/shard_map/ppermute | solution.py:42
  312.9 21.1 %collective-permute-done.39 = bf16[384,1536]{1,0:T(8,128)(2,1)S(1)} collective-permute-done((bf16[384,1536]{1,0:T(8,128)(2,1)S(1)}, bf16[384,1536]{1,0:T(8,128)(2,1)S(1)}, u32[]{:S(2)}, u32[]{:S(2)}) %collective-permute-start.39) | collective-permute-done | bytes 1179680 | tf_op jit(solution)/shard_map/ppermute | solution.py:102
  338.8 15.6 %collective-permute-done.20 = bf16[256,1664]{1,0:T(8,128)(2,1)S(1)} collective-permute-done((bf16[256,1664]{1,0:T(8,128)(2,1)S(1)}, bf16[256,1664]{1,0:T(8,128)(2,1)S(1)}, u32[]{:S(2)}, u32[]{:S(2)}) %collective-permute-start.20) | collective-permute-done | bytes 852000 | tf_op jit(solution)/shard_map/ppermute | solution.py:42
  372.5 16.7 %collective-permute-done.43 = bf16[384,1536]{1,0:T(8,128)(2,1)S(1)} collective-permute-done((bf16[384,1536]{1,0:T(8,128)(2,1)S(1)}, bf16[384,1536]{1,0:T(8,128)(2,1)S(1)}, u32[]{:S(2)}, u32[]{:S(2)}) %collective-permute-start.43) | collective-permute-done | bytes 1179680 | tf_op jit(solution)/shard_map/ppermute | solution.py:42
  395.3 17.7 %shard_map.227 = (f32[256,1536]{1,0:T(8,128)}, f32[256,1536]{1,0:T(8,128)}, bf16[256,1536]{1,0:T(8,128)(2,1)}, bf16[256,1536]{1,0:T(8,128)(2,1)}, bf16[256,1536]...) custom-call(bf16[256,1536]{1,0:T(8,128)(2,1)} %copy-done.3, ...), custom_call_target="tpu_custom_call" | custom-call | flops 3623878656 | bytes 18874368 | tf_op jit(solution)/shard_map/pallas_call | solution.py:393
  434.6 14.0 %shard_map.228 = (f32[512,1664]{1,0:T(8,128)}, f32[512,1664]{1,0:T(8,128)}, f32[16,512]{1,0:T(8,128)}, f32[16,512]{1,0:T(8,128)}, f32[16,512]{1,0:T(8,128)}) custom-call(bf16[512,1536]{1,0:T(8,128)(2,1)} %copy-done.14, bf16[512,1536]{1,0:T(8,128)(2,1)} %copy-done.12, bf16[128,1536]{1,0:T(8,128)(2,1)} %pad.27.refs_2_.refs_11_, ...), custom_call_target="tpu_custom_call" | custom-call | flops 5234491392 | bytes 18743296 | tf_op jit(solution)/shard_map/pallas_call | solution.py:522
  451.0 13.9 %shard_map.231 = (f32[512,1664]{1,0:T(8,128)}, f32[512,1664]{1,0:T(8,128)}, f32[16,512]{1,0:T(8,128)}, f32[16,512]{1,0:T(8,128)}, f32[16,512]{1,0:T(8,128)}) custom-call(bf16[512,1536]{1,0:T(8,128)(2,1)} %copy-done.13, bf16[512,1536]{1,0:T(8,128)(2,1)} %copy-done.11, bf16[128,1536]{1,0:T(8,128)(2,1)} %pad.27.refs_2_.refs_11_, ...), custom_call_target="tpu_custom_call" | custom-call | flops 5234491392 | bytes 18743296 | tf_op jit(solution)/shard_map/pallas_call | solution.py:522
  464.9 16.5 %shard_map.232 = (f32[512,1664]{1,0:T(8,128)}, f32[512,1664]{1,0:T(8,128)}, f32[16,512]{1,0:T(8,128)}, f32[16,512]{1,0:T(8,128)}, f32[16,512]{1,0:T(8,128)}) custom-call(bf16[512,1536]{1,0:T(8,128)(2,1)} %copy-done.13, bf16[512,1536]{1,0:T(8,128)(2,1)} %copy-done.11, bf16[128,1536]{1,0:T(8,128)(2,1)} %pad.27.refs_2_.refs_11_, ...), custom_call_target="tpu_custom_call" | custom-call | flops 5234491392 | bytes 18743296 | tf_op jit(solution)/shard_map/pallas_call | solution.py:522
  481.4 15.0 %shard_map.233 = (bf16[512,1664]{1,0:T(8,128)(2,1)}, bf16[512,1664]{1,0:T(8,128)(2,1)}, f32[16,512]{1,0:T(8,128)}, f32[16,512]{1,0:T(8,128)}, f32[16,512]{1,0:T(8,128)}) custom-call(bf16[512,1536]{1,0:T(8,128)(2,1)} %copy-done.13, bf16[512,1536]{1,0:T(8,128)(2,1)} %copy-done.11, bf16[128,1536]{1,0:T(8,128)(2,1)} %pad.27.refs_2_.refs_11_, ...), custom_call_target="tpu_custom_call" | custom-call | flops 5234491392 | bytes 18743296 | tf_op jit(solution)/shard_map/pallas_call | solution.py:522
  498.2 16.2 %shard_map.229 = (f32[512,1664]{1,0:T(8,128)}, f32[512,1664]{1,0:T(8,128)}, f32[16,512]{1,0:T(8,128)}, f32[16,512]{1,0:T(8,128)}, f32[16,512]{1,0:T(8,128)}) custom-call(bf16[512,1536]{1,0:T(8,128)(2,1)} %copy-done.14, bf16[512,1536]{1,0:T(8,128)(2,1)} %copy-done.12, bf16[128,1536]{1,0:T(8,128)(2,1)} %pad.27.refs_2_.refs_11_, ...), custom_call_target="tpu_custom_call" | custom-call | flops 5234491392 | bytes 18743296 | tf_op jit(solution)/shard_map/pallas_call | solution.py:522
  514.4 15.2 %shard_map.230 = (bf16[512,1664]{1,0:T(8,128)(2,1)}, bf16[512,1664]{1,0:T(8,128)(2,1)}, f32[16,512]{1,0:T(8,128)}, f32[16,512]{1,0:T(8,128)}, f32[16,512]{1,0:T(8,128)}) custom-call(bf16[512,1536]{1,0:T(8,128)(2,1)} %copy-done.14, bf16[512,1536]{1,0:T(8,128)(2,1)} %copy-done.12, bf16[128,1536]{1,0:T(8,128)(2,1)} %pad.27.refs_2_.refs_11_, ...), custom_call_target="tpu_custom_call" | custom-call | flops 5234491392 | bytes 18743296 | tf_op jit(solution)/shard_map/pallas_call | solution.py:522
  536.7 19.3 %collective-permute-done.62 = bf16[256,1664]{1,0:T(8,128)(2,1)S(1)} collective-permute-done((bf16[256,1664]{1,0:T(8,128)(2,1)S(1)}, bf16[256,1664]{1,0:T(8,128)(2,1)S(1)}, u32[]{:S(2)}, u32[]{:S(2)}) %collective-permute-start.62) | collective-permute-done | bytes 852000 | tf_op jit(solution)/shard_map/ppermute | solution.py:42
  557.5 26.4 %shard_map.234 = (f32[256,1536]{1,0:T(8,128)}, bf16[256,1536]{1,0:T(8,128)(2,1)}, f32[16,1536]{1,0:T(8,128)}, f32[16,1536]{1,0:T(8,128)}, f32[16,1536]{1,0:T(8,1...) custom-call(bf16[256,1536]{1,0:T(8,128)(2,1)} %collective-permute-do, ...), custom_call_target="tpu_custom_call" | custom-call | flops 4831838208 | bytes 18874368 | tf_op jit(solution)/shard_map/pallas_call | solution.py:456
  592.0 23.4 %collective-permute-done.72 = bf16[130,768]{1,0:T(8,128)(2,1)S(1)} collective-permute-done((bf16[130,768]{1,0:T(8,128)(2,1)S(1)}, bf16[130,768]{1,0:T(8,128)(2,1)S(1)}, u32[]{:S(2)}, u32[]{:S(2)}) %collective-permute-start.72) | collective-permute-done | bytes 199712 | tf_op jit(solution)/shard_map/ppermute | solution.py:42
  625.7 14.2 %collective-permute-done.80 = bf16[22,16,384]{2,1,0:T(8,128)(2,1)S(1)} collective-permute-done((bf16[22,16,384]{2,1,0:T(8,128)(2,1)S(1)}, bf16[22,16,384]{2,1,0:T(8,128)(2,1)S(1)}, u32[]{:S(2)}, u32[]{:S(2)}) %collective-permute-start.80) | collective-permute-done | bytes 270368 | tf_op jit(solution)/shard_map/ppermute | solution.py:42
  642.3 31.3 %shard_map.235 = (bf16[1024,1152]{1,0:T(8,128)(2,1)}, f32[16,384]{1,0:T(8,128)}, f32[16,1152]{1,0:T(8,128)}) custom-call(bf16[1024,1536]{1,0:T(8,128)(2,1)} %pad_maximum_fusion.1.g_ref, bf16[128,1536]{1,0:T(8,128)(2,1)} %pad.23.refs_2_.up_ref, bf16[1664,384]{1,0:T(8,128)(2,1)} %slice.492.w_ref, bf16[1024,384]{1,0:T(8,128)(2,1)} %get-tuple-element.83.q_ref, ...), custom_call_target="tpu_custom_call" | custom-call | flops 16106127360 | bytes 3932160 | tf_op jit(solution)/shard_map/pallas_call | solution.py:310
  687.4 11.9 %collective-permute-done.83 = bf16[2,22,16,384]{3,2,1,0:T(8,128)(2,1)S(1)} collective-permute-done((bf16[2,22,16,384]{3,2,1,0:T(8,128)(2,1)S(1)}, bf16[2,22,16,384]{3,2,1,0:T(8,128)(2,1)S(1)}, u32[]{:S(2)}, u32[]{:S(2)}) %collective-permute-start.83) | collective-permute-done | bytes 540704 | tf_op jit(solution)/shard_map/ppermute | solution.py:42
  (653 shorter events, 338.9 us)
Async XLA Ops:
  5.7 42.8 %collective-permute-start = (bf16[192,1152]{1,0:T(8,128)(2,1)}, bf16[192,1152]{1,0:T(8,128)(2,1)}, u32[]{:S(2)}, u32[]{:S(2)}) collective-permute-start(bf16[192,1152]{1,0:T(8,128)(2,1)} %get-tuple-element.211), channel_id=1, source_target_pairs={{0,4},{4,0},{1,5},{5,1},{2,6},{6,2},{3,7},{7,3},{8,12},{12,8},{9,1... | collective-permute-start | bytes 1327112 | tf_op jit(solution)/shard_map/ppermute | solution.py:38
  6.2 46.2 %collective-permute-start.11 = (s32[1,1024]{1,0:T(1,128)}, s32[1,1024]{1,0:T(1,128)}, u32[]{:S(2)}, u32[]{:S(2)}) collective-permute-start(s32[1,1024]{1,0:T(1,128)} %param.20), channel_id=1, source_target_pairs={{0,4},{4,0},{1,5},{5,1},{2,6},{6,2},{3,7},{7,3},{8,12},{12,8},{9,1... | collective-permute-start | bytes 12296 | tf_op jit(solution)/shard_map/ppermute | solution.py:38
  10.5 87.1 %collective-permute-start.12 = (bf16[192,1920]{1,0:T(8,128)(2,1)}, bf16[192,1920]{1,0:T(8,128)(2,1)}, u32[]{:S(2)}, u32[]{:S(2)}) collective-permute-start(bf16[192,1920]{1,0:T(8,128)(2,1)} %constant_dynamic-update-slice_fusion), channel_id=1, source_target_pairs={{0,4},{4,0},{1,5},{5,1},{2,6},{6,2},{3,7},{7,3},{8,12},{12,8},{9,1... | collective-permute-start | bytes 2211848 | tf_op jit(solution)/shard_map/ppermute | solution.py:38
  10.6 42.6 %collective-permute-start.24 = (bf16[130,384]{1,0:T(8,128)(2,1)}, bf16[130,384]{1,0:T(8,128)(2,1)}, u32[]{:S(2)}, u32[]{:S(2)}) collective-permute-start(bf16[130,384]{1,0:T(8,128)(2,1)} %bitcast.28), channel_id=1, source_target_pairs={{0,0},{2,4},{4,2},{6,6},{1,1},{3,5},{5,3},{7,7},{8,8},{10,12},{12,... | collective-permute-start | bytes 299528 | tf_op jit(solution)/shard_map/ppermute | solution.py:46
  31.4 60.2 %collective-permute-start.34 = (bf16[192,1536]{1,0:T(8,128)(2,1)}, bf16[192,1536]{1,0:T(8,128)(2,1)}, u32[]{:S(2)}, u32[]{:S(2)}) collective-permute-start(bf16[192,1536]{1,0:T(8,128)(2,1)} %get-tuple-element.200), channel_id=1, source_target_pairs={{0,4},{4,0},{1,5},{5,1},{2,6},{6,2},{3,7},{7,3},{8,12},{12,8},{9,1... | collective-permute-start | bytes 1769480 | tf_op jit(solution)/shard_map/ppermute | solution.py:38
  98.8 50.5 %collective-permute-start.13 = (bf16[384,1920]{1,0:T(8,128)(2,1)S(1)}, bf16[384,1920]{1,0:T(8,128)(2,1)S(1)}, u32[]{:S(2)}, u32[]{:S(2)}) collective-permute-start(bf16[384,1920]{1,0:T(8,128)(2,1)S(1)} %constant_dynamic-update-slice_fusion.105), channel_id=1, source_target_pairs={{0,2},{6,4},{1,3},{7,5},{8,10},{14,12},{9,11},{15,13},{16,18},{22,... | collective-permute-start | bytes 4423688 | tf_op jit(solution)/shard_map/ppermute | solution.py:102
  149.5 44.0 %collective-permute-start.14 = (bf16[384,1920]{1,0:T(8,128)(2,1)S(1)}, bf16[384,1920]{1,0:T(8,128)(2,1)}, u32[]{:S(2)}, u32[]{:S(2)}) collective-permute-start(bf16[384,1920]{1,0:T(8,128)(2,1)S(1)} %broadcast_select_fusion), channel_id=1, source_target_pairs={{0,8},{8,0},{16,24},{24,16},{1,9},{9,1},{17,25},{25,17},{2,10},{10... | collective-permute-start | bytes 4423688 | tf_op jit(solution)/shard_map/ppermute | solution.py:42
  150.9 44.3 %collective-permute-start.15 = (bf16[384,1920]{1,0:T(8,128)(2,1)S(1)}, bf16[384,1920]{1,0:T(8,128)(2,1)}, u32[]{:S(2)}, u32[]{:S(2)}) collective-permute-start(bf16[384,1920]{1,0:T(8,128)(2,1)S(1)} %broadcast_select_fusion), channel_id=1, source_target_pairs={{0,16},{8,24},{16,0},{24,8},{1,17},{9,25},{17,1},{25,9},{2,18},{10... | collective-permute-start | bytes 4423688 | tf_op jit(solution)/shard_map/ppermute | solution.py:42
  159.4 40.9 %collective-permute-start.55 = (bf16[256,1536]{1,0:T(8,128)(2,1)}, bf16[256,1536]{1,0:T(8,128)(2,1)}, u32[]{:S(2)}, u32[]{:S(2)}) collective-permute-start(bf16[256,1536]{1,0:T(8,128)(2,1)} %collective-permute-done.32.refs_0_), channel_id=1, source_target_pairs={{0,1},{1,0},{2,3},{3,2},{4,5},{5,4},{6,7},{7,6},{8,9},{9,8},{10,11... | collective-permute-start | bytes 2359304 | tf_op jit(solution)/shard_map/ppermute | solution.py:42
  200.3 66.5 %collective-permute-start.56 = (bf16[256,1536]{1,0:T(8,128)(2,1)}, bf16[256,1536]{1,0:T(8,128)(2,1)}, u32[]{:S(2)}, u32[]{:S(2)}) collective-permute-start(bf16[256,1536]{1,0:T(8,128)(2,1)} %collective-permute-done.55), channel_id=1, source_target_pairs={{0,4},{4,0},{1,5},{5,1},{2,6},{6,2},{3,7},{7,3},{8,12},{12,8},{9,1... | collective-permute-start | bytes 2359304 | tf_op jit(solution)/shard_map/ppermute | solution.py:38
  208.6 60.2 %collective-permute-start.38 = (bf16[384,1536]{1,0:T(8,128)(2,1)}, bf16[384,1536]{1,0:T(8,128)(2,1)}, u32[]{:S(2)}, u32[]{:S(2)}) collective-permute-start(bf16[384,1536]{1,0:T(8,128)(2,1)} %constant_dynamic-update-slice_fusion.97), channel_id=1, source_target_pairs={{0,2},{6,4},{1,3},{7,5},{8,10},{14,12},{9,11},{15,13},{16,18},{22,... | collective-permute-start | bytes 3538952 | tf_op jit(solution)/shard_map/ppermute | solution.py:102
  213.7 58.9 %collective-permute-start.40 = (bf16[384,1536]{1,0:T(8,128)(2,1)}, bf16[384,1536]{1,0:T(8,128)(2,1)}, u32[]{:S(2)}, u32[]{:S(2)}) collective-permute-start(bf16[384,1536]{1,0:T(8,128)(2,1)} %broadcast_select_fusion.3), channel_id=1, source_target_pairs={{0,8},{8,0},{16,24},{24,16},{1,9},{9,1},{17,25},{25,17},{2,10},{10... | collective-permute-start | bytes 3538952 | tf_op jit(solution)/shard_map/ppermute | solution.py:42
  261.1 74.7 %collective-permute-start.22 = (bf16[1664,768]{1,0:T(8,128)(2,1)S(1)}, bf16[1664,768]{1,0:T(8,128)(2,1)S(1)}, u32[]{:S(2)}, u32[]{:S(2)}) collective-permute-start(bf16[1664,768]{1,0:T(8,128)(2,1)S(1)} %slice.496.refs_7_.refs_15_), channel_id=1, source_target_pairs={{0,1},{1,0},{2,3},{3,2},{4,5},{5,4},{6,7},{7,6},{8,9},{9,8},{10,11... | collective-permute-start | bytes 7667720 | tf_op jit(solution)/shard_map/ppermute | solution.py:42
  271.0 63.0 %collective-permute-start.39 = (bf16[384,1536]{1,0:T(8,128)(2,1)S(1)}, bf16[384,1536]{1,0:T(8,128)(2,1)S(1)}, u32[]{:S(2)}, u32[]{:S(2)}) collective-permute-start(bf16[384,1536]{1,0:T(8,128)(2,1)S(1)} %copy-done.23), channel_id=1, source_target_pairs={{0,2},{6,4},{1,3},{7,5},{8,10},{14,12},{9,11},{15,13},{16,18},{22,... | collective-permute-start | bytes 3538952 | tf_op jit(solution)/shard_map/ppermute | solution.py:102
  272.5 62.6 %collective-permute-start.41 = (bf16[384,1536]{1,0:T(8,128)(2,1)S(1)}, bf16[384,1536]{1,0:T(8,128)(2,1)S(1)}, u32[]{:S(2)}, u32[]{:S(2)}) collective-permute-start(bf16[384,1536]{1,0:T(8,128)(2,1)S(1)} %broadcast_select_fusion.2), channel_id=1, source_target_pairs={{0,8},{8,0},{16,24},{24,16},{1,9},{9,1},{17,25},{25,17},{2,10},{10... | collective-permute-start | bytes 3538952 | tf_op jit(solution)/shard_map/ppermute | solution.py:42
  307.7 86.1 %collective-permute-start.21 = (bf16[1664,768]{1,0:T(8,128)(2,1)S(1)}, bf16[1664,768]{1,0:T(8,128)(2,1)S(1)}, u32[]{:S(2)}, u32[]{:S(2)}) collective-permute-start(bf16[1664,768]{1,0:T(8,128)(2,1)S(1)} %slice.496.refs_7_.refs_15_), channel_id=1, source_target_pairs={{0,4},{4,0},{1,5},{5,1},{2,6},{6,2},{3,7},{7,3},{8,12},{12,8},{9,1... | collective-permute-start | bytes 7667720 | tf_op jit(solution)/shard_map/ppermute | solution.py:38
  335.7 58.8 %collective-permute-start.23 = (bf16[1664,768]{1,0:T(8,128)(2,1)S(1)}, bf16[1664,768]{1,0:T(8,128)(2,1)}, u32[]{:S(2)}, u32[]{:S(2)}) collective-permute-start(bf16[1664,768]{1,0:T(8,128)(2,1)S(1)} %collective-permute-done.22.refs_9_.refs_17_), channel_id=1, source_target_pairs={{0,4},{4,0},{1,5},{5,1},{2,6},{6,2},{3,7},{7,3},{8,12},{12,8},{9,1... | collective-permute-start | bytes 7667720 | tf_op jit(solution)/shard_map/ppermute | solution.py:38
  531.0 53.2 %collective-permute-start.52 = (bf16[256,1664]{1,0:T(8,128)(2,1)S(1)}, bf16[256,1664]{1,0:T(8,128)(2,1)S(1)}, u32[]{:S(2)}, u32[]{:S(2)}) collective-permute-start(bf16[256,1664]{1,0:T(8,128)(2,1)S(1)} %slice.419), channel_id=1, source_target_pairs={{0,4},{4,0},{1,5},{5,1},{2,6},{6,2},{3,7},{7,3},{8,12},{12,8},{9,1... | collective-permute-start | bytes 2555912 | tf_op jit(solution)/shard_map/ppermute | solution.py:38
  536.2 48.1 %collective-permute-start.58 = (bf16[256,1664]{1,0:T(8,128)(2,1)S(1)}, bf16[256,1664]{1,0:T(8,128)(2,1)S(1)}, u32[]{:S(2)}, u32[]{:S(2)}) collective-permute-start(bf16[256,1664]{1,0:T(8,128)(2,1)S(1)} %add_convert_fusion.2), channel_id=1, source_target_pairs={{0,1},{1,0},{2,3},{3,2},{4,5},{5,4},{6,7},{7,6},{8,9},{9,8},{10,11... | collective-permute-start | bytes 2555912 | tf_op jit(solution)/shard_map/ppermute | solution.py:42
  583.9 41.7 %collective-permute-start.64 = (bf16[256,1536]{1,0:T(8,128)(2,1)}, bf16[256,1536]{1,0:T(8,128)(2,1)S(1)}, u32[]{:S(2)}, u32[]{:S(2)}) collective-permute-start(bf16[256,1536]{1,0:T(8,128)(2,1)} %get-tuple-element.118), channel_id=1, source_target_pairs={{0,1},{1,0},{2,3},{3,2},{4,5},{5,4},{6,7},{7,6},{8,9},{9,8},{10,11... | collective-permute-start | bytes 2359304 | tf_op jit(solution)/shard_map/ppermute | solution.py:42
  584.2 55.7 %collective-permute-start.63 = (bf16[256,1536]{1,0:T(8,128)(2,1)}, bf16[256,1536]{1,0:T(8,128)(2,1)S(1)}, u32[]{:S(2)}, u32[]{:S(2)}) collective-permute-start(bf16[256,1536]{1,0:T(8,128)(2,1)} %get-tuple-element.118), channel_id=1, source_target_pairs={{0,4},{4,0},{1,5},{5,1},{2,6},{6,2},{3,7},{7,3},{8,12},{12,8},{9,1... | collective-permute-start | bytes 2359304 | tf_op jit(solution)/shard_map/ppermute | solution.py:38
  585.7 116.3 %collective-permute-start.59 = (bf16[256,1536]{1,0:T(8,128)(2,1)S(1)}, bf16[256,1536]{1,0:T(8,128)(2,1)S(1)}, u32[]{:S(2)}, u32[]{:S(2)}) collective-permute-start(bf16[256,1536]{1,0:T(8,128)(2,1)S(1)} %fusion.19), channel_id=1, source_target_pairs={{0,0},{2,4},{4,2},{6,6},{1,1},{3,5},{5,3},{7,7},{8,8},{10,12},{12,... | collective-permute-start | bytes 2359304 | tf_op jit(solution)/shard_map/ppermute | solution.py:46
  620.7 58.1 %collective-permute-start.74 = (bf16[130,384]{1,0:T(8,128)(2,1)S(1)}, bf16[130,384]{1,0:T(8,128)(2,1)S(1)}, u32[]{:S(2)}, u32[]{:S(2)}) collective-permute-start(bf16[130,384]{1,0:T(8,128)(2,1)S(1)} %get-tuple-element.192), channel_id=1, source_target_pairs={{0,4},{4,0},{1,5},{5,1},{2,6},{6,2},{3,7},{7,3},{8,12},{12,8},{9,1... | collective-permute-start | bytes 299528 | tf_op jit(solution)/shard_map/ppermute | solution.py:38
  639.9 45.9 %collective-permute-start.73 = (bf16[130,384]{1,0:T(8,128)(2,1)S(1)}, bf16[130,384]{1,0:T(8,128)(2,1)S(1)}, u32[]{:S(2)}, u32[]{:S(2)}) collective-permute-start(bf16[130,384]{1,0:T(8,128)(2,1)S(1)} %get-tuple-element.191), channel_id=1, source_target_pairs={{0,4},{4,0},{1,5},{5,1},{2,6},{6,2},{3,7},{7,3},{8,12},{12,8},{9,1... | collective-permute-start | bytes 299528 | tf_op jit(solution)/shard_map/ppermute | solution.py:38
  (180 other events, 2286.8 us)

commit v3 on v2

v3 whole, which is shorter than its diff:
```python
import functools

import jax
import jax.numpy as jnp
from jax import lax
from jax.experimental import pallas as pl
from jax.experimental.pallas import tpu as pltpu
from jax.sharding import Mesh, PartitionSpec as P

HEAD_DIM = 64
ROT = 32
EPSILON = 1e-05
F32 = jnp.float32
BF = jnp.bfloat16
SWAP = ((0, 1), (1, 0))
LANES = 128
VMEM_LIMIT = 56 * 1024 * 1024


def dot(left, right):
    return jnp.dot(left, right, preferred_element_type=F32)


def dot_nt(left, right):
    return lax.dot_general(left, right, (((1,), (1,)), ((), ())), preferred_element_type=F32)


def dot_tn(left, right):
    return lax.dot_general(left, right, (((0,), (0,)), ((), ())), preferred_element_type=F32)


class Order:
    def __init__(self, first):
        self.token = first

    def wait(self, *values):
        *values, self.token = lax.optimization_barrier((*values, self.token))
        return values[0] if len(values) == 1 else values

    mark = wait


def core_swap(x):
    return lax.ppermute(x, "core", SWAP)


def xor_move(x, axis, size, k):
    return lax.ppermute(x, axis, [(i, i ^ k) for i in range(size)])


def home_swap(x):
    return lax.ppermute(x, ("core", "zhi"), [(0, 0), (1, 2), (2, 1), (3, 3)])


def turned(x):
    return lax.ppermute(x, ("core", "zhi"), [(0, 1), (1, 3), (2, 0), (3, 2)])


def turned_back(x):
    return lax.ppermute(x, ("core", "zhi"), [(0, 2), (1, 0), (2, 3), (3, 1)])


class Group:
    def __init__(self, pairs, chips):
        self.pairs, self.chips = pairs, chips
        self.core, self.zhi, self.p = (lax.axis_index(n) for n in ("core", "zhi", "p"))
        self.chip = lax.axis_index("chip")
        self.home = self.core == self.zhi
        self.pieces = [
            (self.core ^ kc) * pairs + (self.p ^ kp) for kp in range(pairs) for kc in (0, 1)
        ]

    def far_p(self, own):
        return [xor_move(own, "p", self.pairs, k) for k in range(1, self.pairs)]

    def near_sums(self, own, other):
        return own.astype(F32) + other.astype(F32)

    def cross(self, shard):
        return xor_move(shard, "zhi", 2, 1)

    def spread_one(self, block):
        if self.chips == 4:
            return [xor_move(block, "chip", 4, k) for k in (1, 2)]
        return [xor_move(block, "chip", self.chips, k) for k in range(1, self.chips)]

    def spread_two(self, got):
        if self.chips != 4:
            return []
        half = got[0].shape[0] // 2
        return [xor_move(got[1][:half], "chip", 4, 1), xor_move(got[0][half:], "chip", 4, 2)]

    def places(self, rows):
        if self.chips == 4:
            diagonal = (self.chip ^ 3) * rows
            return [(self.chip ^ 1) * rows, (self.chip ^ 2) * rows, diagonal, diagonal + rows // 2]
        return [(self.chip ^ k) * rows for k in range(1, self.chips)]


def place_kernel(count, moves, olds, places_ref, *refs):
    sources, refs = refs[:count], refs[count + olds :]
    *targets, sems = refs
    copies = []
    for number, (source, row, rows, target, lead, place, offset) in enumerate(moves):
        at = pl.ds(pl.multiple_of(places_ref[place] + offset, 16), rows)
        to = targets[target].at[at] if lead is None else targets[target].at[lead, at]
        copy = pltpu.make_async_copy(
            sources[source].at[pl.ds(row, rows)], to, sems.at[number]
        )
        copy.start()
        copies.append(copy)
    for copy in copies:
        copy.wait()


def place(sources, moves, places, targets, fresh):
    shapes = [sds(t, BF) if fresh else sds(t.shape, BF) for t in targets]
    olds = () if fresh else tuple(targets)
    any_spec = pl.BlockSpec(memory_space=pl.ANY)
    return pl.pallas_call(
        functools.partial(place_kernel, len(sources), moves, len(olds)),
        grid_spec=pltpu.PrefetchScalarGridSpec(
            num_scalar_prefetch=1,
            grid=(1,),
            in_specs=[whole_spec(a.shape) for a in sources] + [any_spec] * len(olds),
            out_specs=[any_spec] * len(shapes),
            scratch_shapes=[pltpu.SemaphoreType.DMA((len(moves),))],
        ),
        out_shape=shapes,
        input_output_aliases={1 + len(sources) + i: i for i in range(len(olds))},
        compiler_params=params(),
        cost_estimate=cost(0, 0),
    )(places, *sources, *olds)


def stats(stream):
    average = jnp.mean(stream, axis=-1, keepdims=True)
    centred = stream - average
    variance = jnp.mean(centred * centred, axis=-1, keepdims=True)
    scale = lax.rsqrt(variance + EPSILON)
    return centred * scale, scale


def layer_norm(stream, gain, bias):
    return (stats(stream)[0] * gain + bias).astype(BF)


def norm_backward(stream, gain, grad):
    unit, scale = stats(stream)
    grad = grad * gain
    return scale * (
        grad
        - jnp.mean(grad, axis=-1, keepdims=True)
        - unit * jnp.mean(grad * unit, axis=-1, keepdims=True)
    )


def turn(x, cosines, left_sines, right_sines):
    breadth = 2 * HEAD_DIM if x.shape[1] % (2 * HEAD_DIM) == 0 else HEAD_DIM
    half = ROT // 2
    for at in range(0, x.shape[1], breadth):
        group = x[:, at : at + breadth]
        if breadth % 128 == 0:
            left, right = pltpu.roll(group, breadth - half, 1), pltpu.roll(group, half, 1)
        else:
            left = jnp.concatenate([group[:, half:], group[:, :half]], axis=1)
            right = jnp.concatenate([group[:, -half:], group[:, :-half]], axis=1)
        yield (
            at,
            breadth,
            group * cosines[:, :breadth]
            + left * left_sines[:, :breadth]
            + right * right_sines[:, :breadth],
        )


def whole_spec(shape):
    return pl.BlockSpec(shape, lambda *_: (0,) * len(shape))


def row_spec(rows, columns):
    return pl.BlockSpec((rows, columns), lambda t: (t, 0))


def take_tile(refs, tile_ref, step):
    rows, tile = refs[0].shape[0], tile_ref.shape[0]
    for i, ref in enumerate(refs):

        @pl.when(step == i * rows // tile)
        def _(i=i, ref=ref):
            tile_ref[i * rows % tile : i * rows % tile + rows, :] = ref[...]


def give_tile(value, refs, step):
    rows, (tile, columns) = refs[0].shape[0], value.shape
    for i, ref in enumerate(refs):

        @pl.when(step == i * rows // tile)
        def _(i=i, ref=ref):
            ref[:, :columns] = value[i * rows % tile : i * rows % tile + rows]
            ref[:, columns:] = jnp.zeros((rows, ref.shape[1] - columns), ref.dtype)


def total_of(refs):
    total = refs[0][...].astype(F32)
    for ref in refs[1:]:
        total = total + ref[...].astype(F32)
    return total


def by_piece(ref, row, value):
    local = ref.shape[2]
    for k in range(ref.shape[0]):
        ref[k, row : row + value.shape[0], :] = value[:, k * local : (k + 1) * local].astype(
            ref.dtype
        )


def columns_of(weight, start, size):
    if size % 128 == 0:
        return pl.BlockSpec((weight.shape[0], size), lambda *_: (0, start // size)), 0
    return whole_spec(weight.shape), start


def params(semantics=1):
    return pltpu.CompilerParams(
        dimension_semantics=("arbitrary",) * semantics, vmem_limit_bytes=VMEM_LIMIT
    )


def cost(flops, moved, exps=0):
    return pl.CostEstimate(flops=int(flops), bytes_accessed=int(moved), transcendentals=int(exps))


def sds(shape, dtype):
    return jax.ShapeDtypeStruct(shape, dtype)


def query_kernel(count, *refs):
    blocks, (gain_ref, bias_ref, down_ref, w_ref, cos_ref, left_ref, right_ref), refs = (
        refs[:count],
        refs[count : count + 7],
        refs[count + 7 :],
    )
    q_ref, k_ref, v_ref, low_ref, n_ref, x_ref = refs
    take_tile(blocks, x_ref, pl.program_id(0))
    local, width = q_ref.shape[1], x_ref.shape[1]
    normed = layer_norm(x_ref[...].astype(F32), gain_ref[...], bias_ref[...])
    n_ref[...] = normed
    low = dot_nt(normed, down_ref[...]).astype(BF)
    low_ref[...] = low
    mixed = dot(normed, w_ref[:width, : 3 * local]) + dot(low, w_ref[width:, : 3 * local])
    tables = cos_ref[...], left_ref[...], right_ref[...]
    for at, breadth, turned in turn(mixed[:, :local], *tables):
        q_ref[:, at : at + breadth] = (turned * HEAD_DIM**-0.5).astype(BF)
    for at, breadth, turned in turn(mixed[:, local : 2 * local], *tables):
        k_ref[:, at : at + breadth] = turned.astype(BF)
    v_ref[...] = mixed[:, 2 * local :].astype(BF)


def project_self(blocks, gain, bias, down, weight, tables, rows):
    width = blocks[0].shape[1]
    tokens = len(blocks) * blocks[0].shape[0]
    local = weight.shape[1] // 4
    spec, _ = columns_of(weight, 0, 3 * local)
    return pl.pallas_call(
        functools.partial(query_kernel, len(blocks)),
        grid=(tokens // rows,),
        in_specs=[whole_spec(b.shape) for b in blocks]
        + [whole_spec(gain.shape), whole_spec(bias.shape), whole_spec(down.shape), spec]
        + [row_spec(rows, t.shape[1]) for t in tables],
        out_specs=[row_spec(rows, local)] * 3
        + [row_spec(rows, down.shape[0]), row_spec(rows, width)],
        out_shape=[sds((tokens, local), BF)] * 3
        + [sds((tokens, down.shape[0]), BF), sds((tokens, width), BF)],
        scratch_shapes=[pltpu.VMEM((rows, width), BF)],
        compiler_params=params(),
        cost_estimate=cost(2 * tokens * weight.size, 2 * weight.size),
    )(*blocks, gain, bias, down, weight, *tables)


def attend_kernel(start, q_ref, k_ref, v_ref, w_ref, o_ref, lse_ref, *y_refs):
    rows, local = q_ref.shape
    lanes = lax.broadcasted_iota(jnp.int32, (rows, 128), 1)
    logsums = jnp.zeros((rows, 128), F32)
    for head in range(local // HEAD_DIM):
        at = slice(head * HEAD_DIM, (head + 1) * HEAD_DIM)
        scores = dot_nt(q_ref[:, at], k_ref[:, at])
        top = jnp.max(scores, axis=1, keepdims=True)
        powers = jnp.exp(scores - top)
        total = jnp.sum(powers, axis=1, keepdims=True)
        out = dot(powers.astype(BF), v_ref[:, at]) / total
        o_ref[:, at] = out.astype(BF)
        logsums = jnp.where(lanes == head, top + jnp.log(total), logsums)
    lse_ref[...] = logsums.T[: lse_ref.shape[0]]
    y = dot_nt(o_ref[...], w_ref[:, start : start + local]).astype(BF)
    give_tile(y, y_refs, pl.program_id(0))


def attend_self(query, keys, values, weight, rows, first, count, block):
    tokens, local = query.shape
    deep = weight.shape[0] // LANES * LANES + LANES
    heads = -(-local // HEAD_DIM // 8) * 8
    spec, start = columns_of(weight, 3 * local, local)
    return pl.pallas_call(
        functools.partial(attend_kernel, start),
        grid=(count,),
        in_specs=[
            pl.BlockSpec((rows, local), lambda t: (first + t, 0)),
            whole_spec(keys.shape),
            whole_spec(values.shape),
            spec,
        ],
        out_specs=[row_spec(rows, local), pl.BlockSpec((heads, rows), lambda t: (0, t))]
        + [whole_spec((block, deep))] * (count * rows // block),
        out_shape=[sds((count * rows, local), BF), sds((heads, count * rows), F32)]
        + [sds((block, deep), BF)] * (count * rows // block),
        compiler_params=params(),
        cost_estimate=cost(
            16 * count * rows * tokens * local, 4 * weight.size, count * rows * tokens
        ),
    )(query, keys, values, weight)


def project_back_kernel(local, m_ref, w_ref, low_ref, *refs):
    width = w_ref.shape[0] - low_ref.shape[1]
    value = dot_nt(m_ref[...], w_ref[:, : 3 * local]).astype(BF)
    low_ref[...] = value[:, width:]
    give_tile(value, refs, pl.program_id(0))


def project_back(mixed, weight, rows, first, count, block, rank):
    local, deep = weight.shape[1] // 4, weight.shape[0] // LANES * LANES + LANES
    spec, _ = columns_of(weight, 0, 3 * local)
    blocks = count * rows // block
    return pl.pallas_call(
        functools.partial(project_back_kernel, local),
        grid=(count,),
        in_specs=[pl.BlockSpec((rows, 3 * local), lambda t: (first + t, 0)), spec],
        out_specs=[row_spec(rows, rank)] + [whole_spec((block, deep))] * blocks,
        out_shape=[sds((count * rows, rank), BF)] + [sds((block, deep), BF)] * blocks,
        compiler_params=params(),
        cost_estimate=cost(40 * count * rows * deep * local, 2 * weight.size),
    )(mixed, weight)


def attend_back_kernel(
    first, last, tiles, column, number, *refs,
):
    grads, refs = refs[:number], refs[number:]
    (
        up_ref, w_ref, q_ref, k_ref, v_ref, o_ref, lse_ref, cos_ref, left_ref, right_ref, low_ref,
    ), refs = refs[:11], refs[11:]
    *refs, g_ref = refs
    take_tile(grads, g_ref, pl.program_id(0))
    if not first:
        (mq_ref, gk_in, gv_in, down_in), refs = refs[:4], refs[4:]
    if last:
        m_ref, down_ref, gup_ref, gk_ref, gv_ref = refs
    else:
        m_ref, gk_ref, gv_ref, down_ref = refs
    step, rows = pl.program_id(0), q_ref.shape[0]
    width, local = g_ref.shape[1], q_ref.shape[1]
    at_rows = pl.ds(pl.multiple_of((step + tiles) * rows, rows), rows)
    at_query = at_rows if last else pl.ds(pl.multiple_of(step * rows, rows), rows)

    @pl.when(step == 0)
    def _():
        if first:
            gk_ref[...] = jnp.zeros_like(gk_ref)
            gv_ref[...] = jnp.zeros_like(gv_ref)
            down_ref[...] = jnp.zeros_like(down_ref)
        else:
            gk_ref[...] = gk_in[...]
            gv_ref[...] = gv_in[...]
            down_ref[...] = down_in[...]
            m_ref[: mq_ref.shape[0], :local] = mq_ref[...]

    grad = g_ref[...]
    grad_low = dot_nt(grad, up_ref[...]).astype(BF)
    weight = w_ref[:, column : column + local]
    grad_out = dot(grad, weight[:width]) + dot(grad_low, weight[width:])
    grad_out = grad_out.astype(BF)
    out = o_ref[...]
    down_ref[...] += dot_tn(grad_low, out)
    product = grad_out.astype(F32) * out.astype(F32)
    ones = jnp.ones((8, HEAD_DIM), F32)
    parts = []
    for head in range(local // HEAD_DIM):
        at = slice(head * HEAD_DIM, (head + 1) * HEAD_DIM)
        q, k, v, g = q_ref[:, at], k_ref[:, at], v_ref[:, at], grad_out[:, at]
        delta = lax.dot_general(
            ones, product[:, at], (((1,), (1,)), ((), ())),
            precision=lax.Precision.HIGHEST, preferred_element_type=F32,
        )[:1]
        probs = jnp.exp(dot_nt(k, q) - lse_ref[head : head + 1, :])
        grad_scores = (probs * (dot_nt(v, g) - delta)).astype(BF)
        gv_ref[:, at] += dot(probs.astype(BF), g)
        gk_ref[:, at] += dot(grad_scores, q)
        parts.append(dot_tn(grad_scores, k) * HEAD_DIM**-0.5)
    tables = cos_ref[at_rows, :], -left_ref[at_rows, :], -right_ref[at_rows, :]
    for at, breadth, turned in turn(jnp.concatenate(parts, axis=1), *tables):
        m_ref[at_query, at : at + breadth] = turned.astype(BF)

    if last:

        @pl.when(step == pl.num_programs(0) - 1)
        def _():
            tables = cos_ref[...], -left_ref[...], -right_ref[...]
            for at, breadth, turned in turn(gk_ref[...], *tables):
                m_ref[:, local + at : local + at + breadth] = turned.astype(BF)
            m_ref[:, 2 * local :] = gv_ref[...].astype(BF)
            gup_ref[...] = dot_tn(low_ref[...], m_ref[...])


def attend_back(grads, up, weight, query, keys, values, out, lse, tables, low, rank, rows, start, before):
    tokens, local = query.shape
    block, width = grads[0].shape
    count = len(grads) * block // rows
    first, last = before is None, (start + count) * rows == tokens
    before = () if first else before
    sums = [sds((tokens, local), F32)] * 2 + [sds((rank, local), F32)]
    if last:
        shapes = [sds((tokens, 3 * local), BF), sums[2], sds((rank, 3 * local), F32)]
        scratch = [pltpu.VMEM((tokens, local), F32)] * 2
    else:
        shapes, scratch = [sds((count * rows, local), BF), *sums], []
    scratch.append(pltpu.VMEM((rows, width), BF))

    def tile(columns):
        return pl.BlockSpec((rows, columns), lambda t: (start + t, 0))

    spec, column = columns_of(weight, 3 * local, local)
    return pl.pallas_call(
        functools.partial(attend_back_kernel, first, last, start, column, len(grads)),
        grid=(count,),
        in_specs=[
            *[whole_spec(g.shape) for g in grads],
            whole_spec(up.shape),
            spec,
            tile(local),
            whole_spec(keys.shape),
            whole_spec(values.shape),
            row_spec(rows, local),
            pl.BlockSpec((lse.shape[0], rows), lambda t: (0, t)),
            *[whole_spec(t.shape) for t in tables],
            whole_spec(low.shape),
            *[whole_spec(b.shape) for b in before],
        ],
        out_specs=[whole_spec(s.shape) for s in shapes],
        out_shape=shapes,
        scratch_shapes=scratch,
        compiler_params=params(),
        cost_estimate=cost(
            40 * count * rows * tokens * local, 10 * query.size, count * rows * tokens
        ),
    )(*grads, up, weight, query, keys, values, out, lse, *tables, low, *before)


def cross_kernel(members, local, *refs):
    (x_ref, up_self_ref, up_cross_ref, down_ref, gain_ref, bias_ref, w_ref), refs = (
        refs[:7],
        refs[7:],
    )
    kv_refs, refs = refs[:members], refs[members:]
    y_refs, refs = refs[:-10], refs[-10:]
    branch = total_of(y_refs)
    s1_ref, s2_ref, n2_ref, n3_ref, q_ref, o_ref, lse_ref, z2_ref, u_ref, z4_ref = refs
    rows, width = x_ref.shape
    rank = down_ref.shape[0]
    deep = slice(width, width + rank)
    low = branch[:, deep].astype(BF)
    z2_ref[...] = low
    stream = x_ref[...].astype(F32) + branch[:, :width] + dot(low, up_self_ref[...])
    s1_ref[...] = stream
    normed = layer_norm(stream, gain_ref[1:2, :], bias_ref[1:2, :])
    n2_ref[...] = normed
    low = dot_nt(normed, down_ref[...]).astype(BF)
    u_ref[...] = low
    lanes = lax.broadcasted_iota(jnp.int32, (rows, 128), 1)
    logsums = jnp.zeros((rows, 128), F32)
    total = jnp.zeros((rows, width + rank), F32)
    for k in range(members):
        weight, keyval = w_ref[k], kv_refs[k][...]
        query = dot(normed, weight[:width, :local]) + dot(low, weight[deep, :local])
        query = (query * HEAD_DIM**-0.5).astype(BF)
        q_ref[:, k * local : (k + 1) * local] = query
        parts = []
        for head in range(local // HEAD_DIM):
            at = slice(head * HEAD_DIM, (head + 1) * HEAD_DIM)
            scores = dot_nt(query[:, at], keyval[:, at])
            top = jnp.max(scores, axis=1, keepdims=True)
            powers = jnp.exp(scores - top)
            sums = jnp.sum(powers, axis=1, keepdims=True)
            values = keyval[:, local + head * HEAD_DIM : local + (head + 1) * HEAD_DIM]
            parts.append((dot(powers.astype(BF), values) / sums).astype(BF))
            number = k * (local // HEAD_DIM) + head
            logsums = jnp.where(lanes == number, top + jnp.log(sums), logsums)
        out = jnp.concatenate(parts, axis=1)
        o_ref[:, k * local : (k + 1) * local] = out
        total = total + dot_nt(out, weight[:, local:])
    lse_ref[...] = logsums
    low = total[:, deep].astype(BF)
    z4_ref[...] = low
    stream = stream + total[:, :width] + dot(low, up_cross_ref[...])
    s2_ref[...] = stream
    n3_ref[...] = layer_norm(stream, gain_ref[2:3, :], bias_ref[2:3, :])


def cross_forward(x, ys, up_self, up_cross, down, gains, biases, weight, keyvals):
    rows, width = x.shape
    members, local = len(keyvals), weight.shape[2] // 2
    plain, wide = sds((rows, width), BF), sds((rows, width), F32)
    low = sds((rows, down.shape[0]), BF)
    return pl.pallas_call(
        functools.partial(cross_kernel, members, local),
        out_shape=[wide, wide, plain, plain, plain, plain, sds((rows, 128), F32), low, low, low],
        compiler_params=pltpu.CompilerParams(vmem_limit_bytes=VMEM_LIMIT),
        cost_estimate=cost(24 * rows * width * width, 8 * width * width),
    )(x, up_self, up_cross, down, gains, biases, weight, *keyvals, *ys)


def cross_back_kernel(members, local, *refs):
    (
        g_ref, s1_ref, s2_ref, n2_ref, q_ref, o_ref, lse_ref, u_ref, z4_ref,
        up_ref, down5_ref, down2_ref, gain_ref, bias_ref, w_ref,
    ), refs = refs[:15], refs[15:]
    kv_refs, refs = refs[:members], refs[members:]
    dn_refs, (r1_ref, r1b_ref, fixed_ref, near_ref, *gkv_refs) = (
        refs[: -4 - members],
        refs[-4 - members :],
    )
    summed = total_of(dn_refs)
    width = g_ref.shape[1]
    rank = up_ref.shape[0]
    deep = slice(width, width + rank)
    stream = s2_ref[...]
    low = summed[:, deep].astype(BF)
    grad_normed = summed[:, :width] + dot(low, down5_ref[...])
    normed = layer_norm(stream, gain_ref[2:3, :], bias_ref[2:3, :])
    by_piece(fixed_ref, rank, dot_tn(low, normed))
    grad = g_ref[...].astype(F32) + norm_backward(stream, gain_ref[2:3, :], grad_normed)
    branch = grad.astype(BF)
    low = dot_nt(branch, up_ref[...]).astype(BF)
    by_piece(fixed_ref, 2 * rank, dot_tn(z4_ref[...], branch))
    by_piece(near_ref, 0, dot_tn(low, o_ref[...]))
    total = jnp.zeros((g_ref.shape[0], width + rank), F32)
    for k in range(members):
        weight, keyval = w_ref[k], kv_refs[k][...]
        columns = slice(k * local, (k + 1) * local)
        grad_out = dot(branch, weight[:width, local:]) + dot(low, weight[deep, local:])
        grad_out = grad_out.astype(BF)
        out, query = o_ref[:, columns], q_ref[:, columns]
        product = grad_out.astype(F32) * out.astype(F32)
        queries, keys, values = [], [], []
        for head in range(local // HEAD_DIM):
            at = slice(head * HEAD_DIM, (head + 1) * HEAD_DIM)
            number = k * (local // HEAD_DIM) + head
            key, q, g = keyval[:, at], query[:, at], grad_out[:, at]
            value = keyval[:, local + head * HEAD_DIM : local + (head + 1) * HEAD_DIM]
            delta = jnp.sum(product[:, at], axis=1, keepdims=True)
            probs = jnp.exp(dot_nt(q, key) - lse_ref[:, number : number + 1])
            grad_scores = (probs * (dot_nt(g, value) - delta)).astype(BF)
            queries.append((dot(grad_scores, key) * HEAD_DIM**-0.5).astype(BF))
            keys.append(dot_tn(grad_scores, q))
            values.append(dot_tn(probs.astype(BF), g))
        grad_query = jnp.concatenate(queries, axis=1)
        gkv_refs[k][...] = jnp.concatenate(keys + values, axis=1).astype(BF)
        near_ref[k, rank:, :] = dot_tn(u_ref[...], grad_query).astype(BF)
        total = total + dot_nt(grad_query, weight[:, :local])
    low = total[:, deep].astype(BF)
    by_piece(fixed_ref, 0, dot_tn(low, n2_ref[...]))
    grad_normed = total[:, :width] + dot(low, down2_ref[...])
    grad = grad + norm_backward(s1_ref[...], gain_ref[1:2, :], grad_normed)
    r1_ref[...] = grad
    r1b_ref[...] = grad.astype(BF)


def cross_back(
    g, dns, s1, s2, n2, q, o, lse, u, z4, up, down5, down2, gains, biases, weight, keyvals
):
    rows, width = g.shape
    rank = up.shape[0]
    members, local = len(keyvals), weight.shape[2] // 2
    return pl.pallas_call(
        functools.partial(cross_back_kernel, members, local),
        out_shape=[sds((rows, width), F32), sds((rows, width), BF)]
        + [sds((members, n * rank, local), BF) for n in (3, 2)]
        + [sds(keyvals[0].shape, BF)] * members,
        compiler_params=pltpu.CompilerParams(vmem_limit_bytes=VMEM_LIMIT),
        cost_estimate=cost(32 * rows * width * width, 8 * width * width),
    )(g, s1, s2, n2, q, o, lse, u, z4, up, down5, down2, gains, biases, weight, *keyvals, *dns)


def output_kernel(s2_ref, up_ref, g_ref, *refs):
    *y_refs, out_ref, gup_ref = refs
    width, rank = out_ref.shape[1], up_ref.shape[0]
    total = total_of(y_refs)
    low = total[:, width : width + rank].astype(BF)
    out_ref[...] = (s2_ref[...] + total[:, :width] + dot(low, up_ref[...])).astype(BF)
    by_piece(gup_ref, 0, dot_tn(low, g_ref[...]))


def output_end(s2, ys, up, g, members):
    rank, width = up.shape
    return pl.pallas_call(
        output_kernel,
        out_shape=[sds(g.shape, BF), sds((members, rank, width // members), BF)],
        compiler_params=pltpu.CompilerParams(vmem_limit_bytes=VMEM_LIMIT),
        cost_estimate=cost(0, 0),
    )(s2, up, g, *ys)


def input_kernel(x_ref, r_ref, down_ref, gain_ref, *refs):
    *dn_refs, out_ref = refs
    width, rank = out_ref.shape[1], down_ref.shape[0]
    total = total_of(dn_refs)
    low = total[:, width : width + rank].astype(BF)
    grad = total[:, :width] + dot(low, down_ref[...])
    back = norm_backward(x_ref[...].astype(F32), gain_ref[...], grad)
    out_ref[...] = (r_ref[...] + back).astype(BF)


def input_end(x, r1, dns, down, gain):
    return pl.pallas_call(
        input_kernel,
        out_shape=sds(x.shape, BF),
        compiler_params=pltpu.CompilerParams(vmem_limit_bytes=VMEM_LIMIT),
        cost_estimate=cost(0, 0),
    )(x, r1, down, gain, *dns)


def rows_kernel(near_ref, far_ref, n_ref, z_ref, r_ref, out_ref):
    rows, rank = near_ref.shape
    down = dot_tn(near_ref[...], n_ref[:rows, :]) + dot_tn(far_ref[...], n_ref[rows:, :])
    by_piece(out_ref, 0, down)
    by_piece(out_ref, rank, dot_tn(z_ref[...], r_ref[...]))


def self_rows(low_near, low_far, normed, low_two, branch, members):
    rank, width = low_near.shape[1], normed.shape[1]
    return pl.pallas_call(
        rows_kernel,
        out_shape=sds((members, 2 * rank, width // members), BF),
        compiler_params=pltpu.CompilerParams(vmem_limit_bytes=VMEM_LIMIT),
        cost_estimate=cost(0, 0),
    )(low_near, low_far, normed, low_two, branch)


def context_kernel(members, places_ref, *refs):
    blocks, (w_ref, down_ref, kv_ref, low_ref) = refs[:members], refs[members:]
    rank, local = down_ref.shape[1], blocks[0].shape[1]
    width = members * local
    low, keyval = 0.0, 0.0
    for k in range(members):
        at = pl.ds(pl.multiple_of(places_ref[k], local), local)
        low = low + dot(blocks[k][...], down_ref[at, :])
        keyval = keyval + dot(blocks[k][...], w_ref[at, :])
    low = low.astype(BF)
    low_ref[...] = low
    kv_ref[...] = (keyval + dot(low, w_ref[width : width + rank, :])).astype(BF)


def context_forward(places, blocks, weight, down):
    count = blocks[0].shape[0]
    arrays = (*blocks, weight, down)
    shapes = [sds((count, weight.shape[1]), BF), sds((count, down.shape[1]), BF)]
    return pl.pallas_call(
        functools.partial(context_kernel, len(blocks)),
        grid_spec=pltpu.PrefetchScalarGridSpec(
            num_scalar_prefetch=1,
            grid=(1,),
            in_specs=[whole_spec(a.shape) for a in arrays],
            out_specs=[whole_spec(s.shape) for s in shapes],
        ),
        out_shape=shapes,
        compiler_params=params(),
        cost_estimate=cost(0, 0),
    )(places, *arrays)


def context_back_kernel(members, places_ref, *refs):
    blocks, (w_ref, down_ref, low_ref, g_ref), refs = (
        refs[:members],
        refs[members : members + 4],
        refs[members + 4 :],
    )
    gup_ref, *refs = refs
    rank, local = down_ref.shape[1], blocks[0].shape[1]
    width = members * local
    grad = g_ref[...]
    low = dot_nt(grad, w_ref[width : width + rank, :]).astype(BF)
    gup_ref[...] = dot_tn(low_ref[...], grad)
    for k in range(members):
        at = pl.ds(pl.multiple_of(places_ref[k], local), local)
        out = dot_nt(grad, w_ref[at, :]) + dot_nt(low, down_ref[at, :])
        refs[k][...] = out.astype(BF)
        refs[members + k][...] = dot_tn(low, blocks[k][...]).astype(BF)


def context_back(places, blocks, weight, down, low, grad):
    count, local = blocks[0].shape
    rank, members = down.shape[1], len(blocks)
    arrays = (*blocks, weight, down, low, grad)
    shapes = (
        [sds((rank, weight.shape[1]), F32)]
        + [sds((count, local), BF)] * members
        + [sds((rank, local), BF)] * members
    )
    return pl.pallas_call(
        functools.partial(context_back_kernel, members),
        grid_spec=pltpu.PrefetchScalarGridSpec(
            num_scalar_prefetch=1,
            grid=(1,),
            in_specs=[whole_spec(a.shape) for a in arrays],
            out_specs=[whole_spec(s.shape) for s in shapes],
        ),
        out_shape=shapes,
        compiler_params=params(),
        cost_estimate=cost(0, 0),
    )(places, *arrays)


def table_kernel(cos_ref, sin_ref, out_cos_ref, out_left_ref, out_right_ref):
    half, breadth = ROT // 2, 2 * HEAD_DIM
    lane = lax.broadcasted_iota(jnp.int32, (half, breadth), 1)
    row = lax.broadcasted_iota(jnp.int32, (half, breadth), 0)
    within = lane % HEAD_DIM
    first = jnp.where(within == row, 1.0, 0.0)
    second = jnp.where(within == row + half, 1.0, 0.0)

    def spread(ref, pattern):
        return lax.dot_general(
            ref[...], pattern, (((0,), (0,)), ((), ())),
            precision=lax.Precision.HIGHEST, preferred_element_type=F32,
        )

    lanes = lax.broadcasted_iota(jnp.int32, out_cos_ref.shape, 1) % HEAD_DIM
    out_cos_ref[...] = jnp.where(lanes < ROT, spread(cos_ref, first + second), 1.0)
    out_left_ref[...] = -spread(sin_ref, first)
    out_right_ref[...] = spread(sin_ref, second)


def rotary_tables(cosines, sines):
    tokens = cosines.shape[1]
    return pl.pallas_call(
        table_kernel,
        out_shape=[sds((tokens, 2 * HEAD_DIM), F32)] * 3,
        compiler_params=pltpu.CompilerParams(vmem_limit_bytes=VMEM_LIMIT),
        cost_estimate=cost(0, 0),
    )(cosines, sines)


def feed_kernel(first, last, number, *refs):
    n_refs, g_refs, (down_ref, up_ref, w_ref), refs = (
        refs[:number],
        refs[number : 2 * number],
        refs[2 * number : 2 * number + 3],
        refs[2 * number + 3 :],
    )
    if not first:
        (y_in, dn_in), refs = refs[:2], refs[2:]
    *refs, gdown_ref, ggate_ref, gupper_ref, n_ref, g_ref = refs
    step, width = pl.program_id(0), n_ref.shape[1]
    rank, part = gdown_ref.shape
    take_tile(n_refs, n_ref, step)
    take_tile(g_refs, g_ref, step)

    @pl.when(step == 0)
    def _():
        for ref in (gdown_ref, ggate_ref, gupper_ref):
            ref[...] = jnp.zeros_like(ref)

    normed, grad = n_ref[...], g_ref[...]
    low = dot_nt(normed, down_ref[...]).astype(BF)
    grad_low = dot_nt(grad, up_ref[...]).astype(BF)
    deep = slice(width, width + rank)
    both = dot(normed, w_ref[:width, : 2 * part]) + dot(low, w_ref[deep, : 2 * part])
    gate, upper = both[:, :part], both[:, part:]
    grad_unit = dot(grad, w_ref[:width, 2 * part :]) + dot(grad_low, w_ref[deep, 2 * part :])
    sigmoid = 1.0 / (1.0 + jnp.exp(-gate))
    acted = gate * sigmoid
    unit = (acted * upper).astype(BF)
    grad_gate = (grad_unit * upper * (sigmoid + acted * (1.0 - sigmoid))).astype(BF)
    grad_upper = (grad_unit * acted).astype(BF)
    y = dot_nt(unit, w_ref[:, 2 * part :])
    dn = dot_nt(grad_gate, w_ref[:, :part]) + dot_nt(grad_upper, w_ref[:, part : 2 * part])
    if not first:
        y, dn = y + y_in[...].astype(F32), dn + dn_in[...].astype(F32)
    if last:
        give_tile(y.astype(BF), refs[:number], step)
        give_tile(dn.astype(BF), refs[number:], step)
    else:
        refs[0][...] = y.astype(BF)
        refs[1][...] = dn.astype(BF)
    gdown_ref[...] += dot_tn(grad_low, unit)
    ggate_ref[...] += dot_tn(low, grad_gate)
    gupper_ref[...] += dot_tn(low, grad_upper)


def feed(normed, grads, down, up, weight, sums, rows, start, last):
    block, width = normed[0].shape
    rank, number = down.shape[0], len(normed)
    deep, part = weight.shape[0], weight.shape[1] // 3
    narrow = sds((rank, part), F32)
    tokens = number * block
    if last:
        wide = sds((block, deep // LANES * LANES + LANES), BF)
        shapes, specs = [wide] * (2 * number), [whole_spec(wide.shape)] * (2 * number)
    else:
        shapes, specs = [sds((tokens, deep), BF)] * 2, [row_spec(rows, deep)] * 2
    first = not sums
    arrays = (*normed, *grads, down, up, weight)
    return pl.pallas_call(
        functools.partial(feed_kernel, first, last, number),
        grid=(tokens // rows,),
        in_specs=[whole_spec(a.shape) for a in arrays]
        + [pl.BlockSpec((rows, deep), lambda t: (start + t, 0)) for _ in sums],
        out_specs=specs + [whole_spec(narrow.shape)] * 3,
        out_shape=shapes + [narrow] * 3,
        scratch_shapes=[pltpu.VMEM((rows, width), BF)] * 2,
        compiler_params=params(),
        cost_estimate=cost(8 * tokens * weight.size, 2 * weight.size),
    )(*arrays, *sums)


def settle_first_kernel(fold, labels_ref, in_ref, down_ref, up_ref, hid_ref, gate_ref):
    slot = pl.program_id(0)
    local = down_ref.shape[-1]
    for ref in (down_ref, up_ref, hid_ref, gate_ref):
        ref[...] = jnp.zeros_like(ref)
    for s in range(in_ref.shape[0]):

        @pl.when(labels_ref[s] == slot)
        def _(s=s):
            for n, k in enumerate(DOWN_FIRST):
                down_ref[0, k] += in_ref[s, n].astype(F32)
            for n, k in enumerate(UP_FIRST):
                up_ref[0, k] += in_ref[s, len(DOWN_FIRST) + n].astype(F32)
            for k in range(fold):
                at, n = slice(k * local, (k + 1) * local), 6 + k
                hid_ref[0, :, at] += in_ref[s, n].astype(F32)
                gate_ref[0, 0, :, at] += in_ref[s, n + fold].astype(F32)
                gate_ref[0, 1, :, at] += in_ref[s, n + 2 * fold].astype(F32)


def settle_second_kernel(labels_ref, in_ref, down_in, up_in, down_ref, up_ref):
    slot = pl.program_id(0)
    down_ref[...] = down_in[...]
    up_ref[...] = up_in[...]
    for s in range(in_ref.shape[0]):

        @pl.when(labels_ref[s] == slot)
        def _(s=s):
            for n, k in enumerate(DOWN_SECOND):
                down_ref[0, k] += in_ref[s, n].astype(F32)
            for n, k in enumerate(UP_SECOND):
                up_ref[0, k] += in_ref[s, len(DOWN_SECOND) + n].astype(F32)


DOWN_FIRST, UP_FIRST = (2, 4, 5), (4, 7, 8)
DOWN_SECOND, UP_SECOND = (0, 1, 3), (0, 1, 2, 3, 5, 6)


def slot_spec(shape):
    return pl.BlockSpec((1,) + shape[1:], lambda i, *_, n=len(shape): (i,) + (0,) * (n - 1))


def settle_first(labels, grads, slots, fold):
    rank, local = grads.shape[2:]
    hidden = fold * local
    shapes = [
        (slots, 6, rank, local),
        (slots, 9, rank, local),
        (slots, rank, hidden),
        (slots, 2, rank, hidden),
    ]
    return pl.pallas_call(
        functools.partial(settle_first_kernel, fold),
        grid_spec=pltpu.PrefetchScalarGridSpec(
            num_scalar_prefetch=1,
            grid=(slots,),
            in_specs=[whole_spec(grads.shape)],
            out_specs=[slot_spec(s) for s in shapes],
        ),
        out_shape=[sds(s, F32) for s in shapes],
        compiler_params=params(),
        cost_estimate=cost(0, 0),
    )(labels, grads)


def settle_second(labels, grads, down, up):
    return pl.pallas_call(
        settle_second_kernel,
        grid_spec=pltpu.PrefetchScalarGridSpec(
            num_scalar_prefetch=1,
            grid=(down.shape[0],),
            in_specs=[whole_spec(grads.shape), slot_spec(down.shape), slot_spec(up.shape)],
            out_specs=[slot_spec(down.shape), slot_spec(up.shape)],
        ),
        out_shape=[sds(down.shape, F32), sds(up.shape, F32)],
        compiler_params=params(),
        cost_estimate=cost(0, 0),
    )(labels, grads, down, up)


def chunks(hidden):
    return (hidden // 3,) * 3


def body(
    inputs,
    context,
    positions,
    adapter_index,
    self_in_weight,
    self_out_weight,
    cross_query_weight,
    cross_keyval_weight,
    cross_out_weight,
    feed_in_weight,
    feed_out_weight,
    norm_gains,
    norm_biases,
    adapter_down,
    adapter_down_hidden,
    adapter_up,
    adapter_up_hidden,
    out_cotangent,
    *,
    pairs,
    chips,
):
    group = Group(pairs, chips)
    members = 2 * pairs
    rows, width = inputs.shape[1], inputs.shape[2]
    block = self_in_weight.shape[0]
    local = self_in_weight.shape[2]
    hidden = feed_in_weight.shape[2]
    slots, rank = adapter_down.shape[0], adapter_down.shape[3]
    deep = width + rank
    parts = chunks(hidden)
    fold = hidden // local
    pieces = group.pieces
    gains, biases = norm_gains, norm_biases
    tile = min(256, members * rows)
    tiles = members * rows // tile
    near_tiles = tiles // pairs

    def packed(*parts):
        return jnp.concatenate(parts, axis=1)

    def stacked(*parts):
        return jnp.concatenate(parts, axis=0)

    def listed(values):
        return list(values) if isinstance(values, (list, tuple)) else [values]

    def piece(array, k, size):
        return lax.dynamic_slice_in_dim(array, pieces[k] * size, size, array.ndim - 1)

    def own(array):
        return piece(array, 0, local)

    near_chips = [1, 2] if chips == 4 else list(range(1, chips))
    chip_rows = [(group.chip ^ k) * 2 * block for k in range(chips)]
    mine_rows = [c + group.core * block for c in chip_rows]
    other_rows = [c + (1 - group.core) * block for c in chip_rows]
    first_rows = [c + group.zhi * block for c in chip_rows]
    second_rows = [c + (1 - group.zhi) * block for c in chip_rows]
    fixed = [jnp.zeros_like(group.core), group.core * block, (1 - group.core) * block]
    row_places = jnp.stack(
        chip_rows + mine_rows + other_rows + first_rows + second_rows + fixed
    ).astype(jnp.int32)
    zero, mine_at, other_at = 5 * chips, 5 * chips + 1, 5 * chips + 2

    def put_all(own_entry, near, rest, low, columns, by_core=True):
        entries, moves = [own_entry, *near, *rest], []
        for i, k in enumerate([0, *near_chips] + [3] * len(rest)):
            row = entries[i][1]
            if len(rest) == 2 and i > len(near):
                moves.append((i, row, block, 0, None, (2 + i - len(near)) * chips + k, 0))
            elif by_core:
                moves.append((i, row, 2 * block, 0, None, k, 0))
            else:
                moves.append((i, row, block, 0, None, 3 * chips + k, 0))
                moves.append((i, row + block, block, 0, None, 4 * chips + k, 0))
        moves.append((len(entries), 0, rank, 0, None, zero, width))
        sources = [e[0] for e in entries]
        return place([*sources, low], moves, row_places, [(deep, columns)], True)[0]

    def spread(prev, own_block):
        if prev and chips == 4:
            half = prev[0][1]
            turns = [
                prev[1][0][prev[1][2] : prev[1][2] + half],
                prev[0][0][prev[0][2] + half : prev[0][2] + 2 * half],
            ]
            if own_block is not None:
                turns = listed(step.mark(*[stacked(turn, own_block) for turn in turns]))
            return [xor_move(turn, "chip", 4, k) for turn, k in zip(turns, near_chips)]
        if own_block is None:
            return []
        return [xor_move(own_block, "chip", chips, k) for k in near_chips]

    def flat(*groups):
        return [x for g in groups for x in listed(g)]

    def wait_all(*groups):
        groups = [listed(g) for g in groups]
        values = iter(listed(step.wait(*flat(*groups))))
        return [[next(values) for _ in g] for g in groups]

    def swap_all(blocks):
        if not blocks:
            return []
        blocks = listed(step.wait(*blocks))
        return listed(step.wait(*[core_swap(b) for b in blocks]))

    shard_self = packed(*[self_in_weight[:, i] for i in range(3)], self_out_weight.T)
    step = Order(shard_self[:8, :128])
    self_from = [home_swap(shard_self), turned(shard_self)]
    stream_own, context_own = home_swap(inputs[0]), home_swap(context[0])
    index, positions = step.wait(adapter_index, positions)
    index_other, positions_other = step.wait(core_swap(index), core_swap(positions))
    index = jnp.where(group.home, index, index_other)[0]
    positions = jnp.where(group.home, positions, positions_other)[0]
    down = lax.dynamic_index_in_dim(adapter_down.transpose(0, 1, 3, 2), index, 0, keepdims=False)
    up = lax.dynamic_index_in_dim(adapter_up.transpose(0, 2, 1, 3), index, 0, keepdims=False)
    down, up = step.mark(down, up)
    low_self = packed(*[own(up[i]) for i in range(3)], own(down[1]))
    low_keyval = packed(own(up[5]), own(up[6]))
    low_cross = stacked(
        *[packed(piece(up[4], k, local), piece(down[4], k, local)) for k in range(members)]
    )
    low_self, low_keyval, low_cross = step.mark(low_self, low_keyval, low_cross)
    keyval_parts = step.wait(cross_keyval_weight)
    keyval_parts = step.mark(keyval_parts[:, 0], keyval_parts[:, 1])
    shard_cross = step.mark(packed(cross_query_weight, cross_out_weight.T, *keyval_parts))
    stream_own, context_own, *self_from = step.wait(stream_own, context_own, *self_from)
    ready_self = step.mark(stacked(*self_from))

    near_self, far_cross = spread([], ready_self), group.cross(shard_cross)
    stream_other, stream_far = core_swap(stream_own), group.far_p(stream_own)
    blocks_at = [
        lax.dynamic_slice_in_dim(positions, pieces[k] * rows, rows, 0) for k in range(members)
    ]
    half = ROT // 2
    inverse = 10000.0 ** (-jnp.arange(half, dtype=F32) / half)
    angles = inverse[:, None] * step.wait(jnp.concatenate(blocks_at)).astype(F32)[None]
    tables = step.mark(*rotary_tables(*step.mark(jnp.cos(angles), jnp.sin(angles))))
    feed_in, feed_out = step.wait(feed_in_weight, feed_out_weight)
    gate_rows, upper_rows = step.mark(feed_in[:, 0], feed_in[:, 1])
    at = [sum(parts[:i]) for i in range(len(parts))]

    def feed_shard(i):
        to = slice(at[i], at[i] + parts[i])
        gate, upper, out = step.wait(gate_rows, upper_rows, feed_out)
        return step.mark(packed(gate[:, to], upper[:, to], out.T[:, to]))

    shard_feed = [feed_shard(i) for i in range(len(parts))]
    near_self, stream_far, (far_cross, stream_other) = wait_all(
        near_self, stream_far, [far_cross, stream_other]
    )
    mine = jnp.where(group.home, shard_cross, far_cross)
    given = jnp.where(group.home, far_cross, shard_cross)
    keyval_mine, keyval_give = mine[:, 2 * local :], given[:, 2 * local :]
    pair = stacked(mine[:, : 2 * local], given[:, : 2 * local])
    keyval_mine, keyval_give, pair = step.mark(keyval_mine, keyval_give, pair)
    keyval_other, *stream_far_other = swap_all([keyval_give, *stream_far])

    rest_self = spread([(g, block, 0) for g in near_self], None)
    pair_far = group.far_p(pair)
    feed_from = [[home_swap(shard_feed[0]), turned(shard_feed[0])]]
    moves = [
        (0, 0, block, 0, None, mine_at, 0),
        (1, 0, block, 0, None, other_at, 0),
        (2, 0, 2 * block, 0, None, zero, 2 * block),
    ]
    ready_keyval = step.mark(
        place(
            [keyval_mine, keyval_other, pair], moves, row_places, [(4 * block, 2 * local)], True
        )[0]
    )
    stream = [stream_own, stream_other]
    for far, far_other in zip(stream_far, stream_far_other):
        stream += [far, far_other]
    rest_self, pair_far, feed_from[0] = wait_all(rest_self, pair_far, feed_from[0])
    self_weight = step.mark(
        put_all(
            (ready_self, 0), [(g, 0) for g in near_self], [(g, 0) for g in rest_self], low_self,
            4 * local, by_core=False,
        )
    )

    near_keyval = spread([], ready_keyval)
    cotangent_own = home_swap(step.wait(out_cotangent[0]))
    context_far = group.far_p(context_own)
    query, keys, values, low_one, normed_one = project_self(
        listed(step.wait(*stream)), gains[0:1], biases[0:1], down[0], self_weight, tables, tile
    )
    query, keys, values = step.mark(query, keys, values)
    heads_far, logsum_far, *y_far = attend_self(
        query, keys, values, self_weight, tile, near_tiles, tiles - near_tiles, rows
    )
    y_far = listed(step.mark(*y_far))

    def far_sums(*groups):
        others = iter(swap_all([g[2 * k + 1] for g in groups for k in range(pairs - 1)]))
        sums = [
            [group.near_sums(g[2 * k], next(others)).astype(BF) for k in range(pairs - 1)]
            for g in groups
        ]
        values = iter(listed(step.mark(*flat(*sums))))
        return [[next(values) for _ in s] for s in sums]

    def move_p(sums):
        return [xor_move(s, "p", pairs, k + 1) for k, s in enumerate(sums)]

    def sum_up(blocks, other, far):
        total = group.near_sums(blocks[0], other)
        for f in far:
            total = total + f.astype(F32)
        return step.mark(total)

    near_keyval, context_far, (cotangent_own,) = wait_all(
        near_keyval, context_far, [cotangent_own]
    )
    (y_sums,) = far_sums(y_far)

    far = move_p(y_sums)
    if chips == 4:
        both_far = [spread([(g, 2 * block, 0) for g in near_keyval], pair_far[0])]
    else:
        both_far = [spread([], p) for p in pair_far]
    heads_near, logsum_near, *y_rows = attend_self(
        step.wait(query), keys, values, self_weight, tile, 0, near_tiles, rows
    )
    y_rows = listed(step.mark(*y_rows))
    far, *both_far = wait_all(far, *both_far)
    y_other, context_other, *swapped = swap_all([y_rows[1], context_own, *context_far])
    branch = [y_rows[0], y_other, *far]
    context_blocks = [context_own, context_other]
    for far, far_other in zip(context_far, swapped):
        context_blocks += [far, far_other]

    if chips == 4:
        (x_got, y_got), (x_first, y_first) = both_far[0], near_keyval
        at_rest = 2 * block
        keyval_from = [(ready_keyval, 0), (x_first, 0), (y_first, 0)], [(x_got, 0)]
        pair_from = [[(ready_keyval, at_rest), (x_first, at_rest), (y_first, at_rest), (y_got, 0)]]
        pair_from.append([(pair_far[0], 0), (x_got, at_rest), (y_got, at_rest)])
    else:
        at_rest = 0
        keyval_from = [(b, 0) for b in [ready_keyval, *near_keyval]], []
        pair_from = [[(b, 2 * block) for b in [ready_keyval, *near_keyval]]]
        pair_from += [[(b, 0) for b in [p, *n]] for p, n in zip(pair_far, both_far)]
    keyval_weight = step.mark(
        put_all(keyval_from[0][0], keyval_from[0][1:], keyval_from[1], low_keyval, 2 * local)
    )
    context_places = (jnp.stack(pieces) * local).astype(jnp.int32)
    down_context = step.mark(down[3].T)
    keyval, low_context = context_forward(
        context_places, context_blocks, keyval_weight, down_context
    )
    keyval = step.mark(keyval)

    if chips == 4:
        rest_far = spread([(x_got, block, at_rest), (y_got, block, at_rest)], None)
    else:
        rest_far = []
    keyval_far = group.far_p(keyval)
    ready_feed = [step.mark(stacked(*feed_from[0]))]
    keyval_far, rest_far = wait_all(keyval_far, rest_far)
    near_feed = [spread([], ready_feed[0])]
    cotangent_far = group.far_p(cotangent_own)
    distances = [0, *near_chips]
    by_chip = [(n, i, e) for n, found in enumerate(pair_from) for i, e in enumerate(found)]
    swapped = swap_all(
        [
            keyval, *keyval_far, *rest_far, cotangent_own,
            *[e[0][e[1] : e[1] + 2 * block] for _, _, e in by_chip],
        ]
    )
    keyvals = [keyval, swapped[0]]
    for far, far_other in zip(keyval_far, swapped[1:]):
        keyvals += [far, far_other]
    swapped = swapped[1 + len(keyval_far) :]
    rest_other, swapped = swapped[: len(rest_far)], swapped[len(rest_far) :]
    cotangent_blocks = [cotangent_own, swapped[0]]
    swapped = swapped[1:]
    sources, moves = [], []
    for (n, i, (array, row)), other in zip(by_chip, swapped):
        chip = distances[i] if i < len(distances) else 3
        for r in (0, 1):
            at_source = len(sources)
            moves.append((at_source, row + r * block, block, 0, 2 * n + r, chips + chip, 0))
            moves.append((at_source + 1, r * block, block, 0, 2 * n + 1 - r, 2 * chips + chip, 0))
        sources += [array, other]
    for r, (mine, other) in enumerate(zip(rest_far, rest_other)):
        at_source = len(sources)
        moves.append((at_source, 0, block, 0, 2 + r, chips + 3, 0))
        moves.append((at_source + 1, 0, block, 0, 3 - r, 2 * chips + 3, 0))
        sources += [mine, other]
    moves += [(len(sources), r * rank, rank, 0, r, zero, width) for r in range(members)]
    cross_weight = step.mark(
        place([*sources, low_cross], moves, row_places, [(members, deep, 2 * local)], True)[0]
    )

    near_feed[0], cotangent_far = wait_all(near_feed[0], cotangent_far)

    rest_feed = [spread([(g, block, 0) for g in near_feed[0]], None)]
    feed_from.append([home_swap(shard_feed[1]), turned(shard_feed[1])])
    stream_own, *branch = step.wait(stream_own, *branch)

    (
        stream_one, stream_two, normed_two, normed_three, query_cross, heads_cross, logsum_cross,
        low_two, low_three, low_four,
    ) = cross_forward(
        stream_own, branch, up[3], up[7], down[2], gains, biases, cross_weight, keyvals,
    )
    normed_own = step.mark(normed_three)
    rest_feed[0], feed_from[1] = wait_all(rest_feed[0], feed_from[1])
    ready_feed.append(step.mark(stacked(*feed_from[1])))

    normed_far = group.far_p(normed_own)
    near_feed.append(spread([], ready_feed[1]))
    feed_from.append([home_swap(shard_feed[2]), turned(shard_feed[2])])
    down_hidden = lax.dynamic_index_in_dim(
        adapter_down_hidden.transpose(0, 2, 1), index, 0, keepdims=False
    )
    up_hidden = lax.dynamic_index_in_dim(
        adapter_up_hidden.transpose(0, 2, 1, 3), index, 0, keepdims=False
    )
    feed_down, feed_up = piece(down_hidden, 0, hidden), piece(up_hidden, 0, hidden)
    feed_down, feed_gate, feed_upper = step.mark(feed_down, feed_up[0], feed_up[1])
    low_feed = [
        packed(feed_gate[:, to], feed_upper[:, to], feed_down[:, to])
        for to in [slice(a, a + p) for a, p in zip(at, parts)]
    ]
    low_feed = step.mark(*low_feed)
    near_feed[1], normed_far, feed_from[2] = wait_all(near_feed[1], normed_far, feed_from[2])
    normed_other, *swapped = swap_all([normed_own, *normed_far, *cotangent_far])
    normed_blocks = [normed_own, normed_other]
    for far, far_other in zip(normed_far, swapped):
        normed_blocks += [far, far_other]
    for far, far_other in zip(cotangent_far, swapped[len(normed_far) :]):
        cotangent_blocks += [far, far_other]
    ready_feed.append(step.mark(stacked(*feed_from[2])))

    def feed_weight(i, skip, rest):
        return step.mark(
            put_all(
                (ready_feed[i], 0), [(g, skip) for g in near_feed[i]], [(g, 0) for g in rest],
                low_feed[i], 3 * parts[i], by_core=False,
            )
        )

    weight = feed_weight(0, 0, rest_feed[0])
    skip = block if chips == 4 else 0

    near_feed.append(spread([(g, block, 0) for g in near_feed[1]], ready_feed[2]))

    def feed_pass(weight, sums, picked, start, last):
        normed, cotangent = wait_all(normed_blocks[picked], cotangent_blocks[picked])
        found = feed(normed, cotangent, down[5], up[8], weight, sums, tile, start, last)
        *values, gdown, ggate, gupper = found
        values = step.mark(*values)
        half = len(values) // 2
        return values[:half], values[half:], [gdown, ggate, gupper]

    everything, far_only, near_only = slice(0, None), slice(2, None), slice(0, 2)
    y, dn, *feed_grads = feed_pass(weight, (), everything, 0, False)
    (near_feed[2],) = wait_all(near_feed[2])
    weight = feed_weight(1, 0, near_feed[2] if chips == 4 else [])
    rest_feed.append(spread([(g, block, skip) for g in near_feed[2]], None))
    y, dn, grads = feed_pass(weight, (*y, *dn), everything, 0, False)
    feed_grads.append(grads)
    (rest_feed[1],) = wait_all(rest_feed[1]) if rest_feed[1] else ([],)
    weight = feed_weight(2, skip, rest_feed[1])
    y_far, dn_far, grads = feed_pass(weight, (*y, *dn), far_only, near_tiles, True)

    dn_sums, y_sums = far_sums(dn_far, y_far)
    far = move_p(dn_sums)
    y_rows, dn_rows, more = feed_pass(weight, (*y, *dn), near_only, 0, True)
    feed_grads.append([a + b for a, b in zip(grads, more)])
    (far,) = wait_all(far)
    dn_other, y_other = swap_all([dn_rows[1], y_rows[1]])
    grad_normed = [dn_rows[0], dn_other, *far]

    far = move_p(step.mark(*y_sums) if len(y_sums) > 1 else [step.mark(*y_sums)])
    grad_stream, branch_grad, fixed_rows, near_rows, *keyval_rows = cross_back(
        cotangent_own, listed(step.wait(*grad_normed)), stream_one, stream_two, normed_two,
        query_cross, heads_cross, logsum_cross, low_three, low_four, up[7], down[5], down[2],
        gains, biases, cross_weight, keyvals,
    )
    branch_grad, *keyval_rows = step.mark(branch_grad, *keyval_rows)
    (far,) = wait_all(far)

    branch_far = group.far_p(branch_grad)
    (branch_other,) = swap_all([branch_grad])

    def back(grad, heads, logsum, first, before):
        return attend_back(
            grad, up[3], self_weight, query, keys, values, heads, logsum, tables, low_one, rank,
            tile, first, before,
        )

    near_back = step.mark(
        *back([branch_grad, branch_other], heads_near, logsum_near, 0, None)
    )
    (branch_far,) = wait_all(branch_far)
    keyval_other, *branch_swapped = swap_all([keyval_rows[1], *branch_far])
    branch_blocks = []
    for f, o in zip(branch_far, branch_swapped):
        branch_blocks += [f, o]

    output, grad_up_eight = step.mark(
        *output_end(stream_two, [y_rows[0], y_other, *far], up[8], cotangent_own, members)
    )

    def taken(by_piece, k):
        return lax.dynamic_index_in_dim(by_piece, pieces[k], 0, keepdims=False)

    first_rows = listed(
        step.mark(
            *[
                stacked(taken(fixed_rows, k), taken(grad_up_eight, k), near_rows[k])
                for k in range(members)
            ]
        )
    )
    first_sums, keyval_sums = far_sums(first_rows[2:], keyval_rows[2:])
    (first_other,) = swap_all([first_rows[1]])

    def columns(array):
        return array.reshape(rank, -1, local).transpose(1, 0, 2)

    def sent(parts):
        parts.append(jnp.full((1, rank, local), index, F32))
        grads = step.mark(jnp.concatenate(parts, axis=0).astype(BF))
        return [home_swap(grads), turned_back(grads)]

    def to_chips(blocks):
        both = step.mark(stacked(*blocks))
        return [both] + [xor_move(both, "chip", chips, k) for k in range(1, chips)]

    def every(blocks):
        grads = stacked(*blocks)
        grads = grads.reshape(-1, grads.shape[0] // (2 * chips), rank, local)
        return grads, grads[:, -1, 0, 0].astype(jnp.int32)

    first_far, keyval_far, block_output = move_p(first_sums), move_p(keyval_sums), home_swap(output)
    branch_blocks = listed(step.wait(*branch_blocks))
    grad_mixed, grad_down_one, grad_up_self = back(
        branch_blocks, heads_far, logsum_far, near_tiles, near_back
    )
    grad_mixed = step.mark(grad_mixed)
    first_far, keyval_far, (block_output,) = wait_all(first_far, keyval_far, [block_output])
    low_far, *dn_far = step.mark(
        *project_back(grad_mixed, self_weight, tile, near_tiles, tiles - near_tiles, rows, rank)
    )
    (dn_sums,) = far_sums(dn_far)

    summed = sum_up(first_rows, first_other, first_far).reshape(-1, rank, local)
    grad_keyval = step.mark(sum_up(keyval_rows, keyval_other, keyval_far).astype(BF))
    far = move_p(step.mark(*dn_sums) if len(dn_sums) > 1 else [step.mark(*dn_sums)])
    low_near, *dn_rows = step.mark(
        *project_back(step.wait(grad_mixed), self_weight, tile, 0, near_tiles, rows, rank)
    )
    grad_up_keyval, *found = step.mark(
        *context_back(
            context_places, context_blocks, keyval_weight, down_context, low_context,
            step.wait(grad_keyval),
        )
    )
    context_rows, grad_down_three = found[:members], found[members:]
    own_rows = step.mark(
        self_rows(low_near, low_far, normed_one, low_two, branch_grad, members)
    )
    (far,) = wait_all(far)

    first = sent(
        [
            summed[0:1],
            summed[4:5],
            summed[1:2],
            summed[5:6],
            summed[2:4],
            *[columns(jnp.concatenate(g, axis=1)) for g in zip(*feed_grads)],
        ]
    )
    second_rows = listed(
        step.mark(
            *[stacked(taken(own_rows, k), grad_down_three[k]) for k in range(members)]
        )
    )
    dn_other, second_other, context_other, *others = swap_all(
        [dn_rows[1], second_rows[1], context_rows[1], *second_rows[3::2], *context_rows[3::2]]
    )
    grad_inputs = step.mark(
        input_end(stream_own, grad_stream, [dn_rows[0], dn_other, *far], down[0], gains[0:1])
    )
    sums = [
        group.near_sums(b, o).astype(BF)
        for b, o in zip([*second_rows[2::2], *context_rows[2::2]], others)
    ]
    sums = listed(step.mark(*sums))
    second_far, context_far = move_p(sums[: pairs - 1]), move_p(sums[pairs - 1 :])
    second_far, context_far, first = wait_all(second_far, context_far, first)
    grad_inputs = home_swap(grad_inputs)
    summed = sum_up(second_rows, second_other, second_far).reshape(-1, rank, local)
    second = sent(
        [
            summed[0:1],
            grad_down_one[None],
            summed[2:3],
            columns(grad_up_self),
            summed[1:2],
            columns(grad_up_keyval),
        ]
    )
    grad_context = home_swap(step.mark(sum_up(context_rows, context_other, context_far).astype(BF)))
    first = to_chips(first)
    (first,) = wait_all(first)
    first, labels = every(first)
    grad_down, grad_up, grad_hidden, grad_gate = settle_first(labels, first, slots, fold)
    grad_down, grad_up = step.mark(grad_down, grad_up)
    (second,) = wait_all(second)
    (second,) = wait_all(to_chips(second))
    second, labels = every(second)
    grad_down, grad_up = settle_second(labels, second, grad_down, grad_up)
    return (
        block_output[None],
        grad_inputs.astype(F32)[None],
        grad_context.astype(F32)[None],
        grad_down.transpose(0, 1, 3, 2),
        grad_hidden.transpose(0, 2, 1),
        grad_up.transpose(0, 2, 1, 3),
        grad_gate.transpose(0, 2, 1, 3),
    )


def solution(mesh):
    members = mesh.shape["tensor"]
    chips = mesh.shape["dp"] // 2
    mesh = Mesh(
        mesh.devices.reshape(chips, 2, 2, members // 2), ("chip", "core", "zhi", "p")
    )
    dp, tensor = ("chip", "core"), ("zhi", "p")
    in_specs = (
        P(dp, tensor, None),
        P(dp, None, tensor),
        P(dp, None),
        P(dp),
        P(dp, None, tensor),
        P(tensor, dp),
        P(dp, tensor),
        P(dp, None, tensor),
        P(tensor, dp),
        P(dp, None, tensor),
        P(tensor, dp),
        P(),
        P(),
        P(),
        P(),
        P(),
        P(),
        P(dp, tensor, None),
    )
    out_specs = (
        P(dp, tensor, None),
        P(dp, tensor, None),
        P(dp, None, tensor),
        P(None, None, tensor, None),
        P(None, tensor, None),
        P(None, None, None, tensor),
        P(None, None, None, tensor),
    )

    def run(*args):
        return body(*args, pairs=members // 2, chips=chips)

    return jax.shard_map(run, mesh=mesh, in_specs=in_specs, out_specs=out_specs, check_vma=False)
```

time: 776 us -> 674 us (0.87)
  waiting for transfers between devices: 239 us -> 159 us
  Pallas kernels: 206 us -> 278 us
  local copies, waits for them, and re-layouts: 109 us -> 44.6 us
  matrix products: 18.4 us -> 0 us
  other arithmetic: 42 us -> 29.2 us
    ppermute x45 -> x42, waiting for transfers between devices: 210 us -> 122 us  [xor_move(): return lax.ppermute(x, axis, [(i, i ^ k) for i in range(size)])]
    pallas_call x10 -> x26, Pallas kernels: 162 us -> 234 us  [the longest x4 69.8 us: feed(): pl.pallas_call(functools.partial(feed_kernel, first, last, number), grid=...]
    dynamic_update_slice x25 -> x0, local copies, waits for them, and re-layouts: 32.4 us -> none  [the longest x14 14 us: assemble(): whole = lax.dynamic_update_slice(whole, block, ((self.chip ^ k) * rows, 0))]
    ppermute x5 -> x6, starting transfers between devices: 43.5 us -> 15.5 us  [the longest x4 10.2 us: turned(): return lax.ppermute(x, ('core', 'zhi'), [(0, 1), (1, 3), (2, 0), (3, 2)])]
    ppermute x39 -> x40, starting transfers between devices: 36.8 us -> 62.4 us  [core_swap(): return lax.ppermute(x, 'core', SWAP)]
    dot_general x14 -> x0, matrix products: 18.4 us -> none  [the longest x4 14 us: dot_nt(): lax.dot_general(left, right, (((1,), (1,)), ((), ())), preferred_element_...]
    ppermute x6 -> x12, starting transfers between devices: 13.7 us -> 26.2 us  [home_swap(): return lax.ppermute(x, ('core', 'zhi'), [(0, 0), (1, 2), (2, 1), (3, 3)])]
    unnamed x284 -> x238, local copies, waits for them, and re-layouts: 29.7 us -> 19.8 us
  transfers between devices with their start and end apart: 95 -> 100, of which waited for: 32 -> 29; matrix products, arithmetic and copies ran while one was open for 19% -> 7% of each run, Pallas kernels for 21% -> 38%
where the time goes in v3:
time: 674 us; the launch traced here: 663 us
  Pallas kernels  278 us (41%)
  waiting for transfers between devices  159 us (24%)
  starting transfers between devices  148 us (22%)
  local copies, waits for them, and re-layouts  44.6 us (7%)
  other arithmetic  29.2 us (4%)
    ppermute x42, waiting for transfers between devices, xor_move(): return lax.ppermute(x, axis, [(i, i ^ k) for i in range(size)])  122 us
    pallas_call x4, Pallas kernels, feed(): pl.pallas_call(functools.partial(feed_kernel, first, last, number), grid=...  69.8 us
    ppermute x40, starting transfers between devices, core_swap(): return lax.ppermute(x, 'core', SWAP)  62.4 us
    ppermute x42, starting transfers between devices, xor_move(): return lax.ppermute(x, axis, [(i, i ^ k) for i in range(size)])  43.8 us
    pallas_call x7, Pallas kernels, place(): pl.pallas_call(functools.partial(place_kernel, len(sources), moves, len(o...  38.9 us
    pallas_call x2, Pallas kernels, attend_back(): pl.pallas_call(functools.partial(attend_back_kernel, first, last, start,...  37.6 us
    ppermute x12, starting transfers between devices, home_swap(): return lax.ppermute(x, ('core', 'zhi'), [(0, 0), (1, 2), (2, 1), (3, 3)])  26.2 us
    pallas_call x1, Pallas kernels, cross_back(): pl.pallas_call(functools.partial(cross_back_kernel, members, local), out_...  26.1 us
  transfers between devices with their start and end apart: 100, of which 29 were waited for; matrix products, arithmetic and copies ran while one was open for 7% of the time, Pallas kernels for 38%

profile of v3, /device:TPU:0, one launch (start us, length us, event | category | flops | bytes accessed | tf_op | source)
XLA Modules:
  0.0 662.6 jit_solution(7538790947439088918)
XLA Ops:
  10.3 7.5 %collective-permute-start.2 = (bf16[256,1536]{1,0:T(8,128)(2,1)}, bf16[256,1536]{1,0:T(8,128)(2,1)}, u32[]{:S(2)}, u32[]{:S(2)}) collective-permute-start(bf16[256,1536]{1,0:T(8,128)(2,1)} %bitcast.46), channel_id=1, source_target_pairs={{0,0},{2,4},{4,2},{6,6},{1,1},{3,5},{5,3},{7,7},{8,8},{10,12},{12,... | collective-permute-start | bytes 2359304 | tf_op jit(solution)/shard_map/ppermute | solution.py:52
  32.0 46.5 %collective-permute-start.10 = (bf16[256,1536]{1,0:T(8,128)(2,1)}, bf16[256,1536]{1,0:T(8,128)(2,1)S(1)}, u32[]{:S(2)}, u32[]{:S(2)}) collective-permute-start(bf16[256,1536]{1,0:T(8,128)(2,1)} %collective-permute-done.2.refs_0_.x_ref), channel_id=1, source_target_pairs={{0,4},{4,0},{1,5},{5,1},{2,6},{6,2},{3,7},{7,3},{8,12},{12,8},{9,1... | collective-permute-start | bytes 2359304 | tf_op jit(solution)/shard_map/ppermute | solution.py:44
  86.7 11.6 %collective-permute-done.8.refs_2_ = bf16[256,1536]{1,0:T(8,128)(2,1)} collective-permute-done((bf16[256,1536]{1,0:T(8,128)(2,1)}, bf16[256,1536]{1,0:T(8,128)(2,1)}, u32[]{:S(2)}, u32[]{:S(2)}) %collective-permute-start.8) | collective-permute-done | bytes 786464 | tf_op jit(solution)/shard_map/ppermute | solution.py:48
  119.5 12.5 %collective-permute-done.18.refs_8_ = bf16[384,768]{1,0:T(8,128)(2,1)} collective-permute-done((bf16[384,768]{1,0:T(8,128)(2,1)S(1)}, bf16[384,768]{1,0:T(8,128)(2,1)}, u32[]{:S(2)}, u32[]{:S(2)}) %collective-permute-start.18) | collective-permute-done | bytes 589856 | tf_op jit(solution)/shard_map/ppermute | solution.py:48
  143.5 14.1 %shard_map.228 = (bf16[1024,384]{1,0:T(8,128)(2,1)}, bf16[1024,384]{1,0:T(8,128)(2,1)}, bf16[1024,384]{1,0:T(8,128)(2,1)}, bf16[1024,16]{1,0:T(8,128)(2,1)}, bf16[1024,1536]{1,0:T(8,128)(2,1)}) custom-call(bf16[256,1536]{1,0:T(8,128)(2,1)} %collective-permute-done.2.refs_0_.x_ref, bf16[256,1536]{1,0:T(8,128)(2,1)} %copy-done.102, ...), custom_call_target="tpu_custom_call" | custom-call | flops 4882169856 | bytes 4767744 | tf_op jit(solution)/shard_map/pallas_call | solution.py:266
  157.6 10.9 %shard_map.229 = (bf16[512,384]{1,0:T(8,128)(2,1)}, f32[8,512]{1,0:T(8,128)}, bf16[256,1664]{1,0:T(8,128)(2,1)}, bf16[256,1664]{1,0:T(8,128)(2,1)}) custom-call(bf16[1024,384]{1,0:T(8,128)(2,1)} %get-tuple-element.634.q_ref.refs_4_, bf16[1024,384]{1,0:T(8,128)(2,1)} %get-tuple-element.615.k_ref.refs_5_, bf16[1024,384]{1,0:T(8,128)(2,1)} %get-tuple-element.616.v_ref.refs_6_, ...), custom_call_target="tpu_custom_call" | custom-call | flops 3221225472 | bytes 9535488 | tf_op jit(solution)/shard_map/pallas_call | solution.py:305
  179.8 11.3 %shard_map.230 = (bf16[512,384]{1,0:T(8,128)(2,1)}, f32[8,512]{1,0:T(8,128)}, bf16[256,1664]{1,0:T(8,128)(2,1)}, bf16[256,1664]{1,0:T(8,128)(2,1)}) custom-call(bf16[1024,384]{1,0:T(8,128)(2,1)} %get-tuple-element.634.q_ref.refs_4_, bf16[1024,384]{1,0:T(8,128)(2,1)} %get-tuple-element.615.k_ref.refs_5_, bf16[1024,384]{1,0:T(8,128)(2,1)} %get-tuple-element.616.v_ref.refs_6_, ...), custom_call_target="tpu_custom_call" | custom-call | flops 3221225472 | bytes 9535488 | tf_op jit(solution)/shard_map/pallas_call | solution.py:305
  191.1 8.9 %collective-permute-done.23.refs_13_ = bf16[256,1664]{1,0:T(8,128)(2,1)S(1)} collective-permute-done((bf16[256,1664]{1,0:T(8,128)(2,1)S(1)}, bf16[256,1664]{1,0:T(8,128)(2,1)S(1)}, u32[]{:S(2)}, u32[]{:S(2)}) %collective-permute-start.23) | collective-permute-done | bytes 852000 | tf_op jit(solution)/shard_map/ppermute | solution.py:48
  250.7 9.4 %shard_map.233.refs_6_.refs_14_ = bf16[4,1552,768]{2,1,0:T(8,128)(2,1)} custom-call(s32[23]{0:T(128)} %stack.106.places_ref, bf16[768,768]{1,0:T(8,128)(2,1)} %shard_map.226.refs_0_, bf16[384,768]{1,0:T(8,128)(2,1)} %copy-done.35, bf16[768,768]{1,0:T(8,128)(2,1)} %copy-done.10, bf16[384,768]{1,0:T(8,128)(2,1)} %copy-done.36, bf16[768,768]{1,0:T(8,128)(2,1)} %copy-done.4, ...), custom_call_target="tpu_custom_call" | custom-call | tf_op jit(solution)/shard_map/pallas_call | solution.py:120
  260.1 10.4 %collective-permute-done.31.refs_6_.refs_2_ = bf16[256,1536]{1,0:T(8,128)(2,1)} collective-permute-done((bf16[256,1536]{1,0:T(8,128)(2,1)}, bf16[256,1536]{1,0:T(8,128)(2,1)}, u32[]{:S(2)}, u32[]{:S(2)}) %collective-permute-start.31) | collective-permute-done | bytes 786464 | tf_op jit(solution)/shard_map/ppermute | solution.py:48
  273.8 17.5 %shard_map.234 = (f32[256,1536]{1,0:T(8,128)}, f32[256,1536]{1,0:T(8,128)}, bf16[256,1536]{1,0:T(8,128)(2,1)}, bf16[256,1536]{1,0:T(8,128)(2,1)}, bf16[256,1536]...) custom-call(bf16[256,1536]{1,0:T(8,128)(2,1)} %collective-permute-do, ...), custom_call_target="tpu_custom_call" | custom-call | flops 14495514624 | bytes 18874368 | tf_op jit(solution)/shard_map/pallas_call | solution.py:515
  300.5 7.4 %collective-permute-done.55 = bf16[192,1536]{1,0:T(8,128)(2,1)S(1)} collective-permute-done((bf16[192,1536]{1,0:T(8,128)(2,1)S(1)}, bf16[192,1536]{1,0:T(8,128)(2,1)S(1)}, u32[]{:S(2)}, u32[]{:S(2)}) %collective-permute-start.55) | collective-permute-done | bytes 589856 | tf_op jit(solution)/shard_map/ppermute | solution.py:56
  307.9 10.1 %collective-permute-done.53.refs_2_.refs_0_ = bf16[256,1536]{1,0:T(8,128)(2,1)} collective-permute-done((bf16[256,1536]{1,0:T(8,128)(2,1)}, bf16[256,1536]{1,0:T(8,128)(2,1)}, u32[]{:S(2)}, u32[]{:S(2)}) %collective-permute-start.53) | collective-permute-done | bytes 786464 | tf_op jit(solution)/shard_map/ppermute | solution.py:48
  333.8 20.5 %shard_map.236 = (bf16[1024,1552]{1,0:T(8,128)(2,1)}, bf16[1024,1552]{1,0:T(8,128)(2,1)}, f32[16,512]{1,0:T(8,128)}, f32[16,512]{1,0:T(8,128)}, f32[16,512]{1,0:T(8,128)}) custom-call(bf16[256,1536]{1,0:T(8,128)(2,1)} %get-tuple-element.819.refs_0_, bf16[256,1536]{1,0:T(8,128)(2,1)} %copy-done.104, ...), custom_call_target="tpu_custom_call" | custom-call | flops 19528679424 | bytes 4767744 | tf_op jit(solution)/shard_map/pallas_call | solution.py:814
  354.3 18.5 %collective-permute-done.59.refs_3_.refs_1_ = bf16[576,1536]{1,0:T(8,128)(2,1)S(1)} collective-permute-done((bf16[576,1536]{1,0:T(8,128)(2,1)S(1)}, bf16[576,1536]{1,0:T(8,128)(2,1)S(1)}, u32[]{:S(2)}, u32[]{:S(2)}) %collective-permute-start.59) | collective-permute-done | bytes 1769504 | tf_op jit(solution)/shard_map/ppermute | solution.py:48
  382.7 21.2 %shard_map.238 = (bf16[1024,1552]{1,0:T(8,128)(2,1)}, bf16[1024,1552]{1,0:T(8,128)(2,1)}, f32[16,512]{1,0:T(8,128)}, f32[16,512]{1,0:T(8,128)}, f32[16,512]{1,0:T(8,128)}) custom-call(bf16[256,1536]{1,0:T(8,128)(2,1)} %get-tuple-element.819.refs_0_, bf16[256,1536]{1,0:T(8,128)(2,1)} %copy-done.104, ...), custom_call_target="tpu_custom_call" | custom-call | flops 19528679424 | bytes 4767744 | tf_op jit(solution)/shard_map/pallas_call | solution.py:814
  411.2 13.9 %shard_map.240 = (bf16[256,1664]{1,0:T(8,128)(2,1)}, bf16[256,1664]{1,0:T(8,128)(2,1)}, bf16[256,1664]{1,0:T(8,128)(2,1)}, bf16[256,1664]{1,0:T(8,128)(2,1)}, f3...) custom-call(bf16[256,1536]{1,0:T(8,128)(2,1)} %collective-permute-done.53.refs_2_.refs_0_, ...), custom_call_target="tpu_custom_call" | custom-call | flops 9764339712 | bytes 4767744 | tf_op jit(solution)/shard_map/pallas_call | solution.py:814
  431.8 14.2 %shard_map.241 = (bf16[256,1664]{1,0:T(8,128)(2,1)}, bf16[256,1664]{1,0:T(8,128)(2,1)}, bf16[256,1664]{1,0:T(8,128)(2,1)}, bf16[256,1664]{1,0:T(8,128)(2,1)}, f3...) custom-call(bf16[256,1536]{1,0:T(8,128)(2,1)} %get-tuple-element.819.refs_0_, ...), custom_call_target="tpu_custom_call" | custom-call | flops 9764339712 | bytes 4767744 | tf_op jit(solution)/shard_map/pallas_call | solution.py:814
  456.6 26.1 %shard_map.242 = (f32[256,1536]{1,0:T(8,128)}, bf16[256,1536]{1,0:T(8,128)(2,1)}, bf16[4,48,384]{2,1,0:T(8,128)(2,1)}, bf16[4,32,384]{2,1,0:T(8,128)(2,1)}, bf16...) custom-call(bf16[256,1536]{1,0:T(8,128)(2,1)} %copy-done.32, ...), custom_call_target="tpu_custom_call" | custom-call | flops 19327352832 | bytes 18874368 | tf_op jit(solution)/shard_map/pallas_call | solution.py:585
  486.2 17.6 %shard_map.244 = (bf16[512,384]{1,0:T(8,128)(2,1)}, f32[1024,384]{1,0:T(8,128)}, f32[1024,384]{1,0:T(8,128)}, f32[16,384]{1,0:T(8,128)}) custom-call(bf16[256,1536]{1,0:T(8,128)(2,1)} %get-tuple-element.862.refs_0_.r_ref, bf16[256,1536]{1,0:T(8,128)(2,1)} %copy-done.107, bf16[16,1536]{1,0:T(8,128)(2,1)} %get-tuple-element.1083.refs_1_.refs_2_, ...), custom_call_target="tpu_custom_call" | custom-call | flops 8053063680 | bytes 3932160 | tf_op jit(solution)/shard_map/pallas_call | solution.py:434
  515.9 20.0 %shard_map.245 = (bf16[1024,1152]{1,0:T(8,128)(2,1)}, f32[16,384]{1,0:T(8,128)}, f32[16,1152]{1,0:T(8,128)}) custom-call(bf16[256,1536]{1,0:T(8,128)(2,1)} %copy-done.103, bf16[256,1536]{1,0:T(8,128)(2,1)} %copy-done.105, bf16[16,1536]{1,0:T(8,128)(2,1)} %get-tuple-element.1083.refs_1_.refs_2_, bf16[1552,1536]{1,0:T(8,128)(2,1)} %shard_map.227.refs_7_.w_ref.refs_3_, ...), custom_call_target="tpu_custom_call" | custom-call | flops 8053063680 | bytes 3932160 | tf_op jit(solution)/shard_map/pallas_call | solution.py:434
  575.9 8.8 %collective-permute-done.90 = bf16[19,16,384]{2,1,0:T(8,128)(2,1)S(1)} collective-permute-done((bf16[19,16,384]{2,1,0:T(8,128)(2,1)}, bf16[19,16,384]{2,1,0:T(8,128)(2,1)S(1)}, u32[]{:S(2)}, u32[]{:S(2)}) %collective-permute-start.90) | collective-permute-done | bytes 233504 | tf_op jit(solution)/shard_map/ppermute | solution.py:60
  618.9 20.9 %collective-permute-done.96 = bf16[20,16,384]{2,0,1:T(8,128)(2,1)S(1)} collective-permute-done((bf16[20,16,384]{2,0,1:T(8,128)(2,1)S(1)}, bf16[20,16,384]{2,0,1:T(8,128)(2,1)S(1)}, u32[]{:S(2)}, u32[]{:S(2)}) %collective-permute-start.96) | collective-permute-done | bytes 245792 | tf_op jit(solution)/shard_map/ppermute | solution.py:48
  652.3 7.8 %shard_map.252 = (f32[8,6,16,384]{3,2,1,0:T(8,128)}, f32[8,9,16,384]{3,2,1,0:T(8,128)}) custom-call(s32[8]{0:T(128)} %get-tuple-element.1146.labels_ref, bf16[8,10,16,384]{3,2,1,0:T(8,128)(2,1)} %bitcast.219, f32[8,6,16,384]{3,2,1,0:T(8,128)} %get-tuple-element.1031.down_in, f32[8,9,16,384]{3,2,1,0:T(8,128)} %get-tuple-element.1032.up_in), custom_call_target="tpu_custom_call" | custom-call | tf_op jit(solution)/shard_map/pallas_call | solution.py:893
  (581 shorter events, 290.9 us)
Async XLA Ops:
  25.9 60.8 %collective-permute-start.9 = (bf16[192,1536]{1,0:T(8,128)(2,1)S(1)}, bf16[192,1536]{1,0:T(8,128)(2,1)S(1)}, u32[]{:S(2)}, u32[]{:S(2)}) collective-permute-start(bf16[192,1536]{1,0:T(8,128)(2,1)S(1)} %pad_maximum_fusion.10), channel_id=1, source_target_pairs={{0,2},{2,0},{1,3},{3,1},{4,6},{6,4},{5,7},{7,5},{8,10},{10,8},{9,1... | collective-permute-start | bytes 1769480 | tf_op jit(solution)/shard_map/ppermute | solution.py:48
  28.1 70.2 %collective-permute-start.6 = (bf16[384,1536]{1,0:T(8,128)(2,1)S(1)}, bf16[384,1536]{1,0:T(8,128)(2,1)S(1)}, u32[]{:S(2)}, u32[]{:S(2)}) collective-permute-start(bf16[384,1536]{1,0:T(8,128)(2,1)S(1)} %pad_maximum_fusion.5.refs_0_), channel_id=1, source_target_pairs={{0,8},{8,0},{16,24},{24,16},{1,9},{9,1},{17,25},{25,17},{2,10},{10... | collective-permute-start | bytes 3538952 | tf_op jit(solution)/shard_map/ppermute | solution.py:48
  30.5 67.8 %collective-permute-start.7 = (bf16[384,1536]{1,0:T(8,128)(2,1)S(1)}, bf16[384,1536]{1,0:T(8,128)(2,1)S(1)}, u32[]{:S(2)}, u32[]{:S(2)}) collective-permute-start(bf16[384,1536]{1,0:T(8,128)(2,1)S(1)} %pad_maximum_fusion.5.refs_0_), channel_id=1, source_target_pairs={{0,16},{8,24},{16,0},{24,8},{1,17},{9,25},{17,1},{25,9},{2,18},{10... | collective-permute-start | bytes 3538952 | tf_op jit(solution)/shard_map/ppermute | solution.py:48
  32.0 54.7 %collective-permute-start.10 = (bf16[256,1536]{1,0:T(8,128)(2,1)}, bf16[256,1536]{1,0:T(8,128)(2,1)S(1)}, u32[]{:S(2)}, u32[]{:S(2)}) collective-permute-start(bf16[256,1536]{1,0:T(8,128)(2,1)} %collective-permute-done.2.refs_0_.x_ref), channel_id=1, source_target_pairs={{0,4},{4,0},{1,5},{5,1},{2,6},{6,2},{3,7},{7,3},{8,12},{12,8},{9,1... | collective-permute-start | bytes 2359304 | tf_op jit(solution)/shard_map/ppermute | solution.py:44
  113.6 55.0 %collective-permute-start.13 = (bf16[768,768]{1,0:T(8,128)(2,1)}, bf16[768,768]{1,0:T(8,128)(2,1)S(1)}, u32[]{:S(2)}, u32[]{:S(2)}) collective-permute-start(bf16[768,768]{1,0:T(8,128)(2,1)} %shard_map.226.refs_0_), channel_id=1, source_target_pairs={{0,8},{8,0},{16,24},{24,16},{1,9},{9,1},{17,25},{25,17},{2,10},{10... | collective-permute-start | bytes 3538952 | tf_op jit(solution)/shard_map/ppermute | solution.py:48
  118.5 50.1 %collective-permute-start.14 = (bf16[768,768]{1,0:T(8,128)(2,1)}, bf16[768,768]{1,0:T(8,128)(2,1)S(1)}, u32[]{:S(2)}, u32[]{:S(2)}) collective-permute-start(bf16[768,768]{1,0:T(8,128)(2,1)} %shard_map.226.refs_0_), channel_id=1, source_target_pairs={{0,16},{8,24},{16,0},{24,8},{1,17},{9,25},{17,1},{25,9},{2,18},{10... | collective-permute-start | bytes 3538952 | tf_op jit(solution)/shard_map/ppermute | solution.py:48
  138.9 29.7 %collective-permute-start.21 = (bf16[256,1536]{1,0:T(8,128)(2,1)S(1)}, bf16[256,1536]{1,0:T(8,128)(2,1)S(1)}, u32[]{:S(2)}, u32[]{:S(2)}) collective-permute-start(bf16[256,1536]{1,0:T(8,128)(2,1)S(1)} %bitcast.240), channel_id=1, source_target_pairs={{0,0},{2,4},{4,2},{6,6},{1,1},{3,5},{5,3},{7,7},{8,8},{10,12},{12,... | collective-permute-start | bytes 2359304 | tf_op jit(solution)/shard_map/ppermute | solution.py:52
  177.2 28.2 %collective-permute-start.24 = (bf16[768,768]{1,0:T(8,128)(2,1)S(1)}, bf16[768,768]{1,0:T(8,128)(2,1)S(1)}, u32[]{:S(2)}, u32[]{:S(2)}) collective-permute-start(bf16[768,768]{1,0:T(8,128)(2,1)S(1)} %get-tuple-element.642), channel_id=1, source_target_pairs={{0,8},{8,0},{16,24},{24,16},{1,9},{9,1},{17,25},{25,17},{2,10},{10... | collective-permute-start | bytes 3538952 | tf_op jit(solution)/shard_map/ppermute | solution.py:48
  178.0 27.8 %collective-permute-start.25 = (bf16[768,768]{1,0:T(8,128)(2,1)S(1)}, bf16[768,768]{1,0:T(8,128)(2,1)S(1)}, u32[]{:S(2)}, u32[]{:S(2)}) collective-permute-start(bf16[768,768]{1,0:T(8,128)(2,1)S(1)} %get-tuple-element.643), channel_id=1, source_target_pairs={{0,16},{8,24},{16,0},{24,8},{1,17},{9,25},{17,1},{25,9},{2,18},{10... | collective-permute-start | bytes 3538952 | tf_op jit(solution)/shard_map/ppermute | solution.py:48
  238.6 32.6 %collective-permute-start.29 = (bf16[384,1536]{1,0:T(8,128)(2,1)S(1)}, bf16[384,1536]{1,0:T(8,128)(2,1)S(1)}, u32[]{:S(2)}, u32[]{:S(2)}) collective-permute-start(bf16[384,1536]{1,0:T(8,128)(2,1)S(1)} %copy-done.11), channel_id=1, source_target_pairs={{0,8},{8,0},{16,24},{24,16},{1,9},{9,1},{17,25},{25,17},{2,10},{10... | collective-permute-start | bytes 3538952 | tf_op jit(solution)/shard_map/ppermute | solution.py:48
  241.0 30.2 %collective-permute-start.30 = (bf16[384,1536]{1,0:T(8,128)(2,1)S(1)}, bf16[384,1536]{1,0:T(8,128)(2,1)S(1)}, u32[]{:S(2)}, u32[]{:S(2)}) collective-permute-start(bf16[384,1536]{1,0:T(8,128)(2,1)S(1)} %copy-done.11), channel_id=1, source_target_pairs={{0,16},{8,24},{16,0},{24,8},{1,17},{9,25},{17,1},{25,9},{2,18},{10... | collective-permute-start | bytes 3538952 | tf_op jit(solution)/shard_map/ppermute | solution.py:48
  241.9 28.6 %collective-permute-start.31 = (bf16[256,1536]{1,0:T(8,128)(2,1)}, bf16[256,1536]{1,0:T(8,128)(2,1)}, u32[]{:S(2)}, u32[]{:S(2)}) collective-permute-start(bf16[256,1536]{1,0:T(8,128)(2,1)} %copy-done.32), channel_id=1, source_target_pairs={{0,1},{1,0},{2,3},{3,2},{4,5},{5,4},{6,7},{7,6},{8,9},{9,8},{10,11... | collective-permute-start | bytes 2359304 | tf_op jit(solution)/shard_map/ppermute | solution.py:48
  246.0 45.3 %collective-permute-start.49 = (bf16[192,1536]{1,0:T(8,128)(2,1)}, bf16[192,1536]{1,0:T(8,128)(2,1)S(1)}, u32[]{:S(2)}, u32[]{:S(2)}) collective-permute-start(bf16[192,1536]{1,0:T(8,128)(2,1)} %pad_maximum_fusion.13), channel_id=1, source_target_pairs={{0,0},{2,4},{4,2},{6,6},{1,1},{3,5},{5,3},{7,7},{8,8},{10,12},{12,... | collective-permute-start | bytes 1769480 | tf_op jit(solution)/shard_map/ppermute | solution.py:52
  247.9 46.3 %collective-permute-start.50 = (bf16[192,1536]{1,0:T(8,128)(2,1)}, bf16[192,1536]{1,0:T(8,128)(2,1)S(1)}, u32[]{:S(2)}, u32[]{:S(2)}) collective-permute-start(bf16[192,1536]{1,0:T(8,128)(2,1)} %pad_maximum_fusion.13), channel_id=1, source_target_pairs={{0,2},{2,6},{4,0},{6,4},{1,3},{3,7},{5,1},{7,5},{8,10},{10,14},{12... | collective-permute-start | bytes 1769480 | tf_op jit(solution)/shard_map/ppermute | solution.py:56
  270.5 30.0 %collective-permute-start.54 = (bf16[192,1536]{1,0:T(8,128)(2,1)S(1)}, bf16[192,1536]{1,0:T(8,128)(2,1)S(1)}, u32[]{:S(2)}, u32[]{:S(2)}) collective-permute-start(bf16[192,1536]{1,0:T(8,128)(2,1)S(1)} %copy-done.44), channel_id=1, source_target_pairs={{0,0},{2,4},{4,2},{6,6},{1,1},{3,5},{5,3},{7,7},{8,8},{10,12},{12,... | collective-permute-start | bytes 1769480 | tf_op jit(solution)/shard_map/ppermute | solution.py:52
  331.7 41.1 %collective-permute-start.59 = (bf16[576,1536]{1,0:T(8,128)(2,1)S(1)}, bf16[576,1536]{1,0:T(8,128)(2,1)S(1)}, u32[]{:S(2)}, u32[]{:S(2)}) collective-permute-start(bf16[576,1536]{1,0:T(8,128)(2,1)S(1)} %get-tuple-element.754), channel_id=1, source_target_pairs={{0,8},{8,0},{16,24},{24,16},{1,9},{9,1},{17,25},{25,17},{2,10},{10... | collective-permute-start | bytes 5308424 | tf_op jit(solution)/shard_map/ppermute | solution.py:48
  332.9 40.7 %collective-permute-start.60 = (bf16[576,1536]{1,0:T(8,128)(2,1)S(1)}, bf16[576,1536]{1,0:T(8,128)(2,1)S(1)}, u32[]{:S(2)}, u32[]{:S(2)}) collective-permute-start(bf16[576,1536]{1,0:T(8,128)(2,1)S(1)} %get-tuple-element.755), channel_id=1, source_target_pairs={{0,16},{8,24},{16,0},{24,8},{1,17},{9,25},{17,1},{25,9},{2,18},{10... | collective-permute-start | bytes 5308424 | tf_op jit(solution)/shard_map/ppermute | solution.py:48
  455.4 27.4 %collective-permute-start.68 = (bf16[256,1664]{1,0:T(8,128)(2,1)S(1)}, bf16[256,1664]{1,0:T(8,128)(2,1)S(1)}, u32[]{:S(2)}, u32[]{:S(2)}) collective-permute-start(bf16[256,1664]{1,0:T(8,128)(2,1)S(1)} %add_convert_fusion.1), channel_id=1, source_target_pairs={{0,1},{1,0},{2,3},{3,2},{4,5},{5,4},{6,7},{7,6},{8,9},{9,8},{10,11... | collective-permute-start | bytes 2555912 | tf_op jit(solution)/shard_map/ppermute | solution.py:48
  512.1 43.9 %collective-permute-start.77 = (bf16[256,1536]{1,0:T(8,128)(2,1)}, bf16[256,1536]{1,0:T(8,128)(2,1)S(1)}, u32[]{:S(2)}, u32[]{:S(2)}) collective-permute-start(bf16[256,1536]{1,0:T(8,128)(2,1)} %get-tuple-element.896), channel_id=1, source_target_pairs={{0,0},{2,4},{4,2},{6,6},{1,1},{3,5},{5,3},{7,7},{8,8},{10,12},{12,... | collective-permute-start | bytes 2359304 | tf_op jit(solution)/shard_map/ppermute | solution.py:52
  513.9 42.1 %collective-permute-start.76 = (bf16[130,768]{1,0:T(8,128)(2,1)S(1)}, bf16[130,768]{1,0:T(8,128)(2,1)S(1)}, u32[]{:S(2)}, u32[]{:S(2)}) collective-permute-start(bf16[130,768]{1,0:T(8,128)(2,1)S(1)} %add_convert_fusion.4), channel_id=1, source_target_pairs={{0,1},{1,0},{2,3},{3,2},{4,5},{5,4},{6,7},{7,6},{8,9},{9,8},{10,11... | collective-permute-start | bytes 599048 | tf_op jit(solution)/shard_map/ppermute | solution.py:48
  514.8 41.3 %collective-permute-start.75 = (bf16[96,384]{1,0:T(8,128)(2,1)S(1)}, bf16[96,384]{1,0:T(8,128)(2,1)S(1)}, u32[]{:S(2)}, u32[]{:S(2)}) collective-permute-start(bf16[96,384]{1,0:T(8,128)(2,1)S(1)} %add_convert_fusion.6), channel_id=1, source_target_pairs={{0,1},{1,0},{2,3},{3,2},{4,5},{5,4},{6,7},{7,6},{8,9},{9,8},{10,11... | collective-permute-start | bytes 221192 | tf_op jit(solution)/shard_map/ppermute | solution.py:48
  574.9 30.4 %collective-permute-start.80 = (bf16[256,1664]{1,0:T(8,128)(2,1)S(1)}, bf16[256,1664]{1,0:T(8,128)(2,1)S(1)}, u32[]{:S(2)}, u32[]{:S(2)}) collective-permute-start(bf16[256,1664]{1,0:T(8,128)(2,1)S(1)} %add_convert_fusion), channel_id=1, source_target_pairs={{0,1},{1,0},{2,3},{3,2},{4,5},{5,4},{6,7},{7,6},{8,9},{9,8},{10,11... | collective-permute-start | bytes 2555912 | tf_op jit(solution)/shard_map/ppermute | solution.py:48
  610.9 49.2 %collective-permute-start.86 = (bf16[256,1536]{1,0:T(8,128)(2,1)}, bf16[256,1536]{1,0:T(8,128)(2,1)S(1)}, u32[]{:S(2)}, u32[]{:S(2)}) collective-permute-start(bf16[256,1536]{1,0:T(8,128)(2,1)} %shard_map.250), channel_id=1, source_target_pairs={{0,0},{2,4},{4,2},{6,6},{1,1},{3,5},{5,3},{7,7},{8,8},{10,12},{12,... | collective-permute-start | bytes 2359304 | tf_op jit(solution)/shard_map/ppermute | solution.py:52
  612.8 27.5 %collective-permute-start.97 = (bf16[38,16,384]{2,1,0:T(8,128)(2,1)S(1)}, bf16[38,16,384]{2,1,0:T(8,128)(2,1)S(1)}, u32[]{:S(2)}, u32[]{:S(2)}) collective-permute-start(bf16[38,16,384]{2,1,0:T(8,128)(2,1)S(1)} %pad_maximum_fusion.16), channel_id=1, source_target_pairs={{0,8},{8,0},{16,24},{24,16},{1,9},{9,1},{17,25},{25,17},{2,10},{10... | collective-permute-start | bytes 1400840 | tf_op jit(solution)/shard_map/ppermute | solution.py:48
  (191 other events, 2135.8 us)

commit v4 on v3

v4 whole, which is shorter than its diff:
```python
import functools

import jax
import jax.numpy as jnp
from jax import lax
from jax.experimental import pallas as pl
from jax.experimental.pallas import tpu as pltpu
from jax.sharding import Mesh, PartitionSpec as P

HEAD_DIM = 64
ROT = 32
EPSILON = 1e-05
F32 = jnp.float32
BF = jnp.bfloat16
SWAP = ((0, 1), (1, 0))
LANES = 128
VMEM_LIMIT = 56 * 1024 * 1024


def dot(left, right):
    return jnp.dot(left, right, preferred_element_type=F32)


def dot_nt(left, right):
    return lax.dot_general(left, right, (((1,), (1,)), ((), ())), preferred_element_type=F32)


def dot_tn(left, right):
    return lax.dot_general(left, right, (((0,), (0,)), ((), ())), preferred_element_type=F32)


class Order:
    def __init__(self, first):
        self.token = first

    def wait(self, *values):
        *values, self.token = lax.optimization_barrier((*values, self.token))
        return values[0] if len(values) == 1 else values

    mark = wait


def core_swap(x):
    return lax.ppermute(x, "core", SWAP)


def xor_move(x, axis, size, k):
    return lax.ppermute(x, axis, [(i, i ^ k) for i in range(size)])


def home_swap(x):
    return lax.ppermute(x, ("core", "zhi"), [(0, 0), (1, 2), (2, 1), (3, 3)])


def turned(x):
    return lax.ppermute(x, ("core", "zhi"), [(0, 1), (1, 3), (2, 0), (3, 2)])


def turned_back(x):
    return lax.ppermute(x, ("core", "zhi"), [(0, 2), (1, 0), (2, 3), (3, 1)])


class Group:
    def __init__(self, pairs, chips):
        self.pairs, self.chips = pairs, chips
        self.core, self.zhi, self.p = (lax.axis_index(n) for n in ("core", "zhi", "p"))
        self.chip = lax.axis_index("chip")
        self.home = self.core == self.zhi
        self.pieces = [
            (self.core ^ kc) * pairs + (self.p ^ kp) for kp in range(pairs) for kc in (0, 1)
        ]

    def far_p(self, own):
        return [xor_move(own, "p", self.pairs, k) for k in range(1, self.pairs)]

    def near_sums(self, own, other):
        return own.astype(F32) + other.astype(F32)

    def cross(self, shard):
        return xor_move(shard, "zhi", 2, 1)

    def spread_one(self, block):
        if self.chips == 4:
            return [xor_move(block, "chip", 4, k) for k in (1, 2)]
        return [xor_move(block, "chip", self.chips, k) for k in range(1, self.chips)]

    def spread_two(self, got):
        if self.chips != 4:
            return []
        half = got[0].shape[0] // 2
        return [xor_move(got[1][:half], "chip", 4, 1), xor_move(got[0][half:], "chip", 4, 2)]

    def places(self, rows):
        if self.chips == 4:
            diagonal = (self.chip ^ 3) * rows
            return [(self.chip ^ 1) * rows, (self.chip ^ 2) * rows, diagonal, diagonal + rows // 2]
        return [(self.chip ^ k) * rows for k in range(1, self.chips)]


class Weight:
    def __init__(self, shape, places):
        self.shape, self.places, self.arrays, self.moves = shape, places, [], []

    def add(self, array, *parts):
        self.moves += [(len(self.arrays), *part) for part in parts]
        self.arrays.append(array)

    @property
    def count(self):
        return len(self.arrays)

    def specs(self):
        return [pl.BlockSpec(memory_space=pl.ANY)] * self.count

    def columns(self, start, size):
        if size % 128 or start % 128:
            return 0, self.shape[-1], start
        return start, size, 0

    def scratch(self, size=None):
        shape = self.shape if size is None else self.shape[:-1] + (size,)
        return [pltpu.VMEM(shape, BF), pltpu.SemaphoreType.DMA((len(self.moves),))]

    def at_first(self, step, refs, places_ref, target, sems, start=0, size=None):
        def begin():
            @pl.when(step == 0)
            def _():
                self.bring(refs, places_ref, target, sems, start, size)

        def end():
            @pl.when(step == 0)
            def _():
                wait_for(self.bring(refs, places_ref, target, sems, start, size, go=False))

        return begin, end

    def bring(self, refs, places_ref, target, sems, start=0, size=None, go=True):
        copies = []
        for number, (source, row, rows, column, columns, lead, place, offset) in enumerate(self.moves):
            at = pl.ds(pl.multiple_of(places_ref[place] + offset, 16), rows)
            to = target.at[at] if lead is None else target.at[lead, at]
            if size is not None:
                column, columns = column + start, size
            found = refs[source].at[pl.ds(row, rows), pl.ds(column, columns)]
            copies.append(pltpu.make_async_copy(found, to, sems.at[number]))
        if go:
            for copy in copies:
                copy.start()
        return copies


def wait_for(copies):
    for copy in copies:
        copy.wait()


def weight_call(kernel, weight, grid, in_specs, out_specs, out_shape, scratch, estimate, arrays):
    return pl.pallas_call(
        kernel,
        grid_spec=pltpu.PrefetchScalarGridSpec(
            num_scalar_prefetch=1,
            grid=grid,
            in_specs=weight.specs() + in_specs,
            out_specs=out_specs,
            scratch_shapes=scratch,
        ),
        out_shape=out_shape,
        compiler_params=params(),
        cost_estimate=estimate,
    )(weight.places, *weight.arrays, *arrays)


def stats(stream):
    average = jnp.mean(stream, axis=-1, keepdims=True)
    centred = stream - average
    variance = jnp.mean(centred * centred, axis=-1, keepdims=True)
    scale = lax.rsqrt(variance + EPSILON)
    return centred * scale, scale


def layer_norm(stream, gain, bias):
    return (stats(stream)[0] * gain + bias).astype(BF)


def norm_backward(stream, gain, grad):
    unit, scale = stats(stream)
    grad = grad * gain
    return scale * (
        grad
        - jnp.mean(grad, axis=-1, keepdims=True)
        - unit * jnp.mean(grad * unit, axis=-1, keepdims=True)
    )


def turn(x, cosines, left_sines, right_sines):
    breadth = 2 * HEAD_DIM if x.shape[1] % (2 * HEAD_DIM) == 0 else HEAD_DIM
    half = ROT // 2
    for at in range(0, x.shape[1], breadth):
        group = x[:, at : at + breadth]
        if breadth % 128 == 0:
            left, right = pltpu.roll(group, breadth - half, 1), pltpu.roll(group, half, 1)
        else:
            left = jnp.concatenate([group[:, half:], group[:, :half]], axis=1)
            right = jnp.concatenate([group[:, -half:], group[:, :-half]], axis=1)
        yield (
            at,
            breadth,
            group * cosines[:, :breadth]
            + left * left_sines[:, :breadth]
            + right * right_sines[:, :breadth],
        )


def head_sums(product):
    columns = product.shape[1]
    rows = -(-columns // HEAD_DIM // 8) * 8
    head = lax.broadcasted_iota(jnp.int32, (rows, columns), 0)
    lane = lax.broadcasted_iota(jnp.int32, (rows, columns), 1)
    picked = jnp.where(lane // HEAD_DIM == head, 1.0, 0.0).astype(F32)
    return lax.dot_general(
        picked, product, (((1,), (1,)), ((), ())),
        precision=lax.Precision.HIGHEST, preferred_element_type=F32,
    )


def whole_spec(shape):
    return pl.BlockSpec(shape, lambda *_: (0,) * len(shape))


def row_spec(rows, columns):
    return pl.BlockSpec((rows, columns), lambda t, *_: (t, 0))


def take_tile(refs, tile_ref, step):
    rows, tile = refs[0].shape[0], tile_ref.shape[0]
    for i, ref in enumerate(refs):

        @pl.when(step == i * rows // tile)
        def _(i=i, ref=ref):
            tile_ref[i * rows % tile : i * rows % tile + rows, :] = ref[...]


def give_tile(value, refs, step):
    rows, (tile, columns) = refs[0].shape[0], value.shape
    for i, ref in enumerate(refs):

        @pl.when(step == i * rows // tile)
        def _(i=i, ref=ref):
            ref[:, :columns] = value[i * rows % tile : i * rows % tile + rows]
            ref[:, columns:] = jnp.zeros((rows, ref.shape[1] - columns), ref.dtype)


def total_of(refs):
    total = refs[0][...].astype(F32)
    for ref in refs[1:]:
        total = total + ref[...].astype(F32)
    return total


def by_piece(ref, row, value):
    local = ref.shape[2]
    for k in range(ref.shape[0]):
        ref[k, row : row + value.shape[0], :] = value[:, k * local : (k + 1) * local].astype(
            ref.dtype
        )


def params(semantics=1):
    return pltpu.CompilerParams(
        dimension_semantics=("arbitrary",) * semantics, vmem_limit_bytes=VMEM_LIMIT
    )


def cost(flops, moved, exps=0):
    return pl.CostEstimate(
        flops=int(flops) or 1000, bytes_accessed=int(moved) or 1000, transcendentals=int(exps)
    )


def sds(shape, dtype):
    return jax.ShapeDtypeStruct(shape, dtype)


def query_kernel(weight, part, count, places_ref, *refs):
    w_refs, refs = refs[: weight.count], refs[weight.count :]
    blocks, (gain_ref, bias_ref, down_ref, cos_ref, left_ref, right_ref), refs = (
        refs[:count],
        refs[count : count + 6],
        refs[count + 6 :],
    )
    q_ref, k_ref, v_ref, low_ref, n_ref, x_ref, w_ref, sems = refs
    step = pl.program_id(0)

    begin, end = weight.at_first(step, w_refs, places_ref, w_ref, sems, *part[:2])
    begin()
    take_tile(blocks, x_ref, step)
    local, width = q_ref.shape[1], x_ref.shape[1]
    normed = layer_norm(x_ref[...].astype(F32), gain_ref[...], bias_ref[...])
    n_ref[...] = normed
    low = dot_nt(normed, down_ref[...]).astype(BF)
    low_ref[...] = low
    end()
    at = slice(part[2], part[2] + 3 * local)
    mixed = dot(normed, w_ref[:width, at]) + dot(low, w_ref[width:, at])
    tables = cos_ref[...], left_ref[...], right_ref[...]
    for at, breadth, turned in turn(mixed[:, :local], *tables):
        q_ref[:, at : at + breadth] = (turned * HEAD_DIM**-0.5).astype(BF)
    for at, breadth, turned in turn(mixed[:, local : 2 * local], *tables):
        k_ref[:, at : at + breadth] = turned.astype(BF)
    v_ref[...] = mixed[:, 2 * local :].astype(BF)


def project_self(blocks, gain, bias, down, weight, tables, rows):
    width = blocks[0].shape[1]
    tokens = len(blocks) * blocks[0].shape[0]
    local = weight.shape[1] // 4
    part = weight.columns(0, 3 * local)
    return weight_call(
        functools.partial(query_kernel, weight, part, len(blocks)),
        weight,
        (tokens // rows,),
        [whole_spec(b.shape) for b in blocks]
        + [whole_spec(gain.shape), whole_spec(bias.shape), whole_spec(down.shape)]
        + [row_spec(rows, t.shape[1]) for t in tables],
        [row_spec(rows, local)] * 3 + [row_spec(rows, down.shape[0]), row_spec(rows, width)],
        [sds((tokens, local), BF)] * 3
        + [sds((tokens, down.shape[0]), BF), sds((tokens, width), BF)],
        [pltpu.VMEM((rows, width), BF), *weight.scratch(part[1])],
        cost(8 * tokens * width * local, 8 * width * local),
        [*blocks, gain, bias, down, *tables],
    )


def attend_kernel(weight, part, places_ref, *refs):
    w_refs, refs = refs[: weight.count], refs[weight.count :]
    q_ref, k_ref, v_ref, o_ref, lse_ref, *y_refs, w_ref, sems = refs
    rows, local = q_ref.shape
    step = pl.program_id(0)

    begin, end = weight.at_first(step, w_refs, places_ref, w_ref, sems, *part[:2])
    begin()
    lanes = lax.broadcasted_iota(jnp.int32, (rows, 128), 1)
    logsums = jnp.zeros((rows, 128), F32)
    for head in range(local // HEAD_DIM):
        at = slice(head * HEAD_DIM, (head + 1) * HEAD_DIM)
        scores = dot_nt(q_ref[:, at], k_ref[:, at])
        top = jnp.max(scores, axis=1, keepdims=True)
        powers = jnp.exp(scores - top)
        total = jnp.sum(powers, axis=1, keepdims=True)
        out = dot(powers.astype(BF), v_ref[:, at]) / total
        o_ref[:, at] = out.astype(BF)
        logsums = jnp.where(lanes == head, top + jnp.log(total), logsums)
    lse_ref[...] = logsums.T[: lse_ref.shape[0]]
    end()
    y = dot_nt(o_ref[...], w_ref[:, part[2] : part[2] + local]).astype(BF)
    give_tile(y, y_refs, step)


def wide_of(weight):
    return weight.shape[-2] // LANES * LANES + LANES


def attend_self(query, keys, values, weight, rows, first, count, block):
    tokens, local = query.shape
    heads = -(-local // HEAD_DIM // 8) * 8
    part = weight.columns(3 * local, local)
    blocks = count * rows // block
    return weight_call(
        functools.partial(attend_kernel, weight, part),
        weight,
        (count,),
        [
            pl.BlockSpec((rows, local), lambda t, *_: (first + t, 0)),
            whole_spec(keys.shape),
            whole_spec(values.shape),
        ],
        [row_spec(rows, local), pl.BlockSpec((heads, rows), lambda t, *_: (0, t))]
        + [whole_spec((block, wide_of(weight)))] * blocks,
        [sds((count * rows, local), BF), sds((heads, count * rows), F32)]
        + [sds((block, wide_of(weight)), BF)] * blocks,
        weight.scratch(part[1]),
        cost(16 * count * rows * tokens * local, 8 * query.size, count * rows * tokens),
        [query, keys, values],
    )


def project_back_kernel(weight, part, local, places_ref, *refs):
    w_refs, refs = refs[: weight.count], refs[weight.count :]
    m_ref, low_ref, *refs, w_ref, sems = refs
    step = pl.program_id(0)

    @pl.when(step == 0)
    def _():
        wait_for(weight.bring(w_refs, places_ref, w_ref, sems, *part[:2]))

    width = w_ref.shape[0] - low_ref.shape[1]
    value = dot_nt(m_ref[...], w_ref[:, part[2] : part[2] + 3 * local]).astype(BF)
    low_ref[...] = value[:, width:]
    give_tile(value, refs, step)


def project_back(mixed, weight, rows, first, count, block, rank):
    local, wide = weight.shape[1] // 4, wide_of(weight)
    part = weight.columns(0, 3 * local)
    blocks = count * rows // block
    return weight_call(
        functools.partial(project_back_kernel, weight, part, local),
        weight,
        (count,),
        [pl.BlockSpec((rows, 3 * local), lambda t, *_: (first + t, 0))],
        [row_spec(rows, rank)] + [whole_spec((block, wide))] * blocks,
        [sds((count * rows, rank), BF)] + [sds((block, wide), BF)] * blocks,
        weight.scratch(part[1]),
        cost(40 * count * rows * wide * local, 8 * wide * local),
        [mixed],
    )


def attend_back_kernel(weight, part, first, last, tiles, number, places_ref, *refs):
    w_refs, refs = refs[: weight.count], refs[weight.count :]
    grads, refs = refs[:number], refs[number:]
    (
        up_ref, q_ref, k_ref, v_ref, o_ref, lse_ref, cos_ref, left_ref, right_ref, low_ref,
    ), refs = refs[:10], refs[10:]
    *refs, g_ref, w_ref, sems = refs

    @pl.when(pl.program_id(0) == 0)
    def _():
        wait_for(weight.bring(w_refs, places_ref, w_ref, sems, *part[:2]))

    take_tile(grads, g_ref, pl.program_id(0))
    if not first:
        (mq_ref, gk_in, gv_in, down_in), refs = refs[:4], refs[4:]
    if last:
        m_ref, down_ref, gup_ref, gk_ref, gv_ref = refs
    else:
        m_ref, gk_ref, gv_ref, down_ref = refs
    step, rows = pl.program_id(0), q_ref.shape[0]
    width, local = g_ref.shape[1], q_ref.shape[1]
    at_rows = pl.ds(pl.multiple_of((step + tiles) * rows, rows), rows)
    at_query = at_rows if last else pl.ds(pl.multiple_of(step * rows, rows), rows)

    @pl.when(step == 0)
    def _():
        if first:
            gk_ref[...] = jnp.zeros_like(gk_ref)
            gv_ref[...] = jnp.zeros_like(gv_ref)
            down_ref[...] = jnp.zeros_like(down_ref)
        else:
            gk_ref[...] = gk_in[...]
            gv_ref[...] = gv_in[...]
            down_ref[...] = down_in[...]
            m_ref[: mq_ref.shape[0], :local] = mq_ref[...]

    grad = g_ref[...]
    grad_low = dot_nt(grad, up_ref[...]).astype(BF)
    at = slice(part[2], part[2] + local)
    grad_out = dot(grad, w_ref[:width, at]) + dot(grad_low, w_ref[width:, at])
    grad_out = grad_out.astype(BF)
    out = o_ref[...]
    down_ref[...] += dot_tn(grad_low, out)
    product = grad_out.astype(F32) * out.astype(F32)
    deltas = head_sums(product)
    parts = []
    for head in range(local // HEAD_DIM):
        at = slice(head * HEAD_DIM, (head + 1) * HEAD_DIM)
        q, k, v, g = q_ref[:, at], k_ref[:, at], v_ref[:, at], grad_out[:, at]
        delta = deltas[head : head + 1]
        probs = jnp.exp(dot_nt(k, q) - lse_ref[head : head + 1, :])
        grad_scores = (probs * (dot_nt(v, g) - delta)).astype(BF)
        gv_ref[:, at] += dot(probs.astype(BF), g)
        gk_ref[:, at] += dot(grad_scores, q)
        parts.append(dot_tn(grad_scores, k) * HEAD_DIM**-0.5)
    tables = cos_ref[at_rows, :], -left_ref[at_rows, :], -right_ref[at_rows, :]
    for at, breadth, turned in turn(jnp.concatenate(parts, axis=1), *tables):
        m_ref[at_query, at : at + breadth] = turned.astype(BF)

    if last:

        @pl.when(step == pl.num_programs(0) - 1)
        def _():
            tables = cos_ref[...], -left_ref[...], -right_ref[...]
            for at, breadth, turned in turn(gk_ref[...], *tables):
                m_ref[:, local + at : local + at + breadth] = turned.astype(BF)
            m_ref[:, 2 * local :] = gv_ref[...].astype(BF)
            gup_ref[...] = dot_tn(low_ref[...], m_ref[...])


def attend_back(grads, up, weight, query, keys, values, out, lse, tables, low, rank, rows, start, before):
    tokens, local = query.shape
    block, width = grads[0].shape
    count = len(grads) * block // rows
    first, last = before is None, (start + count) * rows == tokens
    before = () if first else before
    sums = [sds((tokens, local), F32)] * 2 + [sds((rank, local), F32)]
    if last:
        shapes = [sds((tokens, 3 * local), BF), sums[2], sds((rank, 3 * local), F32)]
        scratch = [pltpu.VMEM((tokens, local), F32)] * 2
    else:
        shapes, scratch = [sds((count * rows, local), BF), *sums], []
    scratch.append(pltpu.VMEM((rows, width), BF))

    def tile(columns):
        return pl.BlockSpec((rows, columns), lambda t, *_: (start + t, 0))

    part = weight.columns(3 * local, local)
    return weight_call(
        functools.partial(attend_back_kernel, weight, part, first, last, start, len(grads)),
        weight,
        (count,),
        [
            *[whole_spec(g.shape) for g in grads],
            whole_spec(up.shape),
            tile(local),
            whole_spec(keys.shape),
            whole_spec(values.shape),
            row_spec(rows, local),
            pl.BlockSpec((lse.shape[0], rows), lambda t, *_: (0, t)),
            *[whole_spec(t.shape) for t in tables],
            whole_spec(low.shape),
            *[whole_spec(b.shape) for b in before],
        ],
        [whole_spec(s.shape) for s in shapes],
        shapes,
        scratch + weight.scratch(part[1]),
        cost(40 * count * rows * tokens * local, 10 * query.size, count * rows * tokens),
        [*grads, up, query, keys, values, out, lse, *tables, low, *before],
    )


def in_order(swap, first, second):
    keep = swap == 0
    return jnp.where(keep, first, second), jnp.where(keep, second, first)


def cross_kernel(weight, members, local, core_at, places_ref, *refs):
    w_refs, refs = refs[: weight.count], refs[weight.count :]
    *refs, w_ref, sems = refs
    copies = weight.bring(w_refs, places_ref, w_ref, sems)
    (x_ref, up_self_ref, up_cross_ref, down_ref, gain_ref, bias_ref), refs = refs[:6], refs[6:]
    kv_refs, refs = refs[:members], refs[members:]
    y_refs, refs = refs[:-10], refs[-10:]
    branch = total_of(y_refs)
    s1_ref, s2_ref, n2_ref, n3_ref, q_ref, o_ref, lse_ref, z2_ref, u_ref, z4_ref = refs
    rows, width = x_ref.shape
    rank = down_ref.shape[0]
    deep = slice(width, width + rank)
    low = branch[:, deep].astype(BF)
    z2_ref[...] = low
    stream = x_ref[...].astype(F32) + branch[:, :width] + dot(low, up_self_ref[...])
    s1_ref[...] = stream
    normed = layer_norm(stream, gain_ref[1:2, :], bias_ref[1:2, :])
    n2_ref[...] = normed
    low = dot_nt(normed, down_ref[...]).astype(BF)
    u_ref[...] = low
    total = jnp.zeros((rows, width + rank), F32)
    wait_for(copies)
    both = 2 * local
    for n in range(members // 2):
        query = dot(normed, w_ref[n, :width, :both]) + dot(low, w_ref[n, deep, :both])
        query = (query * HEAD_DIM**-0.5).astype(BF)
        q_ref[:, n * both : (n + 1) * both] = query
        found = in_order(places_ref[core_at], kv_refs[2 * n][...], kv_refs[2 * n + 1][...])
        parts, logsums = [], []
        for head in range(both // HEAD_DIM):
            keyval, own = found[head * HEAD_DIM // local], head * HEAD_DIM % local
            keys = keyval[:, own : own + HEAD_DIM]
            values = keyval[:, local + own : local + own + HEAD_DIM]
            scores = dot_nt(keys, query[:, head * HEAD_DIM : (head + 1) * HEAD_DIM])
            top = jnp.max(scores, axis=0, keepdims=True)
            powers = jnp.exp(scores - top)
            sums = jnp.sum(powers, axis=0, keepdims=True)
            parts.append(dot_tn(values, powers.astype(BF)) / sums)
            logsums.append(top + jnp.log(sums))
        out = jnp.concatenate(parts, axis=0).T.astype(BF)
        o_ref[:, n * both : (n + 1) * both] = out
        lse_ref[n] = jnp.concatenate(logsums, axis=0)
        total = total + dot_nt(out, w_ref[n, :, both:])
    low = total[:, deep].astype(BF)
    z4_ref[...] = low
    stream = stream + total[:, :width] + dot(low, up_cross_ref[...])
    s2_ref[...] = stream
    n3_ref[...] = layer_norm(stream, gain_ref[2:3, :], bias_ref[2:3, :])


def cross_forward(x, ys, up_self, up_cross, down, gains, biases, weight, keyvals, core_at):
    rows, width = x.shape
    members, local = len(keyvals), weight.shape[2] // 4
    plain, wide = sds((rows, width), BF), sds((rows, width), F32)
    low = sds((rows, down.shape[0]), BF)
    logsums = sds((members // 2, 2 * local // HEAD_DIM, rows), F32)
    shapes = [wide, wide, plain, plain, plain, plain, logsums, low, low, low]
    arrays = [x, up_self, up_cross, down, gains, biases, *keyvals, *ys]
    return weight_call(
        functools.partial(cross_kernel, weight, members, local, core_at),
        weight,
        (1,),
        [whole_spec(a.shape) for a in arrays],
        [whole_spec(o.shape) for o in shapes],
        shapes,
        weight.scratch(),
        cost(24 * rows * width * width, 8 * width * width),
        arrays,
    )


def cross_back_kernel(weight, members, local, core_at, places_ref, *refs):
    w_refs, refs = refs[: weight.count], refs[weight.count :]
    *refs, w_ref, sems = refs
    copies = weight.bring(w_refs, places_ref, w_ref, sems)
    (
        g_ref, s1_ref, s2_ref, n2_ref, q_ref, o_ref, lse_ref, u_ref, z4_ref,
        up_ref, down5_ref, down2_ref, gain_ref, bias_ref,
    ), refs = refs[:14], refs[14:]
    kv_refs, refs = refs[:members], refs[members:]
    dn_refs, (r1_ref, r1b_ref, fixed_ref, near_ref, *gkv_refs) = (
        refs[: -4 - members],
        refs[-4 - members :],
    )
    summed = total_of(dn_refs)
    width = g_ref.shape[1]
    rank = up_ref.shape[0]
    deep = slice(width, width + rank)
    stream = s2_ref[...]
    low = summed[:, deep].astype(BF)
    grad_normed = summed[:, :width] + dot(low, down5_ref[...])
    normed = layer_norm(stream, gain_ref[2:3, :], bias_ref[2:3, :])
    by_piece(fixed_ref, rank, dot_tn(low, normed))
    grad = g_ref[...].astype(F32) + norm_backward(stream, gain_ref[2:3, :], grad_normed)
    branch = grad.astype(BF)
    low = dot_nt(branch, up_ref[...]).astype(BF)
    by_piece(fixed_ref, 2 * rank, dot_tn(z4_ref[...], branch))
    by_piece(near_ref, 0, dot_tn(low, o_ref[...]))
    total = jnp.zeros((g_ref.shape[0], width + rank), F32)
    wait_for(copies)
    both, swap = 2 * local, places_ref[core_at]
    for n in range(members // 2):
        columns = slice(n * both, (n + 1) * both)
        grad_out = dot(branch, w_ref[n, :width, both:]) + dot(low, w_ref[n, deep, both:])
        grad_out = grad_out.astype(BF)
        query = q_ref[:, columns]
        deltas = head_sums(grad_out.astype(F32) * o_ref[:, columns].astype(F32))
        found = in_order(swap, kv_refs[2 * n][...], kv_refs[2 * n + 1][...])
        queries, keys, values = [], [], []
        for head in range(both // HEAD_DIM):
            keyval, own = found[head * HEAD_DIM // local], head * HEAD_DIM % local
            key = keyval[:, own : own + HEAD_DIM]
            value = keyval[:, local + own : local + own + HEAD_DIM]
            at = slice(head * HEAD_DIM, (head + 1) * HEAD_DIM)
            q, g = query[:, at], grad_out[:, at]
            probs = jnp.exp(dot_nt(key, q) - lse_ref[n, head : head + 1, :])
            grad_scores = (probs * (dot_nt(value, g) - deltas[head : head + 1])).astype(BF)
            queries.append(dot_tn(key, grad_scores))
            keys.append(dot(grad_scores, q))
            values.append(dot(probs.astype(BF), g))
        grad_query = (jnp.concatenate(queries, axis=0).T * HEAD_DIM**-0.5).astype(BF)
        half = len(keys) // 2
        first = jnp.concatenate(keys[:half] + values[:half], axis=1).astype(BF)
        second = jnp.concatenate(keys[half:] + values[half:], axis=1).astype(BF)
        gkv_refs[2 * n][...], gkv_refs[2 * n + 1][...] = in_order(swap, first, second)
        ups = dot_tn(u_ref[...], grad_query).astype(BF)
        near_ref[2 * n, rank:, :] = ups[:, :local]
        near_ref[2 * n + 1, rank:, :] = ups[:, local:]
        total = total + dot_nt(grad_query, w_ref[n, :, :both])
    low = total[:, deep].astype(BF)
    by_piece(fixed_ref, 0, dot_tn(low, n2_ref[...]))
    grad_normed = total[:, :width] + dot(low, down2_ref[...])
    grad = grad + norm_backward(s1_ref[...], gain_ref[1:2, :], grad_normed)
    r1_ref[...] = grad
    r1b_ref[...] = grad.astype(BF)


def cross_back(
    g, dns, s1, s2, n2, q, o, lse, u, z4, up, down5, down2, gains, biases, weight, keyvals, core_at
):
    rows, width = g.shape
    rank = up.shape[0]
    members, local = len(keyvals), weight.shape[2] // 4
    shapes = [sds((rows, width), F32), sds((rows, width), BF)]
    shapes += [sds((members, n * rank, local), BF) for n in (3, 2)]
    shapes += [sds(keyvals[0].shape, BF)] * members
    arrays = [g, s1, s2, n2, q, o, lse, u, z4, up, down5, down2, gains, biases, *keyvals, *dns]
    return weight_call(
        functools.partial(cross_back_kernel, weight, members, local, core_at),
        weight,
        (1,),
        [whole_spec(a.shape) for a in arrays],
        [whole_spec(o.shape) for o in shapes],
        shapes,
        weight.scratch(),
        cost(32 * rows * width * width, 8 * width * width),
        arrays,
    )


def output_kernel(s2_ref, up_ref, g_ref, *refs):
    *y_refs, out_ref, gup_ref = refs
    width, rank = out_ref.shape[1], up_ref.shape[0]
    total = total_of(y_refs)
    low = total[:, width : width + rank].astype(BF)
    out_ref[...] = (s2_ref[...] + total[:, :width] + dot(low, up_ref[...])).astype(BF)
    by_piece(gup_ref, 0, dot_tn(low, g_ref[...]))


def output_end(s2, ys, up, g, members):
    rank, width = up.shape
    return pl.pallas_call(
        output_kernel,
        out_shape=[sds(g.shape, BF), sds((members, rank, width // members), BF)],
        compiler_params=pltpu.CompilerParams(vmem_limit_bytes=VMEM_LIMIT),
        cost_estimate=cost(0, 0),
    )(s2, up, g, *ys)


def input_kernel(x_ref, r_ref, down_ref, gain_ref, *refs):
    *dn_refs, out_ref = refs
    width, rank = out_ref.shape[1], down_ref.shape[0]
    total = total_of(dn_refs)
    low = total[:, width : width + rank].astype(BF)
    grad = total[:, :width] + dot(low, down_ref[...])
    back = norm_backward(x_ref[...].astype(F32), gain_ref[...], grad)
    out_ref[...] = (r_ref[...] + back).astype(BF)


def input_end(x, r1, dns, down, gain):
    return pl.pallas_call(
        input_kernel,
        out_shape=sds(x.shape, BF),
        compiler_params=pltpu.CompilerParams(vmem_limit_bytes=VMEM_LIMIT),
        cost_estimate=cost(0, 0),
    )(x, r1, down, gain, *dns)


def rows_kernel(near_ref, far_ref, n_ref, z_ref, r_ref, out_ref):
    rows, rank = near_ref.shape
    down = dot_tn(near_ref[...], n_ref[:rows, :]) + dot_tn(far_ref[...], n_ref[rows:, :])
    by_piece(out_ref, 0, down)
    by_piece(out_ref, rank, dot_tn(z_ref[...], r_ref[...]))


def self_rows(low_near, low_far, normed, low_two, branch, members):
    rank, width = low_near.shape[1], normed.shape[1]
    return pl.pallas_call(
        rows_kernel,
        out_shape=sds((members, 2 * rank, width // members), BF),
        compiler_params=pltpu.CompilerParams(vmem_limit_bytes=VMEM_LIMIT),
        cost_estimate=cost(0, 0),
    )(low_near, low_far, normed, low_two, branch)


def context_kernel(weight, members, at_pieces, places_ref, *refs):
    w_refs, refs = refs[: weight.count], refs[weight.count :]
    blocks, (down_ref, kv_ref, low_ref, w_ref, sems) = refs[:members], refs[members:]
    wait_for(weight.bring(w_refs, places_ref, w_ref, sems))
    rank, local = down_ref.shape[1], blocks[0].shape[1]
    width = members * local
    low, keyval = 0.0, 0.0
    for k in range(members):
        at = pl.ds(pl.multiple_of(places_ref[at_pieces + k], local), local)
        low = low + dot(blocks[k][...], down_ref[at, :])
        keyval = keyval + dot(blocks[k][...], w_ref[at, :])
    low = low.astype(BF)
    low_ref[...] = low
    kv_ref[...] = (keyval + dot(low, w_ref[width : width + rank, :])).astype(BF)


def context_forward(at_pieces, blocks, weight, down):
    count = blocks[0].shape[0]
    arrays = (*blocks, down)
    shapes = [sds((count, weight.shape[1]), BF), sds((count, down.shape[1]), BF)]
    return weight_call(
        functools.partial(context_kernel, weight, len(blocks), at_pieces),
        weight,
        (1,),
        [whole_spec(a.shape) for a in arrays],
        [whole_spec(s.shape) for s in shapes],
        shapes,
        weight.scratch(),
        cost(0, 0),
        arrays,
    )


def context_back_kernel(weight, members, at_pieces, places_ref, *refs):
    w_refs, refs = refs[: weight.count], refs[weight.count :]
    blocks, (down_ref, low_ref, g_ref), refs = (
        refs[:members],
        refs[members : members + 3],
        refs[members + 3 :],
    )
    gup_ref, *refs, w_ref, sems = refs
    wait_for(weight.bring(w_refs, places_ref, w_ref, sems))
    rank, local = down_ref.shape[1], blocks[0].shape[1]
    width = members * local
    grad = g_ref[...]
    low = dot_nt(grad, w_ref[width : width + rank, :]).astype(BF)
    gup_ref[...] = dot_tn(low_ref[...], grad)
    for k in range(members):
        at = pl.ds(pl.multiple_of(places_ref[at_pieces + k], local), local)
        out = dot_nt(grad, w_ref[at, :]) + dot_nt(low, down_ref[at, :])
        refs[k][...] = out.astype(BF)
        refs[members + k][...] = dot_tn(low, blocks[k][...]).astype(BF)


def context_back(at_pieces, blocks, weight, down, low, grad):
    count, local = blocks[0].shape
    rank, members = down.shape[1], len(blocks)
    arrays = (*blocks, down, low, grad)
    shapes = (
        [sds((rank, weight.shape[1]), F32)]
        + [sds((count, local), BF)] * members
        + [sds((rank, local), BF)] * members
    )
    return weight_call(
        functools.partial(context_back_kernel, weight, members, at_pieces),
        weight,
        (1,),
        [whole_spec(a.shape) for a in arrays],
        [whole_spec(s.shape) for s in shapes],
        shapes,
        weight.scratch(),
        cost(0, 0),
        arrays,
    )


def table_kernel(cos_ref, sin_ref, out_cos_ref, out_left_ref, out_right_ref):
    half, breadth = ROT // 2, 2 * HEAD_DIM
    lane = lax.broadcasted_iota(jnp.int32, (half, breadth), 1)
    row = lax.broadcasted_iota(jnp.int32, (half, breadth), 0)
    within = lane % HEAD_DIM
    first = jnp.where(within == row, 1.0, 0.0)
    second = jnp.where(within == row + half, 1.0, 0.0)

    def spread(ref, pattern):
        return lax.dot_general(
            ref[...], pattern, (((0,), (0,)), ((), ())),
            precision=lax.Precision.HIGHEST, preferred_element_type=F32,
        )

    lanes = lax.broadcasted_iota(jnp.int32, out_cos_ref.shape, 1) % HEAD_DIM
    out_cos_ref[...] = jnp.where(lanes < ROT, spread(cos_ref, first + second), 1.0)
    out_left_ref[...] = -spread(sin_ref, first)
    out_right_ref[...] = spread(sin_ref, second)


def rotary_tables(cosines, sines):
    tokens = cosines.shape[1]
    return pl.pallas_call(
        table_kernel,
        out_shape=[sds((tokens, 2 * HEAD_DIM), F32)] * 3,
        compiler_params=pltpu.CompilerParams(vmem_limit_bytes=VMEM_LIMIT),
        cost_estimate=cost(0, 0),
    )(cosines, sines)


def feed_kernel(weight, first, last, number, places_ref, *refs):
    w_refs, refs = refs[: weight.count], refs[weight.count :]
    n_refs, g_refs, (down_ref, up_ref), refs = (
        refs[:number],
        refs[number : 2 * number],
        refs[2 * number : 2 * number + 2],
        refs[2 * number + 2 :],
    )
    if not first:
        (low_in, glow_in, y_in, dn_in), refs = refs[:4], refs[4:]
    *refs, gdown_ref, ggate_ref, gupper_ref, n_ref, g_ref, w_ref, sems = refs
    step, width = pl.program_id(0), n_ref.shape[1]
    rank, part = gdown_ref.shape
    take_tile(n_refs, n_ref, step)
    take_tile(g_refs, g_ref, step)

    @pl.when(step == 0)
    def _():
        wait_for(weight.bring(w_refs, places_ref, w_ref, sems))
        for ref in (gdown_ref, ggate_ref, gupper_ref):
            ref[...] = jnp.zeros_like(ref)

    normed, grad = n_ref[...], g_ref[...]
    if first:
        low = dot_nt(normed, down_ref[...]).astype(BF)
        grad_low = dot_nt(grad, up_ref[...]).astype(BF)
        refs[2][...] = low
        refs[3][...] = grad_low
    else:
        low, grad_low = low_in[...], glow_in[...]
    deep = slice(width, width + rank)
    both = dot(normed, w_ref[:width, : 2 * part]) + dot(low, w_ref[deep, : 2 * part])
    gate, upper = both[:, :part], both[:, part:]
    grad_unit = dot(grad, w_ref[:width, 2 * part :]) + dot(grad_low, w_ref[deep, 2 * part :])
    sigmoid = 1.0 / (1.0 + jnp.exp(-gate))
    acted = gate * sigmoid
    unit = (acted * upper).astype(BF)
    grad_gate = (grad_unit * upper * (sigmoid + acted * (1.0 - sigmoid))).astype(BF)
    grad_upper = (grad_unit * acted).astype(BF)
    y = dot_nt(unit, w_ref[:, 2 * part :])
    dn = dot_nt(grad_gate, w_ref[:, :part]) + dot_nt(grad_upper, w_ref[:, part : 2 * part])
    if not first:
        y, dn = y + y_in[...].astype(F32), dn + dn_in[...].astype(F32)
    if last:
        give_tile(y.astype(BF), refs[:number], step)
        give_tile(dn.astype(BF), refs[number:], step)
    else:
        refs[0][...] = y.astype(BF)
        refs[1][...] = dn.astype(BF)
    gdown_ref[...] += dot_tn(grad_low, unit)
    ggate_ref[...] += dot_tn(low, grad_gate)
    gupper_ref[...] += dot_tn(low, grad_upper)


def feed(normed, grads, down, up, weight, sums, rows, start, last):
    block, width = normed[0].shape
    rank, number = down.shape[0], len(normed)
    deep, part = weight.shape[0], weight.shape[1] // 3
    narrow = sds((rank, part), F32)
    tokens = number * block
    if last:
        wide = sds((block, deep // LANES * LANES + LANES), BF)
        shapes, specs = [wide] * (2 * number), [whole_spec(wide.shape)] * (2 * number)
    else:
        shapes, specs = [sds((tokens, deep), BF)] * 2, [row_spec(rows, deep)] * 2
    first = not sums
    if first:
        shapes, specs = shapes + [sds((tokens, rank), BF)] * 2, specs + [row_spec(rows, rank)] * 2
    arrays = (*normed, *grads, down, up)
    size = weight.shape[0] * weight.shape[1]
    return weight_call(
        functools.partial(feed_kernel, weight, first, last, number),
        weight,
        (tokens // rows,),
        [whole_spec(a.shape) for a in arrays]
        + [pl.BlockSpec((rows, a.shape[1]), lambda t, *_: (start + t, 0)) for a in sums],
        specs + [whole_spec(narrow.shape)] * 3,
        shapes + [narrow] * 3,
        [pltpu.VMEM((rows, width), BF)] * 2 + weight.scratch(),
        cost(8 * tokens * size, 2 * size),
        [*arrays, *sums],
    )


def settle_first_kernel(fold, labels_ref, in_ref, down_ref, up_ref, hid_ref, gate_ref):
    slot = pl.program_id(0)
    local = down_ref.shape[-1]
    for ref in (down_ref, up_ref, hid_ref, gate_ref):
        ref[...] = jnp.zeros_like(ref)
    for s in range(in_ref.shape[0]):

        @pl.when(labels_ref[s] == slot)
        def _(s=s):
            for n, k in enumerate(DOWN_FIRST):
                down_ref[0, k] += in_ref[s, n].astype(F32)
            for n, k in enumerate(UP_FIRST):
                up_ref[0, k] += in_ref[s, len(DOWN_FIRST) + n].astype(F32)
            for k in range(fold):
                at, n = slice(k * local, (k + 1) * local), 4 + k
                hid_ref[0, :, at] += in_ref[s, n].astype(F32)
                gate_ref[0, 0, :, at] += in_ref[s, n + fold].astype(F32)
                gate_ref[0, 1, :, at] += in_ref[s, n + 2 * fold].astype(F32)


def settle_second_kernel(labels_ref, in_ref, down_in, up_in, down_ref, up_ref):
    del down_in, up_in
    slot = pl.program_id(0)
    downs, ups = down_ref.shape[1], up_ref.shape[1]
    for ref in (down_ref, up_ref):
        ref[...] = jnp.zeros_like(ref)
    for s in range(in_ref.shape[0]):

        @pl.when(labels_ref[s] == slot)
        def _(s=s):
            down_ref[0] += in_ref[s, :downs].astype(F32)
            up_ref[0] += in_ref[s, downs : downs + ups].astype(F32)


DOWN_FIRST, UP_FIRST = (4, 5), (7, 8)


def slot_spec(shape):
    return pl.BlockSpec((1,) + shape[1:], lambda i, *_, n=len(shape): (i,) + (0,) * (n - 1))


def settle_first(labels, grads, slots, fold):
    rank, local = grads.shape[2:]
    hidden = fold * local
    shapes = [
        (slots, 6, rank, local),
        (slots, 9, rank, local),
        (slots, rank, hidden),
        (slots, 2, rank, hidden),
    ]
    return pl.pallas_call(
        functools.partial(settle_first_kernel, fold),
        grid_spec=pltpu.PrefetchScalarGridSpec(
            num_scalar_prefetch=1,
            grid=(slots,),
            in_specs=[whole_spec(grads.shape)],
            out_specs=[slot_spec(s) for s in shapes],
        ),
        out_shape=[sds(s, F32) for s in shapes],
        compiler_params=params(),
        cost_estimate=cost(0, 0),
    )(labels, grads)


def settle_second(labels, grads, down, up):
    downs, ups = DOWN_FIRST[0], UP_FIRST[0]
    return pl.pallas_call(
        settle_second_kernel,
        grid_spec=pltpu.PrefetchScalarGridSpec(
            num_scalar_prefetch=1,
            grid=(down.shape[0],),
            in_specs=[whole_spec(grads.shape)] + [pl.BlockSpec(memory_space=pl.ANY)] * 2,
            out_specs=[
                slot_spec((1, downs) + down.shape[2:]),
                slot_spec((1, ups) + up.shape[2:]),
            ],
        ),
        out_shape=[sds(down.shape, F32), sds(up.shape, F32)],
        input_output_aliases={2: 0, 3: 1},
        compiler_params=params(),
        cost_estimate=cost(0, 0),
    )(labels, grads, down, up)


def chunks(hidden):
    return (hidden // 3,) * 3


def body(
    inputs,
    context,
    positions,
    adapter_index,
    self_in_weight,
    self_out_weight,
    cross_query_weight,
    cross_keyval_weight,
    cross_out_weight,
    feed_in_weight,
    feed_out_weight,
    norm_gains,
    norm_biases,
    adapter_down,
    adapter_down_hidden,
    adapter_up,
    adapter_up_hidden,
    out_cotangent,
    *,
    pairs,
    chips,
):
    group = Group(pairs, chips)
    members = 2 * pairs
    rows, width = inputs.shape[1], inputs.shape[2]
    block = self_in_weight.shape[0]
    local = self_in_weight.shape[2]
    hidden = feed_in_weight.shape[2]
    slots, rank = adapter_down.shape[0], adapter_down.shape[3]
    deep = width + rank
    parts = chunks(hidden)
    fold = hidden // local
    pieces = group.pieces
    gains, biases = norm_gains, norm_biases
    tile = min(256, members * rows)
    tiles = members * rows // tile
    near_tiles = tiles // pairs

    def packed(*parts):
        return jnp.concatenate(parts, axis=1)

    def stacked(*parts):
        return jnp.concatenate(parts, axis=0)

    def listed(values):
        return list(values) if isinstance(values, (list, tuple)) else [values]

    def piece(array, k, size):
        return lax.dynamic_slice_in_dim(array, pieces[k] * size, size, array.ndim - 1)

    def own(array):
        return piece(array, 0, local)

    near_chips = [1, 2] if chips == 4 else list(range(1, chips))
    chip_rows = [(group.chip ^ k) * 2 * block for k in range(chips)]
    one = [[c + o * block for c in chip_rows] for o in (group.core, 1 - group.core)]
    one += [[c + o * block for c in chip_rows] for o in (group.zhi, 1 - group.zhi)]
    row_places = jnp.stack(
        [r for found in one for r in found] + [jnp.zeros_like(group.core)]
        + [p * local for p in pieces] + [group.core]
    ).astype(jnp.int32)
    mine_at, other_at, first_at, second_at, zero = (n * chips for n in range(5))
    at_pieces = zero + 1
    core_at = at_pieces + members

    def chip_weight(own_entry, near, rest, low, columns, halves):
        weight = Weight((deep, columns), row_places)
        entries = [own_entry, *near]
        for k, (array, row) in zip([0, *near_chips], entries):
            weight.add(
                array,
                *[(row + r, block, c, columns, None, at + k, 0) for r, c, at in halves],
            )
        if rest:
            side_by_side = halves[1][0] == 0
            for n, (array, row) in enumerate(rest):
                size = block // 2 if side_by_side else block
                picked = halves if side_by_side else halves[n : n + 1]
                weight.add(
                    array,
                    *[
                        (row, size, c, columns, None, at + 3, n * size if side_by_side else 0)
                        for _, c, at in picked
                    ],
                )
        weight.add(low, (0, rank, 0, columns, None, zero, width))
        return weight

    stacked_halves = [(0, 0, first_at), (block, 0, second_at)]
    packed_halves = [(0, 0, mine_at), (0, 2 * local, other_at)]

    def spread(got, half_at, half, own_block):
        if got and chips == 4:
            turns = [
                got[1][half_at : half_at + half],
                got[0][half_at + half : half_at + 2 * half],
            ]
            if own_block is not None:
                turns = listed(step.mark(*[stacked(turn, own_block) for turn in turns]))
            return [xor_move(turn, "chip", 4, k) for turn, k in zip(turns, near_chips)]
        if own_block is None:
            return []
        return [xor_move(own_block, "chip", chips, k) for k in near_chips]

    def skip(half):
        return half if chips == 4 else 0

    def flat(*groups):
        return [x for g in groups for x in listed(g)]

    def wait_all(*groups):
        groups = [listed(g) for g in groups]
        values = iter(listed(step.wait(*flat(*groups))))
        return [[next(values) for _ in g] for g in groups]

    def swap_all(blocks):
        if not blocks:
            return []
        blocks = listed(step.wait(*blocks))
        return listed(step.wait(*[core_swap(b) for b in blocks]))

    shard_self = packed(*[self_in_weight[:, i] for i in range(3)], self_out_weight.T)
    step = Order(shard_self[:8, :128])
    self_from = [home_swap(shard_self), turned(shard_self)]
    stream_own, context_own = home_swap(inputs[0]), home_swap(context[0])
    index, positions = step.wait(adapter_index, positions)
    index_other, positions_other = step.wait(core_swap(index), core_swap(positions))
    index = jnp.where(group.home, index, index_other)[0]
    positions = jnp.where(group.home, positions, positions_other)[0]
    down = lax.dynamic_index_in_dim(adapter_down.transpose(0, 1, 3, 2), index, 0, keepdims=False)
    up = lax.dynamic_index_in_dim(adapter_up.transpose(0, 2, 1, 3), index, 0, keepdims=False)
    down, up = step.mark(down, up)
    low_self = packed(*[own(up[i]) for i in range(3)], own(down[1]))
    low_keyval = packed(own(up[5]), own(up[6]))
    low_cross = []
    for k in range(pairs):
        two = [
            (group.p ^ k) * local + core * pairs * local for core in (0, 1)
        ]
        low_cross.append(
            packed(
                *[
                    lax.dynamic_slice_in_dim(table[4], where, local, 1)
                    for table in (up, down)
                    for where in two
                ]
            )
        )
    low_cross = stacked(*low_cross)
    low_self, low_keyval, low_cross = step.mark(low_self, low_keyval, low_cross)
    keyval_parts = step.wait(cross_keyval_weight)
    keyval_parts = step.mark(keyval_parts[:, 0], keyval_parts[:, 1])
    shard_cross = step.mark(packed(cross_query_weight, cross_out_weight.T, *keyval_parts))
    far_cross = group.cross(shard_cross)
    blocks_at = [
        lax.dynamic_slice_in_dim(positions, pieces[k] * rows, rows, 0) for k in range(members)
    ]
    half = ROT // 2
    inverse = 10000.0 ** (-jnp.arange(half, dtype=F32) / half)
    angles = inverse[:, None] * step.wait(jnp.concatenate(blocks_at)).astype(F32)[None]
    tables = step.mark(*rotary_tables(*step.mark(jnp.cos(angles), jnp.sin(angles))))
    feed_in, feed_out = step.wait(feed_in_weight, feed_out_weight)
    gate_rows, upper_rows = step.mark(feed_in[:, 0], feed_in[:, 1])
    at = [sum(parts[:i]) for i in range(len(parts))]

    def feed_shard(i):
        to = slice(at[i], at[i] + parts[i])
        gate, upper, out = step.wait(gate_rows, upper_rows, feed_out)
        return step.mark(packed(gate[:, to], upper[:, to], out.T[:, to]))

    shard_feed = [feed_shard(i) for i in range(len(parts))]

    self_from = step.wait(*self_from)
    ready_self = step.mark(stacked(*self_from))
    near_self = spread([], 0, 0, ready_self)
    stream_own, context_own = step.wait(stream_own, context_own)
    stream_far, context_far = group.far_p(stream_own), group.far_p(context_own)
    (near_self,) = wait_all(near_self)
    rest_self = spread(near_self, 0, block, None)
    rest_self, stream_far, context_far, (far_cross,) = wait_all(
        rest_self, stream_far, context_far, [far_cross]
    )
    stream_other, *stream_far_other = swap_all([stream_own, *stream_far])
    stream = [stream_own, stream_other]
    for far, far_other in zip(stream_far, stream_far_other):
        stream += [far, far_other]
    self_weight = chip_weight(
        (ready_self, 0), [(g, 0) for g in near_self], [(g, 0) for g in rest_self], low_self,
        4 * local, stacked_halves,
    )

    mine = jnp.where(group.home, shard_cross, far_cross)
    given = jnp.where(group.home, far_cross, shard_cross)
    keyval_mine, keyval_give = mine[:, 2 * local :], given[:, 2 * local :]
    low_zhi = jnp.where(group.zhi == 0, shard_cross, far_cross)
    high_zhi = jnp.where(group.zhi == 0, far_cross, shard_cross)
    pair = packed(
        *[two[:, n * local : (n + 1) * local] for n in (0, 1) for two in (low_zhi, high_zhi)]
    )
    keyval_mine, keyval_give, pair = step.mark(keyval_mine, keyval_give, pair)
    (keyval_other,) = swap_all([keyval_give])
    ready_keyval = step.mark(stacked(packed(keyval_mine, keyval_other), pair))

    got_one = spread([], 0, 0, ready_keyval)
    pair_far = group.far_p(pair)
    feed_from = [[home_swap(step.wait(shard_feed[0])), turned(step.wait(shard_feed[0]))]]
    query, keys, values, low_one, normed_one = project_self(
        listed(step.wait(*stream)), gains[0:1], biases[0:1], down[0], self_weight, tables, tile
    )
    query, keys, values = step.mark(query, keys, values)
    heads_far, logsum_far, *y_far = attend_self(
        query, keys, values, self_weight, tile, near_tiles, tiles - near_tiles, rows
    )
    y_far = listed(step.mark(*y_far))

    def far_sums(*groups):
        others = iter(swap_all([g[2 * k + 1] for g in groups for k in range(pairs - 1)]))
        sums = [
            [group.near_sums(g[2 * k], next(others)).astype(BF) for k in range(pairs - 1)]
            for g in groups
        ]
        values = iter(listed(step.mark(*flat(*sums))))
        return [[next(values) for _ in s] for s in sums]

    def move_p(sums):
        return [xor_move(s, "p", pairs, k + 1) for k, s in enumerate(sums)]

    def sum_up(blocks, other, far):
        total = group.near_sums(blocks[0], other)
        for f in far:
            total = total + f.astype(F32)
        return step.mark(total)

    got_one, pair_far, feed_from[0] = wait_all(got_one, pair_far, feed_from[0])
    (y_sums,) = far_sums(y_far)

    far = move_p(y_sums)
    quarter = block // 2
    if chips == 4:
        turns = [
            stacked(got[start : start + quarter], got[start + block : start + block + quarter], pair_far[0])
            for got, start in ((got_one[1], 0), (got_one[0], quarter))
        ]
        turns = step.mark(*turns)
        got_two = [xor_move(turn, "chip", 4, k) for turn, k in zip(turns, near_chips)]
    else:
        got_two = flat(*[spread([], 0, 0, p) for p in pair_far])
    early = [ready_keyval, *got_one]
    early_swapped = [core_swap(b) for b in early]
    heads_near, logsum_near, *y_rows = attend_self(
        step.wait(query), keys, values, self_weight, tile, 0, near_tiles, rows
    )
    y_rows = listed(step.mark(*y_rows))
    far, got_two, early_swapped = wait_all(far, got_two, early_swapped)
    y_other, context_other, *swapped = swap_all([y_rows[1], context_own, *context_far])
    branch = [y_rows[0], y_other, *far]
    context_blocks = [context_own, context_other]
    for far, far_other in zip(context_far, swapped):
        context_blocks += [far, far_other]
    keyval_weight = chip_weight(
        (ready_keyval, 0), [(g, 0) for g in got_one],
        [(g, 0) for g in got_two] if chips == 4 else [], low_keyval, 2 * local, packed_halves,
    )
    down_context = step.mark(down[3].T)
    keyval, low_context = context_forward(at_pieces, context_blocks, keyval_weight, down_context)
    keyval = step.mark(keyval)

    keyval_far = group.far_p(keyval)
    cotangent_own = home_swap(step.wait(out_cotangent[0]))
    ready_feed = [step.mark(stacked(*feed_from[0]))]
    found = [(ready_keyval, block, block, 0, 0, 0)]
    found += [(g, block, block, k, 0, 0) for g, k in zip(got_one, near_chips)]
    if chips == 4:
        turns = [got_two[1][block : block + quarter], got_two[0][block + quarter :]]
        got_three = [xor_move(turn, "chip", 4, k) for turn, k in zip(turns, near_chips)]
        keyval_far, got_three = wait_all(keyval_far, got_three)
        found += [(g, 0, quarter, 3, n * quarter, 1) for n, g in enumerate(got_three)]
        found.append((pair_far[0], 0, block, 0, 0, 1))
        for n, (g, k) in enumerate(zip(got_two, near_chips)):
            found += [(g, block, block, k, 0, 1), (g, quarter, quarter, 3, n * quarter, 0)]
    else:
        (keyval_far,) = wait_all(keyval_far)
        count = len(near_chips)
        for n, p in enumerate(pair_far):
            found.append((p, 0, block, 0, 0, n + 1))
            found += [
                (g, 0, block, k, 0, n + 1)
                for g, k in zip(got_two[n * count : (n + 1) * count], near_chips)
            ]
    arrays = []
    for entry in found:
        if not any(entry[0] is a for a in arrays):
            arrays.append(entry[0])
    swapped = swap_all([keyval, *keyval_far, *arrays[len(early) :]])
    keyvals = [keyval, swapped[0]]
    for far, far_other in zip(keyval_far, swapped[1:]):
        keyvals += [far, far_other]
    others = early_swapped + swapped[1 + len(keyval_far) :]
    cotangent_own = step.wait(cotangent_own)
    cross_weight = Weight((pairs, deep, 4 * local), row_places)
    for array, other in zip(arrays, others):
        entries = [e[1:] for e in found if e[0] is array]
        for source, places in ((array, mine_at), (other, other_at)):
            cross_weight.add(
                source,
                *[
                    (row, size, 0, 4 * local, n, places + k, offset)
                    for row, size, k, offset, n in entries
                ],
            )
    cross_weight.add(
        low_cross, *[(n * rank, rank, 0, 4 * local, n, zero, width) for n in range(pairs)]
    )

    near_feed = [spread([], 0, 0, ready_feed[0])]
    feed_from.append([home_swap(step.wait(shard_feed[1])), turned(step.wait(shard_feed[1]))])
    cotangent_far = group.far_p(step.wait(cotangent_own))
    stream_own, *branch = step.wait(stream_own, *branch)

    (
        stream_one, stream_two, normed_two, normed_three, query_cross, heads_cross, logsum_cross,
        low_two, low_three, low_four,
    ) = cross_forward(
        stream_own, branch, up[3], up[7], down[2], gains, biases, cross_weight, keyvals, core_at,
    )
    normed_own = step.mark(normed_three)
    near_feed[0], cotangent_far, feed_from[1] = wait_all(
        near_feed[0], cotangent_far, feed_from[1]
    )
    ready_feed.append(step.mark(stacked(*feed_from[1])))

    normed_far = group.far_p(normed_own)
    near_feed.append(spread(near_feed[0], 0, block, ready_feed[1]))
    down_hidden = lax.dynamic_index_in_dim(
        adapter_down_hidden.transpose(0, 2, 1), index, 0, keepdims=False
    )
    up_hidden = lax.dynamic_index_in_dim(
        adapter_up_hidden.transpose(0, 2, 1, 3), index, 0, keepdims=False
    )
    feed_down, feed_up = piece(down_hidden, 0, hidden), piece(up_hidden, 0, hidden)
    feed_down, feed_gate, feed_upper = step.mark(feed_down, feed_up[0], feed_up[1])
    low_feed = [
        packed(feed_gate[:, to], feed_upper[:, to], feed_down[:, to])
        for to in [slice(a, a + p) for a, p in zip(at, parts)]
    ]
    low_feed = step.mark(*low_feed)
    near_feed[1], normed_far = wait_all(near_feed[1], normed_far)
    normed_other, cotangent_other, *swapped = swap_all(
        [normed_own, cotangent_own, *normed_far, *cotangent_far]
    )
    normed_blocks, cotangent_blocks = [normed_own, normed_other], [cotangent_own, cotangent_other]
    for far, far_other in zip(normed_far, swapped):
        normed_blocks += [far, far_other]
    for far, far_other in zip(cotangent_far, swapped[len(normed_far) :]):
        cotangent_blocks += [far, far_other]

    def feed_weight(i, first, rest):
        return chip_weight(
            (ready_feed[i], 0), [(g, first) for g in near_feed[i]], [(g, 0) for g in rest],
            low_feed[i], 3 * parts[i], stacked_halves,
        )

    def feed_pass(weight, sums, picked, start, last):
        normed, cotangent = wait_all(normed_blocks[picked], cotangent_blocks[picked])
        found = feed(normed, cotangent, down[5], up[8], weight, sums, tile, start, last)
        *values, gdown, ggate, gupper = found
        return listed(step.mark(*values)), [gdown, ggate, gupper]

    everything, far_only, near_only = slice(0, None), slice(2, None), slice(0, 2)

    feed_from.append([home_swap(step.wait(shard_feed[2])), turned(step.wait(shard_feed[2]))])
    rests = near_feed[1] if chips == 4 else []
    weight = feed_weight(0, 0, rests)
    rest_feed = spread(near_feed[1], skip(block), block, None)
    (y, dn, *lows), *feed_grads = feed_pass(weight, (), everything, 0, False)
    rest_feed, feed_from[2] = wait_all(rest_feed, feed_from[2])
    ready_feed.append(step.mark(stacked(*feed_from[2])))

    weight = feed_weight(1, skip(block), rest_feed)
    near_feed.append(spread([], 0, 0, ready_feed[2]))
    (y, dn), grads = feed_pass(weight, (*lows, y, dn), everything, 0, False)
    feed_grads.append(grads)
    (near_feed[2],) = wait_all(near_feed[2])
    (rest_feed,) = wait_all(spread(near_feed[2], 0, block, None)) if chips == 4 else ([],)
    weight = feed_weight(2, 0, rest_feed)
    found, grads = feed_pass(weight, (*lows, y, dn), far_only, near_tiles, True)
    y_far, dn_far = found[: len(found) // 2], found[len(found) // 2 :]

    dn_sums, y_sums = far_sums(dn_far, y_far)
    far = move_p(dn_sums)
    found, more = feed_pass(weight, (*lows, y, dn), near_only, 0, True)
    y_rows, dn_rows = found[:2], found[2:]
    feed_grads.append([a + b for a, b in zip(grads, more)])
    (far,) = wait_all(far)
    dn_other, y_other = swap_all([dn_rows[1], y_rows[1]])
    grad_normed = [dn_rows[0], dn_other, *far]

    far = move_p(step.mark(*y_sums) if len(y_sums) > 1 else [step.mark(*y_sums)])
    grad_stream, branch_grad, fixed_rows, near_rows, *keyval_rows = cross_back(
        cotangent_own, listed(step.wait(*grad_normed)), stream_one, stream_two, normed_two,
        query_cross, heads_cross, logsum_cross, low_three, low_four, up[7], down[5], down[2],
        gains, biases, cross_weight, keyvals, core_at,
    )
    branch_grad, *keyval_rows = step.mark(branch_grad, *keyval_rows)
    (far,) = wait_all(far)

    branch_far = group.far_p(branch_grad)
    (branch_other,) = swap_all([branch_grad])

    def back(grad, heads, logsum, first, before):
        return attend_back(
            grad, up[3], self_weight, query, keys, values, heads, logsum, tables, low_one, rank,
            tile, first, before,
        )

    grads = listed(step.wait(branch_grad, branch_other))
    near_back = step.mark(*back(grads, heads_near, logsum_near, 0, None))
    (branch_far,) = wait_all(branch_far)

    output, grad_up_eight = step.mark(
        *output_end(
            stream_two, [step.wait(y_rows[0]), y_other, *far], up[8], cotangent_own, members
        )
    )

    def taken(by_piece, k):
        return lax.dynamic_index_in_dim(by_piece, pieces[k], 0, keepdims=False)

    def taken_near(by_member, k):
        member = k // 2 * 2 + (group.core ^ (k % 2))
        return lax.dynamic_index_in_dim(by_member, member, 0, keepdims=False)

    first_rows = listed(
        step.mark(
            *[
                stacked(
                    taken(fixed_rows, k)[rank:], taken(grad_up_eight, k),
                    taken_near(near_rows, k)[:rank],
                )
                for k in range(members)
            ]
        )
    )
    swapped = swap_all([*branch_far, *first_rows[1::2], *keyval_rows[1::2]])
    branch_blocks = []
    for f, o in zip(branch_far, swapped):
        branch_blocks += [f, o]
    others = swapped[len(branch_far) :]
    first_sums, keyval_sums = (
        [group.near_sums(a, b) for a, b in zip(even[::2], other)]
        for even, other in ((first_rows, others[:pairs]), (keyval_rows, others[pairs:]))
    )
    moving = listed(step.mark(*[x.astype(BF) for x in first_sums[1:] + keyval_sums[1:]]))

    def columns(array):
        return array.reshape(rank, -1, local).transpose(1, 0, 2)

    def sent(parts):
        parts.append(jnp.full((1, rank, local), index, F32))
        grads = step.mark(jnp.concatenate(parts, axis=0).astype(BF))
        return [home_swap(grads), turned_back(grads)]

    def to_chips(blocks):
        both = step.mark(stacked(*blocks))
        return [both] + [xor_move(both, "chip", chips, k) for k in range(1, chips)]

    def every(blocks):
        grads = stacked(*blocks)
        grads = grads.reshape(-1, grads.shape[0] // (2 * chips), rank, local)
        return grads, grads[:, -1, 0, 0].astype(jnp.int32)

    def total(own, far):
        for f in far:
            own = own + f.astype(F32)
        return own

    first_far, keyval_far = move_p(moving[: pairs - 1]), move_p(moving[pairs - 1 :])
    block_output = home_swap(step.wait(output))
    branch_blocks = listed(step.wait(*branch_blocks))
    grad_mixed, grad_down_one, grad_up_self = back(
        branch_blocks, heads_far, logsum_far, near_tiles, near_back
    )
    grad_mixed = step.mark(grad_mixed)
    first_far, keyval_far, (block_output,) = wait_all(first_far, keyval_far, [block_output])
    summed = total(first_sums[0], first_far).reshape(-1, rank, local)
    first = sent(
        [
            summed[3:4],
            summed[0:1],
            summed[1:3],
            *[columns(jnp.concatenate(g, axis=1)) for g in zip(*feed_grads)],
        ]
    )
    low_far, *dn_far = step.mark(
        *project_back(
            step.wait(grad_mixed), self_weight, tile, near_tiles, tiles - near_tiles, rows, rank
        )
    )
    (first,) = wait_all(first)
    (dn_sums,) = far_sums(dn_far)

    far = move_p(dn_sums)
    low_near, *dn_rows = step.mark(
        *project_back(step.wait(grad_mixed), self_weight, tile, 0, near_tiles, rows, rank)
    )
    (far,) = wait_all(far)
    first = to_chips(first)
    grad_keyval = step.mark(total(keyval_sums[0], keyval_far).astype(BF))
    grad_up_keyval, *found = step.mark(
        *context_back(
            at_pieces, context_blocks, keyval_weight, down_context, low_context, grad_keyval
        )
    )
    context_rows, grad_down_three = found[:members], found[members:]
    own_rows = step.mark(
        self_rows(step.wait(low_near), low_far, normed_one, low_two, branch_grad, members)
    )
    second_rows = listed(
        step.mark(
            *[
                stacked(
                    taken(own_rows, k), taken(fixed_rows, k)[:rank], grad_down_three[k],
                    taken_near(near_rows, k)[rank:],
                )
                for k in range(members)
            ]
        )
    )
    dn_other, *others = swap_all([dn_rows[1], *second_rows[1::2], *context_rows[1::2]])
    second_sums, context_sums = (
        [group.near_sums(a, b) for a, b in zip(even[::2], other)]
        for even, other in ((second_rows, others[:pairs]), (context_rows, others[pairs:]))
    )
    moving = listed(step.mark(*[x.astype(BF) for x in second_sums[1:] + context_sums[1:]]))

    second_far, context_far = move_p(moving[: pairs - 1]), move_p(moving[pairs - 1 :])
    grad_inputs = step.mark(
        input_end(stream_own, grad_stream, [dn_rows[0], dn_other, *far], down[0], gains[0:1])
    )
    second_far, context_far, first = wait_all(second_far, context_far, first)
    summed = total(second_sums[0], second_far).reshape(-1, rank, local)
    second = sent(
        [
            summed[0:1],
            grad_down_one[None],
            summed[2:4],
            columns(grad_up_self),
            summed[1:2],
            summed[4:5],
            columns(grad_up_keyval),
        ]
    )
    grad_inputs = home_swap(step.wait(grad_inputs))
    grad_context = home_swap(step.mark(total(context_sums[0], context_far).astype(BF)))
    first, labels = every(first)
    grad_down, grad_up, grad_hidden, grad_gate = settle_first(labels, first, slots, fold)
    grad_down, grad_up = step.mark(grad_down, grad_up)
    (second,) = wait_all(second)
    (second,) = wait_all(to_chips(second))
    second, labels = every(second)
    labels = labels + (step.token[0, 0].astype(F32) * 0.0).astype(jnp.int32)
    grad_down, grad_up = settle_second(labels, second, grad_down, grad_up)
    return (
        block_output[None],
        grad_inputs.astype(F32)[None],
        grad_context.astype(F32)[None],
        grad_down.transpose(0, 1, 3, 2),
        grad_hidden.transpose(0, 2, 1),
        grad_up.transpose(0, 2, 1, 3),
        grad_gate.transpose(0, 2, 1, 3),
    )


def solution(mesh):
    members = mesh.shape["tensor"]
    chips = mesh.shape["dp"] // 2
    mesh = Mesh(
        mesh.devices.reshape(chips, 2, 2, members // 2), ("chip", "core", "zhi", "p")
    )
    dp, tensor = ("chip", "core"), ("zhi", "p")
    in_specs = (
        P(dp, tensor, None),
        P(dp, None, tensor),
        P(dp, None),
        P(dp),
        P(dp, None, tensor),
        P(tensor, dp),
        P(dp, tensor),
        P(dp, None, tensor),
        P(tensor, dp),
        P(dp, None, tensor),
        P(tensor, dp),
        P(),
        P(),
        P(),
        P(),
        P(),
        P(),
        P(dp, tensor, None),
    )
    out_specs = (
        P(dp, tensor, None),
        P(dp, tensor, None),
        P(dp, None, tensor),
        P(None, None, tensor, None),
        P(None, tensor, None),
        P(None, None, None, tensor),
        P(None, None, None, tensor),
    )

    def run(*args):
        return body(*args, pairs=members // 2, chips=chips)

    return jax.shard_map(run, mesh=mesh, in_specs=in_specs, out_specs=out_specs, check_vma=False)
```

time: 674 us -> 618 us (0.917)
  Pallas kernels: 278 us -> 248 us
  other arithmetic: 29.2 us -> 20.3 us
  starting transfers between devices: 148 us -> 140 us
  local copies, waits for them, and re-layouts: 44.6 us -> 36.7 us
    ppermute x40 -> x39, starting transfers between devices: 62.4 us -> 13.1 us  [core_swap(): return lax.ppermute(x, 'core', SWAP)]
    ppermute x42, starting transfers between devices: 43.8 us -> 79.1 us  [xor_move(): return lax.ppermute(x, axis, [(i, i ^ k) for i in range(size)])]
    pallas_call x22 -> x15, Pallas kernels: 248 us -> 221 us  [weight_call(): pl.pallas_call(kernel, grid_spec=pltpu.PrefetchScalarGridSpec(num_scalar_...]
    ppermute x4, waiting for transfers between devices: 11.3 us -> 0.01 us  [turned(): return lax.ppermute(x, ('core', 'zhi'), [(0, 1), (1, 3), (2, 0), (3, 2)])]
    ppermute x40 -> x39, waiting for transfers between devices: 11.3 us -> 21.7 us  [core_swap(): return lax.ppermute(x, 'core', SWAP)]
    concatenate x20, other arithmetic: 11.7 us -> 4.47 us  [stacked(): return jnp.concatenate(parts, axis=0)]
    unnamed x238 -> x224, local copies, waits for them, and re-layouts: 19.8 us -> 16.5 us
  transfers between devices with their start and end apart: 100 -> 99, of which waited for: 29 -> 39; matrix products, arithmetic and copies ran while one was open for 7% -> 6% of each run, Pallas kernels for 38% -> 36%
where the time goes in v4:
time: 618 us; the launch traced here: 608 us
  Pallas kernels  248 us (40%)
  waiting for transfers between devices  158 us (26%)
  starting transfers between devices  140 us (23%)
  local copies, waits for them, and re-layouts  36.7 us (6%)
  other arithmetic  20.3 us (3%)
    pallas_call x15, Pallas kernels, weight_call(): pl.pallas_call(kernel, grid_spec=pltpu.PrefetchScalarGridSpec(num_scalar_...  221 us
    ppermute x42, waiting for transfers between devices, xor_move(): return lax.ppermute(x, axis, [(i, i ^ k) for i in range(size)])  124 us
    ppermute x42, starting transfers between devices, xor_move(): return lax.ppermute(x, axis, [(i, i ^ k) for i in range(size)])  79.1 us
    ppermute x12, starting transfers between devices, home_swap(): return lax.ppermute(x, ('core', 'zhi'), [(0, 0), (1, 2), (2, 1), (3, 3)])  22.8 us
    ppermute x39, waiting for transfers between devices, core_swap(): return lax.ppermute(x, 'core', SWAP)  21.7 us
    unnamed x224, local copies, waits for them, and re-layouts  16.5 us
    ppermute x4, starting transfers between devices, turned(): return lax.ppermute(x, ('core', 'zhi'), [(0, 1), (1, 3), (2, 0), (3, 2)])  16.5 us
    ppermute x39, starting transfers between devices, core_swap(): return lax.ppermute(x, 'core', SWAP)  13.1 us
  transfers between devices with their start and end apart: 99, of which 39 were waited for; matrix products, arithmetic and copies ran while one was open for 6% of the time, Pallas kernels for 36%

profile of v4, /device:TPU:0, one launch (start us, length us, event | category | flops | bytes accessed | tf_op | source)
XLA Modules:
  0.0 608.3 jit_solution(5131459253259786693)
XLA Ops:
  32.4 10.7 %collective-permute-start.10 = (bf16[256,1536]{1,0:T(8,128)(2,1)S(1)}, bf16[256,1536]{1,0:T(8,128)(2,1)}, u32[]{:S(2)}, u32[]{:S(2)}) collective-permute-start(bf16[256,1536]{1,0:T(8,128)(2,1)S(1)} %collective-permute-done.6.refs_6_.refs_17_.x_ref), channel_id=1, source_target_pairs={{0,1},{1,0},{2,3},{3,2},{4,5},{5,4},{6,7},{7,6},{8,9},{9,8},{10,11... | collective-permute-start | bytes 2359304 | tf_op jit(solution)/shard_map/ppermute | solution.py:48
  43.1 24.5 %collective-permute-start.12 = (bf16[192,1536]{1,0:T(8,128)(2,1)S(1)}, bf16[192,1536]{1,0:T(8,128)(2,1)S(1)}, u32[]{:S(2)}, u32[]{:S(2)}) collective-permute-start(bf16[192,1536]{1,0:T(8,128)(2,1)S(1)} %pad_maximum_fusion.11), channel_id=1, source_target_pairs={{0,2},{2,0},{1,3},{3,1},{4,6},{6,4},{5,7},{7,5},{8,10},{10,8},{9,1... | collective-permute-start | bytes 1769480 | tf_op jit(solution)/shard_map/ppermute | solution.py:48
  70.1 24.3 %collective-permute-done.12 = bf16[192,1536]{1,0:T(8,128)(2,1)S(1)} collective-permute-done((bf16[192,1536]{1,0:T(8,128)(2,1)S(1)}, bf16[192,1536]{1,0:T(8,128)(2,1)S(1)}, u32[]{:S(2)}, u32[]{:S(2)}) %collective-permute-start.12) | collective-permute-done | bytes 589856 | tf_op jit(solution)/shard_map/ppermute | solution.py:48
  108.0 14.8 %shard_map.226 = (bf16[1024,384]{1,0:T(8,128)(2,1)}, bf16[1024,384]{1,0:T(8,128)(2,1)}, bf16[1024,384]{1,0:T(8,128)(2,1)}, bf16[1024,16]{1,0:T(8,128)(2,1)}, bf16[1024,1536]{1,0:T(8,128)(2,1)}) custom-call(s32[22]{0:T(128)} %stack.87.places_ref, bf16[384,1536]{1,0:T(8,128)(2,1)} %copy-done.15, bf16[384,1536]{1,0:T(8,128)(2,1)} %copy-done.39, ...), custom_call_target="tpu_custom_call" | custom-call | flops 4831838208 | bytes 4718592 | tf_op jit(solution)/shard_map/pallas_call | solution.py:158
  122.9 12.9 %shard_map.227 = (bf16[512,384]{1,0:T(8,128)(2,1)}, f32[8,512]{1,0:T(8,128)}, bf16[256,1664]{1,0:T(8,128)(2,1)}, bf16[256,1664]{1,0:T(8,128)(2,1)}) custom-call(s32[22]{0:T(128)} %stack.87.places_ref, bf16[384,1536]{1,0:T(8,128)(2,1)} %copy-done.15, bf16[384,1536]{1,0:T(8,128)(2,1)} %copy-done.39, bf16[384,1536]{1,0:T(8,128)(2,1)} %copy-done.40, ...), custom_call_target="tpu_custom_call" | custom-call | flops 3221225472 | bytes 3145728 | tf_op jit(solution)/shard_map/pallas_call | solution.py:158
  146.9 13.2 %shard_map.228 = (bf16[512,384]{1,0:T(8,128)(2,1)}, f32[8,512]{1,0:T(8,128)}, bf16[256,1664]{1,0:T(8,128)(2,1)}, bf16[256,1664]{1,0:T(8,128)(2,1)}) custom-call(s32[22]{0:T(128)} %stack.87.places_ref, bf16[384,1536]{1,0:T(8,128)(2,1)} %copy-done.15, bf16[384,1536]{1,0:T(8,128)(2,1)} %copy-done.39, bf16[384,1536]{1,0:T(8,128)(2,1)} %copy-done.40, ...), custom_call_target="tpu_custom_call" | custom-call | flops 3221225472 | bytes 3145728 | tf_op jit(solution)/shard_map/pallas_call | solution.py:158
  190.6 7.4 %collective-permute-start.41 = (bf16[256,1536]{1,0:T(8,128)(2,1)}, bf16[256,1536]{1,0:T(8,128)(2,1)}, u32[]{:S(2)}, u32[]{:S(2)}) collective-permute-start(bf16[256,1536]{1,0:T(8,128)(2,1)} %bitcast.62), channel_id=1, source_target_pairs={{0,0},{2,4},{4,2},{6,6},{1,1},{3,5},{5,3},{7,7},{8,8},{10,12},{12,... | collective-permute-start | bytes 2359304 | tf_op jit(solution)/shard_map/ppermute | solution.py:52
  205.2 11.3 %collective-permute-start.46 = (bf16[192,1536]{1,0:T(8,128)(2,1)}, bf16[192,1536]{1,0:T(8,128)(2,1)S(1)}, u32[]{:S(2)}, u32[]{:S(2)}) collective-permute-start(bf16[192,1536]{1,0:T(8,128)(2,1)} %pad_maximum_fusion.14), channel_id=1, source_target_pairs={{0,2},{2,6},{4,0},{6,4},{1,3},{3,7},{5,1},{7,5},{8,10},{10,14},{12... | collective-permute-start | bytes 1769480 | tf_op jit(solution)/shard_map/ppermute | solution.py:56
  218.2 17.9 %shard_map.230 = (f32[256,1536]{1,0:T(8,128)}, f32[256,1536]{1,0:T(8,128)}, bf16[256,1536]{1,0:T(8,128)(2,1)}, bf16[256,1536]{1,0:T(8,128)(2,1)}, bf16[256,1536]...) custom-call(s32[22]{0:T(128)} %stack.87.places_ref, ...), custom_call_target="tpu_custom_call" | custom-call | flops 14495514624 | bytes 18874368 | tf_op jit(solution)/shard_map/pallas_call | solution.py:158
  248.9 16.0 %collective-permute-done.49.refs_8_.refs_6_ = bf16[256,1536]{1,0:T(8,128)(2,1)S(1)} collective-permute-done((bf16[256,1536]{1,0:T(8,128)(2,1)S(1)}, bf16[256,1536]{1,0:T(8,128)(2,1)S(1)}, u32[]{:S(2)}, u32[]{:S(2)}) %collective-permute-start.49) | collective-permute-done | bytes 786464 | tf_op jit(solution)/shard_map/ppermute | solution.py:48
  264.9 10.9 %collective-permute-done.47.refs_3_.refs_1_ = bf16[576,1536]{1,0:T(8,128)(2,1)S(1)} collective-permute-done((bf16[576,1536]{1,0:T(8,128)(2,1)S(1)}, bf16[576,1536]{1,0:T(8,128)(2,1)S(1)}, u32[]{:S(2)}, u32[]{:S(2)}) %collective-permute-start.47) | collective-permute-done | bytes 1769504 | tf_op jit(solution)/shard_map/ppermute | solution.py:48
  292.2 22.0 %shard_map.231 = (bf16[1024,1552]{1,0:T(8,128)(2,1)}, bf16[1024,1552]{1,0:T(8,128)(2,1)}, bf16[1024,16]{1,0:T(8,128)(2,1)}, bf16[1024,16]{1,0:T(8,128)(2,1)}, f3...) custom-call(s32[22]{0:T(128)} %stack.87.places_ref, bf16[384,1536]{1,0:T(8,128)(2,1)} %copy-done.16, ...), custom_call_target="tpu_custom_call" | custom-call | flops 19528679424 | bytes 4767744 | tf_op jit(solution)/shard_map/pallas_call | solution.py:158
  316.2 20.9 %shard_map.232 = (bf16[1024,1552]{1,0:T(8,128)(2,1)}, bf16[1024,1552]{1,0:T(8,128)(2,1)}, f32[16,512]{1,0:T(8,128)}, f32[16,512]{1,0:T(8,128)}, f32[16,512]{1,0:T(8,128)}) custom-call(s32[22]{0:T(128)} %stack.87.places_ref, bf16[384,1536]{1,0:T(8,128)(2,1)} %copy-done.11, bf16[576,1536]{1,0:T(8,128)(2,1)} %copy-done.50, bf16[576,1536]{1,0:T(8,128)(2,1)} %copy-done.51, ...), custom_call_target="tpu_custom_call" | custom-call | flops 19528679424 | bytes 4767744 | tf_op jit(solution)/shard_map/pallas_call | solution.py:158
  345.7 14.0 %collective-permute-done.60.refs_3_ = bf16[192,1536]{1,0:T(8,128)(2,1)S(1)} collective-permute-done((bf16[192,1536]{1,0:T(8,128)(2,1)S(1)}, bf16[192,1536]{1,0:T(8,128)(2,1)S(1)}, u32[]{:S(2)}, u32[]{:S(2)}) %collective-permute-start.60) | collective-permute-done | bytes 589856 | tf_op jit(solution)/shard_map/ppermute | solution.py:48
  361.9 14.7 %shard_map.233 = (bf16[256,1664]{1,0:T(8,128)(2,1)}, bf16[256,1664]{1,0:T(8,128)(2,1)}, bf16[256,1664]{1,0:T(8,128)(2,1)}, bf16[256,1664]{1,0:T(8,128)(2,1)}, f3...) custom-call(s32[22]{0:T(128)} %stack.87.places_ref, bf16[384,1536]{1,0:T(8,128)(2,1)} %copy-done.17, ...), custom_call_target="tpu_custom_call" | custom-call | flops 9764339712 | bytes 4767744 | tf_op jit(solution)/shard_map/pallas_call | solution.py:158
  384.6 15.1 %shard_map.234 = (bf16[256,1664]{1,0:T(8,128)(2,1)}, bf16[256,1664]{1,0:T(8,128)(2,1)}, bf16[256,1664]{1,0:T(8,128)(2,1)}, bf16[256,1664]{1,0:T(8,128)(2,1)}, f3...) custom-call(s32[22]{0:T(128)} %stack.87.places_ref, bf16[384,1536]{1,0:T(8,128)(2,1)} %copy-done.17, ...), custom_call_target="tpu_custom_call" | custom-call | flops 9764339712 | bytes 4767744 | tf_op jit(solution)/shard_map/pallas_call | solution.py:158
  409.5 22.6 %shard_map.235 = (f32[256,1536]{1,0:T(8,128)}, bf16[256,1536]{1,0:T(8,128)(2,1)}, bf16[4,48,384]{2,1,0:T(8,128)(2,1)}, bf16[4,32,384]{2,1,0:T(8,128)(2,1)}, bf16...) custom-call(s32[22]{0:T(128)} %stack.87.places_ref, ...), custom_call_target="tpu_custom_call" | custom-call | flops 19327352832 | bytes 18874368 | tf_op jit(solution)/shard_map/pallas_call | solution.py:158
  435.6 18.8 %shard_map.236 = (bf16[512,384]{1,0:T(8,128)(2,1)}, f32[1024,384]{1,0:T(8,128)}, f32[1024,384]{1,0:T(8,128)}, f32[16,384]{1,0:T(8,128)}) custom-call(s32[22]{0:T(128)} %stack.87.places_ref, bf16[384,1536]{1,0:T(8,128)(2,1)} %copy-done.15, bf16[384,1536]{1,0:T(8,128)(2,1)} %copy-done.39, bf16[384,1536]{1,0:T(8,128)(2,1)} %copy-done.40, ...), custom_call_target="tpu_custom_call" | custom-call | flops 8053063680 | bytes 3932160 | tf_op jit(solution)/shard_map/pallas_call | solution.py:158
  465.6 21.1 %shard_map.238 = (bf16[1024,1152]{1,0:T(8,128)(2,1)}, f32[16,384]{1,0:T(8,128)}, f32[16,1152]{1,0:T(8,128)}) custom-call(s32[22]{0:T(128)} %stack.87.places_ref, bf16[384,1536]{1,0:T(8,128)(2,1)} %copy-done.15, bf16[384,1536]{1,0:T(8,128)(2,1)} %copy-done.39, bf16[384,1536]{1,0:T(8,128)(2,1)} %copy-done.40, ...), custom_call_target="tpu_custom_call" | custom-call | flops 8053063680 | bytes 3932160 | tf_op jit(solution)/shard_map/pallas_call | solution.py:158
  493.0 8.2 %shard_map.239 = (bf16[512,16]{1,0:T(8,128)(2,1)}, bf16[256,1664]{1,0:T(8,128)(2,1)}, bf16[256,1664]{1,0:T(8,128)(2,1)}) custom-call(s32[22]{0:T(128)} %stack.87.places_ref, bf16[384,1536]{1,0:T(8,128)(2,1)} %copy-done.15, bf16[384,1536]{1,0:T(8,128)(2,1)} %copy-done.39, bf16[384,1536]{1,0:T(8,128)(2,1)} %copy-done.40, ...), custom_call_target="tpu_custom_call" | custom-call | flops 13086228480 | bytes 5111808 | tf_op jit(solution)/shard_map/pallas_call | solution.py:158
  506.4 8.0 %shard_map.240 = (bf16[512,16]{1,0:T(8,128)(2,1)}, bf16[256,1664]{1,0:T(8,128)(2,1)}, bf16[256,1664]{1,0:T(8,128)(2,1)}) custom-call(s32[22]{0:T(128)} %stack.87.places_ref, bf16[384,1536]{1,0:T(8,128)(2,1)} %copy-done.15, bf16[384,1536]{1,0:T(8,128)(2,1)} %copy-done.39, bf16[384,1536]{1,0:T(8,128)(2,1)} %copy-done.40, ...), custom_call_target="tpu_custom_call" | custom-call | flops 13086228480 | bytes 5111808 | tf_op jit(solution)/shard_map/pallas_call | solution.py:158
  514.4 12.8 %collective-permute-done.81.refs_2_ = bf16[256,1664]{1,0:T(8,128)(2,1)S(1)} collective-permute-done((bf16[256,1664]{1,0:T(8,128)(2,1)S(1)}, bf16[256,1664]{1,0:T(8,128)(2,1)S(1)}, u32[]{:S(2)}, u32[]{:S(2)}) %collective-permute-start.81) | collective-permute-done | bytes 852000 | tf_op jit(solution)/shard_map/ppermute | solution.py:48
  552.7 8.9 %collective-permute-done.90 = bf16[34,16,384]{2,1,0:T(8,128)(2,1)S(1)} collective-permute-done((bf16[34,16,384]{2,1,0:T(8,128)(2,1)S(1)}, bf16[34,16,384]{2,1,0:T(8,128)(2,1)S(1)}, u32[]{:S(2)}, u32[]{:S(2)}) %collective-permute-start.90) | collective-permute-done | bytes 417824 | tf_op jit(solution)/shard_map/ppermute | solution.py:48
  575.0 10.4 %collective-permute-done.95 = bf16[12,16,384]{2,0,1:T(8,128)(2,1)S(1)} collective-permute-done((bf16[12,16,384]{2,0,1:T(8,128)(2,1)S(1)}, bf16[12,16,384]{2,0,1:T(8,128)(2,1)S(1)}, u32[]{:S(2)}, u32[]{:S(2)}) %collective-permute-start.95) | collective-permute-done | bytes 147488 | tf_op jit(solution)/shard_map/ppermute | solution.py:60
  (560 shorter events, 241.6 us)
Async XLA Ops:
  26.4 41.1 %collective-permute-start.4 = (bf16[384,1536]{1,0:T(8,128)(2,1)S(1)}, bf16[384,1536]{1,0:T(8,128)(2,1)S(1)}, u32[]{:S(2)}, u32[]{:S(2)}) collective-permute-start(bf16[384,1536]{1,0:T(8,128)(2,1)S(1)} %pad_maximum_fusion.5.refs_0_), channel_id=1, source_target_pairs={{0,8},{8,0},{16,24},{24,16},{1,9},{9,1},{17,25},{25,17},{2,10},{10... | collective-permute-start | bytes 3538952 | tf_op jit(solution)/shard_map/ppermute | solution.py:48
  29.5 38.1 %collective-permute-start.5 = (bf16[384,1536]{1,0:T(8,128)(2,1)S(1)}, bf16[384,1536]{1,0:T(8,128)(2,1)S(1)}, u32[]{:S(2)}, u32[]{:S(2)}) collective-permute-start(bf16[384,1536]{1,0:T(8,128)(2,1)S(1)} %pad_maximum_fusion.5.refs_0_), channel_id=1, source_target_pairs={{0,16},{8,24},{16,0},{24,8},{1,17},{9,25},{17,1},{25,9},{2,18},{10... | collective-permute-start | bytes 3538952 | tf_op jit(solution)/shard_map/ppermute | solution.py:48
  32.4 61.9 %collective-permute-start.10 = (bf16[256,1536]{1,0:T(8,128)(2,1)S(1)}, bf16[256,1536]{1,0:T(8,128)(2,1)}, u32[]{:S(2)}, u32[]{:S(2)}) collective-permute-start(bf16[256,1536]{1,0:T(8,128)(2,1)S(1)} %collective-permute-done.6.refs_6_.refs_17_.x_ref), channel_id=1, source_target_pairs={{0,1},{1,0},{2,3},{3,2},{4,5},{5,4},{6,7},{7,6},{8,9},{9,8},{10,11... | collective-permute-start | bytes 2359304 | tf_op jit(solution)/shard_map/ppermute | solution.py:48
  43.1 51.2 %collective-permute-start.12 = (bf16[192,1536]{1,0:T(8,128)(2,1)S(1)}, bf16[192,1536]{1,0:T(8,128)(2,1)S(1)}, u32[]{:S(2)}, u32[]{:S(2)}) collective-permute-start(bf16[192,1536]{1,0:T(8,128)(2,1)S(1)} %pad_maximum_fusion.11), channel_id=1, source_target_pairs={{0,2},{2,0},{1,3},{3,1},{4,6},{6,4},{5,7},{7,5},{8,10},{10,8},{9,1... | collective-permute-start | bytes 1769480 | tf_op jit(solution)/shard_map/ppermute | solution.py:48
  67.7 26.7 %collective-permute-start.8 = (bf16[192,1536]{1,0:T(8,128)(2,1)S(1)}, bf16[192,1536]{1,0:T(8,128)(2,1)}, u32[]{:S(2)}, u32[]{:S(2)}) collective-permute-start(bf16[192,1536]{1,0:T(8,128)(2,1)S(1)} %slice.396), channel_id=1, source_target_pairs={{0,8},{8,0},{16,24},{24,16},{1,9},{9,1},{17,25},{25,17},{2,10},{10... | collective-permute-start | bytes 1769480 | tf_op jit(solution)/shard_map/ppermute | solution.py:48
  99.8 36.5 %collective-permute-start.16 = (bf16[384,1536]{1,0:T(8,128)(2,1)S(1)}, bf16[384,1536]{1,0:T(8,128)(2,1)S(1)}, u32[]{:S(2)}, u32[]{:S(2)}) collective-permute-start(bf16[384,1536]{1,0:T(8,128)(2,1)S(1)} %pad_maximum_fusion.6.refs_0_), channel_id=1, source_target_pairs={{0,8},{8,0},{16,24},{24,16},{1,9},{9,1},{17,25},{25,17},{2,10},{10... | collective-permute-start | bytes 3538952 | tf_op jit(solution)/shard_map/ppermute | solution.py:48
  100.4 35.9 %collective-permute-start.17 = (bf16[384,1536]{1,0:T(8,128)(2,1)S(1)}, bf16[384,1536]{1,0:T(8,128)(2,1)S(1)}, u32[]{:S(2)}, u32[]{:S(2)}) collective-permute-start(bf16[384,1536]{1,0:T(8,128)(2,1)S(1)} %pad_maximum_fusion.6.refs_0_), channel_id=1, source_target_pairs={{0,16},{8,24},{16,0},{24,8},{1,17},{9,25},{17,1},{25,9},{2,18},{10... | collective-permute-start | bytes 3538952 | tf_op jit(solution)/shard_map/ppermute | solution.py:48
  104.2 31.6 %collective-permute-start.18 = (bf16[192,1536]{1,0:T(8,128)(2,1)}, bf16[192,1536]{1,0:T(8,128)(2,1)}, u32[]{:S(2)}, u32[]{:S(2)}) collective-permute-start(bf16[192,1536]{1,0:T(8,128)(2,1)} %copy-done.13), channel_id=1, source_target_pairs={{0,1},{1,0},{2,3},{3,2},{4,5},{5,4},{6,7},{7,6},{8,9},{9,8},{10,11... | collective-permute-start | bytes 1769480 | tf_op jit(solution)/shard_map/ppermute | solution.py:48
  104.2 32.0 %collective-permute-start.20 = (bf16[192,1536]{1,0:T(8,128)(2,1)}, bf16[192,1536]{1,0:T(8,128)(2,1)S(1)}, u32[]{:S(2)}, u32[]{:S(2)}) collective-permute-start(bf16[192,1536]{1,0:T(8,128)(2,1)} %pad_maximum_fusion.13), channel_id=1, source_target_pairs={{0,2},{2,6},{4,0},{6,4},{1,3},{3,7},{5,1},{7,5},{8,10},{10,14},{12... | collective-permute-start | bytes 1769480 | tf_op jit(solution)/shard_map/ppermute | solution.py:56
  106.2 30.1 %collective-permute-start.19 = (bf16[192,1536]{1,0:T(8,128)(2,1)}, bf16[192,1536]{1,0:T(8,128)(2,1)S(1)}, u32[]{:S(2)}, u32[]{:S(2)}) collective-permute-start(bf16[192,1536]{1,0:T(8,128)(2,1)} %pad_maximum_fusion.13), channel_id=1, source_target_pairs={{0,0},{2,4},{4,2},{6,6},{1,1},{3,5},{5,3},{7,7},{8,8},{10,12},{12,... | collective-permute-start | bytes 1769480 | tf_op jit(solution)/shard_map/ppermute | solution.py:52
  142.5 28.2 %collective-permute-start.23 = (bf16[384,1536]{1,0:T(8,128)(2,1)S(1)}, bf16[384,1536]{1,0:T(8,128)(2,1)S(1)}, u32[]{:S(2)}, u32[]{:S(2)}) collective-permute-start(bf16[384,1536]{1,0:T(8,128)(2,1)S(1)} %get-tuple-element.662), channel_id=1, source_target_pairs={{0,8},{8,0},{16,24},{24,16},{1,9},{9,1},{17,25},{25,17},{2,10},{10... | collective-permute-start | bytes 3538952 | tf_op jit(solution)/shard_map/ppermute | solution.py:48
  144.0 27.9 %collective-permute-start.24 = (bf16[384,1536]{1,0:T(8,128)(2,1)S(1)}, bf16[384,1536]{1,0:T(8,128)(2,1)S(1)}, u32[]{:S(2)}, u32[]{:S(2)}) collective-permute-start(bf16[384,1536]{1,0:T(8,128)(2,1)S(1)} %get-tuple-element.663), channel_id=1, source_target_pairs={{0,16},{8,24},{16,0},{24,8},{1,17},{9,25},{17,1},{25,9},{2,18},{10... | collective-permute-start | bytes 3538952 | tf_op jit(solution)/shard_map/ppermute | solution.py:48
  202.7 33.4 %collective-permute-start.42 = (bf16[384,1536]{1,0:T(8,128)(2,1)S(1)}, bf16[384,1536]{1,0:T(8,128)(2,1)S(1)}, u32[]{:S(2)}, u32[]{:S(2)}) collective-permute-start(bf16[384,1536]{1,0:T(8,128)(2,1)S(1)} %pad_maximum_fusion.7.refs_0_), channel_id=1, source_target_pairs={{0,8},{8,0},{16,24},{24,16},{1,9},{9,1},{17,25},{25,17},{2,10},{10... | collective-permute-start | bytes 3538952 | tf_op jit(solution)/shard_map/ppermute | solution.py:48
  204.2 31.9 %collective-permute-start.43 = (bf16[384,1536]{1,0:T(8,128)(2,1)S(1)}, bf16[384,1536]{1,0:T(8,128)(2,1)S(1)}, u32[]{:S(2)}, u32[]{:S(2)}) collective-permute-start(bf16[384,1536]{1,0:T(8,128)(2,1)S(1)} %pad_maximum_fusion.7.refs_0_), channel_id=1, source_target_pairs={{0,16},{8,24},{16,0},{24,8},{1,17},{9,25},{17,1},{25,9},{2,18},{10... | collective-permute-start | bytes 3538952 | tf_op jit(solution)/shard_map/ppermute | solution.py:48
  204.7 32.4 %collective-permute-start.44 = (bf16[256,1536]{1,0:T(8,128)(2,1)}, bf16[256,1536]{1,0:T(8,128)(2,1)}, u32[]{:S(2)}, u32[]{:S(2)}) collective-permute-start(bf16[256,1536]{1,0:T(8,128)(2,1)} %collective-permute-done.41.refs_10_.refs_8_.refs_17_.g_ref), channel_id=1, source_target_pairs={{0,1},{1,0},{2,3},{3,2},{4,5},{5,4},{6,7},{7,6},{8,9},{9,8},{10,11... | collective-permute-start | bytes 2359304 | tf_op jit(solution)/shard_map/ppermute | solution.py:48
  205.2 30.9 %collective-permute-start.46 = (bf16[192,1536]{1,0:T(8,128)(2,1)}, bf16[192,1536]{1,0:T(8,128)(2,1)S(1)}, u32[]{:S(2)}, u32[]{:S(2)}) collective-permute-start(bf16[192,1536]{1,0:T(8,128)(2,1)} %pad_maximum_fusion.14), channel_id=1, source_target_pairs={{0,2},{2,6},{4,0},{6,4},{1,3},{3,7},{5,1},{7,5},{8,10},{10,14},{12... | collective-permute-start | bytes 1769480 | tf_op jit(solution)/shard_map/ppermute | solution.py:56
  239.7 36.1 %collective-permute-start.47 = (bf16[576,1536]{1,0:T(8,128)(2,1)S(1)}, bf16[576,1536]{1,0:T(8,128)(2,1)S(1)}, u32[]{:S(2)}, u32[]{:S(2)}) collective-permute-start(bf16[576,1536]{1,0:T(8,128)(2,1)S(1)} %get-tuple-element.752), channel_id=1, source_target_pairs={{0,8},{8,0},{16,24},{24,16},{1,9},{9,1},{17,25},{25,17},{2,10},{10... | collective-permute-start | bytes 5308424 | tf_op jit(solution)/shard_map/ppermute | solution.py:48
  241.3 36.3 %collective-permute-start.48 = (bf16[576,1536]{1,0:T(8,128)(2,1)S(1)}, bf16[576,1536]{1,0:T(8,128)(2,1)S(1)}, u32[]{:S(2)}, u32[]{:S(2)}) collective-permute-start(bf16[576,1536]{1,0:T(8,128)(2,1)S(1)} %get-tuple-element.753), channel_id=1, source_target_pairs={{0,16},{8,24},{16,0},{24,8},{1,17},{9,25},{17,1},{25,9},{2,18},{10... | collective-permute-start | bytes 5308424 | tf_op jit(solution)/shard_map/ppermute | solution.py:48
  283.2 31.1 %collective-permute-start.50 = (bf16[192,1536]{1,0:T(8,128)(2,1)S(1)}, bf16[192,1536]{1,0:T(8,128)(2,1)S(1)}, u32[]{:S(2)}, u32[]{:S(2)}) collective-permute-start(bf16[192,1536]{1,0:T(8,128)(2,1)S(1)} %slice.431), channel_id=1, source_target_pairs={{0,8},{8,0},{16,24},{24,16},{1,9},{9,1},{17,25},{25,17},{2,10},{10... | collective-permute-start | bytes 1769480 | tf_op jit(solution)/shard_map/ppermute | solution.py:48
  285.6 28.7 %collective-permute-start.51 = (bf16[192,1536]{1,0:T(8,128)(2,1)S(1)}, bf16[192,1536]{1,0:T(8,128)(2,1)S(1)}, u32[]{:S(2)}, u32[]{:S(2)}) collective-permute-start(bf16[192,1536]{1,0:T(8,128)(2,1)S(1)} %slice.432), channel_id=1, source_target_pairs={{0,16},{8,24},{16,0},{24,8},{1,17},{9,25},{17,1},{25,9},{2,18},{10... | collective-permute-start | bytes 1769480 | tf_op jit(solution)/shard_map/ppermute | solution.py:48
  288.1 26.2 %collective-permute-start.57 = (bf16[192,1536]{1,0:T(8,128)(2,1)S(1)}, bf16[192,1536]{1,0:T(8,128)(2,1)S(1)}, u32[]{:S(2)}, u32[]{:S(2)}) collective-permute-start(bf16[192,1536]{1,0:T(8,128)(2,1)S(1)} %copy-done.30), channel_id=1, source_target_pairs={{0,2},{2,6},{4,0},{6,4},{1,3},{3,7},{5,1},{7,5},{8,10},{10,14},{12... | collective-permute-start | bytes 1769480 | tf_op jit(solution)/shard_map/ppermute | solution.py:56
  315.2 27.4 %collective-permute-start.58 = (bf16[384,1536]{1,0:T(8,128)(2,1)S(1)}, bf16[384,1536]{1,0:T(8,128)(2,1)S(1)}, u32[]{:S(2)}, u32[]{:S(2)}) collective-permute-start(bf16[384,1536]{1,0:T(8,128)(2,1)S(1)} %pad_maximum_fusion.9.refs_0_), channel_id=1, source_target_pairs={{0,8},{8,0},{16,24},{24,16},{1,9},{9,1},{17,25},{25,17},{2,10},{10... | collective-permute-start | bytes 3538952 | tf_op jit(solution)/shard_map/ppermute | solution.py:48
  315.7 27.8 %collective-permute-start.59 = (bf16[384,1536]{1,0:T(8,128)(2,1)S(1)}, bf16[384,1536]{1,0:T(8,128)(2,1)S(1)}, u32[]{:S(2)}, u32[]{:S(2)}) collective-permute-start(bf16[384,1536]{1,0:T(8,128)(2,1)S(1)} %pad_maximum_fusion.9.refs_0_), channel_id=1, source_target_pairs={{0,16},{8,24},{16,0},{24,8},{1,17},{9,25},{17,1},{25,9},{2,18},{10... | collective-permute-start | bytes 3538952 | tf_op jit(solution)/shard_map/ppermute | solution.py:48
  567.3 37.7 %collective-permute-start.92 = (bf16[256,1536]{1,0:T(8,128)(2,1)S(1)}, bf16[256,1536]{1,0:T(8,128)(2,1)S(1)}, u32[]{:S(2)}, u32[]{:S(2)}) collective-permute-start(bf16[256,1536]{1,0:T(8,128)(2,1)S(1)} %copy-done.26), channel_id=1, source_target_pairs={{0,0},{2,4},{4,2},{6,6},{1,1},{3,5},{5,3},{7,7},{8,8},{10,12},{12,... | collective-permute-start | bytes 2359304 | tf_op jit(solution)/shard_map/ppermute | solution.py:52
  (183 other events, 1836.2 us)

commit v5 on v4

--- a/solution.py
+++ b/solution.py
@@ -384,55 +384,22 @@
     )
 
 
-def project_back_kernel(weight, part, local, places_ref, *refs):
-    w_refs, refs = refs[: weight.count], refs[weight.count :]
-    m_ref, low_ref, *refs, w_ref, sems = refs
-    step = pl.program_id(0)
-
-    @pl.when(step == 0)
-    def _():
-        wait_for(weight.bring(w_refs, places_ref, w_ref, sems, *part[:2]))
-
-    width = w_ref.shape[0] - low_ref.shape[1]
-    value = dot_nt(m_ref[...], w_ref[:, part[2] : part[2] + 3 * local]).astype(BF)
-    low_ref[...] = value[:, width:]
-    give_tile(value, refs, step)
-
-
-def project_back(mixed, weight, rows, first, count, block, rank):
-    local, wide = weight.shape[1] // 4, wide_of(weight)
-    part = weight.columns(0, 3 * local)
-    blocks = count * rows // block
-    return weight_call(
-        functools.partial(project_back_kernel, weight, part, local),
-        weight,
-        (count,),
-        [pl.BlockSpec((rows, 3 * local), lambda t, *_: (first + t, 0))],
-        [row_spec(rows, rank)] + [whole_spec((block, wide))] * blocks,
-        [sds((count * rows, rank), BF)] + [sds((block, wide), BF)] * blocks,
-        weight.scratch(part[1]),
-        cost(40 * count * rows * wide * local, 8 * wide * local),
-        [mixed],
-    )
-
-
-def attend_back_kernel(weight, part, first, last, tiles, number, places_ref, *refs):
+def attend_back_kernel(weight, part, first, last, tiles, number, blocks, places_ref, *refs):
     w_refs, refs = refs[: weight.count], refs[weight.count :]
     grads, refs = refs[:number], refs[number:]
     (
         up_ref, q_ref, k_ref, v_ref, o_ref, lse_ref, cos_ref, left_ref, right_ref, low_ref,
     ), refs = refs[:10], refs[10:]
     *refs, g_ref, w_ref, sems = refs
-
-    @pl.when(pl.program_id(0) == 0)
-    def _():
-        wait_for(weight.bring(w_refs, places_ref, w_ref, sems, *part[:2]))
-
+    begin, end = weight.at_first(pl.program_id(0), w_refs, places_ref, w_ref, sems, *part[:2])
+    begin()
     take_tile(grads, g_ref, pl.program_id(0))
     if not first:
         (mq_ref, gk_in, gv_in, down_in), refs = refs[:4], refs[4:]
     if last:
-        m_ref, down_ref, gup_ref, gk_ref, gv_ref = refs
+        (n_ref, z_ref, r_ref), refs = refs[:3], refs[3:]
+        (down_ref, gup_ref, rows_ref), refs = refs[:3], refs[3:]
+        dn_refs, (m_ref, gk_ref, gv_ref) = refs[:blocks], refs[blocks:]
     else:
         m_ref, gk_ref, gv_ref, down_ref = refs
     step, rows = pl.program_id(0), q_ref.shape[0]
@@ -454,6 +421,7 @@
 
     grad = g_ref[...]
     grad_low = dot_nt(grad, up_ref[...]).astype(BF)
+    end()
     at = slice(part[2], part[2] + local)
     grad_out = dot(grad, w_ref[:width, at]) + dot(grad_low, w_ref[width:, at])
     grad_out = grad_out.astype(BF)
@@ -484,28 +452,47 @@
                 m_ref[:, local + at : local + at + breadth] = turned.astype(BF)
             m_ref[:, 2 * local :] = gv_ref[...].astype(BF)
             gup_ref[...] = dot_tn(low_ref[...], m_ref[...])
-
-
-def attend_back(grads, up, weight, query, keys, values, out, lse, tables, low, rank, rows, start, before):
+            rank, block = up_ref.shape[0], dn_refs[0].shape[0]
+            down = 0.0
+            for i, ref in enumerate(dn_refs):
+                at = slice(i * block, (i + 1) * block)
+                value = dot_nt(m_ref[at, :], w_ref[:, : 3 * local]).astype(BF)
+                ref[:, : width + rank] = value
+                ref[:, width + rank :] = jnp.zeros((block, ref.shape[1] - width - rank), BF)
+                down = down + dot_tn(value[:, width:], n_ref[at, :])
+            by_piece(rows_ref, 0, down)
+            by_piece(rows_ref, rank, dot_tn(z_ref[...], r_ref[...]))
+
+
+def attend_back(
+    grads, up, weight, query, keys, values, out, lse, tables, low, rows, start, before, ends
+):
     tokens, local = query.shape
     block, width = grads[0].shape
+    rank = up.shape[0]
     count = len(grads) * block // rows
-    first, last = before is None, (start + count) * rows == tokens
+    first, last = before is None, ends is not None
     before = () if first else before
+    ends = ends if last else ()
     sums = [sds((tokens, local), F32)] * 2 + [sds((rank, local), F32)]
+    blocks = tokens // block if last else 0
     if last:
-        shapes = [sds((tokens, 3 * local), BF), sums[2], sds((rank, 3 * local), F32)]
-        scratch = [pltpu.VMEM((tokens, local), F32)] * 2
+        members = width // local
+        shapes = [sums[2], sds((rank, 3 * local), F32), sds((members, 2 * rank, local), BF)]
+        shapes += [sds((block, wide_of(weight)), BF)] * blocks
+        scratch = [pltpu.VMEM((tokens, 3 * local), BF)]
+        scratch += [pltpu.VMEM((tokens, local), F32)] * 2
+        part = 0, 4 * local, 3 * local
     else:
         shapes, scratch = [sds((count * rows, local), BF), *sums], []
+        part = weight.columns(3 * local, local)
     scratch.append(pltpu.VMEM((rows, width), BF))
 
     def tile(columns):
         return pl.BlockSpec((rows, columns), lambda t, *_: (start + t, 0))
 
-    part = weight.columns(3 * local, local)
     return weight_call(
-        functools.partial(attend_back_kernel, weight, part, first, last, start, len(grads)),
+        functools.partial(attend_back_kernel, weight, part, first, last, start, len(grads), blocks),
         weight,
         (count,),
         [
@@ -519,12 +506,13 @@
             *[whole_spec(t.shape) for t in tables],
             whole_spec(low.shape),
             *[whole_spec(b.shape) for b in before],
+            *[whole_spec(e.shape) for e in ends],
         ],
         [whole_spec(s.shape) for s in shapes],
         shapes,
         scratch + weight.scratch(part[1]),
         cost(40 * count * rows * tokens * local, 10 * query.size, count * rows * tokens),
-        [*grads, up, query, keys, values, out, lse, *tables, low, *before],
+        [*grads, up, query, keys, values, out, lse, *tables, low, *before, *ends],
     )
 
 
@@ -731,23 +719,6 @@
     )(x, r1, down, gain, *dns)
 
 
-def rows_kernel(near_ref, far_ref, n_ref, z_ref, r_ref, out_ref):
-    rows, rank = near_ref.shape
-    down = dot_tn(near_ref[...], n_ref[:rows, :]) + dot_tn(far_ref[...], n_ref[rows:, :])
-    by_piece(out_ref, 0, down)
-    by_piece(out_ref, rank, dot_tn(z_ref[...], r_ref[...]))
-
-
-def self_rows(low_near, low_far, normed, low_two, branch, members):
-    rank, width = low_near.shape[1], normed.shape[1]
-    return pl.pallas_call(
-        rows_kernel,
-        out_shape=sds((members, 2 * rank, width // members), BF),
-        compiler_params=pltpu.CompilerParams(vmem_limit_bytes=VMEM_LIMIT),
-        cost_estimate=cost(0, 0),
-    )(low_near, low_far, normed, low_two, branch)
-
-
 def context_kernel(weight, members, at_pieces, places_ref, *refs):
     w_refs, refs = refs[: weight.count], refs[weight.count :]
     blocks, (down_ref, kv_ref, low_ref, w_ref, sems) = refs[:members], refs[members:]
@@ -819,7 +790,7 @@
         [whole_spec(s.shape) for s in shapes],
         shapes,
         weight.scratch(),
-        cost(0, 0),
+        cost(10**10, 10**6),
         arrays,
     )
 
@@ -938,10 +909,10 @@
     )
 
 
-def settle_first_kernel(fold, labels_ref, in_ref, down_ref, up_ref, hid_ref, gate_ref):
+def settle_first_kernel(fold, labels_ref, in_ref, down_ref, hid_ref, gate_ref):
     slot = pl.program_id(0)
     local = down_ref.shape[-1]
-    for ref in (down_ref, up_ref, hid_ref, gate_ref):
+    for ref in (down_ref, hid_ref, gate_ref):
         ref[...] = jnp.zeros_like(ref)
     for s in range(in_ref.shape[0]):
 
@@ -949,17 +920,15 @@
         def _(s=s):
             for n, k in enumerate(DOWN_FIRST):
                 down_ref[0, k] += in_ref[s, n].astype(F32)
-            for n, k in enumerate(UP_FIRST):
-                up_ref[0, k] += in_ref[s, len(DOWN_FIRST) + n].astype(F32)
             for k in range(fold):
-                at, n = slice(k * local, (k + 1) * local), 4 + k
+                at, n = slice(k * local, (k + 1) * local), len(DOWN_FIRST) + k
                 hid_ref[0, :, at] += in_ref[s, n].astype(F32)
                 gate_ref[0, 0, :, at] += in_ref[s, n + fold].astype(F32)
                 gate_ref[0, 1, :, at] += in_ref[s, n + 2 * fold].astype(F32)
 
 
-def settle_second_kernel(labels_ref, in_ref, down_in, up_in, down_ref, up_ref):
-    del down_in, up_in
+def settle_second_kernel(labels_ref, in_ref, down_in, down_ref, up_ref):
+    del down_in
     slot = pl.program_id(0)
     downs, ups = down_ref.shape[1], up_ref.shape[1]
     for ref in (down_ref, up_ref):
@@ -972,7 +941,7 @@
             up_ref[0] += in_ref[s, downs : downs + ups].astype(F32)
 
 
-DOWN_FIRST, UP_FIRST = (4, 5), (7, 8)
+DOWN_FIRST = (4, 5)
 
 
 def slot_spec(shape):
@@ -984,7 +953,6 @@
     hidden = fold * local
     shapes = [
         (slots, 6, rank, local),
-        (slots, 9, rank, local),
         (slots, rank, hidden),
         (slots, 2, rank, hidden),
     ]
@@ -1002,28 +970,26 @@
     )(labels, grads)
 
 
-def settle_second(labels, grads, down, up):
-    downs, ups = DOWN_FIRST[0], UP_FIRST[0]
+def settle_second(labels, grads, down):
+    downs = DOWN_FIRST[0]
+    up = down.shape[:1] + (9,) + down.shape[2:]
     return pl.pallas_call(
         settle_second_kernel,
         grid_spec=pltpu.PrefetchScalarGridSpec(
             num_scalar_prefetch=1,
             grid=(down.shape[0],),
-            in_specs=[whole_spec(grads.shape)] + [pl.BlockSpec(memory_space=pl.ANY)] * 2,
-            out_specs=[
-                slot_spec((1, downs) + down.shape[2:]),
-                slot_spec((1, ups) + up.shape[2:]),
-            ],
+            in_specs=[whole_spec(grads.shape), pl.BlockSpec(memory_space=pl.ANY)],
+            out_specs=[slot_spec((1, downs) + down.shape[2:]), slot_spec(up)],
         ),
-        out_shape=[sds(down.shape, F32), sds(up.shape, F32)],
-        input_output_aliases={2: 0, 3: 1},
+        out_shape=[sds(down.shape, F32), sds(up, F32)],
+        input_output_aliases={2: 0},
         compiler_params=params(),
         cost_estimate=cost(0, 0),
-    )(labels, grads, down, up)
+    )(labels, grads, down)
 
 
 def chunks(hidden):
-    return (hidden // 3,) * 3
+    return 2 * hidden // 3, hidden // 3
 
 
 def body(
@@ -1232,7 +1198,9 @@
 
     got_one = spread([], 0, 0, ready_keyval)
     pair_far = group.far_p(pair)
-    feed_from = [[home_swap(step.wait(shard_feed[0])), turned(step.wait(shard_feed[0]))]]
+    half_columns = shard_feed[0].shape[1] // 2
+    halves = step.wait(shard_feed[0][:, :half_columns], shard_feed[0][:, half_columns:])
+    feed_one = [home_swap(halves[0]), turned(halves[0])]
     query, keys, values, low_one, normed_one = project_self(
         listed(step.wait(*stream)), gains[0:1], biases[0:1], down[0], self_weight, tables, tile
     )
@@ -1260,7 +1228,7 @@
             total = total + f.astype(F32)
         return step.mark(total)
 
-    got_one, pair_far, feed_from[0] = wait_all(got_one, pair_far, feed_from[0])
+    got_one, pair_far, feed_one = wait_all(got_one, pair_far, feed_one)
     (y_sums,) = far_sums(y_far)
 
     far = move_p(y_sums)
@@ -1274,13 +1242,12 @@
         got_two = [xor_move(turn, "chip", 4, k) for turn, k in zip(turns, near_chips)]
     else:
         got_two = flat(*[spread([], 0, 0, p) for p in pair_far])
-    early = [ready_keyval, *got_one]
-    early_swapped = [core_swap(b) for b in early]
+    feed_two = [home_swap(halves[1]), turned(halves[1])]
     heads_near, logsum_near, *y_rows = attend_self(
         step.wait(query), keys, values, self_weight, tile, 0, near_tiles, rows
     )
     y_rows = listed(step.mark(*y_rows))
-    far, got_two, early_swapped = wait_all(far, got_two, early_swapped)
+    far, got_two, feed_two = wait_all(far, got_two, feed_two)
     y_other, context_other, *swapped = swap_all([y_rows[1], context_own, *context_far])
     branch = [y_rows[0], y_other, *far]
     context_blocks = [context_own, context_other]
@@ -1295,8 +1262,7 @@
     keyval = step.mark(keyval)
 
     keyval_far = group.far_p(keyval)
-    cotangent_own = home_swap(step.wait(out_cotangent[0]))
-    ready_feed = [step.mark(stacked(*feed_from[0]))]
+    ready_feed = [step.mark(stacked(*[packed(*two) for two in zip(feed_one, feed_two)]))]
     found = [(ready_keyval, block, block, 0, 0, 0)]
     found += [(g, block, block, k, 0, 0) for g, k in zip(got_one, near_chips)]
     if chips == 4:
@@ -1320,12 +1286,11 @@
     for entry in found:
         if not any(entry[0] is a for a in arrays):
             arrays.append(entry[0])
-    swapped = swap_all([keyval, *keyval_far, *arrays[len(early) :]])
+    swapped = swap_all([keyval, *keyval_far, *arrays])
     keyvals = [keyval, swapped[0]]
     for far, far_other in zip(keyval_far, swapped[1:]):
         keyvals += [far, far_other]
-    others = early_swapped + swapped[1 + len(keyval_far) :]
-    cotangent_own = step.wait(cotangent_own)
+    others = swapped[1 + len(keyval_far) :]
     cross_weight = Weight((pairs, deep, 4 * local), row_places)
     for array, other in zip(arrays, others):
         entries = [e[1:] for e in found if e[0] is array]
@@ -1342,8 +1307,7 @@
     )
 
     near_feed = [spread([], 0, 0, ready_feed[0])]
-    feed_from.append([home_swap(step.wait(shard_feed[1])), turned(step.wait(shard_feed[1]))])
-    cotangent_far = group.far_p(step.wait(cotangent_own))
+    feed_from = [home_swap(step.wait(shard_feed[1])), turned(step.wait(shard_feed[1]))]
     stream_own, *branch = step.wait(stream_own, *branch)
 
     (
@@ -1353,13 +1317,12 @@
         stream_own, branch, up[3], up[7], down[2], gains, biases, cross_weight, keyvals, core_at,
     )
     normed_own = step.mark(normed_three)
-    near_feed[0], cotangent_far, feed_from[1] = wait_all(
-        near_feed[0], cotangent_far, feed_from[1]
-    )
-    ready_feed.append(step.mark(stacked(*feed_from[1])))
+    (feed_from,) = wait_all(feed_from)
+    ready_feed.append(step.mark(stacked(*feed_from)))
 
     normed_far = group.far_p(normed_own)
-    near_feed.append(spread(near_feed[0], 0, block, ready_feed[1]))
+    cotangent_own = home_swap(step.wait(out_cotangent[0]))
+    (normed_other,) = swap_all([normed_own])
     down_hidden = lax.dynamic_index_in_dim(
         adapter_down_hidden.transpose(0, 2, 1), index, 0, keepdims=False
     )
@@ -1373,53 +1336,58 @@
         for to in [slice(a, a + p) for a, p in zip(at, parts)]
     ]
     low_feed = step.mark(*low_feed)
-    near_feed[1], normed_far = wait_all(near_feed[1], normed_far)
-    normed_other, cotangent_other, *swapped = swap_all(
-        [normed_own, cotangent_own, *normed_far, *cotangent_far]
-    )
-    normed_blocks, cotangent_blocks = [normed_own, normed_other], [cotangent_own, cotangent_other]
-    for far, far_other in zip(normed_far, swapped):
-        normed_blocks += [far, far_other]
-    for far, far_other in zip(cotangent_far, swapped[len(normed_far) :]):
-        cotangent_blocks += [far, far_other]
-
-    def feed_weight(i, first, rest):
+    (near_feed[0],) = wait_all(near_feed[0])
+    rest_feed = spread(near_feed[0], 0, block, None)
+    normed_far, (cotangent_own,) = wait_all(normed_far, [cotangent_own])
+    cotangent_other, *normed_swapped = swap_all([cotangent_own, *normed_far])
+
+    def feed_weight(i, rest):
         return chip_weight(
-            (ready_feed[i], 0), [(g, first) for g in near_feed[i]], [(g, 0) for g in rest],
+            (ready_feed[i], 0), [(g, 0) for g in near_feed[i]], [(g, 0) for g in rest],
             low_feed[i], 3 * parts[i], stacked_halves,
         )
 
-    def feed_pass(weight, sums, picked, start, last):
-        normed, cotangent = wait_all(normed_blocks[picked], cotangent_blocks[picked])
-        found = feed(normed, cotangent, down[5], up[8], weight, sums, tile, start, last)
+    normed_blocks = [[normed_own, normed_other], []]
+    cotangent_blocks = [[cotangent_own, cotangent_other], []]
+
+    def feed_pass(weight, half, state, last):
+        normed, cotangent = wait_all(normed_blocks[half], cotangent_blocks[half])
+        found = feed(normed, cotangent, down[5], up[8], weight, state, tile, 0, last)
         *values, gdown, ggate, gupper = found
         return listed(step.mark(*values)), [gdown, ggate, gupper]
 
-    everything, far_only, near_only = slice(0, None), slice(2, None), slice(0, 2)
-
-    feed_from.append([home_swap(step.wait(shard_feed[2])), turned(step.wait(shard_feed[2]))])
-    rests = near_feed[1] if chips == 4 else []
-    weight = feed_weight(0, 0, rests)
-    rest_feed = spread(near_feed[1], skip(block), block, None)
-    (y, dn, *lows), *feed_grads = feed_pass(weight, (), everything, 0, False)
-    rest_feed, feed_from[2] = wait_all(rest_feed, feed_from[2])
-    ready_feed.append(step.mark(stacked(*feed_from[2])))
-
-    weight = feed_weight(1, skip(block), rest_feed)
-    near_feed.append(spread([], 0, 0, ready_feed[2]))
-    (y, dn), grads = feed_pass(weight, (*lows, y, dn), everything, 0, False)
-    feed_grads.append(grads)
-    (near_feed[2],) = wait_all(near_feed[2])
-    (rest_feed,) = wait_all(spread(near_feed[2], 0, block, None)) if chips == 4 else ([],)
-    weight = feed_weight(2, 0, rest_feed)
-    found, grads = feed_pass(weight, (*lows, y, dn), far_only, near_tiles, True)
+    def added(one, two):
+        return [a + b for a, b in zip(one, two)]
+
+    (rest_feed,) = wait_all(rest_feed) if rest_feed else ([],)
+    weight = feed_weight(0, rest_feed)
+    near_feed.append(spread([], 0, 0, ready_feed[1]))
+    cotangent_far = group.far_p(cotangent_own)
+    (y, dn, *lows), grads = feed_pass(weight, 0, (), False)
+    states = [(*lows, y, dn)]
+    near_feed[1], cotangent_far = wait_all(near_feed[1], cotangent_far)
+    swapped = normed_swapped + swap_all(cotangent_far)
+    for blocks, fars, others in (
+        (normed_blocks[1], normed_far, swapped[: pairs - 1]),
+        (cotangent_blocks[1], cotangent_far, swapped[pairs - 1 :]),
+    ):
+        for far, far_other in zip(fars, others):
+            blocks += [far, far_other]
+    rest_feed = spread(near_feed[1], 0, block, None)
+    (y, dn, *lows), more = feed_pass(weight, 1, (), False)
+    states.append((*lows, y, dn))
+    feed_grads = [added(grads, more)]
+    (rest_feed,) = wait_all(rest_feed) if rest_feed else ([],)
+
+    weight = feed_weight(1, rest_feed)
+    found, grads = feed_pass(weight, 1, states[1], True)
     y_far, dn_far = found[: len(found) // 2], found[len(found) // 2 :]
 
     dn_sums, y_sums = far_sums(dn_far, y_far)
     far = move_p(dn_sums)
-    found, more = feed_pass(weight, (*lows, y, dn), near_only, 0, True)
+    found, more = feed_pass(weight, 0, states[0], True)
     y_rows, dn_rows = found[:2], found[2:]
-    feed_grads.append([a + b for a, b in zip(grads, more)])
+    feed_grads.append(added(grads, more))
     (far,) = wait_all(far)
     dn_other, y_other = swap_all([dn_rows[1], y_rows[1]])
     grad_normed = [dn_rows[0], dn_other, *far]
@@ -1436,50 +1404,47 @@
     branch_far = group.far_p(branch_grad)
     (branch_other,) = swap_all([branch_grad])
 
-    def back(grad, heads, logsum, first, before):
+    def back(grad, heads, logsum, first, before, ends):
         return attend_back(
-            grad, up[3], self_weight, query, keys, values, heads, logsum, tables, low_one, rank,
-            tile, first, before,
+            grad, up[3], self_weight, query, keys, values, heads, logsum, tables, low_one, tile,
+            first, before, ends,
         )
 
+    def taken(by_piece, k):
+        return lax.dynamic_index_in_dim(by_piece, pieces[k], 0, keepdims=False)
+
+    def taken_near(by_member, k):
+        member = k // 2 * 2 + (group.core ^ (k % 2))
+        return lax.dynamic_index_in_dim(by_member, member, 0, keepdims=False)
+
+    first_rows = listed(
+        step.mark(
+            *[
+                stacked(taken_near(near_rows, k)[:rank], taken(fixed_rows, k)[rank : 2 * rank])
+                for k in range(members)
+            ]
+        )
+    )
+    others = swap_all([*keyval_rows[1::2], *first_rows[1::2]])
+    keyval_sums, first_sums = (
+        [group.near_sums(a, b) for a, b in zip(own[::2], others[n * pairs : (n + 1) * pairs])]
+        for n, own in enumerate((keyval_rows, first_rows))
+    )
+    moving = listed(step.mark(*[x.astype(BF) for x in keyval_sums[1:] + first_sums[1:]]))
+    keyval_far, first_far = move_p(moving[: pairs - 1]), move_p(moving[pairs - 1 :])
     grads = listed(step.wait(branch_grad, branch_other))
-    near_back = step.mark(*back(grads, heads_near, logsum_near, 0, None))
-    (branch_far,) = wait_all(branch_far)
+    near_back = step.mark(*back(grads, heads_near, logsum_near, 0, None, None))
+    branch_far, keyval_far, first_far = wait_all(branch_far, keyval_far, first_far)
 
     output, grad_up_eight = step.mark(
         *output_end(
             stream_two, [step.wait(y_rows[0]), y_other, *far], up[8], cotangent_own, members
         )
     )
-
-    def taken(by_piece, k):
-        return lax.dynamic_index_in_dim(by_piece, pieces[k], 0, keepdims=False)
-
-    def taken_near(by_member, k):
-        member = k // 2 * 2 + (group.core ^ (k % 2))
-        return lax.dynamic_index_in_dim(by_member, member, 0, keepdims=False)
-
-    first_rows = listed(
-        step.mark(
-            *[
-                stacked(
-                    taken(fixed_rows, k)[rank:], taken(grad_up_eight, k),
-                    taken_near(near_rows, k)[:rank],
-                )
-                for k in range(members)
-            ]
-        )
-    )
-    swapped = swap_all([*branch_far, *first_rows[1::2], *keyval_rows[1::2]])
+    swapped = swap_all(branch_far)
     branch_blocks = []
     for f, o in zip(branch_far, swapped):
         branch_blocks += [f, o]
-    others = swapped[len(branch_far) :]
-    first_sums, keyval_sums = (
-        [group.near_sums(a, b) for a, b in zip(even[::2], other)]
-        for even, other in ((first_rows, others[:pairs]), (keyval_rows, others[pairs:]))
-    )
-    moving = listed(step.mark(*[x.astype(BF) for x in first_sums[1:] + keyval_sums[1:]]))
 
     def columns(array):
         return array.reshape(rank, -1, local).transpose(1, 0, 2)
@@ -1503,37 +1468,6 @@
             own = own + f.astype(F32)
         return own
 
-    first_far, keyval_far = move_p(moving[: pairs - 1]), move_p(moving[pairs - 1 :])
-    block_output = home_swap(step.wait(output))
-    branch_blocks = listed(step.wait(*branch_blocks))
-    grad_mixed, grad_down_one, grad_up_self = back(
-        branch_blocks, heads_far, logsum_far, near_tiles, near_back
-    )
-    grad_mixed = step.mark(grad_mixed)
-    first_far, keyval_far, (block_output,) = wait_all(first_far, keyval_far, [block_output])
-    summed = total(first_sums[0], first_far).reshape(-1, rank, local)
-    first = sent(
-        [
-            summed[3:4],
-            summed[0:1],
-            summed[1:3],
-            *[columns(jnp.concatenate(g, axis=1)) for g in zip(*feed_grads)],
-        ]
-    )
-    low_far, *dn_far = step.mark(
-        *project_back(
-            step.wait(grad_mixed), self_weight, tile, near_tiles, tiles - near_tiles, rows, rank
-        )
-    )
-    (first,) = wait_all(first)
-    (dn_sums,) = far_sums(dn_far)
-
-    far = move_p(dn_sums)
-    low_near, *dn_rows = step.mark(
-        *project_back(step.wait(grad_mixed), self_weight, tile, 0, near_tiles, rows, rank)
-    )
-    (far,) = wait_all(far)
-    first = to_chips(first)
     grad_keyval = step.mark(total(keyval_sums[0], keyval_far).astype(BF))
     grad_up_keyval, *found = step.mark(
         *context_back(
@@ -1541,54 +1475,72 @@
         )
     )
     context_rows, grad_down_three = found[:members], found[members:]
-    own_rows = step.mark(
-        self_rows(step.wait(low_near), low_far, normed_one, low_two, branch_grad, members)
-    )
+    summed = total(first_sums[0], first_far).reshape(-1, rank, local)
+    first = sent([summed, *[columns(jnp.concatenate(g, axis=1)) for g in zip(*feed_grads)]])
+    block_output = home_swap(step.wait(output))
+    branch_blocks = listed(step.wait(*branch_blocks))
+    found = back(
+        branch_blocks, heads_far, logsum_far, near_tiles, near_back,
+        (normed_one, low_two, branch_grad),
+    )
+    first, (block_output,), found = wait_all(first, [block_output], found)
+    grad_down_one, grad_up_self, own_rows, *dn_blocks = found
+
     second_rows = listed(
         step.mark(
             *[
                 stacked(
-                    taken(own_rows, k), taken(fixed_rows, k)[:rank], grad_down_three[k],
+                    taken(own_rows, k), taken(fixed_rows, k)[:rank],
+                    taken(fixed_rows, k)[2 * rank :], taken(grad_up_eight, k), grad_down_three[k],
                     taken_near(near_rows, k)[rank:],
                 )
                 for k in range(members)
             ]
         )
     )
-    dn_other, *others = swap_all([dn_rows[1], *second_rows[1::2], *context_rows[1::2]])
-    second_sums, context_sums = (
-        [group.near_sums(a, b) for a, b in zip(even[::2], other)]
-        for even, other in ((second_rows, others[:pairs]), (context_rows, others[pairs:]))
-    )
-    moving = listed(step.mark(*[x.astype(BF) for x in second_sums[1:] + context_sums[1:]]))
-
-    second_far, context_far = move_p(moving[: pairs - 1]), move_p(moving[pairs - 1 :])
+    swapped = swap_all([*dn_blocks[1::2], *second_rows[1::2], *context_rows[1::2]])
+    dn_sums, second_sums, context_sums = (
+        [group.near_sums(a, b) for a, b in zip(own[::2], swapped[n * pairs : (n + 1) * pairs])]
+        for n, own in enumerate((dn_blocks, second_rows, context_rows))
+    )
+    moving = [x.astype(BF) for x in dn_sums[1:] + second_sums[1:] + context_sums[1:]]
+    moving = listed(step.mark(*moving))
+    count = pairs - 1
+    far = move_p(moving[:count])
+    second_far = move_p(listed(step.wait(*moving[count : 2 * count])))
+    context_far = move_p(listed(step.wait(*moving[2 * count :])))
+    first = to_chips(first)
+    far, second_far, context_far, first = wait_all(far, second_far, context_far, first)
+
     grad_inputs = step.mark(
-        input_end(stream_own, grad_stream, [dn_rows[0], dn_other, *far], down[0], gains[0:1])
-    )
-    second_far, context_far, first = wait_all(second_far, context_far, first)
+        input_end(
+            stream_own, grad_stream, [dn_blocks[0], swapped[0], *far], down[0], gains[0:1]
+        )
+    )
     summed = total(second_sums[0], second_far).reshape(-1, rank, local)
     second = sent(
         [
             summed[0:1],
             grad_down_one[None],
-            summed[2:4],
+            summed[2:3],
+            summed[5:6],
             columns(grad_up_self),
             summed[1:2],
-            summed[4:5],
+            summed[6:7],
             columns(grad_up_keyval),
+            summed[3:5],
         ]
     )
     grad_inputs = home_swap(step.wait(grad_inputs))
     grad_context = home_swap(step.mark(total(context_sums[0], context_far).astype(BF)))
     first, labels = every(first)
-    grad_down, grad_up, grad_hidden, grad_gate = settle_first(labels, first, slots, fold)
-    grad_down, grad_up = step.mark(grad_down, grad_up)
+    grad_down, grad_hidden, grad_gate = settle_first(labels, first, slots, fold)
+    grad_down = step.mark(grad_down)
     (second,) = wait_all(second)
     (second,) = wait_all(to_chips(second))
     second, labels = every(second)
     labels = labels + (step.token[0, 0].astype(F32) * 0.0).astype(jnp.int32)
-    grad_down, grad_up = settle_second(labels, second, grad_down, grad_up)
+    grad_down, grad_up = settle_second(labels, second, grad_down)
     return (
         block_output[None],
         grad_inputs.astype(F32)[None],

time: 618 us -> 586 us (0.948)
  waiting for transfers between devices: 158 us -> 141 us
  Pallas kernels: 248 us -> 235 us
  starting transfers between devices: 140 us -> 128 us
  other arithmetic: 20.3 us -> 27.2 us
    ppermute x42 -> x40, waiting for transfers between devices: 124 us -> 95.3 us  [xor_move(): return lax.ppermute(x, axis, [(i, i ^ k) for i in range(size)])]
    ppermute x4, waiting for transfers between devices: 0.01 us -> 13.8 us  [turned(): return lax.ppermute(x, ('core', 'zhi'), [(0, 1), (1, 3), (2, 0), (3, 2)])]
    pallas_call x15 -> x13, Pallas kernels: 221 us -> 211 us  [weight_call(): pl.pallas_call(kernel, grid_spec=pltpu.PrefetchScalarGridSpec(num_scalar_...]
    ppermute x12, starting transfers between devices: 22.8 us -> 16.3 us  [home_swap(): return lax.ppermute(x, ('core', 'zhi'), [(0, 0), (1, 2), (2, 1), (3, 3)])]
    ppermute x4, starting transfers between devices: 16.5 us -> 10.2 us  [turned(): return lax.ppermute(x, ('core', 'zhi'), [(0, 1), (1, 3), (2, 0), (3, 2)])]
    unnamed x224 -> x227, local copies, waits for them, and re-layouts: 16.5 us -> 19.6 us
    ppermute x42 -> x40, starting transfers between devices: 79.1 us -> 79.2 us  [xor_move(): return lax.ppermute(x, axis, [(i, i ^ k) for i in range(size)])]
  transfers between devices with their start and end apart: 99 -> 97, of which waited for: 39 -> 38; matrix products, arithmetic and copies ran while one was open for 6% -> 7% of each run, Pallas kernels for 36% -> 36%
where the time goes in v5:
time: 586 us; the launch traced here: 576 us
  Pallas kernels  235 us (40%)
  waiting for transfers between devices  141 us (24%)
  starting transfers between devices  128 us (22%)
  local copies, waits for them, and re-layouts  40.7 us (7%)
  other arithmetic  27.2 us (5%)
    pallas_call x13, Pallas kernels, weight_call(): pl.pallas_call(kernel, grid_spec=pltpu.PrefetchScalarGridSpec(num_scalar_...  211 us
    ppermute x40, waiting for transfers between devices, xor_move(): return lax.ppermute(x, axis, [(i, i ^ k) for i in range(size)])  95.3 us
    ppermute x40, starting transfers between devices, xor_move(): return lax.ppermute(x, axis, [(i, i ^ k) for i in range(size)])  79.2 us
    ppermute x39, waiting for transfers between devices, core_swap(): return lax.ppermute(x, 'core', SWAP)  22.2 us
    unnamed x227, local copies, waits for them, and re-layouts  19.6 us
    ppermute x12, starting transfers between devices, home_swap(): return lax.ppermute(x, ('core', 'zhi'), [(0, 0), (1, 2), (2, 1), (3, 3)])  16.3 us
    ppermute x39, starting transfers between devices, core_swap(): return lax.ppermute(x, 'core', SWAP)  14.6 us
    ppermute x4, waiting for transfers between devices, turned(): return lax.ppermute(x, ('core', 'zhi'), [(0, 1), (1, 3), (2, 0), (3, 2)])  13.8 us
  transfers between devices with their start and end apart: 97, of which 38 were waited for; matrix products, arithmetic and copies ran while one was open for 7% of the time, Pallas kernels for 36%

profile of v5, /device:TPU:0, one launch (start us, length us, event | category | flops | bytes accessed | tf_op | source)
XLA Modules:
  0.0 576.1 jit_solution(11613416353716701815)
XLA Ops:
  3.7 6.0 %collective-permute-start.2 = (bf16[192,1536]{1,0:T(8,128)(2,1)}, bf16[192,1536]{1,0:T(8,128)(2,1)}, u32[]{:S(2)}, u32[]{:S(2)}) collective-permute-start(bf16[192,1536]{1,0:T(8,128)(2,1)} %pad_maximum_fusion.9), channel_id=1, source_target_pairs={{0,0},{2,4},{4,2},{6,6},{1,1},{3,5},{5,3},{7,7},{8,8},{10,12},{12,... | collective-permute-start | bytes 1769480 | tf_op jit(solution)/shard_map/ppermute | solution.py:52
  32.2 12.3 %collective-permute-start.10 = (bf16[256,1536]{1,0:T(8,128)(2,1)}, bf16[256,1536]{1,0:T(8,128)(2,1)}, u32[]{:S(2)}, u32[]{:S(2)}) collective-permute-start(bf16[256,1536]{1,0:T(8,128)(2,1)} %collective-permute-done.6.refs_6_.refs_17_.x_ref), channel_id=1, source_target_pairs={{0,1},{1,0},{2,3},{3,2},{4,5},{5,4},{6,7},{7,6},{8,9},{9,8},{10,11... | collective-permute-start | bytes 2359304 | tf_op jit(solution)/shard_map/ppermute | solution.py:48
  44.4 22.4 %collective-permute-start.12 = (bf16[192,1536]{1,0:T(8,128)(2,1)S(1)}, bf16[192,1536]{1,0:T(8,128)(2,1)S(1)}, u32[]{:S(2)}, u32[]{:S(2)}) collective-permute-start(bf16[192,1536]{1,0:T(8,128)(2,1)S(1)} %pad_maximum_fusion.8), channel_id=1, source_target_pairs={{0,2},{2,0},{1,3},{3,1},{4,6},{6,4},{5,7},{7,5},{8,10},{10,8},{9,1... | collective-permute-start | bytes 1769480 | tf_op jit(solution)/shard_map/ppermute | solution.py:48
  71.7 21.5 %collective-permute-done.12 = bf16[192,1536]{1,0:T(8,128)(2,1)S(1)} collective-permute-done((bf16[192,1536]{1,0:T(8,128)(2,1)S(1)}, bf16[192,1536]{1,0:T(8,128)(2,1)S(1)}, u32[]{:S(2)}, u32[]{:S(2)}) %collective-permute-start.12) | collective-permute-done | bytes 589856 | tf_op jit(solution)/shard_map/ppermute | solution.py:48
  108.5 14.8 %shard_map.226 = (bf16[1024,384]{1,0:T(8,128)(2,1)}, bf16[1024,384]{1,0:T(8,128)(2,1)}, bf16[1024,384]{1,0:T(8,128)(2,1)}, bf16[1024,16]{1,0:T(8,128)(2,1)}, bf16[1024,1536]{1,0:T(8,128)(2,1)}) custom-call(s32[22]{0:T(128)} %stack.87.places_ref, bf16[384,1536]{1,0:T(8,128)(2,1)} %copy-done.13, bf16[384,1536]{1,0:T(8,128)(2,1)} %copy-done.37, ...), custom_call_target="tpu_custom_call" | custom-call | flops 4831838208 | bytes 4718592 | tf_op jit(solution)/shard_map/pallas_call | solution.py:158
  123.4 12.9 %shard_map.227 = (bf16[512,384]{1,0:T(8,128)(2,1)}, f32[8,512]{1,0:T(8,128)}, bf16[256,1664]{1,0:T(8,128)(2,1)}, bf16[256,1664]{1,0:T(8,128)(2,1)}) custom-call(s32[22]{0:T(128)} %stack.87.places_ref, bf16[384,1536]{1,0:T(8,128)(2,1)} %copy-done.13, bf16[384,1536]{1,0:T(8,128)(2,1)} %copy-done.37, bf16[384,1536]{1,0:T(8,128)(2,1)} %copy-done.38, ...), custom_call_target="tpu_custom_call" | custom-call | flops 3221225472 | bytes 3145728 | tf_op jit(solution)/shard_map/pallas_call | solution.py:158
  147.8 12.8 %shard_map.228 = (bf16[512,384]{1,0:T(8,128)(2,1)}, f32[8,512]{1,0:T(8,128)}, bf16[256,1664]{1,0:T(8,128)(2,1)}, bf16[256,1664]{1,0:T(8,128)(2,1)}) custom-call(s32[22]{0:T(128)} %stack.87.places_ref, bf16[384,1536]{1,0:T(8,128)(2,1)} %copy-done.13, bf16[384,1536]{1,0:T(8,128)(2,1)} %copy-done.37, bf16[384,1536]{1,0:T(8,128)(2,1)} %copy-done.38, ...), custom_call_target="tpu_custom_call" | custom-call | flops 3221225472 | bytes 3145728 | tf_op jit(solution)/shard_map/pallas_call | solution.py:158
  160.7 13.7 %collective-permute-done.26 = bf16[192,1536]{1,0:T(8,128)(2,1)S(1)} collective-permute-done((bf16[192,1536]{1,0:T(8,128)(2,1)S(1)}, bf16[192,1536]{1,0:T(8,128)(2,1)S(1)}, u32[]{:S(2)}, u32[]{:S(2)}) %collective-permute-start.26) | collective-permute-done | bytes 589856 | tf_op jit(solution)/shard_map/ppermute | solution.py:56
  211.8 17.9 %shard_map.230 = (f32[256,1536]{1,0:T(8,128)}, f32[256,1536]{1,0:T(8,128)}, bf16[256,1536]{1,0:T(8,128)(2,1)}, bf16[256,1536]{1,0:T(8,128)(2,1)}, bf16[256,1536]...) custom-call(s32[22]{0:T(128)} %stack.87.places_ref, ...), custom_call_target="tpu_custom_call" | custom-call | flops 14495514624 | bytes 18874368 | tf_op jit(solution)/shard_map/pallas_call | solution.py:158
  231.1 6.0 %collective-permute-start.49 = (bf16[256,1536]{1,0:T(8,128)(2,1)S(1)}, bf16[256,1536]{1,0:T(8,128)(2,1)S(1)}, u32[]{:S(2)}, u32[]{:S(2)}) collective-permute-start(bf16[256,1536]{1,0:T(8,128)(2,1)S(1)} %copy-done.82), channel_id=1, source_target_pairs={{0,4},{4,0},{1,5},{5,1},{2,6},{6,2},{3,7},{7,3},{8,12},{12,8},{9,1... | collective-permute-start | bytes 2359304 | tf_op jit(solution)/shard_map/ppermute | solution.py:44
  241.6 12.9 %collective-permute-done.47.refs_1_ = bf16[384,3072]{1,0:T(8,128)(2,1)S(1)} collective-permute-done((bf16[384,3072]{1,0:T(8,128)(2,1)}, bf16[384,3072]{1,0:T(8,128)(2,1)S(1)}, u32[]{:S(2)}, u32[]{:S(2)}) %collective-permute-start.47) | collective-permute-done | bytes 2359328 | tf_op jit(solution)/shard_map/ppermute | solution.py:48
  273.5 14.8 %collective-permute-done.53.refs_3_ = bf16[192,3072]{1,0:T(8,128)(2,1)S(1)} collective-permute-done((bf16[192,3072]{1,0:T(8,128)(2,1)S(1)}, bf16[192,3072]{1,0:T(8,128)(2,1)S(1)}, u32[]{:S(2)}, u32[]{:S(2)}) %collective-permute-start.53) | collective-permute-done | bytes 1179680 | tf_op jit(solution)/shard_map/ppermute | solution.py:48
  290.7 20.9 %shard_map.231 = (bf16[512,1552]{1,0:T(8,128)(2,1)}, bf16[512,1552]{1,0:T(8,128)(2,1)}, bf16[512,16]{1,0:T(8,128)(2,1)}, bf16[512,16]{1,0:T(8,128)(2,1)}, f32[16...) custom-call(s32[22]{0:T(128)} %stack.87.places_ref, bf16[384,3072]{1,0:T(8,128)(2,1)} %maximum_maximum_fusion.refs_0_, ...), custom_call_target="tpu_custom_call" | custom-call | flops 19528679424 | bytes 9535488 | tf_op jit(solution)/shard_map/pallas_call | solution.py:158
  316.5 20.7 %shard_map.232 = (bf16[512,1552]{1,0:T(8,128)(2,1)}, bf16[512,1552]{1,0:T(8,128)(2,1)}, bf16[512,16]{1,0:T(8,128)(2,1)}, bf16[512,16]{1,0:T(8,128)(2,1)}, f32[16...) custom-call(s32[22]{0:T(128)} %stack.87.places_ref, bf16[384,3072]{1,0:T(8,128)(2,1)} %maximum_maximum_fusion.refs_0_, ...), custom_call_target="tpu_custom_call" | custom-call | flops 19528679424 | bytes 9535488 | tf_op jit(solution)/shard_map/pallas_call | solution.py:158
  339.0 15.2 %shard_map.233 = (bf16[256,1664]{1,0:T(8,128)(2,1)}, bf16[256,1664]{1,0:T(8,128)(2,1)}, bf16[256,1664]{1,0:T(8,128)(2,1)}, bf16[256,1664]{1,0:T(8,128)(2,1)}, f3...) custom-call(s32[22]{0:T(128)} %stack.87.places_ref, bf16[384,1536]{1,0:T(8,128)(2,1)} %copy-done.14, ...), custom_call_target="tpu_custom_call" | custom-call | flops 9764339712 | bytes 4767744 | tf_op jit(solution)/shard_map/pallas_call | solution.py:158
  361.5 14.8 %shard_map.234 = (bf16[256,1664]{1,0:T(8,128)(2,1)}, bf16[256,1664]{1,0:T(8,128)(2,1)}, bf16[256,1664]{1,0:T(8,128)(2,1)}, bf16[256,1664]{1,0:T(8,128)(2,1)}, f3...) custom-call(s32[22]{0:T(128)} %stack.87.places_ref, bf16[384,1536]{1,0:T(8,128)(2,1)} %copy-done.14, ...), custom_call_target="tpu_custom_call" | custom-call | flops 9764339712 | bytes 4767744 | tf_op jit(solution)/shard_map/pallas_call | solution.py:158
  386.3 22.4 %shard_map.235 = (f32[256,1536]{1,0:T(8,128)}, bf16[256,1536]{1,0:T(8,128)(2,1)}, bf16[4,48,384]{2,1,0:T(8,128)(2,1)}, bf16[4,32,384]{2,1,0:T(8,128)(2,1)}, bf16...) custom-call(s32[22]{0:T(128)} %stack.87.places_ref, ...), custom_call_target="tpu_custom_call" | custom-call | flops 19327352832 | bytes 18874368 | tf_op jit(solution)/shard_map/pallas_call | solution.py:158
  416.6 18.2 %shard_map.236 = (bf16[512,384]{1,0:T(8,128)(2,1)}, f32[1024,384]{1,0:T(8,128)}, f32[1024,384]{1,0:T(8,128)}, f32[16,384]{1,0:T(8,128)}) custom-call(s32[22]{0:T(128)} %stack.87.places_ref, bf16[384,1536]{1,0:T(8,128)(2,1)} %copy-done.13, bf16[384,1536]{1,0:T(8,128)(2,1)} %copy-done.37, bf16[384,1536]{1,0:T(8,128)(2,1)} %copy-done.38, ...), custom_call_target="tpu_custom_call" | custom-call | flops 8053063680 | bytes 3932160 | tf_op jit(solution)/shard_map/pallas_call | solution.py:158
  444.4 5.7 shard_map.238
  456.8 29.6 %shard_map.239 = (f32[16,384]{1,0:T(8,128)}, f32[16,1152]{1,0:T(8,128)}, bf16[4,32,384]{2,1,0:T(8,128)(2,1)}, bf16[256,1664]{1,0:T(8,128)(2,1)}, bf16[256,1664]{...) custom-call(s32[22]{0:T(128)} %stack.87.places_ref, bf16[384,1536]{1,0:T(8,128)(2,1)} %copy-done.13, ...), custom_call_target="tpu_custom_call" | custom-call | flops 8053063680 | bytes 3932160 | tf_op jit(solution)/shard_map/pallas_call | solution.py:158
  500.9 17.2 %collective-permute-done.85 = bf16[112,384]{1,0:T(8,128)(2,1)S(1)} collective-permute-done((bf16[112,384]{1,0:T(8,128)(2,1)}, bf16[112,384]{1,0:T(8,128)(2,1)S(1)}, u32[]{:S(2)}, u32[]{:S(2)}) %collective-permute-start.85) | collective-permute-done | bytes 86048 | tf_op jit(solution)/shard_map/ppermute | solution.py:48
  535.9 5.8 %shard_map.241 = (f32[8,6,16,384]{3,2,1,0:T(8,128)}, f32[8,16,1536]{2,1,0:T(8,128)}, f32[8,2,16,1536]{3,2,1,0:T(8,128)}) custom-call(s32[8]{0:T(128)} %fusion.39.labels_ref, bf16[8,15,16,384]{3,2,1,0:T(8,128)(2,1)} %bitcast.257), custom_call_target="tpu_custom_call" | custom-call | flops 1000 | bytes 1000 | tf_op jit(solution)/shard_map/pallas_call | solution.py:959
  541.7 9.4 %collective-permute-done.93 = bf16[14,16,384]{2,0,1:T(8,128)(2,1)S(1)} collective-permute-done((bf16[14,16,384]{2,0,1:T(8,128)(2,1)S(1)}, bf16[14,16,384]{2,0,1:T(8,128)(2,1)S(1)}, u32[]{:S(2)}, u32[]{:S(2)}) %collective-permute-start.93) | collective-permute-done | bytes 172064 | tf_op jit(solution)/shard_map/ppermute | solution.py:60
  567.8 5.8 %shard_map.242 = (f32[8,6,16,384]{3,2,1,0:T(8,128)}, f32[8,9,16,384]{3,2,1,0:T(8,128)}) custom-call(s32[8]{0:T(128)} %fusion.40.labels_ref, bf16[8,14,16,384]{3,2,1,0:T(8,128)(2,1)} %bitcast.259, f32[8,6,16,384]{3,2,1,0:T(8,128)} %get-tuple-element.1018.down_in), custom_call_target="tpu_custom_call", output_to_operand_aliasing={{0}: (2, {})} | custom-call | flops 1000 | bytes 1000 | tf_op jit(solution)/shard_map/pallas_call | solution.py:976
  (542 shorter events, 217.4 us)
Async XLA Ops:
  24.8 42.0 %collective-permute-start.4 = (bf16[384,1536]{1,0:T(8,128)(2,1)S(1)}, bf16[384,1536]{1,0:T(8,128)(2,1)S(1)}, u32[]{:S(2)}, u32[]{:S(2)}) collective-permute-start(bf16[384,1536]{1,0:T(8,128)(2,1)S(1)} %pad_maximum_fusion.5.refs_0_), channel_id=1, source_target_pairs={{0,8},{8,0},{16,24},{24,16},{1,9},{9,1},{17,25},{25,17},{2,10},{10... | collective-permute-start | bytes 3538952 | tf_op jit(solution)/shard_map/ppermute | solution.py:48
  27.8 39.0 %collective-permute-start.5 = (bf16[384,1536]{1,0:T(8,128)(2,1)S(1)}, bf16[384,1536]{1,0:T(8,128)(2,1)S(1)}, u32[]{:S(2)}, u32[]{:S(2)}) collective-permute-start(bf16[384,1536]{1,0:T(8,128)(2,1)S(1)} %pad_maximum_fusion.5.refs_0_), channel_id=1, source_target_pairs={{0,16},{8,24},{16,0},{24,8},{1,17},{9,25},{17,1},{25,9},{2,18},{10... | collective-permute-start | bytes 3538952 | tf_op jit(solution)/shard_map/ppermute | solution.py:48
  32.2 61.0 %collective-permute-start.10 = (bf16[256,1536]{1,0:T(8,128)(2,1)}, bf16[256,1536]{1,0:T(8,128)(2,1)}, u32[]{:S(2)}, u32[]{:S(2)}) collective-permute-start(bf16[256,1536]{1,0:T(8,128)(2,1)} %collective-permute-done.6.refs_6_.refs_17_.x_ref), channel_id=1, source_target_pairs={{0,1},{1,0},{2,3},{3,2},{4,5},{5,4},{6,7},{7,6},{8,9},{9,8},{10,11... | collective-permute-start | bytes 2359304 | tf_op jit(solution)/shard_map/ppermute | solution.py:48
  44.4 48.8 %collective-permute-start.12 = (bf16[192,1536]{1,0:T(8,128)(2,1)S(1)}, bf16[192,1536]{1,0:T(8,128)(2,1)S(1)}, u32[]{:S(2)}, u32[]{:S(2)}) collective-permute-start(bf16[192,1536]{1,0:T(8,128)(2,1)S(1)} %pad_maximum_fusion.8), channel_id=1, source_target_pairs={{0,2},{2,0},{1,3},{3,1},{4,6},{6,4},{5,7},{7,5},{8,10},{10,8},{9,1... | collective-permute-start | bytes 1769480 | tf_op jit(solution)/shard_map/ppermute | solution.py:48
  101.6 34.8 %collective-permute-start.16 = (bf16[384,1536]{1,0:T(8,128)(2,1)S(1)}, bf16[384,1536]{1,0:T(8,128)(2,1)S(1)}, u32[]{:S(2)}, u32[]{:S(2)}) collective-permute-start(bf16[384,1536]{1,0:T(8,128)(2,1)S(1)} %pad_maximum_fusion.6.refs_0_), channel_id=1, source_target_pairs={{0,8},{8,0},{16,24},{24,16},{1,9},{9,1},{17,25},{25,17},{2,10},{10... | collective-permute-start | bytes 3538952 | tf_op jit(solution)/shard_map/ppermute | solution.py:48
  102.2 34.2 %collective-permute-start.17 = (bf16[384,1536]{1,0:T(8,128)(2,1)S(1)}, bf16[384,1536]{1,0:T(8,128)(2,1)S(1)}, u32[]{:S(2)}, u32[]{:S(2)}) collective-permute-start(bf16[384,1536]{1,0:T(8,128)(2,1)S(1)} %pad_maximum_fusion.6.refs_0_), channel_id=1, source_target_pairs={{0,16},{8,24},{16,0},{24,8},{1,17},{9,25},{17,1},{25,9},{2,18},{10... | collective-permute-start | bytes 3538952 | tf_op jit(solution)/shard_map/ppermute | solution.py:48
  103.1 33.2 %collective-permute-start.18 = (bf16[192,1536]{1,0:T(8,128)(2,1)S(1)}, bf16[192,1536]{1,0:T(8,128)(2,1)S(1)}, u32[]{:S(2)}, u32[]{:S(2)}) collective-permute-start(bf16[192,1536]{1,0:T(8,128)(2,1)S(1)} %copy-done.11), channel_id=1, source_target_pairs={{0,1},{1,0},{2,3},{3,2},{4,5},{5,4},{6,7},{7,6},{8,9},{9,8},{10,11... | collective-permute-start | bytes 1769480 | tf_op jit(solution)/shard_map/ppermute | solution.py:48
  103.1 33.3 %collective-permute-start.19 = (bf16[192,1536]{1,0:T(8,128)(2,1)S(1)}, bf16[192,1536]{1,0:T(8,128)(2,1)S(1)}, u32[]{:S(2)}, u32[]{:S(2)}) collective-permute-start(bf16[192,1536]{1,0:T(8,128)(2,1)S(1)} %get-tuple-element.586), channel_id=1, source_target_pairs={{0,0},{2,4},{4,2},{6,6},{1,1},{3,5},{5,3},{7,7},{8,8},{10,12},{12,... | collective-permute-start | bytes 1769480 | tf_op jit(solution)/shard_map/ppermute | solution.py:52
  103.8 32.6 %collective-permute-start.20 = (bf16[192,1536]{1,0:T(8,128)(2,1)S(1)}, bf16[192,1536]{1,0:T(8,128)(2,1)S(1)}, u32[]{:S(2)}, u32[]{:S(2)}) collective-permute-start(bf16[192,1536]{1,0:T(8,128)(2,1)S(1)} %get-tuple-element.586), channel_id=1, source_target_pairs={{0,2},{2,6},{4,0},{6,4},{1,3},{3,7},{5,1},{7,5},{8,10},{10,14},{12... | collective-permute-start | bytes 1769480 | tf_op jit(solution)/shard_map/ppermute | solution.py:56
  140.0 35.9 %collective-permute-start.23 = (bf16[384,1536]{1,0:T(8,128)(2,1)S(1)}, bf16[384,1536]{1,0:T(8,128)(2,1)}, u32[]{:S(2)}, u32[]{:S(2)}) collective-permute-start(bf16[384,1536]{1,0:T(8,128)(2,1)S(1)} %get-tuple-element.623), channel_id=1, source_target_pairs={{0,8},{8,0},{16,24},{24,16},{1,9},{9,1},{17,25},{25,17},{2,10},{10... | collective-permute-start | bytes 3538952 | tf_op jit(solution)/shard_map/ppermute | solution.py:48
  141.4 34.6 %collective-permute-start.24 = (bf16[384,1536]{1,0:T(8,128)(2,1)S(1)}, bf16[384,1536]{1,0:T(8,128)(2,1)}, u32[]{:S(2)}, u32[]{:S(2)}) collective-permute-start(bf16[384,1536]{1,0:T(8,128)(2,1)S(1)} %get-tuple-element.624), channel_id=1, source_target_pairs={{0,16},{8,24},{16,0},{24,8},{1,17},{9,25},{17,1},{25,9},{2,18},{10... | collective-permute-start | bytes 3538952 | tf_op jit(solution)/shard_map/ppermute | solution.py:48
  142.9 33.1 %collective-permute-start.22 = (bf16[256,1664]{1,0:T(8,128)(2,1)S(1)}, bf16[256,1664]{1,0:T(8,128)(2,1)S(1)}, u32[]{:S(2)}, u32[]{:S(2)}) collective-permute-start(bf16[256,1664]{1,0:T(8,128)(2,1)S(1)} %add_convert_fusion.3), channel_id=1, source_target_pairs={{0,1},{1,0},{2,3},{3,2},{4,5},{5,4},{6,7},{7,6},{8,9},{9,8},{10,11... | collective-permute-start | bytes 2555912 | tf_op jit(solution)/shard_map/ppermute | solution.py:48
  144.5 29.9 %collective-permute-start.26 = (bf16[192,1536]{1,0:T(8,128)(2,1)S(1)}, bf16[192,1536]{1,0:T(8,128)(2,1)S(1)}, u32[]{:S(2)}, u32[]{:S(2)}) collective-permute-start(bf16[192,1536]{1,0:T(8,128)(2,1)S(1)} %get-tuple-element.625), channel_id=1, source_target_pairs={{0,2},{2,6},{4,0},{6,4},{1,3},{3,7},{5,1},{7,5},{8,10},{10,14},{12... | collective-permute-start | bytes 1769480 | tf_op jit(solution)/shard_map/ppermute | solution.py:56
  200.8 53.6 %collective-permute-start.47 = (bf16[384,3072]{1,0:T(8,128)(2,1)}, bf16[384,3072]{1,0:T(8,128)(2,1)S(1)}, u32[]{:S(2)}, u32[]{:S(2)}) collective-permute-start(bf16[384,3072]{1,0:T(8,128)(2,1)} %maximum_maximum_fusion.refs_0_), channel_id=1, source_target_pairs={{0,8},{8,0},{16,24},{24,16},{1,9},{9,1},{17,25},{25,17},{2,10},{10... | collective-permute-start | bytes 7077896 | tf_op jit(solution)/shard_map/ppermute | solution.py:48
  204.2 53.8 %collective-permute-start.48 = (bf16[384,3072]{1,0:T(8,128)(2,1)}, bf16[384,3072]{1,0:T(8,128)(2,1)}, u32[]{:S(2)}, u32[]{:S(2)}) collective-permute-start(bf16[384,3072]{1,0:T(8,128)(2,1)} %maximum_maximum_fusion.refs_0_), channel_id=1, source_target_pairs={{0,16},{8,24},{16,0},{24,8},{1,17},{9,25},{17,1},{25,9},{2,18},{10... | collective-permute-start | bytes 7077896 | tf_op jit(solution)/shard_map/ppermute | solution.py:48
  259.3 29.0 %collective-permute-start.53 = (bf16[192,3072]{1,0:T(8,128)(2,1)S(1)}, bf16[192,3072]{1,0:T(8,128)(2,1)S(1)}, u32[]{:S(2)}, u32[]{:S(2)}) collective-permute-start(bf16[192,3072]{1,0:T(8,128)(2,1)S(1)} %slice.424), channel_id=1, source_target_pairs={{0,8},{8,0},{16,24},{24,16},{1,9},{9,1},{17,25},{25,17},{2,10},{10... | collective-permute-start | bytes 3538952 | tf_op jit(solution)/shard_map/ppermute | solution.py:48
  260.7 29.0 %collective-permute-start.54 = (bf16[192,3072]{1,0:T(8,128)(2,1)S(1)}, bf16[192,3072]{1,0:T(8,128)(2,1)S(1)}, u32[]{:S(2)}, u32[]{:S(2)}) collective-permute-start(bf16[192,3072]{1,0:T(8,128)(2,1)S(1)} %slice.425), channel_id=1, source_target_pairs={{0,16},{8,24},{16,0},{24,8},{1,17},{9,25},{17,1},{25,9},{2,18},{10... | collective-permute-start | bytes 3538952 | tf_op jit(solution)/shard_map/ppermute | solution.py:48
  267.7 44.3 %collective-permute-start.50 = (bf16[384,1536]{1,0:T(8,128)(2,1)S(1)}, bf16[384,1536]{1,0:T(8,128)(2,1)S(1)}, u32[]{:S(2)}, u32[]{:S(2)}) collective-permute-start(bf16[384,1536]{1,0:T(8,128)(2,1)S(1)} %pad_maximum_fusion.7.refs_0_), channel_id=1, source_target_pairs={{0,8},{8,0},{16,24},{24,16},{1,9},{9,1},{17,25},{25,17},{2,10},{10... | collective-permute-start | bytes 3538952 | tf_op jit(solution)/shard_map/ppermute | solution.py:48
  270.0 43.2 %collective-permute-start.51 = (bf16[384,1536]{1,0:T(8,128)(2,1)S(1)}, bf16[384,1536]{1,0:T(8,128)(2,1)S(1)}, u32[]{:S(2)}, u32[]{:S(2)}) collective-permute-start(bf16[384,1536]{1,0:T(8,128)(2,1)S(1)} %pad_maximum_fusion.7.refs_0_), channel_id=1, source_target_pairs={{0,16},{8,24},{16,0},{24,8},{1,17},{9,25},{17,1},{25,9},{2,18},{10... | collective-permute-start | bytes 3538952 | tf_op jit(solution)/shard_map/ppermute | solution.py:48
  271.3 41.9 %collective-permute-start.52 = (bf16[256,1536]{1,0:T(8,128)(2,1)S(1)}, bf16[256,1536]{1,0:T(8,128)(2,1)}, u32[]{:S(2)}, u32[]{:S(2)}) collective-permute-start(bf16[256,1536]{1,0:T(8,128)(2,1)S(1)} %collective-permute-done.46.refs_8_.refs_17_.g_ref), channel_id=1, source_target_pairs={{0,1},{1,0},{2,3},{3,2},{4,5},{5,4},{6,7},{7,6},{8,9},{9,8},{10,11... | collective-permute-start | bytes 2359304 | tf_op jit(solution)/shard_map/ppermute | solution.py:48
  450.1 36.4 %collective-permute-start.77 = (bf16[256,1536]{1,0:T(8,128)(2,1)S(1)}, bf16[256,1536]{1,0:T(8,128)(2,1)S(1)}, u32[]{:S(2)}, u32[]{:S(2)}) collective-permute-start(bf16[256,1536]{1,0:T(8,128)(2,1)S(1)} %copy-done.88), channel_id=1, source_target_pairs={{0,0},{2,4},{4,2},{6,6},{1,1},{3,5},{5,3},{7,7},{8,8},{10,12},{12,... | collective-permute-start | bytes 2359304 | tf_op jit(solution)/shard_map/ppermute | solution.py:52
  450.8 35.7 %collective-permute-start.75 = (bf16[15,16,384]{2,1,0:T(8,128)(2,1)S(1)}, bf16[15,16,384]{2,1,0:T(8,128)(2,1)S(1)}, u32[]{:S(2)}, u32[]{:S(2)}) collective-permute-start(bf16[15,16,384]{2,1,0:T(8,128)(2,1)S(1)} %constant_dynamic-update-slice_fusion), channel_id=1, source_target_pairs={{0,0},{2,4},{4,2},{6,6},{1,1},{3,5},{5,3},{7,7},{8,8},{10,12},{12,... | collective-permute-start | bytes 552968 | tf_op jit(solution)/shard_map/ppermute | solution.py:52
  451.5 35.0 %collective-permute-start.76 = (bf16[15,16,384]{2,1,0:T(8,128)(2,1)S(1)}, bf16[15,16,384]{2,1,0:T(8,128)(2,1)S(1)}, u32[]{:S(2)}, u32[]{:S(2)}) collective-permute-start(bf16[15,16,384]{2,1,0:T(8,128)(2,1)S(1)} %constant_dynamic-update-slice_fusion), channel_id=1, source_target_pairs={{0,4},{2,0},{4,6},{6,2},{1,5},{3,1},{5,7},{7,3},{8,12},{10,8},{12,... | collective-permute-start | bytes 552968 | tf_op jit(solution)/shard_map/ppermute | solution.py:60
  535.1 38.6 %collective-permute-start.90 = (bf16[256,1536]{1,0:T(8,128)(2,1)S(1)}, bf16[256,1536]{1,0:T(8,128)(2,1)S(1)}, u32[]{:S(2)}, u32[]{:S(2)}) collective-permute-start(bf16[256,1536]{1,0:T(8,128)(2,1)S(1)} %copy-done.23), channel_id=1, source_target_pairs={{0,0},{2,4},{4,2},{6,6},{1,1},{3,5},{5,3},{7,7},{8,8},{10,12},{12,... | collective-permute-start | bytes 2359304 | tf_op jit(solution)/shard_map/ppermute | solution.py:52
  (178 other events, 1945.8 us)

commit v6 on v5

--- a/solution.py
+++ b/solution.py
@@ -1468,13 +1468,6 @@
             own = own + f.astype(F32)
         return own
 
-    grad_keyval = step.mark(total(keyval_sums[0], keyval_far).astype(BF))
-    grad_up_keyval, *found = step.mark(
-        *context_back(
-            at_pieces, context_blocks, keyval_weight, down_context, low_context, grad_keyval
-        )
-    )
-    context_rows, grad_down_three = found[:members], found[members:]
     summed = total(first_sums[0], first_far).reshape(-1, rank, local)
     first = sent([summed, *[columns(jnp.concatenate(g, axis=1)) for g in zip(*feed_grads)]])
     block_output = home_swap(step.wait(output))
@@ -1485,6 +1478,20 @@
     )
     first, (block_output,), found = wait_all(first, [block_output], found)
     grad_down_one, grad_up_self, own_rows, *dn_blocks = found
+
+    count = pairs - 1
+    dn_others = swap_all(dn_blocks[1::2])
+    dn_sums = [group.near_sums(a, b) for a, b in zip(dn_blocks[::2], dn_others)]
+    far = move_p(listed(step.mark(*[x.astype(BF) for x in dn_sums[1:]])))
+    first = to_chips(first)
+    grad_keyval = step.mark(total(keyval_sums[0], keyval_far).astype(BF))
+    grad_up_keyval, *found = step.mark(
+        *context_back(
+            at_pieces, context_blocks, keyval_weight, down_context, low_context, grad_keyval
+        )
+    )
+    context_rows, grad_down_three = found[:members], found[members:]
+    far, first = wait_all(far, first)
 
     second_rows = listed(
         step.mark(
@@ -1498,25 +1505,20 @@
             ]
         )
     )
-    swapped = swap_all([*dn_blocks[1::2], *second_rows[1::2], *context_rows[1::2]])
-    dn_sums, second_sums, context_sums = (
+    swapped = swap_all([*second_rows[1::2], *context_rows[1::2]])
+    second_sums, context_sums = (
         [group.near_sums(a, b) for a, b in zip(own[::2], swapped[n * pairs : (n + 1) * pairs])]
-        for n, own in enumerate((dn_blocks, second_rows, context_rows))
-    )
-    moving = [x.astype(BF) for x in dn_sums[1:] + second_sums[1:] + context_sums[1:]]
+        for n, own in enumerate((second_rows, context_rows))
+    )
+    moving = [x.astype(BF) for x in second_sums[1:] + context_sums[1:]]
     moving = listed(step.mark(*moving))
-    count = pairs - 1
-    far = move_p(moving[:count])
-    second_far = move_p(listed(step.wait(*moving[count : 2 * count])))
-    context_far = move_p(listed(step.wait(*moving[2 * count :])))
-    first = to_chips(first)
-    far, second_far, context_far, first = wait_all(far, second_far, context_far, first)
-
+    second_far, context_far = move_p(moving[:count]), move_p(moving[count:])
     grad_inputs = step.mark(
         input_end(
-            stream_own, grad_stream, [dn_blocks[0], swapped[0], *far], down[0], gains[0:1]
+            stream_own, grad_stream, [dn_blocks[0], dn_others[0], *far], down[0], gains[0:1]
         )
     )
+    second_far, context_far = wait_all(second_far, context_far)
     summed = total(second_sums[0], second_far).reshape(-1, rank, local)
     second = sent(
         [
@@ -1531,13 +1533,14 @@
             summed[3:5],
         ]
     )
+    grad_context = home_swap(step.mark(total(context_sums[0], context_far).astype(BF)))
+    (second,) = wait_all(second)
+    second = to_chips(second)
     grad_inputs = home_swap(step.wait(grad_inputs))
-    grad_context = home_swap(step.mark(total(context_sums[0], context_far).astype(BF)))
-    first, labels = every(first)
+    first, labels = every(listed(step.wait(*first)))
     grad_down, grad_hidden, grad_gate = settle_first(labels, first, slots, fold)
     grad_down = step.mark(grad_down)
     (second,) = wait_all(second)
-    (second,) = wait_all(to_chips(second))
     second, labels = every(second)
     labels = labels + (step.token[0, 0].astype(F32) * 0.0).astype(jnp.int32)
     grad_down, grad_up = settle_second(labels, second, grad_down)

time: 586 us -> 576 us (0.983)
  waiting for transfers between devices: 141 us -> 133 us
    ppermute x40, waiting for transfers between devices: 95.3 us -> 86.4 us  [xor_move(): return lax.ppermute(x, axis, [(i, i ^ k) for i in range(size)])]
    unnamed x227 -> x201, local copies, waits for them, and re-layouts: 19.6 us -> 22.1 us
  transfers between devices with their start and end apart: 97 -> 97, of which waited for: 38 -> 42; matrix products, arithmetic and copies ran while one was open for 7% -> 8% of each run, Pallas kernels for 36% -> 38%
where the time goes in v6:
time: 576 us; the launch traced here: 570 us
  Pallas kernels  235 us (41%)
  waiting for transfers between devices  133 us (23%)
  starting transfers between devices  129 us (22%)
  local copies, waits for them, and re-layouts  43.3 us (8%)
  other arithmetic  24.9 us (4%)
    pallas_call x13, Pallas kernels, weight_call(): pl.pallas_call(kernel, grid_spec=pltpu.PrefetchScalarGridSpec(num_scalar_...  211 us
    ppermute x40, waiting for transfers between devices, xor_move(): return lax.ppermute(x, axis, [(i, i ^ k) for i in range(size)])  86.4 us
    ppermute x40, starting transfers between devices, xor_move(): return lax.ppermute(x, axis, [(i, i ^ k) for i in range(size)])  79.2 us
    unnamed x201, local copies, waits for them, and re-layouts  22.1 us
    ppermute x39, waiting for transfers between devices, core_swap(): return lax.ppermute(x, 'core', SWAP)  21.5 us
    ppermute x12, starting transfers between devices, home_swap(): return lax.ppermute(x, ('core', 'zhi'), [(0, 0), (1, 2), (2, 1), (3, 3)])  18.3 us
    ppermute x39, starting transfers between devices, core_swap(): return lax.ppermute(x, 'core', SWAP)  14.9 us
    ppermute x4, waiting for transfers between devices, turned(): return lax.ppermute(x, ('core', 'zhi'), [(0, 1), (1, 3), (2, 0), (3, 2)])  13.8 us
  transfers between devices with their start and end apart: 97, of which 42 were waited for; matrix products, arithmetic and copies ran while one was open for 8% of the time, Pallas kernels for 38%

profile of v6, /device:TPU:0, one launch (start us, length us, event | category | flops | bytes accessed | tf_op | source)
XLA Modules:
  0.0 569.6 jit_solution(475228687903847700)
XLA Ops:
  3.7 5.9 %collective-permute-start.2 = (bf16[192,1536]{1,0:T(8,128)(2,1)}, bf16[192,1536]{1,0:T(8,128)(2,1)}, u32[]{:S(2)}, u32[]{:S(2)}) collective-permute-start(bf16[192,1536]{1,0:T(8,128)(2,1)} %pad_maximum_fusion.9), channel_id=1, source_target_pairs={{0,0},{2,4},{4,2},{6,6},{1,1},{3,5},{5,3},{7,7},{8,8},{10,12},{12,... | collective-permute-start | bytes 1769480 | tf_op jit(solution)/shard_map/ppermute | solution.py:52
  32.0 12.4 %collective-permute-start.10 = (bf16[256,1536]{1,0:T(8,128)(2,1)}, bf16[256,1536]{1,0:T(8,128)(2,1)}, u32[]{:S(2)}, u32[]{:S(2)}) collective-permute-start(bf16[256,1536]{1,0:T(8,128)(2,1)} %collective-permute-done.6.refs_6_.refs_17_.x_ref), channel_id=1, source_target_pairs={{0,1},{1,0},{2,3},{3,2},{4,5},{5,4},{6,7},{7,6},{8,9},{9,8},{10,11... | collective-permute-start | bytes 2359304 | tf_op jit(solution)/shard_map/ppermute | solution.py:48
  44.4 22.4 %collective-permute-start.12 = (bf16[192,1536]{1,0:T(8,128)(2,1)S(1)}, bf16[192,1536]{1,0:T(8,128)(2,1)S(1)}, u32[]{:S(2)}, u32[]{:S(2)}) collective-permute-start(bf16[192,1536]{1,0:T(8,128)(2,1)S(1)} %pad_maximum_fusion.8), channel_id=1, source_target_pairs={{0,2},{2,0},{1,3},{3,1},{4,6},{6,4},{5,7},{7,5},{8,10},{10,8},{9,1... | collective-permute-start | bytes 1769480 | tf_op jit(solution)/shard_map/ppermute | solution.py:48
  71.7 21.5 %collective-permute-done.12 = bf16[192,1536]{1,0:T(8,128)(2,1)S(1)} collective-permute-done((bf16[192,1536]{1,0:T(8,128)(2,1)S(1)}, bf16[192,1536]{1,0:T(8,128)(2,1)S(1)}, u32[]{:S(2)}, u32[]{:S(2)}) %collective-permute-start.12) | collective-permute-done | bytes 589856 | tf_op jit(solution)/shard_map/ppermute | solution.py:48
  108.5 14.8 %shard_map.226 = (bf16[1024,384]{1,0:T(8,128)(2,1)}, bf16[1024,384]{1,0:T(8,128)(2,1)}, bf16[1024,384]{1,0:T(8,128)(2,1)}, bf16[1024,16]{1,0:T(8,128)(2,1)}, bf16[1024,1536]{1,0:T(8,128)(2,1)}) custom-call(s32[22]{0:T(128)} %stack.87.places_ref, bf16[384,1536]{1,0:T(8,128)(2,1)} %copy-done.13, bf16[384,1536]{1,0:T(8,128)(2,1)} %copy-done.38, ...), custom_call_target="tpu_custom_call" | custom-call | flops 4831838208 | bytes 4718592 | tf_op jit(solution)/shard_map/pallas_call | solution.py:158
  123.4 12.9 %shard_map.227 = (bf16[512,384]{1,0:T(8,128)(2,1)}, f32[8,512]{1,0:T(8,128)}, bf16[256,1664]{1,0:T(8,128)(2,1)}, bf16[256,1664]{1,0:T(8,128)(2,1)}) custom-call(s32[22]{0:T(128)} %stack.87.places_ref, bf16[384,1536]{1,0:T(8,128)(2,1)} %copy-done.13, bf16[384,1536]{1,0:T(8,128)(2,1)} %copy-done.38, bf16[384,1536]{1,0:T(8,128)(2,1)} %copy-done.39, ...), custom_call_target="tpu_custom_call" | custom-call | flops 3221225472 | bytes 3145728 | tf_op jit(solution)/shard_map/pallas_call | solution.py:158
  147.9 12.8 %shard_map.228 = (bf16[512,384]{1,0:T(8,128)(2,1)}, f32[8,512]{1,0:T(8,128)}, bf16[256,1664]{1,0:T(8,128)(2,1)}, bf16[256,1664]{1,0:T(8,128)(2,1)}) custom-call(s32[22]{0:T(128)} %stack.87.places_ref, bf16[384,1536]{1,0:T(8,128)(2,1)} %copy-done.13, bf16[384,1536]{1,0:T(8,128)(2,1)} %copy-done.38, bf16[384,1536]{1,0:T(8,128)(2,1)} %copy-done.39, ...), custom_call_target="tpu_custom_call" | custom-call | flops 3221225472 | bytes 3145728 | tf_op jit(solution)/shard_map/pallas_call | solution.py:158
  160.7 13.7 %collective-permute-done.26 = bf16[192,1536]{1,0:T(8,128)(2,1)S(1)} collective-permute-done((bf16[192,1536]{1,0:T(8,128)(2,1)S(1)}, bf16[192,1536]{1,0:T(8,128)(2,1)S(1)}, u32[]{:S(2)}, u32[]{:S(2)}) %collective-permute-start.26) | collective-permute-done | bytes 589856 | tf_op jit(solution)/shard_map/ppermute | solution.py:56
  211.8 17.9 %shard_map.230 = (f32[256,1536]{1,0:T(8,128)}, f32[256,1536]{1,0:T(8,128)}, bf16[256,1536]{1,0:T(8,128)(2,1)}, bf16[256,1536]{1,0:T(8,128)(2,1)}, bf16[256,1536]...) custom-call(s32[22]{0:T(128)} %stack.87.places_ref, ...), custom_call_target="tpu_custom_call" | custom-call | flops 14495514624 | bytes 18874368 | tf_op jit(solution)/shard_map/pallas_call | solution.py:158
  231.1 6.0 %collective-permute-start.49 = (bf16[256,1536]{1,0:T(8,128)(2,1)S(1)}, bf16[256,1536]{1,0:T(8,128)(2,1)S(1)}, u32[]{:S(2)}, u32[]{:S(2)}) collective-permute-start(bf16[256,1536]{1,0:T(8,128)(2,1)S(1)} %copy-done.72), channel_id=1, source_target_pairs={{0,4},{4,0},{1,5},{5,1},{2,6},{6,2},{3,7},{7,3},{8,12},{12,8},{9,1... | collective-permute-start | bytes 2359304 | tf_op jit(solution)/shard_map/ppermute | solution.py:44
  241.6 12.9 %collective-permute-done.47.refs_1_ = bf16[384,3072]{1,0:T(8,128)(2,1)S(1)} collective-permute-done((bf16[384,3072]{1,0:T(8,128)(2,1)}, bf16[384,3072]{1,0:T(8,128)(2,1)S(1)}, u32[]{:S(2)}, u32[]{:S(2)}) %collective-permute-start.47) | collective-permute-done | bytes 2359328 | tf_op jit(solution)/shard_map/ppermute | solution.py:48
  273.5 14.8 %collective-permute-done.53.refs_3_ = bf16[192,3072]{1,0:T(8,128)(2,1)S(1)} collective-permute-done((bf16[192,3072]{1,0:T(8,128)(2,1)S(1)}, bf16[192,3072]{1,0:T(8,128)(2,1)S(1)}, u32[]{:S(2)}, u32[]{:S(2)}) %collective-permute-start.53) | collective-permute-done | bytes 1179680 | tf_op jit(solution)/shard_map/ppermute | solution.py:48
  290.7 20.9 %shard_map.231 = (bf16[512,1552]{1,0:T(8,128)(2,1)}, bf16[512,1552]{1,0:T(8,128)(2,1)}, bf16[512,16]{1,0:T(8,128)(2,1)}, bf16[512,16]{1,0:T(8,128)(2,1)}, f32[16...) custom-call(s32[22]{0:T(128)} %stack.87.places_ref, bf16[384,3072]{1,0:T(8,128)(2,1)} %maximum_maximum_fusion.refs_0_, ...), custom_call_target="tpu_custom_call" | custom-call | flops 19528679424 | bytes 9535488 | tf_op jit(solution)/shard_map/pallas_call | solution.py:158
  316.6 20.7 %shard_map.232 = (bf16[512,1552]{1,0:T(8,128)(2,1)}, bf16[512,1552]{1,0:T(8,128)(2,1)}, bf16[512,16]{1,0:T(8,128)(2,1)}, bf16[512,16]{1,0:T(8,128)(2,1)}, f32[16...) custom-call(s32[22]{0:T(128)} %stack.87.places_ref, bf16[384,3072]{1,0:T(8,128)(2,1)} %maximum_maximum_fusion.refs_0_, ...), custom_call_target="tpu_custom_call" | custom-call | flops 19528679424 | bytes 9535488 | tf_op jit(solution)/shard_map/pallas_call | solution.py:158
  339.1 15.2 %shard_map.233 = (bf16[256,1664]{1,0:T(8,128)(2,1)}, bf16[256,1664]{1,0:T(8,128)(2,1)}, bf16[256,1664]{1,0:T(8,128)(2,1)}, bf16[256,1664]{1,0:T(8,128)(2,1)}, f3...) custom-call(s32[22]{0:T(128)} %stack.87.places_ref, bf16[384,1536]{1,0:T(8,128)(2,1)} %copy-done.14, ...), custom_call_target="tpu_custom_call" | custom-call | flops 9764339712 | bytes 4767744 | tf_op jit(solution)/shard_map/pallas_call | solution.py:158
  361.5 14.8 %shard_map.234 = (bf16[256,1664]{1,0:T(8,128)(2,1)}, bf16[256,1664]{1,0:T(8,128)(2,1)}, bf16[256,1664]{1,0:T(8,128)(2,1)}, bf16[256,1664]{1,0:T(8,128)(2,1)}, f3...) custom-call(s32[22]{0:T(128)} %stack.87.places_ref, bf16[384,1536]{1,0:T(8,128)(2,1)} %copy-done.14, ...), custom_call_target="tpu_custom_call" | custom-call | flops 9764339712 | bytes 4767744 | tf_op jit(solution)/shard_map/pallas_call | solution.py:158
  386.4 22.4 %shard_map.235 = (f32[256,1536]{1,0:T(8,128)}, bf16[256,1536]{1,0:T(8,128)(2,1)}, bf16[4,48,384]{2,1,0:T(8,128)(2,1)}, bf16[4,32,384]{2,1,0:T(8,128)(2,1)}, bf16...) custom-call(s32[22]{0:T(128)} %stack.87.places_ref, ...), custom_call_target="tpu_custom_call" | custom-call | flops 19327352832 | bytes 18874368 | tf_op jit(solution)/shard_map/pallas_call | solution.py:158
  416.6 18.2 %shard_map.236 = (bf16[512,384]{1,0:T(8,128)(2,1)}, f32[1024,384]{1,0:T(8,128)}, f32[1024,384]{1,0:T(8,128)}, f32[16,384]{1,0:T(8,128)}) custom-call(s32[22]{0:T(128)} %stack.87.places_ref, bf16[384,1536]{1,0:T(8,128)(2,1)} %copy-done.13, bf16[384,1536]{1,0:T(8,128)(2,1)} %copy-done.38, bf16[384,1536]{1,0:T(8,128)(2,1)} %copy-done.39, ...), custom_call_target="tpu_custom_call" | custom-call | flops 8053063680 | bytes 3932160 | tf_op jit(solution)/shard_map/pallas_call | solution.py:158
  451.1 29.6 %shard_map.238 = (f32[16,384]{1,0:T(8,128)}, f32[16,1152]{1,0:T(8,128)}, bf16[4,32,384]{2,1,0:T(8,128)(2,1)}, bf16[256,1664]{1,0:T(8,128)(2,1)}, bf16[256,1664]{...) custom-call(s32[22]{0:T(128)} %stack.87.places_ref, bf16[384,1536]{1,0:T(8,128)(2,1)} %copy-done.13, ...), custom_call_target="tpu_custom_call" | custom-call | flops 8053063680 | bytes 3932160 | tf_op jit(solution)/shard_map/pallas_call | solution.py:158
  489.6 5.7 shard_map.239
  498.1 5.5 collective-permute-done.82
  524.6 11.2 %collective-permute-done.91 = bf16[14,16,384]{2,0,1:T(8,128)(2,1)S(1)} collective-permute-done((bf16[14,16,384]{2,0,1:T(8,128)(2,1)S(1)}, bf16[14,16,384]{2,0,1:T(8,128)(2,1)S(1)}, u32[]{:S(2)}, u32[]{:S(2)}) %collective-permute-start.91) | collective-permute-done | bytes 172064 | tf_op jit(solution)/shard_map/ppermute | solution.py:60
  544.6 5.7 %shard_map.241 = (f32[8,6,16,384]{3,2,1,0:T(8,128)}, f32[8,16,1536]{2,1,0:T(8,128)}, f32[8,2,16,1536]{3,2,1,0:T(8,128)}) custom-call(s32[8]{0:T(128)} %fusion.39.labels_ref, bf16[8,15,16,384]{3,2,1,0:T(8,128)(2,1)} %bitcast.257), custom_call_target="tpu_custom_call" | custom-call | flops 1000 | bytes 1000 | tf_op jit(solution)/shard_map/pallas_call | solution.py:959
  561.3 5.8 %shard_map.242 = (f32[8,6,16,384]{3,2,1,0:T(8,128)}, f32[8,9,16,384]{3,2,1,0:T(8,128)}) custom-call(s32[8]{0:T(128)} %fusion.40.labels_ref, bf16[8,14,16,384]{3,2,1,0:T(8,128)(2,1)} %bitcast.259, f32[8,6,16,384]{3,2,1,0:T(8,128)} %get-tuple-element.1028.down_in), custom_call_target="tpu_custom_call", output_to_operand_aliasing={{0}: (2, {})} | custom-call | flops 1000 | bytes 1000 | tf_op jit(solution)/shard_map/pallas_call | solution.py:976
  (516 shorter events, 221.0 us)
Async XLA Ops:
  24.7 42.2 %collective-permute-start.4 = (bf16[384,1536]{1,0:T(8,128)(2,1)S(1)}, bf16[384,1536]{1,0:T(8,128)(2,1)S(1)}, u32[]{:S(2)}, u32[]{:S(2)}) collective-permute-start(bf16[384,1536]{1,0:T(8,128)(2,1)S(1)} %pad_maximum_fusion.5.refs_0_), channel_id=1, source_target_pairs={{0,8},{8,0},{16,24},{24,16},{1,9},{9,1},{17,25},{25,17},{2,10},{10... | collective-permute-start | bytes 3538952 | tf_op jit(solution)/shard_map/ppermute | solution.py:48
  27.7 39.2 %collective-permute-start.5 = (bf16[384,1536]{1,0:T(8,128)(2,1)S(1)}, bf16[384,1536]{1,0:T(8,128)(2,1)S(1)}, u32[]{:S(2)}, u32[]{:S(2)}) collective-permute-start(bf16[384,1536]{1,0:T(8,128)(2,1)S(1)} %pad_maximum_fusion.5.refs_0_), channel_id=1, source_target_pairs={{0,16},{8,24},{16,0},{24,8},{1,17},{9,25},{17,1},{25,9},{2,18},{10... | collective-permute-start | bytes 3538952 | tf_op jit(solution)/shard_map/ppermute | solution.py:48
  32.0 61.2 %collective-permute-start.10 = (bf16[256,1536]{1,0:T(8,128)(2,1)}, bf16[256,1536]{1,0:T(8,128)(2,1)}, u32[]{:S(2)}, u32[]{:S(2)}) collective-permute-start(bf16[256,1536]{1,0:T(8,128)(2,1)} %collective-permute-done.6.refs_6_.refs_17_.x_ref), channel_id=1, source_target_pairs={{0,1},{1,0},{2,3},{3,2},{4,5},{5,4},{6,7},{7,6},{8,9},{9,8},{10,11... | collective-permute-start | bytes 2359304 | tf_op jit(solution)/shard_map/ppermute | solution.py:48
  44.4 48.8 %collective-permute-start.12 = (bf16[192,1536]{1,0:T(8,128)(2,1)S(1)}, bf16[192,1536]{1,0:T(8,128)(2,1)S(1)}, u32[]{:S(2)}, u32[]{:S(2)}) collective-permute-start(bf16[192,1536]{1,0:T(8,128)(2,1)S(1)} %pad_maximum_fusion.8), channel_id=1, source_target_pairs={{0,2},{2,0},{1,3},{3,1},{4,6},{6,4},{5,7},{7,5},{8,10},{10,8},{9,1... | collective-permute-start | bytes 1769480 | tf_op jit(solution)/shard_map/ppermute | solution.py:48
  101.6 34.8 %collective-permute-start.16 = (bf16[384,1536]{1,0:T(8,128)(2,1)S(1)}, bf16[384,1536]{1,0:T(8,128)(2,1)S(1)}, u32[]{:S(2)}, u32[]{:S(2)}) collective-permute-start(bf16[384,1536]{1,0:T(8,128)(2,1)S(1)} %pad_maximum_fusion.6.refs_0_), channel_id=1, source_target_pairs={{0,8},{8,0},{16,24},{24,16},{1,9},{9,1},{17,25},{25,17},{2,10},{10... | collective-permute-start | bytes 3538952 | tf_op jit(solution)/shard_map/ppermute | solution.py:48
  102.2 34.2 %collective-permute-start.17 = (bf16[384,1536]{1,0:T(8,128)(2,1)S(1)}, bf16[384,1536]{1,0:T(8,128)(2,1)S(1)}, u32[]{:S(2)}, u32[]{:S(2)}) collective-permute-start(bf16[384,1536]{1,0:T(8,128)(2,1)S(1)} %pad_maximum_fusion.6.refs_0_), channel_id=1, source_target_pairs={{0,16},{8,24},{16,0},{24,8},{1,17},{9,25},{17,1},{25,9},{2,18},{10... | collective-permute-start | bytes 3538952 | tf_op jit(solution)/shard_map/ppermute | solution.py:48
  103.1 33.2 %collective-permute-start.18 = (bf16[192,1536]{1,0:T(8,128)(2,1)S(1)}, bf16[192,1536]{1,0:T(8,128)(2,1)S(1)}, u32[]{:S(2)}, u32[]{:S(2)}) collective-permute-start(bf16[192,1536]{1,0:T(8,128)(2,1)S(1)} %copy-done.11), channel_id=1, source_target_pairs={{0,1},{1,0},{2,3},{3,2},{4,5},{5,4},{6,7},{7,6},{8,9},{9,8},{10,11... | collective-permute-start | bytes 1769480 | tf_op jit(solution)/shard_map/ppermute | solution.py:48
  103.1 33.3 %collective-permute-start.19 = (bf16[192,1536]{1,0:T(8,128)(2,1)S(1)}, bf16[192,1536]{1,0:T(8,128)(2,1)S(1)}, u32[]{:S(2)}, u32[]{:S(2)}) collective-permute-start(bf16[192,1536]{1,0:T(8,128)(2,1)S(1)} %get-tuple-element.591), channel_id=1, source_target_pairs={{0,0},{2,4},{4,2},{6,6},{1,1},{3,5},{5,3},{7,7},{8,8},{10,12},{12,... | collective-permute-start | bytes 1769480 | tf_op jit(solution)/shard_map/ppermute | solution.py:52
  103.8 32.6 %collective-permute-start.20 = (bf16[192,1536]{1,0:T(8,128)(2,1)S(1)}, bf16[192,1536]{1,0:T(8,128)(2,1)S(1)}, u32[]{:S(2)}, u32[]{:S(2)}) collective-permute-start(bf16[192,1536]{1,0:T(8,128)(2,1)S(1)} %get-tuple-element.591), channel_id=1, source_target_pairs={{0,2},{2,6},{4,0},{6,4},{1,3},{3,7},{5,1},{7,5},{8,10},{10,14},{12... | collective-permute-start | bytes 1769480 | tf_op jit(solution)/shard_map/ppermute | solution.py:56
  140.1 35.9 %collective-permute-start.23 = (bf16[384,1536]{1,0:T(8,128)(2,1)S(1)}, bf16[384,1536]{1,0:T(8,128)(2,1)}, u32[]{:S(2)}, u32[]{:S(2)}) collective-permute-start(bf16[384,1536]{1,0:T(8,128)(2,1)S(1)} %get-tuple-element.628), channel_id=1, source_target_pairs={{0,8},{8,0},{16,24},{24,16},{1,9},{9,1},{17,25},{25,17},{2,10},{10... | collective-permute-start | bytes 3538952 | tf_op jit(solution)/shard_map/ppermute | solution.py:48
  141.4 34.6 %collective-permute-start.24 = (bf16[384,1536]{1,0:T(8,128)(2,1)S(1)}, bf16[384,1536]{1,0:T(8,128)(2,1)}, u32[]{:S(2)}, u32[]{:S(2)}) collective-permute-start(bf16[384,1536]{1,0:T(8,128)(2,1)S(1)} %get-tuple-element.629), channel_id=1, source_target_pairs={{0,16},{8,24},{16,0},{24,8},{1,17},{9,25},{17,1},{25,9},{2,18},{10... | collective-permute-start | bytes 3538952 | tf_op jit(solution)/shard_map/ppermute | solution.py:48
  142.9 33.1 %collective-permute-start.22 = (bf16[256,1664]{1,0:T(8,128)(2,1)S(1)}, bf16[256,1664]{1,0:T(8,128)(2,1)S(1)}, u32[]{:S(2)}, u32[]{:S(2)}) collective-permute-start(bf16[256,1664]{1,0:T(8,128)(2,1)S(1)} %add_convert_fusion.3), channel_id=1, source_target_pairs={{0,1},{1,0},{2,3},{3,2},{4,5},{5,4},{6,7},{7,6},{8,9},{9,8},{10,11... | collective-permute-start | bytes 2555912 | tf_op jit(solution)/shard_map/ppermute | solution.py:48
  144.6 29.9 %collective-permute-start.26 = (bf16[192,1536]{1,0:T(8,128)(2,1)S(1)}, bf16[192,1536]{1,0:T(8,128)(2,1)S(1)}, u32[]{:S(2)}, u32[]{:S(2)}) collective-permute-start(bf16[192,1536]{1,0:T(8,128)(2,1)S(1)} %get-tuple-element.630), channel_id=1, source_target_pairs={{0,2},{2,6},{4,0},{6,4},{1,3},{3,7},{5,1},{7,5},{8,10},{10,14},{12... | collective-permute-start | bytes 1769480 | tf_op jit(solution)/shard_map/ppermute | solution.py:56
  200.8 53.7 %collective-permute-start.47 = (bf16[384,3072]{1,0:T(8,128)(2,1)}, bf16[384,3072]{1,0:T(8,128)(2,1)S(1)}, u32[]{:S(2)}, u32[]{:S(2)}) collective-permute-start(bf16[384,3072]{1,0:T(8,128)(2,1)} %maximum_maximum_fusion.refs_0_), channel_id=1, source_target_pairs={{0,8},{8,0},{16,24},{24,16},{1,9},{9,1},{17,25},{25,17},{2,10},{10... | collective-permute-start | bytes 7077896 | tf_op jit(solution)/shard_map/ppermute | solution.py:48
  204.2 53.8 %collective-permute-start.48 = (bf16[384,3072]{1,0:T(8,128)(2,1)}, bf16[384,3072]{1,0:T(8,128)(2,1)}, u32[]{:S(2)}, u32[]{:S(2)}) collective-permute-start(bf16[384,3072]{1,0:T(8,128)(2,1)} %maximum_maximum_fusion.refs_0_), channel_id=1, source_target_pairs={{0,16},{8,24},{16,0},{24,8},{1,17},{9,25},{17,1},{25,9},{2,18},{10... | collective-permute-start | bytes 7077896 | tf_op jit(solution)/shard_map/ppermute | solution.py:48
  259.3 29.0 %collective-permute-start.53 = (bf16[192,3072]{1,0:T(8,128)(2,1)S(1)}, bf16[192,3072]{1,0:T(8,128)(2,1)S(1)}, u32[]{:S(2)}, u32[]{:S(2)}) collective-permute-start(bf16[192,3072]{1,0:T(8,128)(2,1)S(1)} %slice.424), channel_id=1, source_target_pairs={{0,8},{8,0},{16,24},{24,16},{1,9},{9,1},{17,25},{25,17},{2,10},{10... | collective-permute-start | bytes 3538952 | tf_op jit(solution)/shard_map/ppermute | solution.py:48
  260.7 29.0 %collective-permute-start.54 = (bf16[192,3072]{1,0:T(8,128)(2,1)S(1)}, bf16[192,3072]{1,0:T(8,128)(2,1)S(1)}, u32[]{:S(2)}, u32[]{:S(2)}) collective-permute-start(bf16[192,3072]{1,0:T(8,128)(2,1)S(1)} %slice.425), channel_id=1, source_target_pairs={{0,16},{8,24},{16,0},{24,8},{1,17},{9,25},{17,1},{25,9},{2,18},{10... | collective-permute-start | bytes 3538952 | tf_op jit(solution)/shard_map/ppermute | solution.py:48
  267.7 44.3 %collective-permute-start.50 = (bf16[384,1536]{1,0:T(8,128)(2,1)S(1)}, bf16[384,1536]{1,0:T(8,128)(2,1)S(1)}, u32[]{:S(2)}, u32[]{:S(2)}) collective-permute-start(bf16[384,1536]{1,0:T(8,128)(2,1)S(1)} %pad_maximum_fusion.7.refs_0_), channel_id=1, source_target_pairs={{0,8},{8,0},{16,24},{24,16},{1,9},{9,1},{17,25},{25,17},{2,10},{10... | collective-permute-start | bytes 3538952 | tf_op jit(solution)/shard_map/ppermute | solution.py:48
  270.0 43.2 %collective-permute-start.51 = (bf16[384,1536]{1,0:T(8,128)(2,1)S(1)}, bf16[384,1536]{1,0:T(8,128)(2,1)S(1)}, u32[]{:S(2)}, u32[]{:S(2)}) collective-permute-start(bf16[384,1536]{1,0:T(8,128)(2,1)S(1)} %pad_maximum_fusion.7.refs_0_), channel_id=1, source_target_pairs={{0,16},{8,24},{16,0},{24,8},{1,17},{9,25},{17,1},{25,9},{2,18},{10... | collective-permute-start | bytes 3538952 | tf_op jit(solution)/shard_map/ppermute | solution.py:48
  271.3 41.9 %collective-permute-start.52 = (bf16[256,1536]{1,0:T(8,128)(2,1)S(1)}, bf16[256,1536]{1,0:T(8,128)(2,1)}, u32[]{:S(2)}, u32[]{:S(2)}) collective-permute-start(bf16[256,1536]{1,0:T(8,128)(2,1)S(1)} %collective-permute-done.46.refs_8_.refs_17_.g_ref), channel_id=1, source_target_pairs={{0,1},{1,0},{2,3},{3,2},{4,5},{5,4},{6,7},{7,6},{8,9},{9,8},{10,11... | collective-permute-start | bytes 2359304 | tf_op jit(solution)/shard_map/ppermute | solution.py:48
  444.4 36.3 %collective-permute-start.77 = (bf16[256,1536]{1,0:T(8,128)(2,1)}, bf16[256,1536]{1,0:T(8,128)(2,1)S(1)}, u32[]{:S(2)}, u32[]{:S(2)}) collective-permute-start(bf16[256,1536]{1,0:T(8,128)(2,1)} %get-tuple-element.907), channel_id=1, source_target_pairs={{0,0},{2,4},{4,2},{6,6},{1,1},{3,5},{5,3},{7,7},{8,8},{10,12},{12,... | collective-permute-start | bytes 2359304 | tf_op jit(solution)/shard_map/ppermute | solution.py:52
  446.2 34.5 %collective-permute-start.75 = (bf16[15,16,384]{2,1,0:T(8,128)(2,1)S(1)}, bf16[15,16,384]{2,1,0:T(8,128)(2,1)S(1)}, u32[]{:S(2)}, u32[]{:S(2)}) collective-permute-start(bf16[15,16,384]{2,1,0:T(8,128)(2,1)S(1)} %constant_dynamic-update-slice_fusion), channel_id=1, source_target_pairs={{0,0},{2,4},{4,2},{6,6},{1,1},{3,5},{5,3},{7,7},{8,8},{10,12},{12,... | collective-permute-start | bytes 552968 | tf_op jit(solution)/shard_map/ppermute | solution.py:52
  446.9 33.9 %collective-permute-start.76 = (bf16[15,16,384]{2,1,0:T(8,128)(2,1)S(1)}, bf16[15,16,384]{2,1,0:T(8,128)(2,1)S(1)}, u32[]{:S(2)}, u32[]{:S(2)}) collective-permute-start(bf16[15,16,384]{2,1,0:T(8,128)(2,1)S(1)} %constant_dynamic-update-slice_fusion), channel_id=1, source_target_pairs={{0,4},{2,0},{4,6},{6,2},{1,5},{3,1},{5,7},{7,3},{8,12},{10,8},{12,... | collective-permute-start | bytes 552968 | tf_op jit(solution)/shard_map/ppermute | solution.py:60
  535.9 31.2 %collective-permute-start.92 = (bf16[256,1536]{1,0:T(8,128)(2,1)}, bf16[256,1536]{1,0:T(8,128)(2,1)S(1)}, u32[]{:S(2)}, u32[]{:S(2)}) collective-permute-start(bf16[256,1536]{1,0:T(8,128)(2,1)} %shard_map.240), channel_id=1, source_target_pairs={{0,0},{2,4},{4,2},{6,6},{1,1},{3,5},{5,3},{7,7},{8,8},{10,12},{12,... | collective-permute-start | bytes 2359304 | tf_op jit(solution)/shard_map/ppermute | solution.py:52
  (165 other events, 1788.5 us)

commit v7 on v6

--- a/solution.py
+++ b/solution.py
@@ -1175,7 +1175,13 @@
     rest_self, stream_far, context_far, (far_cross,) = wait_all(
         rest_self, stream_far, context_far, [far_cross]
     )
-    stream_other, *stream_far_other = swap_all([stream_own, *stream_far])
+    stream_other, context_other, *found = swap_all(
+        [stream_own, context_own, *stream_far, *context_far]
+    )
+    stream_far_other, swapped = found[: pairs - 1], found[pairs - 1 :]
+    context_blocks = [context_own, context_other]
+    for far, far_other in zip(context_far, swapped):
+        context_blocks += [far, far_other]
     stream = [stream_own, stream_other]
     for far, far_other in zip(stream_far, stream_far_other):
         stream += [far, far_other]
@@ -1247,12 +1253,7 @@
         step.wait(query), keys, values, self_weight, tile, 0, near_tiles, rows
     )
     y_rows = listed(step.mark(*y_rows))
-    far, got_two, feed_two = wait_all(far, got_two, feed_two)
-    y_other, context_other, *swapped = swap_all([y_rows[1], context_own, *context_far])
-    branch = [y_rows[0], y_other, *far]
-    context_blocks = [context_own, context_other]
-    for far, far_other in zip(context_far, swapped):
-        context_blocks += [far, far_other]
+    (got_two,) = wait_all(got_two)
     keyval_weight = chip_weight(
         (ready_keyval, 0), [(g, 0) for g in got_one],
         [(g, 0) for g in got_two] if chips == 4 else [], low_keyval, 2 * local, packed_halves,
@@ -1261,6 +1262,9 @@
     keyval, low_context = context_forward(at_pieces, context_blocks, keyval_weight, down_context)
     keyval = step.mark(keyval)
 
+    far, feed_two = wait_all(far, feed_two)
+    (y_other,) = swap_all([y_rows[1]])
+    branch = [y_rows[0], y_other, *far]
     keyval_far = group.far_p(keyval)
     ready_feed = [step.mark(stacked(*[packed(*two) for two in zip(feed_one, feed_two)]))]
     found = [(ready_keyval, block, block, 0, 0, 0)]

time: 576 us -> 571 us (level)
    ppermute x4, waiting for transfers between devices: 13.8 us -> 0.01 us  [turned(): return lax.ppermute(x, ('core', 'zhi'), [(0, 1), (1, 3), (2, 0), (3, 2)])]
    ppermute x40, waiting for transfers between devices: 86.4 us -> 97.3 us  [xor_move(): return lax.ppermute(x, axis, [(i, i ^ k) for i in range(size)])]
    unnamed x201 -> x207, local copies, waits for them, and re-layouts: 22.1 us -> 21.9 us
  transfers between devices with their start and end apart: 97 -> 97, of which waited for: 42 -> 41; matrix products, arithmetic and copies ran while one was open for 8% -> 8% of each run, Pallas kernels for 38% -> 38%
where the time goes in v7:
time: 571 us; the launch traced here: 564 us
  Pallas kernels  234 us (41%)
  waiting for transfers between devices  131 us (23%)
  starting transfers between devices  127 us (22%)
  local copies, waits for them, and re-layouts  42.7 us (7%)
  other arithmetic  24.9 us (4%)
    pallas_call x13, Pallas kernels, weight_call(): pl.pallas_call(kernel, grid_spec=pltpu.PrefetchScalarGridSpec(num_scalar_...  211 us
    ppermute x40, waiting for transfers between devices, xor_move(): return lax.ppermute(x, axis, [(i, i ^ k) for i in range(size)])  97.3 us
    ppermute x40, starting transfers between devices, xor_move(): return lax.ppermute(x, axis, [(i, i ^ k) for i in range(size)])  76.1 us
    ppermute x39, waiting for transfers between devices, core_swap(): return lax.ppermute(x, 'core', SWAP)  22.8 us
    unnamed x207, local copies, waits for them, and re-layouts  21.9 us
    ppermute x12, starting transfers between devices, home_swap(): return lax.ppermute(x, ('core', 'zhi'), [(0, 0), (1, 2), (2, 1), (3, 3)])  19.3 us
    ppermute x39, starting transfers between devices, core_swap(): return lax.ppermute(x, 'core', SWAP)  16.1 us
  transfers between devices with their start and end apart: 97, of which 41 were waited for; matrix products, arithmetic and copies ran while one was open for 8% of the time, Pallas kernels for 38%

profile of v7, /device:TPU:0, one launch (start us, length us, event | category | flops | bytes accessed | tf_op | source)
XLA Modules:
  0.0 564.2 jit_solution(10443354840084876829)
XLA Ops:
  3.7 6.0 %collective-permute-start.2 = (bf16[192,1536]{1,0:T(8,128)(2,1)}, bf16[192,1536]{1,0:T(8,128)(2,1)}, u32[]{:S(2)}, u32[]{:S(2)}) collective-permute-start(bf16[192,1536]{1,0:T(8,128)(2,1)} %pad_maximum_fusion.9), channel_id=1, source_target_pairs={{0,0},{2,4},{4,2},{6,6},{1,1},{3,5},{5,3},{7,7},{8,8},{10,12},{12,... | collective-permute-start | bytes 1769480 | tf_op jit(solution)/shard_map/ppermute | solution.py:52
  32.1 12.4 %collective-permute-start.10 = (bf16[256,1536]{1,0:T(8,128)(2,1)}, bf16[256,1536]{1,0:T(8,128)(2,1)}, u32[]{:S(2)}, u32[]{:S(2)}) collective-permute-start(bf16[256,1536]{1,0:T(8,128)(2,1)} %collective-permute-done.6.refs_6_.refs_17_.x_ref), channel_id=1, source_target_pairs={{0,1},{1,0},{2,3},{3,2},{4,5},{5,4},{6,7},{7,6},{8,9},{9,8},{10,11... | collective-permute-start | bytes 2359304 | tf_op jit(solution)/shard_map/ppermute | solution.py:48
  44.4 22.4 %collective-permute-start.12 = (bf16[192,1536]{1,0:T(8,128)(2,1)S(1)}, bf16[192,1536]{1,0:T(8,128)(2,1)S(1)}, u32[]{:S(2)}, u32[]{:S(2)}) collective-permute-start(bf16[192,1536]{1,0:T(8,128)(2,1)S(1)} %pad_maximum_fusion.8), channel_id=1, source_target_pairs={{0,2},{2,0},{1,3},{3,1},{4,6},{6,4},{5,7},{7,5},{8,10},{10,8},{9,1... | collective-permute-start | bytes 1769480 | tf_op jit(solution)/shard_map/ppermute | solution.py:48
  71.7 21.5 %collective-permute-done.12 = bf16[192,1536]{1,0:T(8,128)(2,1)S(1)} collective-permute-done((bf16[192,1536]{1,0:T(8,128)(2,1)S(1)}, bf16[192,1536]{1,0:T(8,128)(2,1)S(1)}, u32[]{:S(2)}, u32[]{:S(2)}) %collective-permute-start.12) | collective-permute-done | bytes 589856 | tf_op jit(solution)/shard_map/ppermute | solution.py:48
  109.7 14.9 %shard_map.226 = (bf16[1024,384]{1,0:T(8,128)(2,1)}, bf16[1024,384]{1,0:T(8,128)(2,1)}, bf16[1024,384]{1,0:T(8,128)(2,1)}, bf16[1024,16]{1,0:T(8,128)(2,1)}, bf16[1024,1536]{1,0:T(8,128)(2,1)}) custom-call(s32[22]{0:T(128)} %stack.87.places_ref, bf16[384,1536]{1,0:T(8,128)(2,1)} %copy-done.13, bf16[384,1536]{1,0:T(8,128)(2,1)} %copy-done.37, ...), custom_call_target="tpu_custom_call" | custom-call | flops 4831838208 | bytes 4718592 | tf_op jit(solution)/shard_map/pallas_call | solution.py:158
  124.6 12.9 %shard_map.227 = (bf16[512,384]{1,0:T(8,128)(2,1)}, f32[8,512]{1,0:T(8,128)}, bf16[256,1664]{1,0:T(8,128)(2,1)}, bf16[256,1664]{1,0:T(8,128)(2,1)}) custom-call(s32[22]{0:T(128)} %stack.87.places_ref, bf16[384,1536]{1,0:T(8,128)(2,1)} %copy-done.13, bf16[384,1536]{1,0:T(8,128)(2,1)} %copy-done.37, bf16[384,1536]{1,0:T(8,128)(2,1)} %copy-done.38, ...), custom_call_target="tpu_custom_call" | custom-call | flops 3221225472 | bytes 3145728 | tf_op jit(solution)/shard_map/pallas_call | solution.py:158
  149.2 12.8 %shard_map.228 = (bf16[512,384]{1,0:T(8,128)(2,1)}, f32[8,512]{1,0:T(8,128)}, bf16[256,1664]{1,0:T(8,128)(2,1)}, bf16[256,1664]{1,0:T(8,128)(2,1)}) custom-call(s32[22]{0:T(128)} %stack.87.places_ref, bf16[384,1536]{1,0:T(8,128)(2,1)} %copy-done.13, bf16[384,1536]{1,0:T(8,128)(2,1)} %copy-done.37, bf16[384,1536]{1,0:T(8,128)(2,1)} %copy-done.38, ...), custom_call_target="tpu_custom_call" | custom-call | flops 3221225472 | bytes 3145728 | tf_op jit(solution)/shard_map/pallas_call | solution.py:158
  162.1 7.3 %collective-permute-done.24.refs_3_.refs_12_ = bf16[384,1536]{1,0:T(8,128)(2,1)} collective-permute-done((bf16[384,1536]{1,0:T(8,128)(2,1)S(1)}, bf16[384,1536]{1,0:T(8,128)(2,1)}, u32[]{:S(2)}, u32[]{:S(2)}) %collective-permute-start.24) | collective-permute-done | bytes 1179680 | tf_op jit(solution)/shard_map/ppermute | solution.py:48
  206.8 17.9 %shard_map.230 = (f32[256,1536]{1,0:T(8,128)}, f32[256,1536]{1,0:T(8,128)}, bf16[256,1536]{1,0:T(8,128)(2,1)}, bf16[256,1536]{1,0:T(8,128)(2,1)}, bf16[256,1536]...) custom-call(s32[22]{0:T(128)} %stack.87.places_ref, ...), custom_call_target="tpu_custom_call" | custom-call | flops 14495514624 | bytes 18874368 | tf_op jit(solution)/shard_map/pallas_call | solution.py:158
  226.0 7.1 %collective-permute-start.49 = (bf16[256,1536]{1,0:T(8,128)(2,1)S(1)}, bf16[256,1536]{1,0:T(8,128)(2,1)S(1)}, u32[]{:S(2)}, u32[]{:S(2)}) collective-permute-start(bf16[256,1536]{1,0:T(8,128)(2,1)S(1)} %copy-done.73), channel_id=1, source_target_pairs={{0,4},{4,0},{1,5},{5,1},{2,6},{6,2},{3,7},{7,3},{8,12},{12,8},{9,1... | collective-permute-start | bytes 2359304 | tf_op jit(solution)/shard_map/ppermute | solution.py:44
  237.4 13.4 %collective-permute-done.47.refs_1_ = bf16[384,3072]{1,0:T(8,128)(2,1)S(1)} collective-permute-done((bf16[384,3072]{1,0:T(8,128)(2,1)}, bf16[384,3072]{1,0:T(8,128)(2,1)S(1)}, u32[]{:S(2)}, u32[]{:S(2)}) %collective-permute-start.47) | collective-permute-done | bytes 2359328 | tf_op jit(solution)/shard_map/ppermute | solution.py:48
  269.3 15.3 %collective-permute-done.53.refs_3_ = bf16[192,3072]{1,0:T(8,128)(2,1)S(1)} collective-permute-done((bf16[192,3072]{1,0:T(8,128)(2,1)S(1)}, bf16[192,3072]{1,0:T(8,128)(2,1)S(1)}, u32[]{:S(2)}, u32[]{:S(2)}) %collective-permute-start.53) | collective-permute-done | bytes 1179680 | tf_op jit(solution)/shard_map/ppermute | solution.py:48
  287.3 20.9 %shard_map.231 = (bf16[512,1552]{1,0:T(8,128)(2,1)}, bf16[512,1552]{1,0:T(8,128)(2,1)}, bf16[512,16]{1,0:T(8,128)(2,1)}, bf16[512,16]{1,0:T(8,128)(2,1)}, f32[16...) custom-call(s32[22]{0:T(128)} %stack.87.places_ref, bf16[384,3072]{1,0:T(8,128)(2,1)} %maximum_maximum_fusion.refs_0_, ...), custom_call_target="tpu_custom_call" | custom-call | flops 19528679424 | bytes 9535488 | tf_op jit(solution)/shard_map/pallas_call | solution.py:158
  313.0 20.7 %shard_map.232 = (bf16[512,1552]{1,0:T(8,128)(2,1)}, bf16[512,1552]{1,0:T(8,128)(2,1)}, bf16[512,16]{1,0:T(8,128)(2,1)}, bf16[512,16]{1,0:T(8,128)(2,1)}, f32[16...) custom-call(s32[22]{0:T(128)} %stack.87.places_ref, bf16[384,3072]{1,0:T(8,128)(2,1)} %maximum_maximum_fusion.refs_0_, ...), custom_call_target="tpu_custom_call" | custom-call | flops 19528679424 | bytes 9535488 | tf_op jit(solution)/shard_map/pallas_call | solution.py:158
  335.4 15.2 %shard_map.233 = (bf16[256,1664]{1,0:T(8,128)(2,1)}, bf16[256,1664]{1,0:T(8,128)(2,1)}, bf16[256,1664]{1,0:T(8,128)(2,1)}, bf16[256,1664]{1,0:T(8,128)(2,1)}, f3...) custom-call(s32[22]{0:T(128)} %stack.87.places_ref, bf16[384,1536]{1,0:T(8,128)(2,1)} %copy-done.14, ...), custom_call_target="tpu_custom_call" | custom-call | flops 9764339712 | bytes 4767744 | tf_op jit(solution)/shard_map/pallas_call | solution.py:158
  356.5 14.8 %shard_map.234 = (bf16[256,1664]{1,0:T(8,128)(2,1)}, bf16[256,1664]{1,0:T(8,128)(2,1)}, bf16[256,1664]{1,0:T(8,128)(2,1)}, bf16[256,1664]{1,0:T(8,128)(2,1)}, f3...) custom-call(s32[22]{0:T(128)} %stack.87.places_ref, bf16[384,1536]{1,0:T(8,128)(2,1)} %copy-done.14, ...), custom_call_target="tpu_custom_call" | custom-call | flops 9764339712 | bytes 4767744 | tf_op jit(solution)/shard_map/pallas_call | solution.py:158
  371.3 5.9 %collective-permute-done.62.refs_37_ = bf16[256,1664]{1,0:T(8,128)(2,1)S(1)} collective-permute-done((bf16[256,1664]{1,0:T(8,128)(2,1)S(1)}, bf16[256,1664]{1,0:T(8,128)(2,1)S(1)}, u32[]{:S(2)}, u32[]{:S(2)}) %collective-permute-start.62) | collective-permute-done | bytes 852000 | tf_op jit(solution)/shard_map/ppermute | solution.py:48
  381.3 22.4 %shard_map.235 = (f32[256,1536]{1,0:T(8,128)}, bf16[256,1536]{1,0:T(8,128)(2,1)}, bf16[4,48,384]{2,1,0:T(8,128)(2,1)}, bf16[4,32,384]{2,1,0:T(8,128)(2,1)}, bf16...) custom-call(s32[22]{0:T(128)} %stack.87.places_ref, ...), custom_call_target="tpu_custom_call" | custom-call | flops 19327352832 | bytes 18874368 | tf_op jit(solution)/shard_map/pallas_call | solution.py:158
  412.4 18.2 %shard_map.236 = (bf16[512,384]{1,0:T(8,128)(2,1)}, f32[1024,384]{1,0:T(8,128)}, f32[1024,384]{1,0:T(8,128)}, f32[16,384]{1,0:T(8,128)}) custom-call(s32[22]{0:T(128)} %stack.87.places_ref, bf16[384,1536]{1,0:T(8,128)(2,1)} %copy-done.13, bf16[384,1536]{1,0:T(8,128)(2,1)} %copy-done.37, bf16[384,1536]{1,0:T(8,128)(2,1)} %copy-done.38, ...), custom_call_target="tpu_custom_call" | custom-call | flops 8053063680 | bytes 3932160 | tf_op jit(solution)/shard_map/pallas_call | solution.py:158
  446.1 29.6 %shard_map.238 = (f32[16,384]{1,0:T(8,128)}, f32[16,1152]{1,0:T(8,128)}, bf16[4,32,384]{2,1,0:T(8,128)(2,1)}, bf16[256,1664]{1,0:T(8,128)(2,1)}, bf16[256,1664]{...) custom-call(s32[22]{0:T(128)} %stack.87.places_ref, bf16[384,1536]{1,0:T(8,128)(2,1)} %copy-done.13, ...), custom_call_target="tpu_custom_call" | custom-call | flops 8053063680 | bytes 3932160 | tf_op jit(solution)/shard_map/pallas_call | solution.py:158
  485.9 5.7 %shard_map.239 = (f32[16,768]{1,0:T(8,128)}, bf16[130,384]{1,0:T(8,128)(2,1)}, bf16[130,384]{1,0:T(8,128)(2,1)}, bf16[130,384]{1,0:T(8,128)(2,1)}, bf16[130,384]...) custom-call(s32[22]{0:T(128)} %stack.87.places_ref, ...), custom_call_target="tpu_custom_call" | custom-call | flops 10000000000 | bytes 1000000 | tf_op jit(solution)/shard_map/pallas_call | solution.py:158
  520.2 10.7 %collective-permute-done.91 = bf16[14,16,384]{2,0,1:T(8,128)(2,1)S(1)} collective-permute-done((bf16[14,16,384]{2,0,1:T(8,128)(2,1)S(1)}, bf16[14,16,384]{2,0,1:T(8,128)(2,1)S(1)}, u32[]{:S(2)}, u32[]{:S(2)}) %collective-permute-start.91) | collective-permute-done | bytes 172064 | tf_op jit(solution)/shard_map/ppermute | solution.py:60
  539.7 5.7 %shard_map.241 = (f32[8,6,16,384]{3,2,1,0:T(8,128)}, f32[8,16,1536]{2,1,0:T(8,128)}, f32[8,2,16,1536]{3,2,1,0:T(8,128)}) custom-call(s32[8]{0:T(128)} %fusion.39.labels_ref, bf16[8,15,16,384]{3,2,1,0:T(8,128)(2,1)} %bitcast.257), custom_call_target="tpu_custom_call" | custom-call | flops 1000 | bytes 1000 | tf_op jit(solution)/shard_map/pallas_call | solution.py:959
  555.9 5.8 %shard_map.242 = (f32[8,6,16,384]{3,2,1,0:T(8,128)}, f32[8,9,16,384]{3,2,1,0:T(8,128)}) custom-call(s32[8]{0:T(128)} %fusion.40.labels_ref, bf16[8,14,16,384]{3,2,1,0:T(8,128)(2,1)} %bitcast.259, f32[8,6,16,384]{3,2,1,0:T(8,128)} %get-tuple-element.1030.down_in), custom_call_target="tpu_custom_call", output_to_operand_aliasing={{0}: (2, {})} | custom-call | flops 1000 | bytes 1000 | tf_op jit(solution)/shard_map/pallas_call | solution.py:976
  (522 shorter events, 219.9 us)
Async XLA Ops:
  24.7 42.1 %collective-permute-start.4 = (bf16[384,1536]{1,0:T(8,128)(2,1)S(1)}, bf16[384,1536]{1,0:T(8,128)(2,1)S(1)}, u32[]{:S(2)}, u32[]{:S(2)}) collective-permute-start(bf16[384,1536]{1,0:T(8,128)(2,1)S(1)} %pad_maximum_fusion.5.refs_0_), channel_id=1, source_target_pairs={{0,8},{8,0},{16,24},{24,16},{1,9},{9,1},{17,25},{25,17},{2,10},{10... | collective-permute-start | bytes 3538952 | tf_op jit(solution)/shard_map/ppermute | solution.py:48
  27.7 39.1 %collective-permute-start.5 = (bf16[384,1536]{1,0:T(8,128)(2,1)S(1)}, bf16[384,1536]{1,0:T(8,128)(2,1)S(1)}, u32[]{:S(2)}, u32[]{:S(2)}) collective-permute-start(bf16[384,1536]{1,0:T(8,128)(2,1)S(1)} %pad_maximum_fusion.5.refs_0_), channel_id=1, source_target_pairs={{0,16},{8,24},{16,0},{24,8},{1,17},{9,25},{17,1},{25,9},{2,18},{10... | collective-permute-start | bytes 3538952 | tf_op jit(solution)/shard_map/ppermute | solution.py:48
  32.1 61.1 %collective-permute-start.10 = (bf16[256,1536]{1,0:T(8,128)(2,1)}, bf16[256,1536]{1,0:T(8,128)(2,1)}, u32[]{:S(2)}, u32[]{:S(2)}) collective-permute-start(bf16[256,1536]{1,0:T(8,128)(2,1)} %collective-permute-done.6.refs_6_.refs_17_.x_ref), channel_id=1, source_target_pairs={{0,1},{1,0},{2,3},{3,2},{4,5},{5,4},{6,7},{7,6},{8,9},{9,8},{10,11... | collective-permute-start | bytes 2359304 | tf_op jit(solution)/shard_map/ppermute | solution.py:48
  44.4 48.8 %collective-permute-start.12 = (bf16[192,1536]{1,0:T(8,128)(2,1)S(1)}, bf16[192,1536]{1,0:T(8,128)(2,1)S(1)}, u32[]{:S(2)}, u32[]{:S(2)}) collective-permute-start(bf16[192,1536]{1,0:T(8,128)(2,1)S(1)} %pad_maximum_fusion.8), channel_id=1, source_target_pairs={{0,2},{2,0},{1,3},{3,1},{4,6},{6,4},{5,7},{7,5},{8,10},{10,8},{9,1... | collective-permute-start | bytes 1769480 | tf_op jit(solution)/shard_map/ppermute | solution.py:48
  102.2 35.4 %collective-permute-start.18 = (bf16[384,1536]{1,0:T(8,128)(2,1)S(1)}, bf16[384,1536]{1,0:T(8,128)(2,1)S(1)}, u32[]{:S(2)}, u32[]{:S(2)}) collective-permute-start(bf16[384,1536]{1,0:T(8,128)(2,1)S(1)} %pad_maximum_fusion.6.refs_0_), channel_id=1, source_target_pairs={{0,8},{8,0},{16,24},{24,16},{1,9},{9,1},{17,25},{25,17},{2,10},{10... | collective-permute-start | bytes 3538952 | tf_op jit(solution)/shard_map/ppermute | solution.py:48
  102.8 34.8 %collective-permute-start.19 = (bf16[384,1536]{1,0:T(8,128)(2,1)S(1)}, bf16[384,1536]{1,0:T(8,128)(2,1)S(1)}, u32[]{:S(2)}, u32[]{:S(2)}) collective-permute-start(bf16[384,1536]{1,0:T(8,128)(2,1)S(1)} %pad_maximum_fusion.6.refs_0_), channel_id=1, source_target_pairs={{0,16},{8,24},{16,0},{24,8},{1,17},{9,25},{17,1},{25,9},{2,18},{10... | collective-permute-start | bytes 3538952 | tf_op jit(solution)/shard_map/ppermute | solution.py:48
  104.2 33.3 %collective-permute-start.20 = (bf16[192,1536]{1,0:T(8,128)(2,1)S(1)}, bf16[192,1536]{1,0:T(8,128)(2,1)S(1)}, u32[]{:S(2)}, u32[]{:S(2)}) collective-permute-start(bf16[192,1536]{1,0:T(8,128)(2,1)S(1)} %copy-done.11), channel_id=1, source_target_pairs={{0,1},{1,0},{2,3},{3,2},{4,5},{5,4},{6,7},{7,6},{8,9},{9,8},{10,11... | collective-permute-start | bytes 1769480 | tf_op jit(solution)/shard_map/ppermute | solution.py:48
  104.2 33.3 %collective-permute-start.21 = (bf16[192,1536]{1,0:T(8,128)(2,1)S(1)}, bf16[192,1536]{1,0:T(8,128)(2,1)S(1)}, u32[]{:S(2)}, u32[]{:S(2)}) collective-permute-start(bf16[192,1536]{1,0:T(8,128)(2,1)S(1)} %get-tuple-element.595), channel_id=1, source_target_pairs={{0,0},{2,4},{4,2},{6,6},{1,1},{3,5},{5,3},{7,7},{8,8},{10,12},{12,... | collective-permute-start | bytes 1769480 | tf_op jit(solution)/shard_map/ppermute | solution.py:52
  104.9 32.6 %collective-permute-start.22 = (bf16[192,1536]{1,0:T(8,128)(2,1)S(1)}, bf16[192,1536]{1,0:T(8,128)(2,1)S(1)}, u32[]{:S(2)}, u32[]{:S(2)}) collective-permute-start(bf16[192,1536]{1,0:T(8,128)(2,1)S(1)} %get-tuple-element.595), channel_id=1, source_target_pairs={{0,2},{2,6},{4,0},{6,4},{1,3},{3,7},{5,1},{7,5},{8,10},{10,14},{12... | collective-permute-start | bytes 1769480 | tf_op jit(solution)/shard_map/ppermute | solution.py:56
  141.2 28.2 %collective-permute-start.24 = (bf16[384,1536]{1,0:T(8,128)(2,1)S(1)}, bf16[384,1536]{1,0:T(8,128)(2,1)}, u32[]{:S(2)}, u32[]{:S(2)}) collective-permute-start(bf16[384,1536]{1,0:T(8,128)(2,1)S(1)} %get-tuple-element.631), channel_id=1, source_target_pairs={{0,8},{8,0},{16,24},{24,16},{1,9},{9,1},{17,25},{25,17},{2,10},{10... | collective-permute-start | bytes 3538952 | tf_op jit(solution)/shard_map/ppermute | solution.py:48
  144.3 33.1 %collective-permute-start.29 = (bf16[256,1664]{1,0:T(8,128)(2,1)S(1)}, bf16[256,1664]{1,0:T(8,128)(2,1)S(1)}, u32[]{:S(2)}, u32[]{:S(2)}) collective-permute-start(bf16[256,1664]{1,0:T(8,128)(2,1)S(1)} %add_convert_fusion.3), channel_id=1, source_target_pairs={{0,1},{1,0},{2,3},{3,2},{4,5},{5,4},{6,7},{7,6},{8,9},{9,8},{10,11... | collective-permute-start | bytes 2555912 | tf_op jit(solution)/shard_map/ppermute | solution.py:48
  145.3 31.5 %collective-permute-start.30 = (bf16[192,1536]{1,0:T(8,128)(2,1)}, bf16[192,1536]{1,0:T(8,128)(2,1)S(1)}, u32[]{:S(2)}, u32[]{:S(2)}) collective-permute-start(bf16[192,1536]{1,0:T(8,128)(2,1)} %get-tuple-element.651), channel_id=1, source_target_pairs={{0,0},{2,4},{4,2},{6,6},{1,1},{3,5},{5,3},{7,7},{8,8},{10,12},{12,... | collective-permute-start | bytes 1769480 | tf_op jit(solution)/shard_map/ppermute | solution.py:52
  147.0 29.8 %collective-permute-start.31 = (bf16[192,1536]{1,0:T(8,128)(2,1)}, bf16[192,1536]{1,0:T(8,128)(2,1)}, u32[]{:S(2)}, u32[]{:S(2)}) collective-permute-start(bf16[192,1536]{1,0:T(8,128)(2,1)} %get-tuple-element.651), channel_id=1, source_target_pairs={{0,2},{2,6},{4,0},{6,4},{1,3},{3,7},{5,1},{7,5},{8,10},{10,14},{12... | collective-permute-start | bytes 1769480 | tf_op jit(solution)/shard_map/ppermute | solution.py:56
  197.3 53.5 %collective-permute-start.47 = (bf16[384,3072]{1,0:T(8,128)(2,1)}, bf16[384,3072]{1,0:T(8,128)(2,1)S(1)}, u32[]{:S(2)}, u32[]{:S(2)}) collective-permute-start(bf16[384,3072]{1,0:T(8,128)(2,1)} %maximum_maximum_fusion.refs_0_), channel_id=1, source_target_pairs={{0,8},{8,0},{16,24},{24,16},{1,9},{9,1},{17,25},{25,17},{2,10},{10... | collective-permute-start | bytes 7077896 | tf_op jit(solution)/shard_map/ppermute | solution.py:48
  200.7 53.6 %collective-permute-start.48 = (bf16[384,3072]{1,0:T(8,128)(2,1)}, bf16[384,3072]{1,0:T(8,128)(2,1)}, u32[]{:S(2)}, u32[]{:S(2)}) collective-permute-start(bf16[384,3072]{1,0:T(8,128)(2,1)} %maximum_maximum_fusion.refs_0_), channel_id=1, source_target_pairs={{0,16},{8,24},{16,0},{24,8},{1,17},{9,25},{17,1},{25,9},{2,18},{10... | collective-permute-start | bytes 7077896 | tf_op jit(solution)/shard_map/ppermute | solution.py:48
  255.6 29.0 %collective-permute-start.53 = (bf16[192,3072]{1,0:T(8,128)(2,1)S(1)}, bf16[192,3072]{1,0:T(8,128)(2,1)S(1)}, u32[]{:S(2)}, u32[]{:S(2)}) collective-permute-start(bf16[192,3072]{1,0:T(8,128)(2,1)S(1)} %slice.424), channel_id=1, source_target_pairs={{0,8},{8,0},{16,24},{24,16},{1,9},{9,1},{17,25},{25,17},{2,10},{10... | collective-permute-start | bytes 3538952 | tf_op jit(solution)/shard_map/ppermute | solution.py:48
  257.3 29.0 %collective-permute-start.54 = (bf16[192,3072]{1,0:T(8,128)(2,1)S(1)}, bf16[192,3072]{1,0:T(8,128)(2,1)S(1)}, u32[]{:S(2)}, u32[]{:S(2)}) collective-permute-start(bf16[192,3072]{1,0:T(8,128)(2,1)S(1)} %slice.425), channel_id=1, source_target_pairs={{0,16},{8,24},{16,0},{24,8},{1,17},{9,25},{17,1},{25,9},{2,18},{10... | collective-permute-start | bytes 3538952 | tf_op jit(solution)/shard_map/ppermute | solution.py:48
  263.9 44.4 %collective-permute-start.50 = (bf16[384,1536]{1,0:T(8,128)(2,1)S(1)}, bf16[384,1536]{1,0:T(8,128)(2,1)S(1)}, u32[]{:S(2)}, u32[]{:S(2)}) collective-permute-start(bf16[384,1536]{1,0:T(8,128)(2,1)S(1)} %pad_maximum_fusion.7.refs_0_), channel_id=1, source_target_pairs={{0,8},{8,0},{16,24},{24,16},{1,9},{9,1},{17,25},{25,17},{2,10},{10... | collective-permute-start | bytes 3538952 | tf_op jit(solution)/shard_map/ppermute | solution.py:48
  266.1 43.4 %collective-permute-start.51 = (bf16[384,1536]{1,0:T(8,128)(2,1)S(1)}, bf16[384,1536]{1,0:T(8,128)(2,1)S(1)}, u32[]{:S(2)}, u32[]{:S(2)}) collective-permute-start(bf16[384,1536]{1,0:T(8,128)(2,1)S(1)} %pad_maximum_fusion.7.refs_0_), channel_id=1, source_target_pairs={{0,16},{8,24},{16,0},{24,8},{1,17},{9,25},{17,1},{25,9},{2,18},{10... | collective-permute-start | bytes 3538952 | tf_op jit(solution)/shard_map/ppermute | solution.py:48
  266.8 42.8 %collective-permute-start.52 = (bf16[256,1536]{1,0:T(8,128)(2,1)S(1)}, bf16[256,1536]{1,0:T(8,128)(2,1)}, u32[]{:S(2)}, u32[]{:S(2)}) collective-permute-start(bf16[256,1536]{1,0:T(8,128)(2,1)S(1)} %collective-permute-done.46.refs_8_.refs_17_.g_ref), channel_id=1, source_target_pairs={{0,1},{1,0},{2,3},{3,2},{4,5},{5,4},{6,7},{7,6},{8,9},{9,8},{10,11... | collective-permute-start | bytes 2359304 | tf_op jit(solution)/shard_map/ppermute | solution.py:48
  439.4 36.3 %collective-permute-start.77 = (bf16[256,1536]{1,0:T(8,128)(2,1)}, bf16[256,1536]{1,0:T(8,128)(2,1)S(1)}, u32[]{:S(2)}, u32[]{:S(2)}) collective-permute-start(bf16[256,1536]{1,0:T(8,128)(2,1)} %get-tuple-element.909), channel_id=1, source_target_pairs={{0,0},{2,4},{4,2},{6,6},{1,1},{3,5},{5,3},{7,7},{8,8},{10,12},{12,... | collective-permute-start | bytes 2359304 | tf_op jit(solution)/shard_map/ppermute | solution.py:52
  441.2 34.5 %collective-permute-start.75 = (bf16[15,16,384]{2,1,0:T(8,128)(2,1)S(1)}, bf16[15,16,384]{2,1,0:T(8,128)(2,1)S(1)}, u32[]{:S(2)}, u32[]{:S(2)}) collective-permute-start(bf16[15,16,384]{2,1,0:T(8,128)(2,1)S(1)} %constant_dynamic-update-slice_fusion), channel_id=1, source_target_pairs={{0,0},{2,4},{4,2},{6,6},{1,1},{3,5},{5,3},{7,7},{8,8},{10,12},{12,... | collective-permute-start | bytes 552968 | tf_op jit(solution)/shard_map/ppermute | solution.py:52
  441.8 33.9 %collective-permute-start.76 = (bf16[15,16,384]{2,1,0:T(8,128)(2,1)S(1)}, bf16[15,16,384]{2,1,0:T(8,128)(2,1)S(1)}, u32[]{:S(2)}, u32[]{:S(2)}) collective-permute-start(bf16[15,16,384]{2,1,0:T(8,128)(2,1)S(1)} %constant_dynamic-update-slice_fusion), channel_id=1, source_target_pairs={{0,4},{2,0},{4,6},{6,2},{1,5},{3,1},{5,7},{7,3},{8,12},{10,8},{12,... | collective-permute-start | bytes 552968 | tf_op jit(solution)/shard_map/ppermute | solution.py:60
  531.1 30.7 %collective-permute-start.92 = (bf16[256,1536]{1,0:T(8,128)(2,1)}, bf16[256,1536]{1,0:T(8,128)(2,1)S(1)}, u32[]{:S(2)}, u32[]{:S(2)}) collective-permute-start(bf16[256,1536]{1,0:T(8,128)(2,1)} %shard_map.240), channel_id=1, source_target_pairs={{0,0},{2,4},{4,2},{6,6},{1,1},{3,5},{5,3},{7,7},{8,8},{10,12},{12,... | collective-permute-start | bytes 2359304 | tf_op jit(solution)/shard_map/ppermute | solution.py:52
  (168 other events, 1779.7 us)

commit v8 on v7

--- a/solution.py
+++ b/solution.py
@@ -909,83 +909,89 @@
     )
 
 
-def settle_first_kernel(fold, labels_ref, in_ref, down_ref, hid_ref, gate_ref):
-    slot = pl.program_id(0)
+STEP_SLOTS = 4
+
+
+def each_slot(labels_ref, in_refs):
+    for j in range(STEP_SLOTS):
+        slot = pl.program_id(0) * STEP_SLOTS + j
+        for n, ref in enumerate(in_refs):
+            for s in range(ref.shape[0]):
+                yield j, labels_ref[n * ref.shape[0] + s] == slot, ref.at[s]
+
+
+def settle_first_kernel(fold, labels_ref, *refs):
+    *in_refs, down_ref, hid_ref, gate_ref = refs
     local = down_ref.shape[-1]
     for ref in (down_ref, hid_ref, gate_ref):
         ref[...] = jnp.zeros_like(ref)
-    for s in range(in_ref.shape[0]):
-
-        @pl.when(labels_ref[s] == slot)
-        def _(s=s):
+    for j, here, found in each_slot(labels_ref, in_refs):
+
+        @pl.when(here)
+        def _(j=j, found=found):
             for n, k in enumerate(DOWN_FIRST):
-                down_ref[0, k] += in_ref[s, n].astype(F32)
+                down_ref[j, k] += found[n].astype(F32)
             for k in range(fold):
                 at, n = slice(k * local, (k + 1) * local), len(DOWN_FIRST) + k
-                hid_ref[0, :, at] += in_ref[s, n].astype(F32)
-                gate_ref[0, 0, :, at] += in_ref[s, n + fold].astype(F32)
-                gate_ref[0, 1, :, at] += in_ref[s, n + 2 * fold].astype(F32)
-
-
-def settle_second_kernel(labels_ref, in_ref, down_in, down_ref, up_ref):
-    del down_in
-    slot = pl.program_id(0)
+                hid_ref[j, :, at] += found[n].astype(F32)
+                gate_ref[j, 0, :, at] += found[n + fold].astype(F32)
+                gate_ref[j, 1, :, at] += found[n + 2 * fold].astype(F32)
+
+
+def settle_second_kernel(labels_ref, *refs):
+    *in_refs, _, down_ref, up_ref = refs
     downs, ups = down_ref.shape[1], up_ref.shape[1]
     for ref in (down_ref, up_ref):
         ref[...] = jnp.zeros_like(ref)
-    for s in range(in_ref.shape[0]):
-
-        @pl.when(labels_ref[s] == slot)
-        def _(s=s):
-            down_ref[0] += in_ref[s, :downs].astype(F32)
-            up_ref[0] += in_ref[s, downs : downs + ups].astype(F32)
+    for j, here, found in each_slot(labels_ref, in_refs):
+
+        @pl.when(here)
+        def _(j=j, found=found):
+            down_ref[j] += found[:downs].astype(F32)
+            up_ref[j] += found[downs : downs + ups].astype(F32)
 
 
 DOWN_FIRST = (4, 5)
 
 
 def slot_spec(shape):
-    return pl.BlockSpec((1,) + shape[1:], lambda i, *_, n=len(shape): (i,) + (0,) * (n - 1))
-
-
-def settle_first(labels, grads, slots, fold):
-    rank, local = grads.shape[2:]
-    hidden = fold * local
-    shapes = [
-        (slots, 6, rank, local),
-        (slots, rank, hidden),
-        (slots, 2, rank, hidden),
-    ]
+    block = (STEP_SLOTS,) + shape[1:]
+    return pl.BlockSpec(block, lambda i, *_, n=len(shape): (i,) + (0,) * (n - 1))
+
+
+def settle_call(kernel, labels, grads, before, shapes, blocks, aliases):
+    slots = shapes[0][0]
     return pl.pallas_call(
-        functools.partial(settle_first_kernel, fold),
+        kernel,
         grid_spec=pltpu.PrefetchScalarGridSpec(
             num_scalar_prefetch=1,
-            grid=(slots,),
-            in_specs=[whole_spec(grads.shape)],
-            out_specs=[slot_spec(s) for s in shapes],
+            grid=(slots // STEP_SLOTS,),
+            in_specs=[whole_spec(g.shape) for g in grads]
+            + [pl.BlockSpec(memory_space=pl.ANY) for _ in before],
+            out_specs=[slot_spec(b) for b in blocks],
         ),
         out_shape=[sds(s, F32) for s in shapes],
+        input_output_aliases=aliases,
         compiler_params=params(),
         cost_estimate=cost(0, 0),
-    )(labels, grads)
+    )(labels, *grads, *before)
+
+
+def settle_first(labels, grads, slots, fold):
+    rank, local = grads[0].shape[2:]
+    hidden = fold * local
+    shapes = [(slots, 6, rank, local), (slots, rank, hidden), (slots, 2, rank, hidden)]
+    kernel = functools.partial(settle_first_kernel, fold)
+    return settle_call(kernel, labels, grads, [], shapes, shapes, {})
 
 
 def settle_second(labels, grads, down):
-    downs = DOWN_FIRST[0]
     up = down.shape[:1] + (9,) + down.shape[2:]
-    return pl.pallas_call(
-        settle_second_kernel,
-        grid_spec=pltpu.PrefetchScalarGridSpec(
-            num_scalar_prefetch=1,
-            grid=(down.shape[0],),
-            in_specs=[whole_spec(grads.shape), pl.BlockSpec(memory_space=pl.ANY)],
-            out_specs=[slot_spec((1, downs) + down.shape[2:]), slot_spec(up)],
-        ),
-        out_shape=[sds(down.shape, F32), sds(up, F32)],
-        input_output_aliases={2: 0},
-        compiler_params=params(),
-        cost_estimate=cost(0, 0),
-    )(labels, grads, down)
+    part = (down.shape[0], DOWN_FIRST[0]) + down.shape[2:]
+    aliases = {1 + len(grads): 0}
+    return settle_call(
+        settle_second_kernel, labels, grads, [down], [down.shape, up], [part, up], aliases
+    )
 
 
 def chunks(hidden):
@@ -1455,7 +1461,8 @@
 
     def sent(parts):
         parts.append(jnp.full((1, rank, local), index, F32))
-        grads = step.mark(jnp.concatenate(parts, axis=0).astype(BF))
+        grads = jnp.concatenate(parts, axis=0).astype(BF).reshape(-1, local)
+        grads = step.mark(grads)
         return [home_swap(grads), turned_back(grads)]
 
     def to_chips(blocks):
@@ -1463,9 +1470,9 @@
         return [both] + [xor_move(both, "chip", chips, k) for k in range(1, chips)]
 
     def every(blocks):
-        grads = stacked(*blocks)
-        grads = grads.reshape(-1, grads.shape[0] // (2 * chips), rank, local)
-        return grads, grads[:, -1, 0, 0].astype(jnp.int32)
+        blocks = [b.reshape(2, -1, rank, local) for b in blocks]
+        labels = jnp.concatenate([b[:, -1, 0, 0] for b in blocks])
+        return blocks, labels.astype(jnp.int32)
 
     def total(own, far):
         for f in far:

time: 571 us -> 567 us (level)
    unnamed x207 -> x213, local copies, waits for them, and re-layouts: 21.9 us -> 22.1 us
  transfers between devices with their start and end apart: 97 -> 97, of which waited for: 41 -> 43; matrix products, arithmetic and copies ran while one was open for 8% -> 8% of each run, Pallas kernels for 38% -> 38%
where the time goes in v8:
time: 567 us; the launch traced here: 560 us
  Pallas kernels  231 us (41%)
  starting transfers between devices  130 us (23%)
  waiting for transfers between devices  128 us (23%)
  local copies, waits for them, and re-layouts  45 us (8%)
  other arithmetic  21 us (4%)
    pallas_call x13, Pallas kernels, weight_call(): pl.pallas_call(kernel, grid_spec=pltpu.PrefetchScalarGridSpec(num_scalar_...  211 us
    ppermute x40, waiting for transfers between devices, xor_move(): return lax.ppermute(x, axis, [(i, i ^ k) for i in range(size)])  93.4 us
    ppermute x40, starting transfers between devices, xor_move(): return lax.ppermute(x, axis, [(i, i ^ k) for i in range(size)])  76.6 us
    ppermute x39, waiting for transfers between devices, core_swap(): return lax.ppermute(x, 'core', SWAP)  23.6 us
    ppermute x12, starting transfers between devices, home_swap(): return lax.ppermute(x, ('core', 'zhi'), [(0, 0), (1, 2), (2, 1), (3, 3)])  22.5 us
    unnamed x213, local copies, waits for them, and re-layouts  22.1 us
    ppermute x39, starting transfers between devices, core_swap(): return lax.ppermute(x, 'core', SWAP)  15.7 us
  transfers between devices with their start and end apart: 97, of which 43 were waited for; matrix products, arithmetic and copies ran while one was open for 8% of the time, Pallas kernels for 38%

profile of v8, /device:TPU:0, one launch (start us, length us, event | category | flops | bytes accessed | tf_op | source)
XLA Modules:
  0.0 559.8 jit_solution(15536079922636936738)
XLA Ops:
  3.7 5.9 %collective-permute-start.2 = (bf16[192,1536]{1,0:T(8,128)(2,1)}, bf16[192,1536]{1,0:T(8,128)(2,1)}, u32[]{:S(2)}, u32[]{:S(2)}) collective-permute-start(bf16[192,1536]{1,0:T(8,128)(2,1)} %pad_maximum_fusion.7), channel_id=1, source_target_pairs={{0,0},{2,4},{4,2},{6,6},{1,1},{3,5},{5,3},{7,7},{8,8},{10,12},{12,... | collective-permute-start | bytes 1769480 | tf_op jit(solution)/shard_map/ppermute | solution.py:52
  32.1 12.3 %collective-permute-start.10 = (bf16[256,1536]{1,0:T(8,128)(2,1)}, bf16[256,1536]{1,0:T(8,128)(2,1)}, u32[]{:S(2)}, u32[]{:S(2)}) collective-permute-start(bf16[256,1536]{1,0:T(8,128)(2,1)} %collective-permute-done.6.refs_6_.refs_17_.x_ref), channel_id=1, source_target_pairs={{0,1},{1,0},{2,3},{3,2},{4,5},{5,4},{6,7},{7,6},{8,9},{9,8},{10,11... | collective-permute-start | bytes 2359304 | tf_op jit(solution)/shard_map/ppermute | solution.py:48
  44.4 22.4 %collective-permute-start.12 = (bf16[192,1536]{1,0:T(8,128)(2,1)S(1)}, bf16[192,1536]{1,0:T(8,128)(2,1)S(1)}, u32[]{:S(2)}, u32[]{:S(2)}) collective-permute-start(bf16[192,1536]{1,0:T(8,128)(2,1)S(1)} %pad_maximum_fusion.6), channel_id=1, source_target_pairs={{0,2},{2,0},{1,3},{3,1},{4,6},{6,4},{5,7},{7,5},{8,10},{10,8},{9,1... | collective-permute-start | bytes 1769480 | tf_op jit(solution)/shard_map/ppermute | solution.py:48
  71.7 21.5 %collective-permute-done.12 = bf16[192,1536]{1,0:T(8,128)(2,1)S(1)} collective-permute-done((bf16[192,1536]{1,0:T(8,128)(2,1)S(1)}, bf16[192,1536]{1,0:T(8,128)(2,1)S(1)}, u32[]{:S(2)}, u32[]{:S(2)}) %collective-permute-start.12) | collective-permute-done | bytes 589856 | tf_op jit(solution)/shard_map/ppermute | solution.py:48
  109.6 14.8 %shard_map.226 = (bf16[1024,384]{1,0:T(8,128)(2,1)}, bf16[1024,384]{1,0:T(8,128)(2,1)}, bf16[1024,384]{1,0:T(8,128)(2,1)}, bf16[1024,16]{1,0:T(8,128)(2,1)}, bf16[1024,1536]{1,0:T(8,128)(2,1)}) custom-call(s32[22]{0:T(128)} %stack.87.places_ref, bf16[384,1536]{1,0:T(8,128)(2,1)} %copy-done.13, bf16[384,1536]{1,0:T(8,128)(2,1)} %copy-done.40, ...), custom_call_target="tpu_custom_call" | custom-call | flops 4831838208 | bytes 4718592 | tf_op jit(solution)/shard_map/pallas_call | solution.py:158
  124.5 12.9 %shard_map.227 = (bf16[512,384]{1,0:T(8,128)(2,1)}, f32[8,512]{1,0:T(8,128)}, bf16[256,1664]{1,0:T(8,128)(2,1)}, bf16[256,1664]{1,0:T(8,128)(2,1)}) custom-call(s32[22]{0:T(128)} %stack.87.places_ref, bf16[384,1536]{1,0:T(8,128)(2,1)} %copy-done.13, bf16[384,1536]{1,0:T(8,128)(2,1)} %copy-done.40, bf16[384,1536]{1,0:T(8,128)(2,1)} %copy-done.41, ...), custom_call_target="tpu_custom_call" | custom-call | flops 3221225472 | bytes 3145728 | tf_op jit(solution)/shard_map/pallas_call | solution.py:158
  145.2 5.9 %collective-permute-start.30 = (bf16[192,1536]{1,0:T(8,128)(2,1)}, bf16[192,1536]{1,0:T(8,128)(2,1)}, u32[]{:S(2)}, u32[]{:S(2)}) collective-permute-start(bf16[192,1536]{1,0:T(8,128)(2,1)} %get-tuple-element.651), channel_id=1, source_target_pairs={{0,0},{2,4},{4,2},{6,6},{1,1},{3,5},{5,3},{7,7},{8,8},{10,12},{12,... | collective-permute-start | bytes 1769480 | tf_op jit(solution)/shard_map/ppermute | solution.py:52
  151.2 12.9 %shard_map.228 = (bf16[512,384]{1,0:T(8,128)(2,1)}, f32[8,512]{1,0:T(8,128)}, bf16[256,1664]{1,0:T(8,128)(2,1)}, bf16[256,1664]{1,0:T(8,128)(2,1)}) custom-call(s32[22]{0:T(128)} %stack.87.places_ref, bf16[384,1536]{1,0:T(8,128)(2,1)} %copy-done.13, bf16[384,1536]{1,0:T(8,128)(2,1)} %copy-done.40, bf16[384,1536]{1,0:T(8,128)(2,1)} %copy-done.41, ...), custom_call_target="tpu_custom_call" | custom-call | flops 3221225472 | bytes 3145728 | tf_op jit(solution)/shard_map/pallas_call | solution.py:158
  171.4 5.2 shard_map.229
  206.8 17.9 %shard_map.230 = (f32[256,1536]{1,0:T(8,128)}, f32[256,1536]{1,0:T(8,128)}, bf16[256,1536]{1,0:T(8,128)(2,1)}, bf16[256,1536]{1,0:T(8,128)(2,1)}, bf16[256,1536]...) custom-call(s32[22]{0:T(128)} %stack.87.places_ref, ...), custom_call_target="tpu_custom_call" | custom-call | flops 14495514624 | bytes 18874368 | tf_op jit(solution)/shard_map/pallas_call | solution.py:158
  226.1 6.8 %collective-permute-start.49 = (bf16[256,1536]{1,0:T(8,128)(2,1)S(1)}, bf16[256,1536]{1,0:T(8,128)(2,1)S(1)}, u32[]{:S(2)}, u32[]{:S(2)}) collective-permute-start(bf16[256,1536]{1,0:T(8,128)(2,1)S(1)} %copy-done.79), channel_id=1, source_target_pairs={{0,4},{4,0},{1,5},{5,1},{2,6},{6,2},{3,7},{7,3},{8,12},{12,8},{9,1... | collective-permute-start | bytes 2359304 | tf_op jit(solution)/shard_map/ppermute | solution.py:44
  237.2 13.3 %collective-permute-done.47.refs_1_ = bf16[384,3072]{1,0:T(8,128)(2,1)S(1)} collective-permute-done((bf16[384,3072]{1,0:T(8,128)(2,1)}, bf16[384,3072]{1,0:T(8,128)(2,1)S(1)}, u32[]{:S(2)}, u32[]{:S(2)}) %collective-permute-start.47) | collective-permute-done | bytes 2359328 | tf_op jit(solution)/shard_map/ppermute | solution.py:48
  257.6 5.4 collective-permute-done.43.refs_6_
  269.2 15.2 %collective-permute-done.53.refs_3_ = bf16[192,3072]{1,0:T(8,128)(2,1)S(1)} collective-permute-done((bf16[192,3072]{1,0:T(8,128)(2,1)S(1)}, bf16[192,3072]{1,0:T(8,128)(2,1)S(1)}, u32[]{:S(2)}, u32[]{:S(2)}) %collective-permute-start.53) | collective-permute-done | bytes 1179680 | tf_op jit(solution)/shard_map/ppermute | solution.py:48
  287.0 20.9 %shard_map.231 = (bf16[512,1552]{1,0:T(8,128)(2,1)}, bf16[512,1552]{1,0:T(8,128)(2,1)}, bf16[512,16]{1,0:T(8,128)(2,1)}, bf16[512,16]{1,0:T(8,128)(2,1)}, f32[16...) custom-call(s32[22]{0:T(128)} %stack.87.places_ref, bf16[384,3072]{1,0:T(8,128)(2,1)} %maximum_maximum_fusion.refs_0_, ...), custom_call_target="tpu_custom_call" | custom-call | flops 19528679424 | bytes 9535488 | tf_op jit(solution)/shard_map/pallas_call | solution.py:158
  312.6 20.7 %shard_map.232 = (bf16[512,1552]{1,0:T(8,128)(2,1)}, bf16[512,1552]{1,0:T(8,128)(2,1)}, bf16[512,16]{1,0:T(8,128)(2,1)}, bf16[512,16]{1,0:T(8,128)(2,1)}, f32[16...) custom-call(s32[22]{0:T(128)} %stack.87.places_ref, bf16[384,3072]{1,0:T(8,128)(2,1)} %maximum_maximum_fusion.refs_0_, ...), custom_call_target="tpu_custom_call" | custom-call | flops 19528679424 | bytes 9535488 | tf_op jit(solution)/shard_map/pallas_call | solution.py:158
  335.1 15.2 %shard_map.233 = (bf16[256,1664]{1,0:T(8,128)(2,1)}, bf16[256,1664]{1,0:T(8,128)(2,1)}, bf16[256,1664]{1,0:T(8,128)(2,1)}, bf16[256,1664]{1,0:T(8,128)(2,1)}, f3...) custom-call(s32[22]{0:T(128)} %stack.87.places_ref, bf16[384,1536]{1,0:T(8,128)(2,1)} %copy-done.14, ...), custom_call_target="tpu_custom_call" | custom-call | flops 9764339712 | bytes 4767744 | tf_op jit(solution)/shard_map/pallas_call | solution.py:158
  356.2 14.8 %shard_map.234 = (bf16[256,1664]{1,0:T(8,128)(2,1)}, bf16[256,1664]{1,0:T(8,128)(2,1)}, bf16[256,1664]{1,0:T(8,128)(2,1)}, bf16[256,1664]{1,0:T(8,128)(2,1)}, f3...) custom-call(s32[22]{0:T(128)} %stack.87.places_ref, bf16[384,1536]{1,0:T(8,128)(2,1)} %copy-done.14, ...), custom_call_target="tpu_custom_call" | custom-call | flops 9764339712 | bytes 4767744 | tf_op jit(solution)/shard_map/pallas_call | solution.py:158
  371.0 5.8 %collective-permute-done.62.refs_37_ = bf16[256,1664]{1,0:T(8,128)(2,1)S(1)} collective-permute-done((bf16[256,1664]{1,0:T(8,128)(2,1)S(1)}, bf16[256,1664]{1,0:T(8,128)(2,1)S(1)}, u32[]{:S(2)}, u32[]{:S(2)}) %collective-permute-start.62) | collective-permute-done | bytes 852000 | tf_op jit(solution)/shard_map/ppermute | solution.py:48
  381.0 22.6 %shard_map.235 = (f32[256,1536]{1,0:T(8,128)}, bf16[256,1536]{1,0:T(8,128)(2,1)}, bf16[4,48,384]{2,1,0:T(8,128)(2,1)}, bf16[4,32,384]{2,1,0:T(8,128)(2,1)}, bf16...) custom-call(s32[22]{0:T(128)} %stack.87.places_ref, ...), custom_call_target="tpu_custom_call" | custom-call | flops 19327352832 | bytes 18874368 | tf_op jit(solution)/shard_map/pallas_call | solution.py:158
  412.2 18.2 %shard_map.236 = (bf16[512,384]{1,0:T(8,128)(2,1)}, f32[1024,384]{1,0:T(8,128)}, f32[1024,384]{1,0:T(8,128)}, f32[16,384]{1,0:T(8,128)}) custom-call(s32[22]{0:T(128)} %stack.87.places_ref, bf16[384,1536]{1,0:T(8,128)(2,1)} %copy-done.13, bf16[384,1536]{1,0:T(8,128)(2,1)} %copy-done.40, bf16[384,1536]{1,0:T(8,128)(2,1)} %copy-done.41, ...), custom_call_target="tpu_custom_call" | custom-call | flops 8053063680 | bytes 3932160 | tf_op jit(solution)/shard_map/pallas_call | solution.py:158
  445.3 29.7 %shard_map.238 = (f32[16,384]{1,0:T(8,128)}, f32[16,1152]{1,0:T(8,128)}, bf16[4,32,384]{2,1,0:T(8,128)(2,1)}, bf16[256,1664]{1,0:T(8,128)(2,1)}, bf16[256,1664]{...) custom-call(s32[22]{0:T(128)} %stack.87.places_ref, bf16[384,1536]{1,0:T(8,128)(2,1)} %copy-done.13, ...), custom_call_target="tpu_custom_call" | custom-call | flops 8053063680 | bytes 3932160 | tf_op jit(solution)/shard_map/pallas_call | solution.py:158
  485.1 5.7 %shard_map.239 = (f32[16,768]{1,0:T(8,128)}, bf16[130,384]{1,0:T(8,128)(2,1)}, bf16[130,384]{1,0:T(8,128)(2,1)}, bf16[130,384]{1,0:T(8,128)(2,1)}, bf16[130,384]...) custom-call(s32[22]{0:T(128)} %stack.87.places_ref, ...), custom_call_target="tpu_custom_call" | custom-call | flops 10000000000 | bytes 1000000 | tf_op jit(solution)/shard_map/pallas_call | solution.py:158
  522.6 10.9 %collective-permute-done.91 = bf16[224,384]{1,0:T(8,128)(2,1)S(1)} collective-permute-done((bf16[224,384]{1,0:T(8,128)(2,1)S(1)}, bf16[224,384]{1,0:T(8,128)(2,1)S(1)}, u32[]{:S(2)}, u32[]{:S(2)}) %collective-permute-start.91) | collective-permute-done | bytes 172064 | tf_op jit(solution)/shard_map/ppermute | solution.py:60
  (539 shorter events, 218.0 us)
Async XLA Ops:
  24.8 42.1 %collective-permute-start.4 = (bf16[384,1536]{1,0:T(8,128)(2,1)S(1)}, bf16[384,1536]{1,0:T(8,128)(2,1)S(1)}, u32[]{:S(2)}, u32[]{:S(2)}) collective-permute-start(bf16[384,1536]{1,0:T(8,128)(2,1)S(1)} %pad_maximum_fusion.3.refs_0_), channel_id=1, source_target_pairs={{0,8},{8,0},{16,24},{24,16},{1,9},{9,1},{17,25},{25,17},{2,10},{10... | collective-permute-start | bytes 3538952 | tf_op jit(solution)/shard_map/ppermute | solution.py:48
  27.8 39.1 %collective-permute-start.5 = (bf16[384,1536]{1,0:T(8,128)(2,1)S(1)}, bf16[384,1536]{1,0:T(8,128)(2,1)S(1)}, u32[]{:S(2)}, u32[]{:S(2)}) collective-permute-start(bf16[384,1536]{1,0:T(8,128)(2,1)S(1)} %pad_maximum_fusion.3.refs_0_), channel_id=1, source_target_pairs={{0,16},{8,24},{16,0},{24,8},{1,17},{9,25},{17,1},{25,9},{2,18},{10... | collective-permute-start | bytes 3538952 | tf_op jit(solution)/shard_map/ppermute | solution.py:48
  32.1 61.1 %collective-permute-start.10 = (bf16[256,1536]{1,0:T(8,128)(2,1)}, bf16[256,1536]{1,0:T(8,128)(2,1)}, u32[]{:S(2)}, u32[]{:S(2)}) collective-permute-start(bf16[256,1536]{1,0:T(8,128)(2,1)} %collective-permute-done.6.refs_6_.refs_17_.x_ref), channel_id=1, source_target_pairs={{0,1},{1,0},{2,3},{3,2},{4,5},{5,4},{6,7},{7,6},{8,9},{9,8},{10,11... | collective-permute-start | bytes 2359304 | tf_op jit(solution)/shard_map/ppermute | solution.py:48
  44.4 48.8 %collective-permute-start.12 = (bf16[192,1536]{1,0:T(8,128)(2,1)S(1)}, bf16[192,1536]{1,0:T(8,128)(2,1)S(1)}, u32[]{:S(2)}, u32[]{:S(2)}) collective-permute-start(bf16[192,1536]{1,0:T(8,128)(2,1)S(1)} %pad_maximum_fusion.6), channel_id=1, source_target_pairs={{0,2},{2,0},{1,3},{3,1},{4,6},{6,4},{5,7},{7,5},{8,10},{10,8},{9,1... | collective-permute-start | bytes 1769480 | tf_op jit(solution)/shard_map/ppermute | solution.py:48
  102.2 35.3 %collective-permute-start.18 = (bf16[384,1536]{1,0:T(8,128)(2,1)S(1)}, bf16[384,1536]{1,0:T(8,128)(2,1)S(1)}, u32[]{:S(2)}, u32[]{:S(2)}) collective-permute-start(bf16[384,1536]{1,0:T(8,128)(2,1)S(1)} %pad_maximum_fusion.4.refs_0_), channel_id=1, source_target_pairs={{0,8},{8,0},{16,24},{24,16},{1,9},{9,1},{17,25},{25,17},{2,10},{10... | collective-permute-start | bytes 3538952 | tf_op jit(solution)/shard_map/ppermute | solution.py:48
  102.8 34.7 %collective-permute-start.19 = (bf16[384,1536]{1,0:T(8,128)(2,1)S(1)}, bf16[384,1536]{1,0:T(8,128)(2,1)S(1)}, u32[]{:S(2)}, u32[]{:S(2)}) collective-permute-start(bf16[384,1536]{1,0:T(8,128)(2,1)S(1)} %pad_maximum_fusion.4.refs_0_), channel_id=1, source_target_pairs={{0,16},{8,24},{16,0},{24,8},{1,17},{9,25},{17,1},{25,9},{2,18},{10... | collective-permute-start | bytes 3538952 | tf_op jit(solution)/shard_map/ppermute | solution.py:48
  104.2 33.2 %collective-permute-start.20 = (bf16[192,1536]{1,0:T(8,128)(2,1)S(1)}, bf16[192,1536]{1,0:T(8,128)(2,1)S(1)}, u32[]{:S(2)}, u32[]{:S(2)}) collective-permute-start(bf16[192,1536]{1,0:T(8,128)(2,1)S(1)} %copy-done.9), channel_id=1, source_target_pairs={{0,1},{1,0},{2,3},{3,2},{4,5},{5,4},{6,7},{7,6},{8,9},{9,8},{10,11... | collective-permute-start | bytes 1769480 | tf_op jit(solution)/shard_map/ppermute | solution.py:48
  104.2 33.3 %collective-permute-start.21 = (bf16[192,1536]{1,0:T(8,128)(2,1)S(1)}, bf16[192,1536]{1,0:T(8,128)(2,1)S(1)}, u32[]{:S(2)}, u32[]{:S(2)}) collective-permute-start(bf16[192,1536]{1,0:T(8,128)(2,1)S(1)} %get-tuple-element.595), channel_id=1, source_target_pairs={{0,0},{2,4},{4,2},{6,6},{1,1},{3,5},{5,3},{7,7},{8,8},{10,12},{12,... | collective-permute-start | bytes 1769480 | tf_op jit(solution)/shard_map/ppermute | solution.py:52
  104.9 32.6 %collective-permute-start.22 = (bf16[192,1536]{1,0:T(8,128)(2,1)S(1)}, bf16[192,1536]{1,0:T(8,128)(2,1)S(1)}, u32[]{:S(2)}, u32[]{:S(2)}) collective-permute-start(bf16[192,1536]{1,0:T(8,128)(2,1)S(1)} %get-tuple-element.595), channel_id=1, source_target_pairs={{0,2},{2,6},{4,0},{6,4},{1,3},{3,7},{5,1},{7,5},{8,10},{10,14},{12... | collective-permute-start | bytes 1769480 | tf_op jit(solution)/shard_map/ppermute | solution.py:56
  141.1 28.2 %collective-permute-start.24 = (bf16[384,1536]{1,0:T(8,128)(2,1)S(1)}, bf16[384,1536]{1,0:T(8,128)(2,1)}, u32[]{:S(2)}, u32[]{:S(2)}) collective-permute-start(bf16[384,1536]{1,0:T(8,128)(2,1)S(1)} %get-tuple-element.631), channel_id=1, source_target_pairs={{0,8},{8,0},{16,24},{24,16},{1,9},{9,1},{17,25},{25,17},{2,10},{10... | collective-permute-start | bytes 3538952 | tf_op jit(solution)/shard_map/ppermute | solution.py:48
  144.2 33.2 %collective-permute-start.29 = (bf16[256,1664]{1,0:T(8,128)(2,1)S(1)}, bf16[256,1664]{1,0:T(8,128)(2,1)}, u32[]{:S(2)}, u32[]{:S(2)}) collective-permute-start(bf16[256,1664]{1,0:T(8,128)(2,1)S(1)} %add_convert_fusion.3), channel_id=1, source_target_pairs={{0,1},{1,0},{2,3},{3,2},{4,5},{5,4},{6,7},{7,6},{8,9},{9,8},{10,11... | collective-permute-start | bytes 2555912 | tf_op jit(solution)/shard_map/ppermute | solution.py:48
  145.2 31.6 %collective-permute-start.30 = (bf16[192,1536]{1,0:T(8,128)(2,1)}, bf16[192,1536]{1,0:T(8,128)(2,1)}, u32[]{:S(2)}, u32[]{:S(2)}) collective-permute-start(bf16[192,1536]{1,0:T(8,128)(2,1)} %get-tuple-element.651), channel_id=1, source_target_pairs={{0,0},{2,4},{4,2},{6,6},{1,1},{3,5},{5,3},{7,7},{8,8},{10,12},{12,... | collective-permute-start | bytes 1769480 | tf_op jit(solution)/shard_map/ppermute | solution.py:52
  197.0 53.5 %collective-permute-start.47 = (bf16[384,3072]{1,0:T(8,128)(2,1)}, bf16[384,3072]{1,0:T(8,128)(2,1)S(1)}, u32[]{:S(2)}, u32[]{:S(2)}) collective-permute-start(bf16[384,3072]{1,0:T(8,128)(2,1)} %maximum_maximum_fusion.refs_0_), channel_id=1, source_target_pairs={{0,8},{8,0},{16,24},{24,16},{1,9},{9,1},{17,25},{25,17},{2,10},{10... | collective-permute-start | bytes 7077896 | tf_op jit(solution)/shard_map/ppermute | solution.py:48
  200.4 53.6 %collective-permute-start.48 = (bf16[384,3072]{1,0:T(8,128)(2,1)}, bf16[384,3072]{1,0:T(8,128)(2,1)}, u32[]{:S(2)}, u32[]{:S(2)}) collective-permute-start(bf16[384,3072]{1,0:T(8,128)(2,1)} %maximum_maximum_fusion.refs_0_), channel_id=1, source_target_pairs={{0,16},{8,24},{16,0},{24,8},{1,17},{9,25},{17,1},{25,9},{2,18},{10... | collective-permute-start | bytes 7077896 | tf_op jit(solution)/shard_map/ppermute | solution.py:48
  234.9 28.1 %collective-permute-start.43 = (bf16[256,1536]{1,0:T(8,128)(2,1)S(1)}, bf16[256,1536]{1,0:T(8,128)(2,1)S(1)}, u32[]{:S(2)}, u32[]{:S(2)}) collective-permute-start(bf16[256,1536]{1,0:T(8,128)(2,1)S(1)} %copy-done.79), channel_id=1, source_target_pairs={{0,1},{1,0},{2,3},{3,2},{4,5},{5,4},{6,7},{7,6},{8,9},{9,8},{10,11... | collective-permute-start | bytes 2359304 | tf_op jit(solution)/shard_map/ppermute | solution.py:48
  235.1 27.9 %collective-permute-start.46 = (bf16[256,1536]{1,0:T(8,128)(2,1)S(1)}, bf16[256,1536]{1,0:T(8,128)(2,1)S(1)}, u32[]{:S(2)}, u32[]{:S(2)}) collective-permute-start(bf16[256,1536]{1,0:T(8,128)(2,1)S(1)} %bitcast.281), channel_id=1, source_target_pairs={{0,0},{2,4},{4,2},{6,6},{1,1},{3,5},{5,3},{7,7},{8,8},{10,12},{12,... | collective-permute-start | bytes 2359304 | tf_op jit(solution)/shard_map/ppermute | solution.py:52
  255.4 29.0 %collective-permute-start.53 = (bf16[192,3072]{1,0:T(8,128)(2,1)S(1)}, bf16[192,3072]{1,0:T(8,128)(2,1)S(1)}, u32[]{:S(2)}, u32[]{:S(2)}) collective-permute-start(bf16[192,3072]{1,0:T(8,128)(2,1)S(1)} %slice.442), channel_id=1, source_target_pairs={{0,8},{8,0},{16,24},{24,16},{1,9},{9,1},{17,25},{25,17},{2,10},{10... | collective-permute-start | bytes 3538952 | tf_op jit(solution)/shard_map/ppermute | solution.py:48
  257.0 29.0 %collective-permute-start.54 = (bf16[192,3072]{1,0:T(8,128)(2,1)S(1)}, bf16[192,3072]{1,0:T(8,128)(2,1)S(1)}, u32[]{:S(2)}, u32[]{:S(2)}) collective-permute-start(bf16[192,3072]{1,0:T(8,128)(2,1)S(1)} %slice.443), channel_id=1, source_target_pairs={{0,16},{8,24},{16,0},{24,8},{1,17},{9,25},{17,1},{25,9},{2,18},{10... | collective-permute-start | bytes 3538952 | tf_op jit(solution)/shard_map/ppermute | solution.py:48
  263.6 44.4 %collective-permute-start.50 = (bf16[384,1536]{1,0:T(8,128)(2,1)S(1)}, bf16[384,1536]{1,0:T(8,128)(2,1)S(1)}, u32[]{:S(2)}, u32[]{:S(2)}) collective-permute-start(bf16[384,1536]{1,0:T(8,128)(2,1)S(1)} %pad_maximum_fusion.5.refs_0_), channel_id=1, source_target_pairs={{0,8},{8,0},{16,24},{24,16},{1,9},{9,1},{17,25},{25,17},{2,10},{10... | collective-permute-start | bytes 3538952 | tf_op jit(solution)/shard_map/ppermute | solution.py:48
  265.8 43.4 %collective-permute-start.51 = (bf16[384,1536]{1,0:T(8,128)(2,1)S(1)}, bf16[384,1536]{1,0:T(8,128)(2,1)S(1)}, u32[]{:S(2)}, u32[]{:S(2)}) collective-permute-start(bf16[384,1536]{1,0:T(8,128)(2,1)S(1)} %pad_maximum_fusion.5.refs_0_), channel_id=1, source_target_pairs={{0,16},{8,24},{16,0},{24,8},{1,17},{9,25},{17,1},{25,9},{2,18},{10... | collective-permute-start | bytes 3538952 | tf_op jit(solution)/shard_map/ppermute | solution.py:48
  266.5 42.8 %collective-permute-start.52 = (bf16[256,1536]{1,0:T(8,128)(2,1)S(1)}, bf16[256,1536]{1,0:T(8,128)(2,1)}, u32[]{:S(2)}, u32[]{:S(2)}) collective-permute-start(bf16[256,1536]{1,0:T(8,128)(2,1)S(1)} %collective-permute-done.46.refs_8_.refs_17_.g_ref), channel_id=1, source_target_pairs={{0,1},{1,0},{2,3},{3,2},{4,5},{5,4},{6,7},{7,6},{8,9},{9,8},{10,11... | collective-permute-start | bytes 2359304 | tf_op jit(solution)/shard_map/ppermute | solution.py:48
  438.6 36.4 %collective-permute-start.77 = (bf16[256,1536]{1,0:T(8,128)(2,1)}, bf16[256,1536]{1,0:T(8,128)(2,1)S(1)}, u32[]{:S(2)}, u32[]{:S(2)}) collective-permute-start(bf16[256,1536]{1,0:T(8,128)(2,1)} %get-tuple-element.909), channel_id=1, source_target_pairs={{0,0},{2,4},{4,2},{6,6},{1,1},{3,5},{5,3},{7,7},{8,8},{10,12},{12,... | collective-permute-start | bytes 2359304 | tf_op jit(solution)/shard_map/ppermute | solution.py:52
  440.4 34.6 %collective-permute-start.75 = (bf16[240,384]{1,0:T(8,128)(2,1)S(1)}, bf16[240,384]{1,0:T(8,128)(2,1)S(1)}, u32[]{:S(2)}, u32[]{:S(2)}) collective-permute-start(bf16[240,384]{1,0:T(8,128)(2,1)S(1)} %bitcast.266), channel_id=1, source_target_pairs={{0,0},{2,4},{4,2},{6,6},{1,1},{3,5},{5,3},{7,7},{8,8},{10,12},{12,... | collective-permute-start | bytes 552968 | tf_op jit(solution)/shard_map/ppermute | solution.py:52
  441.0 33.9 %collective-permute-start.76 = (bf16[240,384]{1,0:T(8,128)(2,1)S(1)}, bf16[240,384]{1,0:T(8,128)(2,1)S(1)}, u32[]{:S(2)}, u32[]{:S(2)}) collective-permute-start(bf16[240,384]{1,0:T(8,128)(2,1)S(1)} %bitcast.267), channel_id=1, source_target_pairs={{0,4},{2,0},{4,6},{6,2},{1,5},{3,1},{5,7},{7,3},{8,12},{10,8},{12,... | collective-permute-start | bytes 552968 | tf_op jit(solution)/shard_map/ppermute | solution.py:60
  (173 other events, 1860.9 us)

commit v9 on v8

--- a/solution.py
+++ b/solution.py
@@ -825,7 +825,7 @@
     )(cosines, sines)
 
 
-def feed_kernel(weight, first, last, number, places_ref, *refs):
+def feed_kernel(weight, first, last, number, tile, places_ref, *refs):
     w_refs, refs = refs[: weight.count], refs[weight.count :]
     n_refs, g_refs, (down_ref, up_ref), refs = (
         refs[:number],
@@ -835,19 +835,24 @@
     )
     if not first:
         (low_in, glow_in, y_in, dn_in), refs = refs[:4], refs[4:]
-    *refs, gdown_ref, ggate_ref, gupper_ref, n_ref, g_ref, w_ref, sems = refs
+    *refs, gdown_ref, ggate_ref, gupper_ref, n_ref, g_ref, block_sems, w_ref, sems = refs
     step, width = pl.program_id(0), n_ref.shape[1]
     rank, part = gdown_ref.shape
-    take_tile(n_refs, n_ref, step)
-    take_tile(g_refs, g_ref, step)
+    block = n_refs[0].shape[0]
 
     @pl.when(step == 0)
     def _():
-        wait_for(weight.bring(w_refs, places_ref, w_ref, sems))
+        copies = weight.bring(w_refs, places_ref, w_ref, sems)
+        for i, ref in enumerate([*n_refs, *g_refs]):
+            to = (n_ref, g_ref)[i // number].at[pl.ds(i % number * block, block)]
+            copies.append(pltpu.make_async_copy(ref, to, block_sems.at[i]))
+            copies[-1].start()
+        wait_for(copies)
         for ref in (gdown_ref, ggate_ref, gupper_ref):
             ref[...] = jnp.zeros_like(ref)
 
-    normed, grad = n_ref[...], g_ref[...]
+    at_tile = pl.ds(pl.multiple_of(step * tile, tile), tile)
+    normed, grad = n_ref[at_tile, :], g_ref[at_tile, :]
     if first:
         low = dot_nt(normed, down_ref[...]).astype(BF)
         grad_low = dot_nt(grad, up_ref[...]).astype(BF)
@@ -896,14 +901,17 @@
     arrays = (*normed, *grads, down, up)
     size = weight.shape[0] * weight.shape[1]
     return weight_call(
-        functools.partial(feed_kernel, weight, first, last, number),
+        functools.partial(feed_kernel, weight, first, last, number, rows),
         weight,
         (tokens // rows,),
-        [whole_spec(a.shape) for a in arrays]
+        [pl.BlockSpec(memory_space=pl.ANY)] * (2 * number)
+        + [whole_spec(down.shape), whole_spec(up.shape)]
         + [pl.BlockSpec((rows, a.shape[1]), lambda t, *_: (start + t, 0)) for a in sums],
         specs + [whole_spec(narrow.shape)] * 3,
         shapes + [narrow] * 3,
-        [pltpu.VMEM((rows, width), BF)] * 2 + weight.scratch(),
+        [pltpu.VMEM((tokens, width), BF)] * 2
+        + [pltpu.SemaphoreType.DMA((2 * number,))]
+        + weight.scratch(),
         cost(8 * tokens * size, 2 * size),
         [*arrays, *sums],
     )
@@ -1393,16 +1401,19 @@
     found, grads = feed_pass(weight, 1, states[1], True)
     y_far, dn_far = found[: len(found) // 2], found[len(found) // 2 :]
 
-    dn_sums, y_sums = far_sums(dn_far, y_far)
+    (dn_sums,) = far_sums(dn_far)
     far = move_p(dn_sums)
     found, more = feed_pass(weight, 0, states[0], True)
     y_rows, dn_rows = found[:2], found[2:]
     feed_grads.append(added(grads, more))
     (far,) = wait_all(far)
-    dn_other, y_other = swap_all([dn_rows[1], y_rows[1]])
+    dn_other, y_other, *y_others = swap_all([dn_rows[1], y_rows[1], *y_far[1::2]])
+    y_sums = listed(
+        step.mark(*[group.near_sums(a, b).astype(BF) for a, b in zip(y_far[::2], y_others)])
+    )
     grad_normed = [dn_rows[0], dn_other, *far]
 
-    far = move_p(step.mark(*y_sums) if len(y_sums) > 1 else [step.mark(*y_sums)])
+    far = move_p(y_sums)
     grad_stream, branch_grad, fixed_rows, near_rows, *keyval_rows = cross_back(
         cotangent_own, listed(step.wait(*grad_normed)), stream_one, stream_two, normed_two,
         query_cross, heads_cross, logsum_cross, low_three, low_four, up[7], down[5], down[2],

time: 567 us -> 567 us (level)
    unnamed x213 -> x215, local copies, waits for them, and re-layouts: 22.1 us -> 22.8 us
  transfers between devices with their start and end apart: 97 -> 97, of which waited for: 43 -> 42; matrix products, arithmetic and copies ran while one was open for 8% -> 7% of each run, Pallas kernels for 38% -> 38%
where the time goes in v9:
time: 567 us; the launch traced here: 560 us
  Pallas kernels  230 us (41%)
  starting transfers between devices  130 us (23%)
  waiting for transfers between devices  129 us (23%)
  local copies, waits for them, and re-layouts  45.6 us (8%)
  other arithmetic  20.9 us (4%)
    pallas_call x13, Pallas kernels, weight_call(): pl.pallas_call(kernel, grid_spec=pltpu.PrefetchScalarGridSpec(num_scalar_...  210 us
    ppermute x40, waiting for transfers between devices, xor_move(): return lax.ppermute(x, axis, [(i, i ^ k) for i in range(size)])  93.5 us
    ppermute x40, starting transfers between devices, xor_move(): return lax.ppermute(x, axis, [(i, i ^ k) for i in range(size)])  76.5 us
    ppermute x39, waiting for transfers between devices, core_swap(): return lax.ppermute(x, 'core', SWAP)  24.1 us
    ppermute x12, starting transfers between devices, home_swap(): return lax.ppermute(x, ('core', 'zhi'), [(0, 0), (1, 2), (2, 1), (3, 3)])  23 us
    unnamed x215, local copies, waits for them, and re-layouts  22.8 us
    ppermute x39, starting transfers between devices, core_swap(): return lax.ppermute(x, 'core', SWAP)  15.6 us
  transfers between devices with their start and end apart: 97, of which 42 were waited for; matrix products, arithmetic and copies ran while one was open for 7% of the time, Pallas kernels for 38%

profile of v9, /device:TPU:0, one launch (start us, length us, event | category | flops | bytes accessed | tf_op | source)
XLA Modules:
  0.0 559.7 jit_solution(10831857433651365496)
XLA Ops:
  3.7 6.0 %collective-permute-start.2 = (bf16[192,1536]{1,0:T(8,128)(2,1)}, bf16[192,1536]{1,0:T(8,128)(2,1)}, u32[]{:S(2)}, u32[]{:S(2)}) collective-permute-start(bf16[192,1536]{1,0:T(8,128)(2,1)} %pad_maximum_fusion.7), channel_id=1, source_target_pairs={{0,0},{2,4},{4,2},{6,6},{1,1},{3,5},{5,3},{7,7},{8,8},{10,12},{12,... | collective-permute-start | bytes 1769480 | tf_op jit(solution)/shard_map/ppermute | solution.py:52
  32.2 12.2 %collective-permute-start.10 = (bf16[256,1536]{1,0:T(8,128)(2,1)}, bf16[256,1536]{1,0:T(8,128)(2,1)}, u32[]{:S(2)}, u32[]{:S(2)}) collective-permute-start(bf16[256,1536]{1,0:T(8,128)(2,1)} %collective-permute-done.6.refs_6_.refs_17_.x_ref), channel_id=1, source_target_pairs={{0,1},{1,0},{2,3},{3,2},{4,5},{5,4},{6,7},{7,6},{8,9},{9,8},{10,11... | collective-permute-start | bytes 2359304 | tf_op jit(solution)/shard_map/ppermute | solution.py:48
  44.5 22.4 %collective-permute-start.12 = (bf16[192,1536]{1,0:T(8,128)(2,1)S(1)}, bf16[192,1536]{1,0:T(8,128)(2,1)S(1)}, u32[]{:S(2)}, u32[]{:S(2)}) collective-permute-start(bf16[192,1536]{1,0:T(8,128)(2,1)S(1)} %pad_maximum_fusion.6), channel_id=1, source_target_pairs={{0,2},{2,0},{1,3},{3,1},{4,6},{6,4},{5,7},{7,5},{8,10},{10,8},{9,1... | collective-permute-start | bytes 1769480 | tf_op jit(solution)/shard_map/ppermute | solution.py:48
  71.7 21.5 %collective-permute-done.12 = bf16[192,1536]{1,0:T(8,128)(2,1)S(1)} collective-permute-done((bf16[192,1536]{1,0:T(8,128)(2,1)S(1)}, bf16[192,1536]{1,0:T(8,128)(2,1)S(1)}, u32[]{:S(2)}, u32[]{:S(2)}) %collective-permute-start.12) | collective-permute-done | bytes 589856 | tf_op jit(solution)/shard_map/ppermute | solution.py:48
  109.6 14.8 %shard_map.226 = (bf16[1024,384]{1,0:T(8,128)(2,1)}, bf16[1024,384]{1,0:T(8,128)(2,1)}, bf16[1024,384]{1,0:T(8,128)(2,1)}, bf16[1024,16]{1,0:T(8,128)(2,1)}, bf16[1024,1536]{1,0:T(8,128)(2,1)}) custom-call(s32[22]{0:T(128)} %stack.87.places_ref, bf16[384,1536]{1,0:T(8,128)(2,1)} %copy-done.13, bf16[384,1536]{1,0:T(8,128)(2,1)} %copy-done.40, ...), custom_call_target="tpu_custom_call" | custom-call | flops 4831838208 | bytes 4718592 | tf_op jit(solution)/shard_map/pallas_call | solution.py:158
  124.5 12.9 %shard_map.227 = (bf16[512,384]{1,0:T(8,128)(2,1)}, f32[8,512]{1,0:T(8,128)}, bf16[256,1664]{1,0:T(8,128)(2,1)}, bf16[256,1664]{1,0:T(8,128)(2,1)}) custom-call(s32[22]{0:T(128)} %stack.87.places_ref, bf16[384,1536]{1,0:T(8,128)(2,1)} %copy-done.13, bf16[384,1536]{1,0:T(8,128)(2,1)} %copy-done.40, bf16[384,1536]{1,0:T(8,128)(2,1)} %copy-done.41, ...), custom_call_target="tpu_custom_call" | custom-call | flops 3221225472 | bytes 3145728 | tf_op jit(solution)/shard_map/pallas_call | solution.py:158
  145.1 5.9 %collective-permute-start.30 = (bf16[192,1536]{1,0:T(8,128)(2,1)}, bf16[192,1536]{1,0:T(8,128)(2,1)}, u32[]{:S(2)}, u32[]{:S(2)}) collective-permute-start(bf16[192,1536]{1,0:T(8,128)(2,1)} %get-tuple-element.650), channel_id=1, source_target_pairs={{0,0},{2,4},{4,2},{6,6},{1,1},{3,5},{5,3},{7,7},{8,8},{10,12},{12,... | collective-permute-start | bytes 1769480 | tf_op jit(solution)/shard_map/ppermute | solution.py:52
  151.3 12.9 %shard_map.228 = (bf16[512,384]{1,0:T(8,128)(2,1)}, f32[8,512]{1,0:T(8,128)}, bf16[256,1664]{1,0:T(8,128)(2,1)}, bf16[256,1664]{1,0:T(8,128)(2,1)}) custom-call(s32[22]{0:T(128)} %stack.87.places_ref, bf16[384,1536]{1,0:T(8,128)(2,1)} %copy-done.13, bf16[384,1536]{1,0:T(8,128)(2,1)} %copy-done.40, bf16[384,1536]{1,0:T(8,128)(2,1)} %copy-done.41, ...), custom_call_target="tpu_custom_call" | custom-call | flops 3221225472 | bytes 3145728 | tf_op jit(solution)/shard_map/pallas_call | solution.py:158
  171.5 5.2 shard_map.229
  206.8 17.9 %shard_map.230 = (f32[256,1536]{1,0:T(8,128)}, f32[256,1536]{1,0:T(8,128)}, bf16[256,1536]{1,0:T(8,128)(2,1)}, bf16[256,1536]{1,0:T(8,128)(2,1)}, bf16[256,1536]...) custom-call(s32[22]{0:T(128)} %stack.87.places_ref, ...), custom_call_target="tpu_custom_call" | custom-call | flops 14495514624 | bytes 18874368 | tf_op jit(solution)/shard_map/pallas_call | solution.py:158
  226.0 6.9 %collective-permute-start.49 = (bf16[256,1536]{1,0:T(8,128)(2,1)S(1)}, bf16[256,1536]{1,0:T(8,128)(2,1)S(1)}, u32[]{:S(2)}, u32[]{:S(2)}) collective-permute-start(bf16[256,1536]{1,0:T(8,128)(2,1)S(1)} %copy-done.80), channel_id=1, source_target_pairs={{0,4},{4,0},{1,5},{5,1},{2,6},{6,2},{3,7},{7,3},{8,12},{12,8},{9,1... | collective-permute-start | bytes 2359304 | tf_op jit(solution)/shard_map/ppermute | solution.py:44
  237.7 12.8 %collective-permute-done.47.refs_1_ = bf16[384,3072]{1,0:T(8,128)(2,1)S(1)} collective-permute-done((bf16[384,3072]{1,0:T(8,128)(2,1)}, bf16[384,3072]{1,0:T(8,128)(2,1)S(1)}, u32[]{:S(2)}, u32[]{:S(2)}) %collective-permute-start.47) | collective-permute-done | bytes 2359328 | tf_op jit(solution)/shard_map/ppermute | solution.py:48
  257.6 5.4 collective-permute-done.43.refs_6_
  269.2 15.2 %collective-permute-done.53.refs_3_ = bf16[192,3072]{1,0:T(8,128)(2,1)S(1)} collective-permute-done((bf16[192,3072]{1,0:T(8,128)(2,1)S(1)}, bf16[192,3072]{1,0:T(8,128)(2,1)S(1)}, u32[]{:S(2)}, u32[]{:S(2)}) %collective-permute-start.53) | collective-permute-done | bytes 1179680 | tf_op jit(solution)/shard_map/ppermute | solution.py:48
  287.0 20.4 %shard_map.231 = (bf16[512,1552]{1,0:T(8,128)(2,1)}, bf16[512,1552]{1,0:T(8,128)(2,1)}, bf16[512,16]{1,0:T(8,128)(2,1)}, bf16[512,16]{1,0:T(8,128)(2,1)}, f32[16...) custom-call(s32[22]{0:T(128)} %stack.87.places_ref, bf16[384,3072]{1,0:T(8,128)(2,1)} %maximum_maximum_fusion.refs_0_, ...), custom_call_target="tpu_custom_call" | custom-call | flops 19528679424 | bytes 9535488 | tf_op jit(solution)/shard_map/pallas_call | solution.py:158
  312.7 20.4 %shard_map.232 = (bf16[512,1552]{1,0:T(8,128)(2,1)}, bf16[512,1552]{1,0:T(8,128)(2,1)}, bf16[512,16]{1,0:T(8,128)(2,1)}, bf16[512,16]{1,0:T(8,128)(2,1)}, f32[16...) custom-call(s32[22]{0:T(128)} %stack.87.places_ref, bf16[384,3072]{1,0:T(8,128)(2,1)} %maximum_maximum_fusion.refs_0_, ...), custom_call_target="tpu_custom_call" | custom-call | flops 19528679424 | bytes 9535488 | tf_op jit(solution)/shard_map/pallas_call | solution.py:158
  334.8 14.7 %shard_map.233 = (bf16[256,1664]{1,0:T(8,128)(2,1)}, bf16[256,1664]{1,0:T(8,128)(2,1)}, bf16[256,1664]{1,0:T(8,128)(2,1)}, bf16[256,1664]{1,0:T(8,128)(2,1)}, f3...) custom-call(s32[22]{0:T(128)} %stack.87.places_ref, bf16[384,1536]{1,0:T(8,128)(2,1)} %copy-done.14, ...), custom_call_target="tpu_custom_call" | custom-call | flops 9764339712 | bytes 4767744 | tf_op jit(solution)/shard_map/pallas_call | solution.py:158
  354.0 14.7 %shard_map.234 = (bf16[256,1664]{1,0:T(8,128)(2,1)}, bf16[256,1664]{1,0:T(8,128)(2,1)}, bf16[256,1664]{1,0:T(8,128)(2,1)}, bf16[256,1664]{1,0:T(8,128)(2,1)}, f3...) custom-call(s32[22]{0:T(128)} %stack.87.places_ref, bf16[384,1536]{1,0:T(8,128)(2,1)} %copy-done.14, ...), custom_call_target="tpu_custom_call" | custom-call | flops 9764339712 | bytes 4767744 | tf_op jit(solution)/shard_map/pallas_call | solution.py:158
  368.7 5.9 %collective-permute-done.61.refs_37_ = bf16[256,1664]{1,0:T(8,128)(2,1)S(1)} collective-permute-done((bf16[256,1664]{1,0:T(8,128)(2,1)S(1)}, bf16[256,1664]{1,0:T(8,128)(2,1)S(1)}, u32[]{:S(2)}, u32[]{:S(2)}) %collective-permute-start.61) | collective-permute-done | bytes 852000 | tf_op jit(solution)/shard_map/ppermute | solution.py:48
  380.9 22.6 %shard_map.235 = (f32[256,1536]{1,0:T(8,128)}, bf16[256,1536]{1,0:T(8,128)(2,1)}, bf16[4,48,384]{2,1,0:T(8,128)(2,1)}, bf16[4,32,384]{2,1,0:T(8,128)(2,1)}, bf16...) custom-call(s32[22]{0:T(128)} %stack.87.places_ref, ...), custom_call_target="tpu_custom_call" | custom-call | flops 19327352832 | bytes 18874368 | tf_op jit(solution)/shard_map/pallas_call | solution.py:158
  412.3 18.2 %shard_map.236 = (bf16[512,384]{1,0:T(8,128)(2,1)}, f32[1024,384]{1,0:T(8,128)}, f32[1024,384]{1,0:T(8,128)}, f32[16,384]{1,0:T(8,128)}) custom-call(s32[22]{0:T(128)} %stack.87.places_ref, bf16[384,1536]{1,0:T(8,128)(2,1)} %copy-done.13, bf16[384,1536]{1,0:T(8,128)(2,1)} %copy-done.40, bf16[384,1536]{1,0:T(8,128)(2,1)} %copy-done.41, ...), custom_call_target="tpu_custom_call" | custom-call | flops 8053063680 | bytes 3932160 | tf_op jit(solution)/shard_map/pallas_call | solution.py:158
  445.4 29.5 %shard_map.238 = (f32[16,384]{1,0:T(8,128)}, f32[16,1152]{1,0:T(8,128)}, bf16[4,32,384]{2,1,0:T(8,128)(2,1)}, bf16[256,1664]{1,0:T(8,128)(2,1)}, bf16[256,1664]{...) custom-call(s32[22]{0:T(128)} %stack.87.places_ref, bf16[384,1536]{1,0:T(8,128)(2,1)} %copy-done.13, ...), custom_call_target="tpu_custom_call" | custom-call | flops 8053063680 | bytes 3932160 | tf_op jit(solution)/shard_map/pallas_call | solution.py:158
  485.1 5.7 %shard_map.239 = (f32[16,768]{1,0:T(8,128)}, bf16[130,384]{1,0:T(8,128)(2,1)}, bf16[130,384]{1,0:T(8,128)(2,1)}, bf16[130,384]{1,0:T(8,128)(2,1)}, bf16[130,384]...) custom-call(s32[22]{0:T(128)} %stack.87.places_ref, ...), custom_call_target="tpu_custom_call" | custom-call | flops 10000000000 | bytes 1000000 | tf_op jit(solution)/shard_map/pallas_call | solution.py:158
  522.5 10.9 %collective-permute-done.91 = bf16[224,384]{1,0:T(8,128)(2,1)S(1)} collective-permute-done((bf16[224,384]{1,0:T(8,128)(2,1)S(1)}, bf16[224,384]{1,0:T(8,128)(2,1)S(1)}, u32[]{:S(2)}, u32[]{:S(2)}) %collective-permute-start.91) | collective-permute-done | bytes 172064 | tf_op jit(solution)/shard_map/ppermute | solution.py:60
  (541 shorter events, 220.0 us)
Async XLA Ops:
  24.9 42.0 %collective-permute-start.4 = (bf16[384,1536]{1,0:T(8,128)(2,1)S(1)}, bf16[384,1536]{1,0:T(8,128)(2,1)S(1)}, u32[]{:S(2)}, u32[]{:S(2)}) collective-permute-start(bf16[384,1536]{1,0:T(8,128)(2,1)S(1)} %pad_maximum_fusion.3.refs_0_), channel_id=1, source_target_pairs={{0,8},{8,0},{16,24},{24,16},{1,9},{9,1},{17,25},{25,17},{2,10},{10... | collective-permute-start | bytes 3538952 | tf_op jit(solution)/shard_map/ppermute | solution.py:48
  27.9 39.0 %collective-permute-start.5 = (bf16[384,1536]{1,0:T(8,128)(2,1)S(1)}, bf16[384,1536]{1,0:T(8,128)(2,1)S(1)}, u32[]{:S(2)}, u32[]{:S(2)}) collective-permute-start(bf16[384,1536]{1,0:T(8,128)(2,1)S(1)} %pad_maximum_fusion.3.refs_0_), channel_id=1, source_target_pairs={{0,16},{8,24},{16,0},{24,8},{1,17},{9,25},{17,1},{25,9},{2,18},{10... | collective-permute-start | bytes 3538952 | tf_op jit(solution)/shard_map/ppermute | solution.py:48
  32.2 61.0 %collective-permute-start.10 = (bf16[256,1536]{1,0:T(8,128)(2,1)}, bf16[256,1536]{1,0:T(8,128)(2,1)}, u32[]{:S(2)}, u32[]{:S(2)}) collective-permute-start(bf16[256,1536]{1,0:T(8,128)(2,1)} %collective-permute-done.6.refs_6_.refs_17_.x_ref), channel_id=1, source_target_pairs={{0,1},{1,0},{2,3},{3,2},{4,5},{5,4},{6,7},{7,6},{8,9},{9,8},{10,11... | collective-permute-start | bytes 2359304 | tf_op jit(solution)/shard_map/ppermute | solution.py:48
  44.5 48.7 %collective-permute-start.12 = (bf16[192,1536]{1,0:T(8,128)(2,1)S(1)}, bf16[192,1536]{1,0:T(8,128)(2,1)S(1)}, u32[]{:S(2)}, u32[]{:S(2)}) collective-permute-start(bf16[192,1536]{1,0:T(8,128)(2,1)S(1)} %pad_maximum_fusion.6), channel_id=1, source_target_pairs={{0,2},{2,0},{1,3},{3,1},{4,6},{6,4},{5,7},{7,5},{8,10},{10,8},{9,1... | collective-permute-start | bytes 1769480 | tf_op jit(solution)/shard_map/ppermute | solution.py:48
  102.2 35.3 %collective-permute-start.18 = (bf16[384,1536]{1,0:T(8,128)(2,1)S(1)}, bf16[384,1536]{1,0:T(8,128)(2,1)S(1)}, u32[]{:S(2)}, u32[]{:S(2)}) collective-permute-start(bf16[384,1536]{1,0:T(8,128)(2,1)S(1)} %pad_maximum_fusion.4.refs_0_), channel_id=1, source_target_pairs={{0,8},{8,0},{16,24},{24,16},{1,9},{9,1},{17,25},{25,17},{2,10},{10... | collective-permute-start | bytes 3538952 | tf_op jit(solution)/shard_map/ppermute | solution.py:48
  102.8 34.7 %collective-permute-start.19 = (bf16[384,1536]{1,0:T(8,128)(2,1)S(1)}, bf16[384,1536]{1,0:T(8,128)(2,1)S(1)}, u32[]{:S(2)}, u32[]{:S(2)}) collective-permute-start(bf16[384,1536]{1,0:T(8,128)(2,1)S(1)} %pad_maximum_fusion.4.refs_0_), channel_id=1, source_target_pairs={{0,16},{8,24},{16,0},{24,8},{1,17},{9,25},{17,1},{25,9},{2,18},{10... | collective-permute-start | bytes 3538952 | tf_op jit(solution)/shard_map/ppermute | solution.py:48
  104.2 33.2 %collective-permute-start.20 = (bf16[192,1536]{1,0:T(8,128)(2,1)S(1)}, bf16[192,1536]{1,0:T(8,128)(2,1)S(1)}, u32[]{:S(2)}, u32[]{:S(2)}) collective-permute-start(bf16[192,1536]{1,0:T(8,128)(2,1)S(1)} %copy-done.9), channel_id=1, source_target_pairs={{0,1},{1,0},{2,3},{3,2},{4,5},{5,4},{6,7},{7,6},{8,9},{9,8},{10,11... | collective-permute-start | bytes 1769480 | tf_op jit(solution)/shard_map/ppermute | solution.py:48
  104.2 33.3 %collective-permute-start.21 = (bf16[192,1536]{1,0:T(8,128)(2,1)S(1)}, bf16[192,1536]{1,0:T(8,128)(2,1)S(1)}, u32[]{:S(2)}, u32[]{:S(2)}) collective-permute-start(bf16[192,1536]{1,0:T(8,128)(2,1)S(1)} %get-tuple-element.594), channel_id=1, source_target_pairs={{0,0},{2,4},{4,2},{6,6},{1,1},{3,5},{5,3},{7,7},{8,8},{10,12},{12,... | collective-permute-start | bytes 1769480 | tf_op jit(solution)/shard_map/ppermute | solution.py:52
  104.9 32.6 %collective-permute-start.22 = (bf16[192,1536]{1,0:T(8,128)(2,1)S(1)}, bf16[192,1536]{1,0:T(8,128)(2,1)S(1)}, u32[]{:S(2)}, u32[]{:S(2)}) collective-permute-start(bf16[192,1536]{1,0:T(8,128)(2,1)S(1)} %get-tuple-element.594), channel_id=1, source_target_pairs={{0,2},{2,6},{4,0},{6,4},{1,3},{3,7},{5,1},{7,5},{8,10},{10,14},{12... | collective-permute-start | bytes 1769480 | tf_op jit(solution)/shard_map/ppermute | solution.py:56
  141.1 28.2 %collective-permute-start.24 = (bf16[384,1536]{1,0:T(8,128)(2,1)S(1)}, bf16[384,1536]{1,0:T(8,128)(2,1)}, u32[]{:S(2)}, u32[]{:S(2)}) collective-permute-start(bf16[384,1536]{1,0:T(8,128)(2,1)S(1)} %get-tuple-element.630), channel_id=1, source_target_pairs={{0,8},{8,0},{16,24},{24,16},{1,9},{9,1},{17,25},{25,17},{2,10},{10... | collective-permute-start | bytes 3538952 | tf_op jit(solution)/shard_map/ppermute | solution.py:48
  144.2 33.2 %collective-permute-start.29 = (bf16[256,1664]{1,0:T(8,128)(2,1)S(1)}, bf16[256,1664]{1,0:T(8,128)(2,1)}, u32[]{:S(2)}, u32[]{:S(2)}) collective-permute-start(bf16[256,1664]{1,0:T(8,128)(2,1)S(1)} %add_convert_fusion.3), channel_id=1, source_target_pairs={{0,1},{1,0},{2,3},{3,2},{4,5},{5,4},{6,7},{7,6},{8,9},{9,8},{10,11... | collective-permute-start | bytes 2555912 | tf_op jit(solution)/shard_map/ppermute | solution.py:48
  145.1 31.6 %collective-permute-start.30 = (bf16[192,1536]{1,0:T(8,128)(2,1)}, bf16[192,1536]{1,0:T(8,128)(2,1)}, u32[]{:S(2)}, u32[]{:S(2)}) collective-permute-start(bf16[192,1536]{1,0:T(8,128)(2,1)} %get-tuple-element.650), channel_id=1, source_target_pairs={{0,0},{2,4},{4,2},{6,6},{1,1},{3,5},{5,3},{7,7},{8,8},{10,12},{12,... | collective-permute-start | bytes 1769480 | tf_op jit(solution)/shard_map/ppermute | solution.py:52
  197.0 53.5 %collective-permute-start.47 = (bf16[384,3072]{1,0:T(8,128)(2,1)}, bf16[384,3072]{1,0:T(8,128)(2,1)S(1)}, u32[]{:S(2)}, u32[]{:S(2)}) collective-permute-start(bf16[384,3072]{1,0:T(8,128)(2,1)} %maximum_maximum_fusion.refs_0_), channel_id=1, source_target_pairs={{0,8},{8,0},{16,24},{24,16},{1,9},{9,1},{17,25},{25,17},{2,10},{10... | collective-permute-start | bytes 7077896 | tf_op jit(solution)/shard_map/ppermute | solution.py:48
  200.4 53.6 %collective-permute-start.48 = (bf16[384,3072]{1,0:T(8,128)(2,1)}, bf16[384,3072]{1,0:T(8,128)(2,1)}, u32[]{:S(2)}, u32[]{:S(2)}) collective-permute-start(bf16[384,3072]{1,0:T(8,128)(2,1)} %maximum_maximum_fusion.refs_0_), channel_id=1, source_target_pairs={{0,16},{8,24},{16,0},{24,8},{1,17},{9,25},{17,1},{25,9},{2,18},{10... | collective-permute-start | bytes 7077896 | tf_op jit(solution)/shard_map/ppermute | solution.py:48
  234.9 28.1 %collective-permute-start.43 = (bf16[256,1536]{1,0:T(8,128)(2,1)S(1)}, bf16[256,1536]{1,0:T(8,128)(2,1)S(1)}, u32[]{:S(2)}, u32[]{:S(2)}) collective-permute-start(bf16[256,1536]{1,0:T(8,128)(2,1)S(1)} %copy-done.80), channel_id=1, source_target_pairs={{0,1},{1,0},{2,3},{3,2},{4,5},{5,4},{6,7},{7,6},{8,9},{9,8},{10,11... | collective-permute-start | bytes 2359304 | tf_op jit(solution)/shard_map/ppermute | solution.py:48
  235.1 27.9 %collective-permute-start.46 = (bf16[256,1536]{1,0:T(8,128)(2,1)S(1)}, bf16[256,1536]{1,0:T(8,128)(2,1)S(1)}, u32[]{:S(2)}, u32[]{:S(2)}) collective-permute-start(bf16[256,1536]{1,0:T(8,128)(2,1)S(1)} %bitcast.281), channel_id=1, source_target_pairs={{0,0},{2,4},{4,2},{6,6},{1,1},{3,5},{5,3},{7,7},{8,8},{10,12},{12,... | collective-permute-start | bytes 2359304 | tf_op jit(solution)/shard_map/ppermute | solution.py:52
  255.4 29.0 %collective-permute-start.53 = (bf16[192,3072]{1,0:T(8,128)(2,1)S(1)}, bf16[192,3072]{1,0:T(8,128)(2,1)S(1)}, u32[]{:S(2)}, u32[]{:S(2)}) collective-permute-start(bf16[192,3072]{1,0:T(8,128)(2,1)S(1)} %slice.442), channel_id=1, source_target_pairs={{0,8},{8,0},{16,24},{24,16},{1,9},{9,1},{17,25},{25,17},{2,10},{10... | collective-permute-start | bytes 3538952 | tf_op jit(solution)/shard_map/ppermute | solution.py:48
  257.0 29.0 %collective-permute-start.54 = (bf16[192,3072]{1,0:T(8,128)(2,1)S(1)}, bf16[192,3072]{1,0:T(8,128)(2,1)S(1)}, u32[]{:S(2)}, u32[]{:S(2)}) collective-permute-start(bf16[192,3072]{1,0:T(8,128)(2,1)S(1)} %slice.443), channel_id=1, source_target_pairs={{0,16},{8,24},{16,0},{24,8},{1,17},{9,25},{17,1},{25,9},{2,18},{10... | collective-permute-start | bytes 3538952 | tf_op jit(solution)/shard_map/ppermute | solution.py:48
  263.6 44.3 %collective-permute-start.50 = (bf16[384,1536]{1,0:T(8,128)(2,1)S(1)}, bf16[384,1536]{1,0:T(8,128)(2,1)S(1)}, u32[]{:S(2)}, u32[]{:S(2)}) collective-permute-start(bf16[384,1536]{1,0:T(8,128)(2,1)S(1)} %pad_maximum_fusion.5.refs_0_), channel_id=1, source_target_pairs={{0,8},{8,0},{16,24},{24,16},{1,9},{9,1},{17,25},{25,17},{2,10},{10... | collective-permute-start | bytes 3538952 | tf_op jit(solution)/shard_map/ppermute | solution.py:48
  265.8 43.4 %collective-permute-start.51 = (bf16[384,1536]{1,0:T(8,128)(2,1)S(1)}, bf16[384,1536]{1,0:T(8,128)(2,1)S(1)}, u32[]{:S(2)}, u32[]{:S(2)}) collective-permute-start(bf16[384,1536]{1,0:T(8,128)(2,1)S(1)} %pad_maximum_fusion.5.refs_0_), channel_id=1, source_target_pairs={{0,16},{8,24},{16,0},{24,8},{1,17},{9,25},{17,1},{25,9},{2,18},{10... | collective-permute-start | bytes 3538952 | tf_op jit(solution)/shard_map/ppermute | solution.py:48
  266.5 42.8 %collective-permute-start.52 = (bf16[256,1536]{1,0:T(8,128)(2,1)S(1)}, bf16[256,1536]{1,0:T(8,128)(2,1)}, u32[]{:S(2)}, u32[]{:S(2)}) collective-permute-start(bf16[256,1536]{1,0:T(8,128)(2,1)S(1)} %collective-permute-done.46.refs_8_.refs_17_.g_ref), channel_id=1, source_target_pairs={{0,1},{1,0},{2,3},{3,2},{4,5},{5,4},{6,7},{7,6},{8,9},{9,8},{10,11... | collective-permute-start | bytes 2359304 | tf_op jit(solution)/shard_map/ppermute | solution.py:48
  438.7 36.2 %collective-permute-start.77 = (bf16[256,1536]{1,0:T(8,128)(2,1)}, bf16[256,1536]{1,0:T(8,128)(2,1)S(1)}, u32[]{:S(2)}, u32[]{:S(2)}) collective-permute-start(bf16[256,1536]{1,0:T(8,128)(2,1)} %get-tuple-element.907), channel_id=1, source_target_pairs={{0,0},{2,4},{4,2},{6,6},{1,1},{3,5},{5,3},{7,7},{8,8},{10,12},{12,... | collective-permute-start | bytes 2359304 | tf_op jit(solution)/shard_map/ppermute | solution.py:52
  440.5 34.4 %collective-permute-start.75 = (bf16[240,384]{1,0:T(8,128)(2,1)S(1)}, bf16[240,384]{1,0:T(8,128)(2,1)S(1)}, u32[]{:S(2)}, u32[]{:S(2)}) collective-permute-start(bf16[240,384]{1,0:T(8,128)(2,1)S(1)} %bitcast.266), channel_id=1, source_target_pairs={{0,0},{2,4},{4,2},{6,6},{1,1},{3,5},{5,3},{7,7},{8,8},{10,12},{12,... | collective-permute-start | bytes 552968 | tf_op jit(solution)/shard_map/ppermute | solution.py:52
  441.2 33.7 %collective-permute-start.76 = (bf16[240,384]{1,0:T(8,128)(2,1)S(1)}, bf16[240,384]{1,0:T(8,128)(2,1)S(1)}, u32[]{:S(2)}, u32[]{:S(2)}) collective-permute-start(bf16[240,384]{1,0:T(8,128)(2,1)S(1)} %bitcast.267), channel_id=1, source_target_pairs={{0,4},{2,0},{4,6},{6,2},{1,5},{3,1},{5,7},{7,3},{8,12},{10,8},{12,... | collective-permute-start | bytes 552968 | tf_op jit(solution)/shard_map/ppermute | solution.py:60
  (174 other events, 1885.0 us)
